TPU v7x, 32 devices: a whole 2x2x4 slice. The times are simulated.
32 devices in a mesh: group: 4 (over x, core), sub: 8 (over z, y).
Axes of the slice: x: 2, y: 2, z: 4, core: 2. Of those that a mesh axis runs over, the one named last changes fastest.
Arguments:
- users: float32 [32768, 512], P(('group', 'sub')), may hold values from -1.2 to 1.2
- items: float32 [2048, 512], P(('group', 'sub')), may hold values from -1.2 to 1.2
- ratings: bfloat16 [4, 32768, 512], P(None, ('group', 'sub')), may hold values from -5 to 5
- occupancy: int32 [4, 256, 4], P(None, ('group', 'sub')), may hold values 0 or 1
Outputs:
- users_out: float32 [32768, 512], P(('group', 'sub'))
- items_out: float32 [2048, 512], P(('group', 'sub'))
All inputs are finite; a program needn't handle non-finite values. No bound on the sum of `occupancy` on one device may be relied on, other than what follows from the above.
Results may differ from a plain program's by a relative error of at most 0.0003.
Values sent between devices are 32-bit elements; how exact they have to be, the bound alone decides.
No kernel may reach another device: no remote copies, remote signals or barrier semaphores. Data moves between devices by JAX's collectives and lax.ppermute only.
A program may use at most 64 MiB of HBM per device.

v0:
```python
import jax
import jax.numpy as jnp
from jax import lax
from jax.sharding import PartitionSpec as P

TILE = 128
STRATA = 4


def passed_along(block, axis, distance):
    devices = range(lax.axis_size(axis))
    route = [((i - distance) % len(devices), i) for i in devices]
    return lax.ppermute(block, axis, route)


def expand_mask(occ, rows, cols):
    tiles = occ.astype(jnp.float32)[:, None, :, None]
    tiles = jnp.broadcast_to(tiles, (rows // TILE, TILE, cols // TILE, TILE))
    return tiles.reshape(rows, cols)


def errors(user_rows, block, rate, occ):
    pred = lax.dot_general(
        user_rows,
        block,
        (((1,), (1,)), ((), ())),
        precision=lax.Precision.HIGHEST,
        preferred_element_type=jnp.float32,
    )
    mask = expand_mask(occ, user_rows.shape[0], block.shape[0])
    return mask * (rate.astype(jnp.float32) - pred)


def user_step(user_rows, block, err):
    pull = jnp.dot(err, block, precision=lax.Precision.HIGHEST, preferred_element_type=jnp.float32)
    return user_rows + 0.02 * (pull - 0.05 * user_rows)


def item_term(err, user_rows):
    return lax.dot_general(
        err,
        user_rows,
        (((0,), (0,)), ((), ())),
        precision=lax.Precision.HIGHEST,
        preferred_element_type=jnp.float32,
    )


def per_device(users, items, ratings, occupancy):
    share_rows = items.shape[0]
    block = lax.all_gather(items, "sub", axis=0, tiled=True)
    for section in range(STRATA):
        err = errors(users, block, ratings[section], occupancy[section])
        new_users = user_step(users, block, err)
        total = lax.psum(item_term(err, users), "sub")
        block = block + 0.005 * (total - 0.05 * block)
        block = passed_along(block, "group", 1)
        users = new_users
    shard = lax.dynamic_slice_in_dim(block, lax.axis_index("sub") * share_rows, share_rows, 0)
    return (users, shard)


def solution(mesh):
    return jax.shard_map(
        per_device,
        mesh=mesh,
        in_specs=(
            P(("group", "sub"), None),
            P(("group", "sub"), None),
            P(None, ("group", "sub"), None),
            P(None, ("group", "sub"), None),
        ),
        out_specs=(P(("group", "sub"), None), P(("group", "sub"), None)),
        check_vma=False,
    )
```

profile of v0, /device:TPU:0, one launch (start us, length us, event | category | flops | bytes accessed | tf_op | source)
XLA Modules:
  0.0 485.3 jit_solution(10683281102510726278)
XLA Ops:
  8.8 44.2 %all-gather.2.cloned.1.call-done = f32[512,512]{1,0:T(8,128)} async-done(((f32[64,512]{1,0:T(8,128)}), f32[512,512]{1,0:T(8,128)}) %all-gather.2.cloned.1.call-update) | async-done | bytes 1048592 | tf_op jit(solution)/shard_map/all_gather | solution.py:51
  53.4 5.1 %bitcast_multiply_fusion.3 = f32[1024,512]{1,0:T(8,128)S(1)} fusion(f32[128,8,4,128]{3,2,1,0:T(4,128)S(1)} %bitcast.60, f32[1024,512]{1,0:T(8,128)S(1)} %copy-done.1, f32[512,512]{1,0:T(8,128)} %all-gather.2.cloned.1.call-done, bf16[4,1024,512]{2,1,0:T(8,128)(2,1)} %param.6), kind=kOutput, calls=%fused_computation.3 | convolution fusion | flops 3222798336 | bytes 8388608 | tf_op jit(solution)/shard_map/dot_general | solution.py:23
  59.8 4.6 fusion
  64.4 76.9 %all-reduce.5.cloned.1.call-done = f32[512,512]{1,0:T(8,128)} async-done(((f32[512,512]{1,0:T(8,128)}), f32[512,512]{1,0:T(8,128)}) %all-reduce.5.cloned.1.call-update) | async-done | bytes 1048592 | tf_op jit(solution)/shard_map/psum | solution.py:55
  141.3 2.4 multiply_add_fusion.7
  144.0 5.8 %multiply_add_fusion.3 = f32[1024,512]{1,0:T(8,128)S(1)} fusion(f32[1024,512]{1,0:T(8,128)} %param.4, f32[1024,512]{1,0:T(8,128)} %copy-done.5, f32[512,512]{1,0:T(8,128)S(1)} %copy-done.6), kind=kOutput, calls=%fused_computation.11 | convolution fusion | flops 3223322624 | bytes 7340032 | tf_op jit(solution)/shard_map/dot_general | solution.py:35
  149.8 8.7 %collective-permute-done = f32[512,512]{1,0:T(8,128)} collective-permute-done((f32[512,512]{1,0:T(8,128)}, f32[512,512]{1,0:T(8,128)}, u32[]{:S(2)}, u32[]{:S(2)}) %collective-permute-start) | collective-permute-done | bytes 1048608 | tf_op jit(solution)/shard_map/ppermute | solution.py:13
  158.8 5.1 %bitcast_multiply_fusion.2 = f32[1024,512]{1,0:T(8,128)S(1)} fusion(f32[128,8,4,128]{3,2,1,0:T(4,128)S(1)} %bitcast.61, f32[1024,512]{1,0:T(8,128)S(1)} %multiply_add_fusion.3, f32[512,512]{1,0:T(8,128)} %collective-permute-done, bf16[4,1024,512]{2,1,0:T(8,128)(2,1)} %param.6), kind=kOutput, calls=%fused_computation.2 | convolution fusion | flops 3222798336 | bytes 8388608 | tf_op jit(solution)/shard_map/dot_general | solution.py:23
  165.1 4.6 fusion.1
  169.8 77.7 %all-reduce.7.cloned.1.call-done = f32[512,512]{1,0:T(8,128)} async-done(((f32[512,512]{1,0:T(8,128)}), f32[512,512]{1,0:T(8,128)}) %all-reduce.7.cloned.1.call-update) | async-done | bytes 1048592 | tf_op jit(solution)/shard_map/psum | solution.py:55
  247.5 2.8 multiply_add_fusion.6
  250.5 5.4 %multiply_add_fusion.2 = f32[1024,512]{1,0:T(8,128)S(1)} fusion(f32[1024,512]{1,0:T(8,128)S(1)} %multiply_add_fusion.3, f32[1024,512]{1,0:T(8,128)} %copy-done.4, f32[512,512]{1,0:T(8,128)} %collective-permute-done), kind=kOutput, calls=%fused_computation.10 | convolution fusion | flops 3223322624 | bytes 7340032 | tf_op jit(solution)/shard_map/dot_general | solution.py:35
  256.0 8.9 %collective-permute-done.1 = f32[512,512]{1,0:T(8,128)S(1)} collective-permute-done((f32[512,512]{1,0:T(8,128)}, f32[512,512]{1,0:T(8,128)S(1)}, u32[]{:S(2)}, u32[]{:S(2)}) %collective-permute-start.1) | collective-permute-done | bytes 1048608 | tf_op jit(solution)/shard_map/ppermute | solution.py:13
  265.2 4.8 bitcast_multiply_fusion.1
  271.4 4.6 fusion.2
  276.0 77.8 %all-reduce.9.cloned.1.call-done = f32[512,512]{1,0:T(8,128)} async-done(((f32[512,512]{1,0:T(8,128)}), f32[512,512]{1,0:T(8,128)}) %all-reduce.9.cloned.1.call-update) | async-done | bytes 1048592 | tf_op jit(solution)/shard_map/psum | solution.py:55
  353.8 2.5 multiply_add_fusion.5
  356.8 6.1 %multiply_add_fusion.1 = f32[1024,512]{1,0:T(8,128)S(1)} fusion(f32[1024,512]{1,0:T(8,128)} %copy-done, f32[1024,512]{1,0:T(8,128)} %copy-done.3, f32[512,512]{1,0:T(8,128)} %copy-done.7), kind=kOutput, calls=%fused_computation.9 | convolution fusion | flops 3223322624 | bytes 7340032 | tf_op jit(solution)/shard_map/dot_general | solution.py:35
  362.9 8.2 %collective-permute-done.2 = f32[512,512]{1,0:T(8,128)S(1)} collective-permute-done((f32[512,512]{1,0:T(8,128)}, f32[512,512]{1,0:T(8,128)S(1)}, u32[]{:S(2)}, u32[]{:S(2)}) %collective-permute-start.2) | collective-permute-done | bytes 1048608 | tf_op jit(solution)/shard_map/ppermute | solution.py:13
  371.5 4.8 bitcast_multiply_fusion
  377.6 4.6 fusion.3
  382.2 77.7 %all-reduce.11.cloned.1.call-done = f32[512,512]{1,0:T(8,128)} async-done(((f32[512,512]{1,0:T(8,128)}), f32[512,512]{1,0:T(8,128)}) %all-reduce.11.cloned.1.call-update) | async-done | bytes 1048592 | tf_op jit(solution)/shard_map/psum | solution.py:55
  462.5 6.5 %multiply_add_fusion = f32[1024,512]{1,0:T(8,128)} fusion(f32[1024,512]{1,0:T(8,128)S(1)} %multiply_add_fusion.1, f32[1024,512]{1,0:T(8,128)} %copy-done.2, f32[512,512]{1,0:T(8,128)S(1)} %collective-permute-done.2), kind=kOutput, calls=%fused_computation.8 | convolution fusion | flops 3223322624 | bytes 7340032 | tf_op jit(solution)/shard_map/dot_general | solution.py:35
  469.0 8.0 %collective-permute-done.3 = f32[512,512]{1,0:T(8,128)} collective-permute-done((f32[512,512]{1,0:T(8,128)}, f32[512,512]{1,0:T(8,128)}, u32[]{:S(2)}, u32[]{:S(2)}) %collective-permute-start.3) | collective-permute-done | bytes 1048608 | tf_op jit(solution)/shard_map/ppermute | solution.py:13
  (41 shorter events, 13.5 us)
Async XLA Ops:
  7.2 46.2 %copy-start.1 = (f32[1024,512]{1,0:T(8,128)S(1)}, f32[1024,512]{1,0:T(8,128)}, u32[]{:S(2)}) copy-start(f32[1024,512]{1,0:T(8,128)} %param.4) | copy-start | bytes 6291460
  7.2 45.8 %all-gather.2.cloned.1.call-start = ((), (), s32[]{:S(2)}) async-start(), calls=%async_computation | async-start | bytes 1179648 | tf_op jit(solution)/shard_map/all_gather | solution.py:51
  7.9 133.4 %all-reduce.5.cloned.1.call-start = ((), (), s32[]{:S(2)}) async-start(), calls=%async_computation.1 | async-start | bytes 2097152 | tf_op jit(solution)/shard_map/psum | solution.py:55
  58.4 1.3 copy-start.5
  59.8 81.5 %copy-start.6 = (f32[512,512]{1,0:T(8,128)S(1)}, f32[512,512]{1,0:T(8,128)}, u32[]{:S(2)}) copy-start(f32[512,512]{1,0:T(8,128)} %all-gather.2.cloned.1.call-done) | copy-start | bytes 3145732
  64.4 183.1 %all-reduce.7.cloned.1.call-start = ((), (), s32[]{:S(2)}) async-start(), calls=%async_computation.2 | async-start | bytes 2097152 | tf_op jit(solution)/shard_map/psum | solution.py:55
  143.7 14.7 %collective-permute-start = (f32[512,512]{1,0:T(8,128)}, f32[512,512]{1,0:T(8,128)}, u32[]{:S(2)}, u32[]{:S(2)}) collective-permute-start(f32[512,512]{1,0:T(8,128)} %multiply_add_fusion.7), channel_id=1, source_target_pairs={{24,0},{0,8},{8,16},{16,24},{25,1},{1,9},{9,17},{17,25},{26,2},{2,... | collective-permute-start | bytes 3145736 | tf_op jit(solution)/shard_map/ppermute | solution.py:13
  163.8 1.3 copy-start.4
  169.7 184.1 %all-reduce.9.cloned.1.call-start = ((), (), s32[]{:S(2)}) async-start(), calls=%async_computation.3 | async-start | bytes 2097152 | tf_op jit(solution)/shard_map/psum | solution.py:55
  250.3 14.6 %collective-permute-start.1 = (f32[512,512]{1,0:T(8,128)}, f32[512,512]{1,0:T(8,128)S(1)}, u32[]{:S(2)}, u32[]{:S(2)}) collective-permute-start(f32[512,512]{1,0:T(8,128)} %multiply_add_fusion.6), channel_id=1, source_target_pairs={{24,0},{0,8},{8,16},{16,24},{25,1},{1,9},{9,17},{17,25},{26,2},{2,... | collective-permute-start | bytes 3145736 | tf_op jit(solution)/shard_map/ppermute | solution.py:13
  256.0 14.0 %copy-start = (f32[1024,512]{1,0:T(8,128)}, f32[1024,512]{1,0:T(8,128)S(1)}, u32[]{:S(2)}) copy-start(f32[1024,512]{1,0:T(8,128)S(1)} %multiply_add_fusion.2) | copy-start | bytes 6291460
  264.9 88.9 %copy-start.7 = (f32[512,512]{1,0:T(8,128)}, f32[512,512]{1,0:T(8,128)S(1)}, u32[]{:S(2)}) copy-start(f32[512,512]{1,0:T(8,128)S(1)} %collective-permute-done.1) | copy-start | bytes 3145732
  270.0 1.3 copy-start.3
  276.0 183.9 %all-reduce.11.cloned.1.call-start = ((), (), s32[]{:S(2)}) async-start(), calls=%async_computation.4 | async-start | bytes 2097152 | tf_op jit(solution)/shard_map/psum | solution.py:55
  356.3 14.8 %collective-permute-start.2 = (f32[512,512]{1,0:T(8,128)}, f32[512,512]{1,0:T(8,128)S(1)}, u32[]{:S(2)}, u32[]{:S(2)}) collective-permute-start(f32[512,512]{1,0:T(8,128)} %multiply_add_fusion.5), channel_id=1, source_target_pairs={{24,0},{0,8},{8,16},{16,24},{25,1},{1,9},{9,17},{17,25},{26,2},{2,... | collective-permute-start | bytes 3145736 | tf_op jit(solution)/shard_map/ppermute | solution.py:13
  376.2 1.3 copy-start.2
  462.4 14.7 %collective-permute-start.3 = (f32[512,512]{1,0:T(8,128)}, f32[512,512]{1,0:T(8,128)}, u32[]{:S(2)}, u32[]{:S(2)}) collective-permute-start(f32[512,512]{1,0:T(8,128)} %multiply_add_fusion.4), channel_id=1, source_target_pairs={{24,0},{0,8},{8,16},{16,24},{25,1},{1,9},{9,17},{17,25},{26,2},{2,... | collective-permute-start | bytes 3145736 | tf_op jit(solution)/shard_map/ppermute | solution.py:13
Sparse Core Ops, SparseCore 0:
  10.1 42.8 all-gather.1
  64.5 76.7 all-reduce.4
  169.9 77.5 all-reduce.6
  276.1 77.6 all-reduce.8
  382.3 77.5 all-reduce.10
where the time goes:
time: 492 us; the launch traced here: 485 us
  waiting for transfers between devices  389 us (79%)
  matrix products  61.8 us (13%)
  between operations  14.2 us (3%)
  other arithmetic  10.9 us (2%)
  local copies, waits for them, and re-layouts  8.52 us (2%)
    psum x4, waiting for transfers between devices, per_device(): total = lax.psum(item_term(err, users), 'sub')  310 us
    all_gather x1, waiting for transfers between devices, per_device(): block = lax.all_gather(items, 'sub', axis=0, tiled=True)  44.2 us
    ppermute x4, waiting for transfers between devices, passed_along(): return lax.ppermute(block, axis, route)  33.8 us
    dot_general x4, matrix products, user_step(): jnp.dot(err, block, precision=lax.Precision.HIGHEST, preferred_element_ty...  23.8 us
    dot_general x4, matrix products, errors(): lax.dot_general(user_rows, block, (((1,), (1,)), ((), ())), precision=lax...  19.6 us
    dot_general x4, matrix products, item_term(): lax.dot_general(err, user_rows, (((0,), (0,)), ((), ())), precision=lax.P...  18.4 us
    add x4, other arithmetic, per_device(): block = block + 0.005 * (total - 0.05 * block)  10.1 us
  transfers between devices with their start and end apart: 9, of which 9 were waited for; matrix products, arithmetic and copies ran while one was open for 5% of the time, Pallas kernels for 0%

commit v1 on v0

v1 whole, which is shorter than its diff:
```python
import functools

import jax
import jax.numpy as jnp
from jax import lax
from jax.experimental import pallas as pl
from jax.experimental.pallas import tpu as pltpu
from jax.sharding import PartitionSpec as P

TILE = 128
CHUNKS = 2
BLOCK = 256
ANY = pl.BlockSpec(memory_space=pltpu.VMEM)
SMEM = pl.BlockSpec(memory_space=pltpu.SMEM)
F32 = jnp.float32
BF16 = jnp.bfloat16


def split(x):
    hi = x.astype(BF16)
    return hi, (x - hi.astype(F32)).astype(BF16)


def dot3(a, b, dims):
    (ah, al), (bh, bl) = a, b
    dot = functools.partial(lax.dot_general, dimension_numbers=(dims, ((), ())), preferred_element_type=F32)
    return dot(ah, bh) + (dot(ah, bl) + dot(al, bh))


def params(mib):
    return pltpu.CompilerParams(vmem_limit_bytes=mib * 1024 * 1024)


def grad_kernel(ny, first_tile, stratum, out_q, *refs):
    where, occ, users, rate = refs[:4]
    pieces = refs[4:4 + ny]
    err_hi, err_lo, v_hi, v_lo = refs[4 + ny:8 + ny]
    grads = refs[8 + ny:8 + 2 * ny]
    block, total = refs[8 + 2 * ny:]
    step = pl.program_id(0)
    mine = where[0]
    rows, rank = total.shape

    @pl.when(step == 0)
    def _():
        for r in range(ny):
            block[:, mine ^ r] = pieces[r][...]
        hi, lo = split(block[...].reshape(rows, rank))
        v_hi[...] = hi
        v_lo[...] = lo

    u = split(users[...])
    pred = dot3(u, (v_hi[...], v_lo[...]), ((1,), (1,)))
    err = rate[...].reshape(pred.shape).astype(F32) - pred
    tiles = err.shape[0] // TILE
    parts = []
    for a in range(tiles):
        line = []
        for b in range(rows // TILE):
            seen = occ[stratum, step * tiles + a, first_tile + b]
            part = err[a * TILE:(a + 1) * TILE, b * TILE:(b + 1) * TILE]
            line.append(jnp.where(seen == 1, part, 0.0))
        parts.append(jnp.concatenate(line, axis=1))
    e = split(jnp.concatenate(parts, axis=0))
    err_hi[...], err_lo[...] = e
    term = dot3(e, u, ((0,), (0,)))

    @pl.when(step == 0)
    def _():
        total[...] = term

    @pl.when(step > 0)
    def _():
        total[...] += term

    @pl.when(step == pl.num_programs(0) - 1)
    def _():
        block[...] = total[...].reshape(block.shape)
        view = block if out_q == block.shape[2] else None
        if view is not None:
            for r in range(ny):
                grads[r][...] = block[:, mine ^ r]
        else:
            whole = total[...].reshape(-1, ny, out_q, rank)
            for r in range(ny):
                for y in range(ny):
                    @pl.when((mine ^ r) == y)
                    def _():
                        grads[r][...] = whole[:, y]


def gradients(where, occ, users, ratings, pieces, stratum, chunk, out_q):
    ny = len(pieces)
    nz, q, rank = pieces[0].shape
    rows = nz * ny * q
    n_users = users.shape[0]
    full = lambda shape: pl.BlockSpec(shape, lambda i: (0,) * len(shape))
    gshape = (rows // (ny * out_q), out_q, rank)
    return pl.pallas_call(
        functools.partial(grad_kernel, ny, chunk * rows // TILE, stratum, out_q),
        grid=(n_users // BLOCK,),
        in_specs=[SMEM, SMEM, pl.BlockSpec((BLOCK, rank), lambda i: (i, 0)),
                  pl.BlockSpec((1, BLOCK, rows), lambda i: (stratum, i, chunk))] + [full(p.shape) for p in pieces],
        out_specs=[pl.BlockSpec((BLOCK, rows), lambda i: (i, 0))] * 2 + [full((rows, rank))] * 2 + [full(gshape)] * ny,
        out_shape=[jax.ShapeDtypeStruct((n_users, rows), BF16)] * 2 + [jax.ShapeDtypeStruct((rows, rank), BF16)] * 2
        + [jax.ShapeDtypeStruct(gshape, F32)] * ny,
        scratch_shapes=[pltpu.VMEM((nz, ny, q, rank), F32), pltpu.VMEM((rows, rank), F32)],
        compiler_params=params(28),
        cost_estimate=pl.CostEstimate(flops=12 * n_users * rows * rank, bytes_accessed=4 * n_users * rank, transcendentals=0),
        name="gradients",
    )(where, occ, users, ratings, *pieces)


def step_kernel(n, *refs):
    users, out = refs[0], refs[-1]
    pull = None
    for i in range(n):
        eh, el, vh, vl = refs[1 + 4 * i:5 + 4 * i]
        part = dot3((eh[...], el[...]), (vh[...], vl[...]), ((1,), (0,)))
        pull = part if pull is None else pull + part
    u = users[...]
    out[...] = u + 0.02 * (pull - 0.05 * u)


def user_step(users, parts):
    n_users, rank = users.shape
    specs, flat = [], []
    for eh, el, vh, vl in parts:
        flat += [eh, el, vh, vl]
        specs += [pl.BlockSpec((BLOCK, eh.shape[1]), lambda i: (i, 0))] * 2 + [pl.BlockSpec(vh.shape, lambda i: (0, 0))] * 2
    rows = sum(p[2].shape[0] for p in parts)
    own = pl.BlockSpec((BLOCK, rank), lambda i: (i, 0))
    return pl.pallas_call(
        functools.partial(step_kernel, len(parts)),
        grid=(n_users // BLOCK,),
        in_specs=[own] + specs,
        out_specs=own,
        out_shape=jax.ShapeDtypeStruct(users.shape, F32),
        compiler_params=params(28),
        cost_estimate=pl.CostEstimate(flops=6 * n_users * rows * rank, bytes_accessed=8 * n_users * rank, transcendentals=0),
        name="user_step",
    )(users, *flat)


def cut_kernel(ny, nz, *refs):
    where = refs[0]
    terms, outs = refs[1:1 + ny], refs[1 + ny:]
    z = where[1]
    for r in range(nz):
        total = terms[0][z ^ r]
        for t in terms[1:]:
            total = total + t[z ^ r]
        outs[r][...] = total


def cut(where, terms):
    nz, q, rank = terms[0].shape
    return pl.pallas_call(
        functools.partial(cut_kernel, len(terms), nz),
        in_specs=[SMEM] + [ANY] * len(terms),
        out_specs=[ANY] * nz,
        out_shape=[jax.ShapeDtypeStruct((q, rank), F32)] * nz,
        compiler_params=params(8),
        name="cut",
    )(where, *terms)


def join_kernel(nz, *refs):
    where, pieces, out = refs[0], refs[1:-1], refs[-1]
    for r in range(nz):
        out[where[1] ^ r] = pieces[r][...]


def join(where, pieces):
    nz = len(pieces)
    return pl.pallas_call(
        functools.partial(join_kernel, nz),
        in_specs=[SMEM] + [ANY] * nz,
        out_specs=ANY,
        out_shape=jax.ShapeDtypeStruct((nz,) + pieces[0].shape, F32),
        compiler_params=params(8),
        name="join",
    )(where, *pieces)


def new_rows(old, terms):
    total = functools.reduce(jnp.add, terms)
    return old + 0.005 * (total - 0.05 * old)


def per_device(n_group, n_sub, users, items, ratings, occupancy):
    strata = ratings.shape[0]
    share, rank = items.shape
    ny = 1
    while ny * ny * 2 <= n_sub:
        ny *= 2
    nz = n_sub // ny
    chunks = max(1, min(CHUNKS, share // 16))
    k = lax.axis_index("sub")
    where = jnp.stack([k % ny, k // ny]).astype(jnp.int32)

    def over_y(x, r):
        return lax.ppermute(x, "sub", [(i, i ^ r) for i in range(n_sub)])

    def over_z(x, r):
        return lax.ppermute(x, "sub", [(i, i ^ (r * ny)) for i in range(n_sub)])

    def onward(x, r):
        route = []
        for g in range(n_group):
            for i in range(n_sub):
                route.append((g * n_sub + i, (g + 1) % n_group * n_sub + (i ^ (r * ny))))
        return lax.ppermute(x, ("group", "sub"), route)

    q = share // chunks
    own = join(where, [items] + [over_z(items, r) for r in range(1, nz)])
    owns = [own] + [over_y(own, r) for r in range(1, ny)]
    if chunks == 1:
        pieces = [owns]
        olds = [items]
    else:
        order = jnp.stack([owns[r] for r in range(ny)])
        order = order if ny == 1 else jnp.take(order, jnp.arange(ny) ^ where[0], axis=0)
        block = order.transpose(1, 0, 2, 3).reshape(chunks, nz, ny, q, rank)
        pieces = [[jnp.take(block[c], where[0] ^ r, axis=1) for r in range(ny)] for c in range(chunks)]
        olds = [jnp.take(pieces[c][0], where[1], axis=0) for c in range(chunks)]

    for s in range(strata):
        last = s == strata - 1
        parts, grads = [], []
        for c in range(chunks):
            res = gradients(where, occupancy, users, ratings, pieces[c], s, c, share if last else q)
            parts.append(res[:4])
            grads.append([res[4]] + [over_y(res[4 + r], r) for r in range(1, ny)])
        new_users = user_step(users, parts)
        if last:
            terms = [jnp.concatenate([g[r] for g in grads]) if chunks > 1 else grads[0][r] for r in range(ny)]
            cuts = cut(where, terms)
            old = olds[0]
            if chunks > 1:
                mine = [jnp.take(v, where[0], axis=1) for v in lasts(pieces, where, share)]
                old = jnp.take(jnp.concatenate(mine), where[1], axis=0)
            rows = new_rows(old, [cuts[0]] + [over_z(cuts[r], r) for r in range(1, nz)])
            rows = lax.ppermute(rows, "group", [(g, (g + 1) % n_group) for g in range(n_group)])
            return new_users, rows
        for c in range(chunks):
            cuts = cut(where, grads[c])
            rows = new_rows(olds[c], [cuts[0]] + [over_z(cuts[r], r) for r in range(1, nz)])
            moved = [onward(rows, r) for r in range(nz)]
            olds[c] = moved[0]
            own = join(where, moved)
            pieces[c] = [own] + [over_y(own, r) for r in range(1, ny)]
        users = new_users


def lasts(pieces, where, share):
    out = []
    for p in pieces:
        ny = len(p)
        nz, q, rank = p[0].shape
        order = jnp.take(jnp.stack(p), jnp.arange(ny) ^ where[0], axis=0)
        out.append(order.transpose(1, 0, 2, 3).reshape(-1, ny, share, rank))
    return out


def solution(mesh):
    spec = P(("group", "sub"), None)
    third = P(None, ("group", "sub"), None)
    return jax.shard_map(
        functools.partial(per_device, mesh.shape["group"], mesh.shape["sub"]),
        mesh=mesh,
        in_specs=(spec, spec, third, third),
        out_specs=(spec, spec),
        check_vma=False,
    )
```

time: 492 us -> 227 us (0.46); the launches traced: 485 us -> 227 us
  waiting for transfers between devices: 389 us -> 41.4 us
  starting transfers between devices: 1.1 us -> 85.8 us
  Pallas kernels: 0 us -> 69.7 us
  matrix products: 61.8 us -> 0 us
  between operations: 14.2 us -> 1.34 us
  local copies, waits for them, and re-layouts: 8.52 us -> 21 us
    psum x4 -> x0, waiting for transfers between devices: 310 us -> none  [per_device(): total = lax.psum(item_term(err, users), 'sub')]
    ppermute x4 -> x66, starting transfers between devices: 0.9 us -> 85.8 us  [the longest x45 53.6 us: over_y(): return lax.ppermute(x, 'sub', [(i, i ^ r) for i in range(n_sub)])]
    pallas_call x0 -> x26, Pallas kernels: none -> 69.7 us  [the longest x8 50.3 us: gradients(): pl.pallas_call(functools.partial(grad_kernel, ny, chunk * rows // TILE, s...]
    dot_general x12 -> x0, matrix products: 61.8 us -> none  [the longest x4 23.8 us: user_step(): jnp.dot(err, block, precision=lax.Precision.HIGHEST, preferred_element_ty...]
    all_gather x1 -> x0, waiting for transfers between devices: 44.2 us -> none  [per_device(): block = lax.all_gather(items, 'sub', axis=0, tiled=True)]
    add x4 -> x7, other arithmetic: 10.1 us -> 1.01 us  [new_rows(): return old + 0.005 * (total - 0.05 * old)]
    unnamed x16 -> x68, local copies, waits for them, and re-layouts: 5.29 us -> 14 us
    ppermute x4 -> x66, waiting for transfers between devices: 33.8 us -> 41.4 us  [the longest x45 20.9 us: over_y(): return lax.ppermute(x, 'sub', [(i, i ^ r) for i in range(n_sub)])]
  transfers between devices with their start and end apart: 9 -> 66, of which waited for: 9 -> 19; matrix products, arithmetic and copies ran while one was open for 5% -> 5% of each run, Pallas kernels for 0% -> 28%
where the time goes in v1:
time: 227 us
  starting transfers between devices  85.8 us (38%)
  Pallas kernels  69.7 us (31%)
  waiting for transfers between devices  41.4 us (18%)
  local copies, waits for them, and re-layouts  21 us (9%)
  other arithmetic  7.34 us (3%)
    ppermute x45, starting transfers between devices, over_y(): return lax.ppermute(x, 'sub', [(i, i ^ r) for i in range(n_sub)])  53.6 us
    pallas_call x8, Pallas kernels, gradients(): pl.pallas_call(functools.partial(grad_kernel, ny, chunk * rows // TILE, s...  50.3 us
    ppermute x45, waiting for transfers between devices, over_y(): return lax.ppermute(x, 'sub', [(i, i ^ r) for i in range(n_sub)])  20.9 us
    ppermute x8, starting transfers between devices, over_z(): return lax.ppermute(x, 'sub', [(i, i ^ r * ny) for i in range(n_sub)])  16.2 us
    ppermute x12, starting transfers between devices, onward(): return lax.ppermute(x, ('group', 'sub'), route)  16 us
    ppermute x8, waiting for transfers between devices, over_z(): return lax.ppermute(x, 'sub', [(i, i ^ r * ny) for i in range(n_sub)])  15.2 us
    unnamed x68, local copies, waits for them, and re-layouts  14 us
    pallas_call x4, Pallas kernels, user_step(): pl.pallas_call(functools.partial(step_kernel, len(parts)), grid=(n_users...  10.4 us
  transfers between devices with their start and end apart: 66, of which 19 were waited for; matrix products, arithmetic and copies ran while one was open for 5% of the time, Pallas kernels for 28%

profile of v1, /device:TPU:0, one launch (start us, length us, event | category | flops | bytes accessed | tf_op | source)
XLA Modules:
  0.0 226.6 jit_solution(17412711075110718087)
XLA Ops:
  0.6 4.1 %collective-permute-start = (f32[64,512]{1,0:T(8,128)}, f32[64,512]{1,0:T(8,128)S(1)}, u32[]{:S(2)}, u32[]{:S(2)}) collective-permute-start(f32[64,512]{1,0:T(8,128)} %refs_1_.9), channel_id=1, source_target_pairs={{0,4},{1,5},{2,6},{3,7},{4,0},{5,1},{6,2},{7,3},{8,12},{9,13},{10,... | collective-permute-start | bytes 393224 | tf_op jit(solution)/shard_map/ppermute | solution.py:206
  4.8 6.4 %collective-permute-done.refs_2_ = f32[64,512]{1,0:T(8,128)S(1)} collective-permute-done((f32[64,512]{1,0:T(8,128)}, f32[64,512]{1,0:T(8,128)S(1)}, u32[]{:S(2)}, u32[]{:S(2)}) %collective-permute-start) | collective-permute-done | bytes 131104 | tf_op jit(solution)/shard_map/ppermute | solution.py:206
  17.1 4.0 %collective-permute-done.1 = f32[2,64,512]{2,1,0:T(8,128)S(1)} collective-permute-done((f32[2,64,512]{2,1,0:T(8,128)S(1)}, f32[2,64,512]{2,1,0:T(8,128)S(1)}, u32[]{:S(2)}, u32[]{:S(2)}) %collective-permute-start.1) | collective-permute-done | bytes 262176 | tf_op jit(solution)/shard_map/ppermute | solution.py:203
  23.6 3.5 %collective-permute-done.3 = f32[2,64,512]{2,1,0:T(8,128)S(1)} collective-permute-done((f32[2,64,512]{2,1,0:T(8,128)S(1)}, f32[2,64,512]{2,1,0:T(8,128)S(1)}, u32[]{:S(2)}, u32[]{:S(2)}) %collective-permute-start.3) | collective-permute-done | bytes 262176 | tf_op jit(solution)/shard_map/ppermute | solution.py:203
  32.4 6.0 %gradients.9 = (bf16[1024,256]{1,0:T(8,128)(2,1)S(1)}, bf16[1024,256]{1,0:T(8,128)(2,1)S(1)}, bf16[256,512]{1,0:T(8,128)(2,1)S(1)}, bf16[256,512]{1,0:T(8,128)(2...) custom-call(s32[2]{0:T(128)S(1)} %pad_add_fusion.refs_0_, ...), custom_call_target="tpu_custom_call" | custom-call | flops 1610612736 | bytes 2097152 | tf_op jit(solution)/shard_map/gradients/pallas_call | solution.py:99
  42.0 6.7 %gradients.8 = (bf16[1024,256]{1,0:T(8,128)(2,1)S(1)}, bf16[1024,256]{1,0:T(8,128)(2,1)S(1)}, bf16[256,512]{1,0:T(8,128)(2,1)S(1)}, bf16[256,512]{1,0:T(8,128)(2...) custom-call(s32[2]{0:T(128)S(1)} %pad_add_fusion.refs_0_, ...), custom_call_target="tpu_custom_call" | custom-call | flops 1610612736 | bytes 2097152 | tf_op jit(solution)/shard_map/gradients/pallas_call | solution.py:99
  56.5 3.1 %collective-permute-start.16 = (f32[32,512]{1,0:T(8,128)}, f32[32,512]{1,0:T(8,128)}, u32[]{:S(2)}, u32[]{:S(2)}) collective-permute-start(f32[32,512]{1,0:T(8,128)} %get-tuple-element.107), channel_id=1, source_target_pairs={{0,4},{1,5},{2,6},{3,7},{4,0},{5,1},{6,2},{7,3},{8,12},{9,13},{10,... | collective-permute-start | bytes 196616 | tf_op jit(solution)/shard_map/ppermute | solution.py:206
  63.2 3.1 %collective-permute-start.7 = (f32[32,512]{1,0:T(8,128)S(1)}, f32[32,512]{1,0:T(8,128)S(1)}, u32[]{:S(2)}, u32[]{:S(2)}) collective-permute-start(f32[32,512]{1,0:T(8,128)S(1)} %get-tuple-element.97), channel_id=1, source_target_pairs={{0,4},{1,5},{2,6},{3,7},{4,0},{5,1},{6,2},{7,3},{8,12},{9,13},{10,... | collective-permute-start | bytes 196616 | tf_op jit(solution)/shard_map/ppermute | solution.py:206
  69.4 3.5 %collective-permute-start.9 = (f32[32,512]{1,0:T(8,128)S(1)}, f32[32,512]{1,0:T(8,128)S(1)}, u32[]{:S(2)}, u32[]{:S(2)}) collective-permute-start(f32[32,512]{1,0:T(8,128)S(1)} %bitcast_add_fusion.1), channel_id=1, source_target_pairs={{0,12},{1,13},{2,14},{3,15},{4,8},{5,9},{6,10},{7,11},{8,20},{9,21... | collective-permute-start | bytes 196616 | tf_op jit(solution)/shard_map/ppermute | solution.py:213
  74.9 3.4 %collective-permute-start.20 = (f32[2,32,512]{2,1,0:T(8,128)S(1)}, f32[2,32,512]{2,1,0:T(8,128)S(1)}, u32[]{:S(2)}, u32[]{:S(2)}) collective-permute-start(f32[2,32,512]{2,1,0:T(8,128)S(1)} %join.9.refs_4_), channel_id=1, source_target_pairs={{0,2},{1,3},{2,0},{3,1},{4,6},{5,7},{6,4},{7,5},{8,10},{9,11},{10,... | collective-permute-start | bytes 393224 | tf_op jit(solution)/shard_map/ppermute | solution.py:203
  90.8 6.0 %gradients.11 = (bf16[1024,256]{1,0:T(8,128)(2,1)S(1)}, bf16[1024,256]{1,0:T(8,128)(2,1)S(1)}, bf16[256,512]{1,0:T(8,128)(2,1)S(1)}, bf16[256,512]{1,0:T(8,128)(...) custom-call(s32[2]{0:T(128)S(1)} %pad_add_fusion.refs_0_, ...), custom_call_target="tpu_custom_call" | custom-call | flops 1610612736 | bytes 2097152 | tf_op jit(solution)/shard_map/gradients/pallas_call | solution.py:99
  100.4 6.0 %gradients.10 = (bf16[1024,256]{1,0:T(8,128)(2,1)S(1)}, bf16[1024,256]{1,0:T(8,128)(2,1)S(1)}, bf16[256,512]{1,0:T(8,128)(2,1)S(1)}, bf16[256,512]{1,0:T(8,128)(...) custom-call(s32[2]{0:T(128)S(1)} %pad_add_fusion.refs_0_, ...), custom_call_target="tpu_custom_call" | custom-call | flops 1610612736 | bytes 2097152 | tf_op jit(solution)/shard_map/gradients/pallas_call | solution.py:99
  113.0 2.7 %collective-permute-done.24.refs_4_ = f32[2,32,512]{2,1,0:T(8,128)S(1)} collective-permute-done((f32[2,32,512]{2,1,0:T(8,128)S(1)}, f32[2,32,512]{2,1,0:T(8,128)S(1)}, u32[]{:S(2)}, u32[]{:S(2)}) %collective-permute-start.24) | collective-permute-done | bytes 131104 | tf_op jit(solution)/shard_map/ppermute | solution.py:203
  116.6 4.2 %collective-permute-start.36 = (f32[32,512]{1,0:T(8,128)S(1)}, f32[32,512]{1,0:T(8,128)S(1)}, u32[]{:S(2)}, u32[]{:S(2)}) collective-permute-start(f32[32,512]{1,0:T(8,128)S(1)} %multiply_add_fusion.3), channel_id=1, source_target_pairs={{0,12},{1,13},{2,14},{3,15},{4,8},{5,9},{6,10},{7,11},{8,20},{9,21... | collective-permute-start | bytes 196616 | tf_op jit(solution)/shard_map/ppermute | solution.py:213
  121.6 3.0 %collective-permute-start.27 = (f32[32,512]{1,0:T(8,128)S(1)}, f32[32,512]{1,0:T(8,128)S(1)}, u32[]{:S(2)}, u32[]{:S(2)}) collective-permute-start(f32[32,512]{1,0:T(8,128)S(1)} %multiply_add_fusion.4), channel_id=1, source_target_pairs={{0,12},{1,13},{2,14},{3,15},{4,8},{5,9},{6,10},{7,11},{8,20},{9,21... | collective-permute-start | bytes 196616 | tf_op jit(solution)/shard_map/ppermute | solution.py:213
  135.5 6.0 %gradients.13 = (bf16[1024,256]{1,0:T(8,128)(2,1)S(1)}, bf16[1024,256]{1,0:T(8,128)(2,1)S(1)}, bf16[256,512]{1,0:T(8,128)(2,1)S(1)}, bf16[256,512]{1,0:T(8,128)(...) custom-call(s32[2]{0:T(128)S(1)} %pad_add_fusion.refs_0_, ...), custom_call_target="tpu_custom_call" | custom-call | flops 1610612736 | bytes 2097152 | tf_op jit(solution)/shard_map/gradients/pallas_call | solution.py:99
  145.4 6.0 %gradients.12 = (bf16[1024,256]{1,0:T(8,128)(2,1)S(1)}, bf16[1024,256]{1,0:T(8,128)(2,1)S(1)}, bf16[256,512]{1,0:T(8,128)(2,1)S(1)}, bf16[256,512]{1,0:T(8,128)(...) custom-call(s32[2]{0:T(128)S(1)} %pad_add_fusion.refs_0_, ...), custom_call_target="tpu_custom_call" | custom-call | flops 1610612736 | bytes 2097152 | tf_op jit(solution)/shard_map/gradients/pallas_call | solution.py:99
  155.5 2.8 %collective-permute-start.52 = (f32[32,512]{1,0:T(8,128)S(1)}, f32[32,512]{1,0:T(8,128)S(1)}, u32[]{:S(2)}, u32[]{:S(2)}) collective-permute-start(f32[32,512]{1,0:T(8,128)S(1)} %get-tuple-element.147), channel_id=1, source_target_pairs={{0,4},{1,5},{2,6},{3,7},{4,0},{5,1},{6,2},{7,3},{8,12},{9,13},{10,... | collective-permute-start | bytes 196616 | tf_op jit(solution)/shard_map/ppermute | solution.py:206
  167.5 2.9 %collective-permute-done.54.refs_2_ = f32[32,512]{1,0:T(8,128)S(1)} collective-permute-done((f32[32,512]{1,0:T(8,128)S(1)}, f32[32,512]{1,0:T(8,128)S(1)}, u32[]{:S(2)}, u32[]{:S(2)}) %collective-permute-start.54) | collective-permute-done | bytes 65568 | tf_op jit(solution)/shard_map/ppermute | solution.py:213
  181.0 6.8 %gradients.15 = (bf16[1024,256]{1,0:T(8,128)(2,1)S(1)}, bf16[1024,256]{1,0:T(8,128)(2,1)S(1)}, bf16[256,512]{1,0:T(8,128)(2,1)S(1)}, bf16[256,512]{1,0:T(8,128)(...) custom-call(s32[2]{0:T(128)S(1)} %pad_add_fusion.refs_0_, ...), custom_call_target="tpu_custom_call" | custom-call | flops 1610612736 | bytes 2097152 | tf_op jit(solution)/shard_map/gradients/pallas_call | solution.py:99
  188.9 6.8 %gradients.14 = (bf16[1024,256]{1,0:T(8,128)(2,1)S(1)}, bf16[1024,256]{1,0:T(8,128)(2,1)S(1)}, bf16[256,512]{1,0:T(8,128)(2,1)S(1)}, bf16[256,512]{1,0:T(8,128)(...) custom-call(s32[2]{0:T(128)S(1)} %pad_add_fusion.refs_0_, ...), custom_call_target="tpu_custom_call" | custom-call | flops 1610612736 | bytes 2097152 | tf_op jit(solution)/shard_map/gradients/pallas_call | solution.py:99
  210.4 2.7 %collective-permute-done.58 = f32[1,64,512]{2,1,0:T(8,128)S(1)} collective-permute-done((f32[1,64,512]{2,1,0:T(8,128)}, f32[1,64,512]{2,1,0:T(8,128)S(1)}, u32[]{:S(2)}, u32[]{:S(2)}) %collective-permute-start.58) | collective-permute-done | bytes 131104 | tf_op jit(solution)/shard_map/ppermute | solution.py:203
  215.2 6.3 %collective-permute-done.64 = f32[64,512]{1,0:T(8,128)S(1)} collective-permute-done((f32[64,512]{1,0:T(8,128)S(1)}, f32[64,512]{1,0:T(8,128)S(1)}, u32[]{:S(2)}, u32[]{:S(2)}) %collective-permute-start.64) | collective-permute-done | bytes 131104 | tf_op jit(solution)/shard_map/ppermute | solution.py:206
  221.6 3.4 %user_step.7 = f32[1024,512]{1,0:T(8,128)} custom-call(f32[1024,512]{1,0:T(8,128)S(1)} %user_step.6.refs_2_.refs_0_, bf16[1024,256]{1,0:T(8,128)(2,1)S(1)} %copy-done.8, bf16[1024,256]{1,0:T(8,128)(2,1)S(1)} %copy-done.10, bf16[256,512]{1,0:T(8,128)(2,1)S(1)} %copy-done.24, bf16[256,512]{1,0:T(8,128)(2,1)S(1)} %copy-done.26, ...), custom_call_target="tpu_custom_call" | custom-call | flops 1610612736 | bytes 4194304 | tf_op jit(solution)/shard_map/user_step/pallas_call | solution.py:133
  (233 shorter events, 115.8 us)
Async XLA Ops:
  15.1 11.9 %collective-permute-start.3 = (f32[2,64,512]{2,1,0:T(8,128)S(1)}, f32[2,64,512]{2,1,0:T(8,128)S(1)}, u32[]{:S(2)}, u32[]{:S(2)}) collective-permute-start(f32[2,64,512]{2,1,0:T(8,128)S(1)} %join.7), channel_id=1, source_target_pairs={{0,3},{1,2},{2,1},{3,0},{4,7},{5,6},{6,5},{7,4},{8,11},{9,10},{10,... | collective-permute-start | bytes 786440 | tf_op jit(solution)/shard_map/ppermute | solution.py:203
  38.4 16.5 %collective-permute-start.13 = (f32[2,32,512]{2,1,0:T(8,128)S(1)}, f32[2,32,512]{2,1,0:T(8,128)S(1)}, u32[]{:S(2)}, u32[]{:S(2)}) collective-permute-start(f32[2,32,512]{2,1,0:T(8,128)S(1)} %get-tuple-element.103), channel_id=1, source_target_pairs={{0,1},{1,0},{2,3},{3,2},{4,5},{5,4},{6,7},{7,6},{8,9},{9,8},{10,11... | collective-permute-start | bytes 393224 | tf_op jit(solution)/shard_map/ppermute | solution.py:203
  39.8 15.5 %collective-permute-start.14 = (f32[2,32,512]{2,1,0:T(8,128)S(1)}, f32[2,32,512]{2,1,0:T(8,128)S(1)}, u32[]{:S(2)}, u32[]{:S(2)}) collective-permute-start(f32[2,32,512]{2,1,0:T(8,128)S(1)} %get-tuple-element.104), channel_id=1, source_target_pairs={{0,2},{1,3},{2,0},{3,1},{4,6},{5,7},{6,4},{7,5},{8,10},{9,11},{10,... | collective-permute-start | bytes 393224 | tf_op jit(solution)/shard_map/ppermute | solution.py:203
  41.5 13.7 %collective-permute-start.15 = (f32[2,32,512]{2,1,0:T(8,128)S(1)}, f32[2,32,512]{2,1,0:T(8,128)S(1)}, u32[]{:S(2)}, u32[]{:S(2)}) collective-permute-start(f32[2,32,512]{2,1,0:T(8,128)S(1)} %get-tuple-element.105), channel_id=1, source_target_pairs={{0,3},{1,2},{2,1},{3,0},{4,7},{5,6},{6,5},{7,4},{8,11},{9,10},{10,... | collective-permute-start | bytes 393224 | tf_op jit(solution)/shard_map/ppermute | solution.py:203
  69.3 17.4 %collective-permute-start.8 = (f32[32,512]{1,0:T(8,128)S(1)}, f32[32,512]{1,0:T(8,128)S(1)}, u32[]{:S(2)}, u32[]{:S(2)}) collective-permute-start(f32[32,512]{1,0:T(8,128)S(1)} %bitcast_add_fusion.1), channel_id=1, source_target_pairs={{0,8},{1,9},{2,10},{3,11},{4,12},{5,13},{6,14},{7,15},{8,16},{9,17... | collective-permute-start | bytes 196616 | tf_op jit(solution)/shard_map/ppermute | solution.py:213
  69.4 17.3 %collective-permute-start.9 = (f32[32,512]{1,0:T(8,128)S(1)}, f32[32,512]{1,0:T(8,128)S(1)}, u32[]{:S(2)}, u32[]{:S(2)}) collective-permute-start(f32[32,512]{1,0:T(8,128)S(1)} %bitcast_add_fusion.1), channel_id=1, source_target_pairs={{0,12},{1,13},{2,14},{3,15},{4,8},{5,9},{6,10},{7,11},{8,20},{9,21... | collective-permute-start | bytes 196616 | tf_op jit(solution)/shard_map/ppermute | solution.py:213
  74.8 15.9 %collective-permute-start.19 = (f32[2,32,512]{2,1,0:T(8,128)S(1)}, f32[2,32,512]{2,1,0:T(8,128)S(1)}, u32[]{:S(2)}, u32[]{:S(2)}) collective-permute-start(f32[2,32,512]{2,1,0:T(8,128)S(1)} %join.9.refs_4_), channel_id=1, source_target_pairs={{0,1},{1,0},{2,3},{3,2},{4,5},{5,4},{6,7},{7,6},{8,9},{9,8},{10,11... | collective-permute-start | bytes 393224 | tf_op jit(solution)/shard_map/ppermute | solution.py:203
  74.9 15.9 %collective-permute-start.20 = (f32[2,32,512]{2,1,0:T(8,128)S(1)}, f32[2,32,512]{2,1,0:T(8,128)S(1)}, u32[]{:S(2)}, u32[]{:S(2)}) collective-permute-start(f32[2,32,512]{2,1,0:T(8,128)S(1)} %join.9.refs_4_), channel_id=1, source_target_pairs={{0,2},{1,3},{2,0},{3,1},{4,6},{5,7},{6,4},{7,5},{8,10},{9,11},{10,... | collective-permute-start | bytes 393224 | tf_op jit(solution)/shard_map/ppermute | solution.py:203
  78.3 12.5 %collective-permute-start.21 = (f32[2,32,512]{2,1,0:T(8,128)S(1)}, f32[2,32,512]{2,1,0:T(8,128)S(1)}, u32[]{:S(2)}, u32[]{:S(2)}) collective-permute-start(f32[2,32,512]{2,1,0:T(8,128)S(1)} %join.9.refs_4_), channel_id=1, source_target_pairs={{0,3},{1,2},{2,1},{3,0},{4,7},{5,6},{6,5},{7,4},{8,11},{9,10},{10,... | collective-permute-start | bytes 393224 | tf_op jit(solution)/shard_map/ppermute | solution.py:203
  87.3 13.0 %collective-permute-start.10 = (f32[2,32,512]{2,1,0:T(8,128)S(1)}, f32[2,32,512]{2,1,0:T(8,128)S(1)}, u32[]{:S(2)}, u32[]{:S(2)}) collective-permute-start(f32[2,32,512]{2,1,0:T(8,128)S(1)} %join.8.refs_4_), channel_id=1, source_target_pairs={{0,1},{1,0},{2,3},{3,2},{4,5},{5,4},{6,7},{7,6},{8,9},{9,8},{10,11... | collective-permute-start | bytes 393224 | tf_op jit(solution)/shard_map/ppermute | solution.py:203
  88.7 11.7 %collective-permute-start.11 = (f32[2,32,512]{2,1,0:T(8,128)S(1)}, f32[2,32,512]{2,1,0:T(8,128)S(1)}, u32[]{:S(2)}, u32[]{:S(2)}) collective-permute-start(f32[2,32,512]{2,1,0:T(8,128)S(1)} %join.8.refs_4_), channel_id=1, source_target_pairs={{0,2},{1,3},{2,0},{3,1},{4,6},{5,7},{6,4},{7,5},{8,10},{9,11},{10,... | collective-permute-start | bytes 393224 | tf_op jit(solution)/shard_map/ppermute | solution.py:203
  96.9 13.0 %collective-permute-start.31 = (f32[2,32,512]{2,1,0:T(8,128)S(1)}, f32[2,32,512]{2,1,0:T(8,128)S(1)}, u32[]{:S(2)}, u32[]{:S(2)}) collective-permute-start(f32[2,32,512]{2,1,0:T(8,128)S(1)} %get-tuple-element.123), channel_id=1, source_target_pairs={{0,1},{1,0},{2,3},{3,2},{4,5},{5,4},{6,7},{7,6},{8,9},{9,8},{10,11... | collective-permute-start | bytes 393224 | tf_op jit(solution)/shard_map/ppermute | solution.py:203
  98.3 11.7 %collective-permute-start.32 = (f32[2,32,512]{2,1,0:T(8,128)S(1)}, f32[2,32,512]{2,1,0:T(8,128)S(1)}, u32[]{:S(2)}, u32[]{:S(2)}) collective-permute-start(f32[2,32,512]{2,1,0:T(8,128)S(1)} %get-tuple-element.124), channel_id=1, source_target_pairs={{0,2},{1,3},{2,0},{3,1},{4,6},{5,7},{6,4},{7,5},{8,10},{9,11},{10,... | collective-permute-start | bytes 393224 | tf_op jit(solution)/shard_map/ppermute | solution.py:203
  131.6 12.2 %collective-permute-start.28 = (f32[2,32,512]{2,1,0:T(8,128)S(1)}, f32[2,32,512]{2,1,0:T(8,128)S(1)}, u32[]{:S(2)}, u32[]{:S(2)}) collective-permute-start(f32[2,32,512]{2,1,0:T(8,128)S(1)} %join.10.refs_4_), channel_id=1, source_target_pairs={{0,1},{1,0},{2,3},{3,2},{4,5},{5,4},{6,7},{7,6},{8,9},{9,8},{10,11... | collective-permute-start | bytes 393224 | tf_op jit(solution)/shard_map/ppermute | solution.py:203
  133.5 11.9 %collective-permute-start.29 = (f32[2,32,512]{2,1,0:T(8,128)S(1)}, f32[2,32,512]{2,1,0:T(8,128)S(1)}, u32[]{:S(2)}, u32[]{:S(2)}) collective-permute-start(f32[2,32,512]{2,1,0:T(8,128)S(1)} %join.10.refs_4_), channel_id=1, source_target_pairs={{0,2},{1,3},{2,0},{3,1},{4,6},{5,7},{6,4},{7,5},{8,10},{9,11},{10,... | collective-permute-start | bytes 393224 | tf_op jit(solution)/shard_map/ppermute | solution.py:203
  133.5 11.9 %collective-permute-start.30 = (f32[2,32,512]{2,1,0:T(8,128)S(1)}, f32[2,32,512]{2,1,0:T(8,128)S(1)}, u32[]{:S(2)}, u32[]{:S(2)}) collective-permute-start(f32[2,32,512]{2,1,0:T(8,128)S(1)} %join.10.refs_4_), channel_id=1, source_target_pairs={{0,3},{1,2},{2,1},{3,0},{4,7},{5,6},{6,5},{7,4},{8,11},{9,10},{10,... | collective-permute-start | bytes 393224 | tf_op jit(solution)/shard_map/ppermute | solution.py:203
  141.5 11.9 %collective-permute-start.49 = (f32[2,32,512]{2,1,0:T(8,128)S(1)}, f32[2,32,512]{2,1,0:T(8,128)S(1)}, u32[]{:S(2)}, u32[]{:S(2)}) collective-permute-start(f32[2,32,512]{2,1,0:T(8,128)S(1)} %get-tuple-element.143), channel_id=1, source_target_pairs={{0,1},{1,0},{2,3},{3,2},{4,5},{5,4},{6,7},{7,6},{8,9},{9,8},{10,11... | collective-permute-start | bytes 393224 | tf_op jit(solution)/shard_map/ppermute | solution.py:203
  143.8 11.1 %collective-permute-start.50 = (f32[2,32,512]{2,1,0:T(8,128)S(1)}, f32[2,32,512]{2,1,0:T(8,128)S(1)}, u32[]{:S(2)}, u32[]{:S(2)}) collective-permute-start(f32[2,32,512]{2,1,0:T(8,128)S(1)} %get-tuple-element.144), channel_id=1, source_target_pairs={{0,2},{1,3},{2,0},{3,1},{4,6},{5,7},{6,4},{7,5},{8,10},{9,11},{10,... | collective-permute-start | bytes 393224 | tf_op jit(solution)/shard_map/ppermute | solution.py:203
  143.8 11.1 %collective-permute-start.51 = (f32[2,32,512]{2,1,0:T(8,128)S(1)}, f32[2,32,512]{2,1,0:T(8,128)S(1)}, u32[]{:S(2)}, u32[]{:S(2)}) collective-permute-start(f32[2,32,512]{2,1,0:T(8,128)S(1)} %get-tuple-element.145), channel_id=1, source_target_pairs={{0,3},{1,2},{2,1},{3,0},{4,7},{5,6},{6,5},{7,4},{8,11},{9,10},{10,... | collective-permute-start | bytes 393224 | tf_op jit(solution)/shard_map/ppermute | solution.py:203
  177.4 11.4 %collective-permute-start.46 = (f32[2,32,512]{2,1,0:T(8,128)S(1)}, f32[2,32,512]{2,1,0:T(8,128)S(1)}, u32[]{:S(2)}, u32[]{:S(2)}) collective-permute-start(f32[2,32,512]{2,1,0:T(8,128)S(1)} %join.12.refs_4_), channel_id=1, source_target_pairs={{0,1},{1,0},{2,3},{3,2},{4,5},{5,4},{6,7},{7,6},{8,9},{9,8},{10,11... | collective-permute-start | bytes 393224 | tf_op jit(solution)/shard_map/ppermute | solution.py:203
  187.8 20.0 %collective-permute-start.63 = (f32[1,64,512]{2,1,0:T(8,128)}, f32[1,64,512]{2,1,0:T(8,128)}, u32[]{:S(2)}, u32[]{:S(2)}) collective-permute-start(f32[1,64,512]{2,1,0:T(8,128)} %get-tuple-element.159), channel_id=1, source_target_pairs={{0,3},{1,2},{2,1},{3,0},{4,7},{5,6},{6,5},{7,4},{8,11},{9,10},{10,... | collective-permute-start | bytes 393224 | tf_op jit(solution)/shard_map/ppermute | solution.py:203
  195.7 12.6 %collective-permute-start.62 = (f32[1,64,512]{2,1,0:T(8,128)}, f32[1,64,512]{2,1,0:T(8,128)}, u32[]{:S(2)}, u32[]{:S(2)}) collective-permute-start(f32[1,64,512]{2,1,0:T(8,128)} %get-tuple-element.158), channel_id=1, source_target_pairs={{0,3},{1,2},{2,1},{3,0},{4,7},{5,6},{6,5},{7,4},{8,11},{9,10},{10,... | collective-permute-start | bytes 393224 | tf_op jit(solution)/shard_map/ppermute | solution.py:203
  197.7 11.7 %collective-permute-start.61 = (f32[1,64,512]{2,1,0:T(8,128)}, f32[1,64,512]{2,1,0:T(8,128)}, u32[]{:S(2)}, u32[]{:S(2)}) collective-permute-start(f32[1,64,512]{2,1,0:T(8,128)} %get-tuple-element.157), channel_id=1, source_target_pairs={{0,2},{1,3},{2,0},{3,1},{4,6},{5,7},{6,4},{7,5},{8,10},{9,11},{10,... | collective-permute-start | bytes 393224 | tf_op jit(solution)/shard_map/ppermute | solution.py:203
  197.9 11.5 %collective-permute-start.60 = (f32[1,64,512]{2,1,0:T(8,128)}, f32[1,64,512]{2,1,0:T(8,128)}, u32[]{:S(2)}, u32[]{:S(2)}) collective-permute-start(f32[1,64,512]{2,1,0:T(8,128)} %get-tuple-element.156), channel_id=1, source_target_pairs={{0,2},{1,3},{2,0},{3,1},{4,6},{5,7},{6,4},{7,5},{8,10},{9,11},{10,... | collective-permute-start | bytes 393224 | tf_op jit(solution)/shard_map/ppermute | solution.py:203
  (75 other events, 462.3 us)

commit v2 on v0

v2 whole, which is shorter than its diff:
```python
import functools

import jax
import jax.numpy as jnp
from jax import lax
from jax.experimental import pallas as pl
from jax.experimental.pallas import tpu as pltpu
from jax.sharding import PartitionSpec as P

TILE = 128
CHUNKS = 2
BLOCK = 512
VMEM = pl.BlockSpec(memory_space=pltpu.VMEM)
SMEM = pl.BlockSpec(memory_space=pltpu.SMEM)
F32 = jnp.float32
BF16 = jnp.bfloat16


def split(x):
    hi = x.astype(BF16)
    return hi, (x - hi.astype(F32)).astype(BF16)


def dot3(a, b, dims):
    (ah, al), (bh, bl) = a, b
    dot = functools.partial(lax.dot_general, dimension_numbers=(dims, ((), ())), preferred_element_type=F32)
    return dot(ah, bh) + (dot(ah, bl) + dot(al, bh))


def params(mib):
    return pltpu.CompilerParams(vmem_limit_bytes=mib * 1024 * 1024)


def grad_kernel(ny, chunk, stratum, *refs):
    where, occ, users, rate = refs[:4]
    pieces = refs[4:4 + ny]
    err_hi, err_lo, v_hi, v_lo, old = refs[4 + ny:9 + ny]
    grads = refs[9 + ny:9 + 2 * ny]
    block, total, vt_hi, vt_lo = refs[9 + 2 * ny:]
    mine = where[0]
    rows, rank = total.shape
    steps, q_in, _ = pieces[0].shape
    for r in range(ny):
        for z in range(steps):
            block[pl.ds((z * ny + (mine ^ r)) * q_in, q_in), :] = pieces[r][z]
    v = block[...]
    v_hi[...], v_lo[...] = split(v)
    vt_hi[...], vt_lo[...] = split(v.T)
    cut, q, _ = grads[0].shape
    old[...] = block[pl.ds((lax.rem(where[1], cut) * ny + mine) * q, q), :]
    for first in range(0, users.shape[0], BLOCK):
        at = slice(first, first + BLOCK)
        u = split(users[at, :])
        pred = dot3(u, (vt_hi[...], vt_lo[...]), ((1,), (0,)))
        err = rate[stratum, at, chunk * rows:(chunk + 1) * rows].astype(F32) - pred
        parts = []
        for a in range(BLOCK // TILE):
            line = []
            for b in range(rows // TILE):
                seen = occ[stratum, first // TILE + a, chunk * rows // TILE + b]
                part = err[a * TILE:(a + 1) * TILE, b * TILE:(b + 1) * TILE]
                line.append(jnp.where(seen == 1, part, 0.0))
            parts.append(jnp.concatenate(line, axis=1))
        err = jnp.concatenate(parts, axis=0)
        err_hi[at, :], err_lo[at, :] = split(err)
        term = dot3(split(err.T), u, ((1,), (0,)))
        if first == 0:
            total[...] = term
        else:
            total[...] += term
    for r in range(ny):
        for z in range(cut):
            grads[r][z] = total[pl.ds((z * ny + (mine ^ r)) * q, q), :]


def gradients(where, occ, users, ratings, pieces, stratum, chunk, q):
    ny = len(pieces)
    steps, q_in, rank = pieces[0].shape
    rows = steps * ny * q_in
    n_users = users.shape[0]
    gshape = (rows // (ny * q), q, rank)
    return pl.pallas_call(
        functools.partial(grad_kernel, ny, chunk, stratum),
        in_specs=[SMEM, SMEM] + [VMEM] * (2 + ny),
        out_specs=[VMEM] * (5 + ny),
        out_shape=[jax.ShapeDtypeStruct((n_users, rows), BF16)] * 2 + [jax.ShapeDtypeStruct((rows, rank), BF16)] * 2
        + [jax.ShapeDtypeStruct((q, rank), F32)] + [jax.ShapeDtypeStruct(gshape, F32)] * ny,
        scratch_shapes=[pltpu.VMEM((rows, rank), F32)] * 2 + [pltpu.VMEM((rank, rows), BF16)] * 2,
        compiler_params=params(24),
        cost_estimate=pl.CostEstimate(flops=12 * n_users * rows * rank, bytes_accessed=4 * n_users * rank, transcendentals=0),
        name="gradients",
    )(where, occ, users, ratings, *pieces)


def step_kernel(n, *refs):
    users, out = refs[0], refs[-1]
    for first in range(0, users.shape[0], BLOCK):
        at = slice(first, first + BLOCK)
        u = users[at, :]
        pull = None
        for i in range(n):
            eh, el, vh, vl = refs[1 + 4 * i:5 + 4 * i]
            part = dot3((eh[at, :], el[at, :]), (vh[...], vl[...]), ((1,), (0,)))
            pull = part if pull is None else pull + part
        out[at, :] = u + 0.02 * (pull - 0.05 * u)


def user_step(users, parts):
    n_users, rank = users.shape
    rows = sum(p[2].shape[0] for p in parts)
    return pl.pallas_call(
        functools.partial(step_kernel, len(parts)),
        in_specs=[VMEM] * (1 + 4 * len(parts)),
        out_specs=VMEM,
        out_shape=jax.ShapeDtypeStruct(users.shape, F32),
        compiler_params=params(24),
        cost_estimate=pl.CostEstimate(flops=6 * n_users * rows * rank, bytes_accessed=8 * n_users * rank, transcendentals=0),
        name="user_step",
    )(users, *[x for p in parts for x in p])


def new_rows(old, terms):
    return old + 0.005 * (jnp.sum(terms, axis=0) - 0.05 * old)


def per_device(n_group, n_sub, users, items, ratings, occupancy):
    strata = ratings.shape[0]
    share, rank = items.shape
    ny = 1
    while ny * ny * 4 <= n_sub:
        ny *= 2
    nz = n_sub // ny
    chunks = max(1, min(CHUNKS, share // 8))
    k = lax.axis_index("sub")
    where = jnp.stack([k % ny, k // ny]).astype(jnp.int32)
    lines = [[z * ny + y for z in range(nz)] for y in range(ny)]

    def over_y(x, r):
        return lax.ppermute(x, "sub", [(i, i ^ r) for i in range(n_sub)])

    def over_z(x):
        return lax.all_to_all(x, "sub", 0, 0, axis_index_groups=lines)

    def gather_z(x):
        return over_z(jnp.broadcast_to(x, (nz,) + x.shape))

    def onward(x, r):
        route = []
        for g in range(n_group):
            for i in range(n_sub):
                route.append((g * n_sub + i, (g + 1) % n_group * n_sub + (i ^ r)))
        return lax.ppermute(x, ("group", "sub"), route)

    q = share // chunks
    own = gather_z(items)
    pieces = []
    for c in range(chunks):
        part = own[c * (nz // chunks):(c + 1) * (nz // chunks)]
        pieces.append([part] + [over_y(part, r) for r in range(1, ny)])

    for s in range(strata):
        last = s == strata - 1
        parts, grads, olds = [], [], []
        for c in range(chunks):
            res = gradients(where, occupancy, users, ratings, pieces[c], s, c, share if last else q)
            parts.append(res[:4])
            olds.append(res[4])
            term = res[5]
            for r in range(1, ny):
                term = term + over_y(res[5 + r], r)
            grads.append(term)
        new_users = user_step(users, parts)
        if last:
            old = olds[0]
            for c in range(1, chunks):
                old = jnp.where(where[1] // (nz // chunks) == c, olds[c], old)
            rows = new_rows(old, over_z(jnp.concatenate(grads)))
            rows = lax.ppermute(rows, "group", [(g, (g + 1) % n_group) for g in range(n_group)])
            return new_users, rows
        for c in range(chunks):
            own = gather_z(new_rows(olds[c], over_z(grads[c])))
            pieces[c] = [onward(own, r) for r in range(ny)]
        users = new_users


def solution(mesh):
    spec = P(("group", "sub"), None)
    third = P(None, ("group", "sub"), None)
    return jax.shard_map(
        functools.partial(per_device, mesh.shape["group"], mesh.shape["sub"]),
        mesh=mesh,
        in_specs=(spec, spec, third, third),
        out_specs=(spec, spec),
        check_vma=False,
    )
```

time: 492 us -> 331 us (0.67)
  waiting for transfers between devices: 389 us -> 103 us
  starting transfers between devices: 1.1 us -> 81.3 us
  matrix products: 61.8 us -> 0 us
  local copies, waits for them, and re-layouts: 8.52 us -> 62.7 us
  Pallas kernels: 0 us -> 41.6 us
  blocking collectives: 0 us -> 20.6 us
  between operations: 14.2 us -> 1.2 us
  other arithmetic: 10.9 us -> 17.9 us
    psum x4 -> x0, waiting for transfers between devices: 310 us -> none  [per_device(): total = lax.psum(item_term(err, users), 'sub')]
    dot_general x12 -> x0, matrix products: 61.8 us -> none  [the longest x4 23.8 us: user_step(): jnp.dot(err, block, precision=lax.Precision.HIGHEST, preferred_element_ty...]
    all_to_all x0 -> x13, starting transfers between devices: none -> 56.7 us  [over_z(): return lax.all_to_all(x, 'sub', 0, 0, axis_index_groups=lines)]
    all_to_all x0 -> x13, waiting for transfers between devices: none -> 51.4 us  [over_z(): return lax.all_to_all(x, 'sub', 0, 0, axis_index_groups=lines)]
    unnamed x16 -> x142, local copies, waits for them, and re-layouts: 5.29 us -> 56.3 us
    all_gather x1 -> x0, waiting for transfers between devices: 44.2 us -> none  [per_device(): block = lax.all_gather(items, 'sub', axis=0, tiled=True)]
    pallas_call x0 -> x12, Pallas kernels: none -> 41.6 us  [the longest x8 32.9 us: gradients(): pl.pallas_call(functools.partial(grad_kernel, ny, chunk, stratum), in_spe...]
    ppermute x4 -> x23, starting transfers between devices: 0.9 us -> 24.5 us  [the longest x10 13 us: over_y(): return lax.ppermute(x, 'sub', [(i, i ^ r) for i in range(n_sub)])]
  transfers between devices with their start and end apart: 9 -> 36, of which waited for: 9 -> 16; matrix products, arithmetic and copies ran while one was open for 5% -> 5% of each run, Pallas kernels for 0% -> 12%
where the time goes in v2:
time: 331 us; the launch traced here: 328 us
  waiting for transfers between devices  103 us (31%)
  starting transfers between devices  81.3 us (25%)
  local copies, waits for them, and re-layouts  62.7 us (19%)
  Pallas kernels  41.6 us (13%)
  blocking collectives  20.6 us (6%)
  other arithmetic  17.9 us (5%)
    all_to_all x13, starting transfers between devices, over_z(): return lax.all_to_all(x, 'sub', 0, 0, axis_index_groups=lines)  56.7 us
    unnamed x142, local copies, waits for them, and re-layouts  56.3 us
    ppermute x10, waiting for transfers between devices, over_y(): return lax.ppermute(x, 'sub', [(i, i ^ r) for i in range(n_sub)])  51.5 us
    all_to_all x13, waiting for transfers between devices, over_z(): return lax.all_to_all(x, 'sub', 0, 0, axis_index_groups=lines)  51.4 us
    pallas_call x8, Pallas kernels, gradients(): pl.pallas_call(functools.partial(grad_kernel, ny, chunk, stratum), in_spe...  32.9 us
    all_to_all x1, blocking collectives, over_z(): return lax.all_to_all(x, 'sub', 0, 0, axis_index_groups=lines)  20.6 us
    ppermute x10, starting transfers between devices, over_y(): return lax.ppermute(x, 'sub', [(i, i ^ r) for i in range(n_sub)])  13 us
    ppermute x12, starting transfers between devices, onward(): return lax.ppermute(x, ('group', 'sub'), route)  11.5 us
  transfers between devices with their start and end apart: 36, of which 16 were waited for; matrix products, arithmetic and copies ran while one was open for 5% of the time, Pallas kernels for 12%

profile of v2, /device:TPU:0, one launch (start us, length us, event | category | flops | bytes accessed | tf_op | source)
XLA Modules:
  0.0 328.1 jit_solution(7190347756824497430)
XLA Ops:
  1.8 20.6 %all_to_all.70 = f32[4,64,512]{2,1,0:T(8,128)S(1)} all-to-all(f32[4,64,512]{2,1,0:T(8,128)S(1)} %broadcast_in_dim.21), channel_id=1, replica_groups={{0,2,4,6},{1,3,5,7},{8,10,12,14},{9,11,13,15},{16,18,20,22},{17,19,21,2..., dimensions={0} | all-to-all | bytes 1048576 | tf_op jit(solution)/shard_map/all_to_all | solution.py:142
  24.2 5.2 %collective-permute-done.1.refs_5_ = f32[2,64,512]{2,1,0:T(8,128)S(1)} collective-permute-done((f32[2,64,512]{2,1,0:T(8,128)S(1)}, f32[2,64,512]{2,1,0:T(8,128)S(1)}, u32[]{:S(2)}, u32[]{:S(2)}) %collective-permute-start.1) | collective-permute-done | bytes 262176 | tf_op jit(solution)/shard_map/ppermute | solution.py:139
  41.0 6.8 %collective-permute-done.5 = f32[4,32,512]{2,1,0:T(8,128)S(1)} collective-permute-done((f32[4,32,512]{2,1,0:T(8,128)S(1)}, f32[4,32,512]{2,1,0:T(8,128)S(1)}, u32[]{:S(2)}, u32[]{:S(2)}) %collective-permute-start.5) | collective-permute-done | bytes 262176 | tf_op jit(solution)/shard_map/ppermute | solution.py:139
  65.4 4.9 %collective-permute-done.2 = f32[4,32,512]{2,1,0:T(8,128)S(1)} collective-permute-done((f32[4,32,512]{2,1,0:T(8,128)S(1)}, f32[4,32,512]{2,1,0:T(8,128)S(1)}, u32[]{:S(2)}, u32[]{:S(2)}) %collective-permute-start.2) | collective-permute-done | bytes 262176 | tf_op jit(solution)/shard_map/ppermute | solution.py:139
  71.0 5.0 %all-to-all-start.1 = ((f32[4,32,512]{2,1,0:T(8,128)}), f32[4,32,512]{2,1,0:T(8,128)S(1)}, u32[]{:S(2)}, u32[]{:S(2)}) async-start(f32[4,32,512]{2,1,0:T(8,128)} %add.52), calls=%async_computation.1 | async-start | bytes 524288 | tf_op jit(solution)/shard_map/all_to_all | solution.py:142
  77.0 5.8 %all-to-all-done.1 = f32[4,32,512]{2,1,0:T(8,128)S(1)} async-done(((f32[4,32,512]{2,1,0:T(8,128)}), f32[4,32,512]{2,1,0:T(8,128)S(1)}, u32[]{:S(2)}, u32[]{:S(2)}) %all-to-all-start.1) | async-done | bytes 262176 | tf_op jit(solution)/shard_map/all_to_all | solution.py:142
  87.7 6.8 %all-to-all-done.4 = f32[4,32,512]{2,1,0:T(8,128)} async-done(((f32[4,32,512]{2,1,0:T(8,128)}), f32[4,32,512]{2,1,0:T(8,128)}, u32[]{:S(2)}, u32[]{:S(2)}) %all-to-all-start.4) | async-done | bytes 262176 | tf_op jit(solution)/shard_map/all_to_all | solution.py:142
  110.6 5.0 %gradients.11 = (bf16[1024,256]{1,0:T(8,128)(2,1)S(1)}, bf16[1024,256]{1,0:T(8,128)(2,1)S(1)}, bf16[256,512]{1,0:T(8,128)(2,1)S(1)}, bf16[256,512]{1,0:T(8,128)(...) custom-call(s32[2]{0:T(128)S(1)} %copy-done.64, s32[4,8,4]{2,1,0:T(8,128)S(1)} %copy.6.refs_1_, ...), custom_call_target="tpu_custom_call" | custom-call | flops 1610612736 | bytes 2097152 | tf_op jit(solution)/shard_map/gradients/pallas_call | solution.py:82
  119.1 9.3 %collective-permute-done.11 = f32[4,32,512]{2,1,0:T(8,128)} collective-permute-done((f32[4,32,512]{2,1,0:T(8,128)}, f32[4,32,512]{2,1,0:T(8,128)}, u32[]{:S(2)}, u32[]{:S(2)}) %collective-permute-start.11) | collective-permute-done | bytes 262176 | tf_op jit(solution)/shard_map/ppermute | solution.py:139
  130.2 4.8 %all-to-all-start.7 = ((f32[4,32,512]{2,1,0:T(8,128)}), f32[4,32,512]{2,1,0:T(8,128)}, u32[]{:S(2)}, u32[]{:S(2)}) async-start(f32[4,32,512]{2,1,0:T(8,128)} %add.58), calls=%async_computation.7 | async-start | bytes 524288 | tf_op jit(solution)/shard_map/all_to_all | solution.py:142
  146.2 5.4 %collective-permute-done.8 = f32[4,32,512]{2,1,0:T(8,128)S(1)} collective-permute-done((f32[4,32,512]{2,1,0:T(8,128)S(1)}, f32[4,32,512]{2,1,0:T(8,128)S(1)}, u32[]{:S(2)}, u32[]{:S(2)}) %collective-permute-start.8) | collective-permute-done | bytes 262176 | tf_op jit(solution)/shard_map/ppermute | solution.py:139
  152.4 4.8 %all-to-all-start.5 = ((f32[4,32,512]{2,1,0:T(8,128)}), f32[4,32,512]{2,1,0:T(8,128)S(1)}, u32[]{:S(2)}, u32[]{:S(2)}) async-start(f32[4,32,512]{2,1,0:T(8,128)} %add.56), calls=%async_computation.5 | async-start | bytes 524288 | tf_op jit(solution)/shard_map/all_to_all | solution.py:142
  158.2 5.8 %all-to-all-done.5 = f32[4,32,512]{2,1,0:T(8,128)S(1)} async-done(((f32[4,32,512]{2,1,0:T(8,128)}), f32[4,32,512]{2,1,0:T(8,128)S(1)}, u32[]{:S(2)}, u32[]{:S(2)}) %all-to-all-start.5) | async-done | bytes 262176 | tf_op jit(solution)/shard_map/all_to_all | solution.py:142
  164.7 4.2 %all-to-all-start.8 = ((f32[4,32,512]{2,1,0:T(8,128)}), f32[4,32,512]{2,1,0:T(8,128)}, u32[]{:S(2)}, u32[]{:S(2)}) async-start(f32[4,32,512]{2,1,0:T(8,128)} %broadcast_in_dim.25), calls=%async_computation.8 | async-start | bytes 524288 | tf_op jit(solution)/shard_map/all_to_all | solution.py:142
  169.0 6.8 %all-to-all-done.8 = f32[4,32,512]{2,1,0:T(8,128)} async-done(((f32[4,32,512]{2,1,0:T(8,128)}), f32[4,32,512]{2,1,0:T(8,128)}, u32[]{:S(2)}, u32[]{:S(2)}) %all-to-all-start.8) | async-done | bytes 262176 | tf_op jit(solution)/shard_map/all_to_all | solution.py:142
  189.8 4.6 %gradients.13 = (bf16[1024,256]{1,0:T(8,128)(2,1)S(1)}, bf16[1024,256]{1,0:T(8,128)(2,1)S(1)}, bf16[256,512]{1,0:T(8,128)(2,1)S(1)}, bf16[256,512]{1,0:T(8,128)(...) custom-call(s32[2]{0:T(128)S(1)} %copy-done.66, s32[4,8,4]{2,1,0:T(8,128)S(1)} %copy.6.refs_1_, ...), custom_call_target="tpu_custom_call" | custom-call | flops 1610612736 | bytes 2097152 | tf_op jit(solution)/shard_map/gradients/pallas_call | solution.py:82
  199.9 7.3 %collective-permute-done.17 = f32[4,32,512]{2,1,0:T(8,128)} collective-permute-done((f32[4,32,512]{2,1,0:T(8,128)}, f32[4,32,512]{2,1,0:T(8,128)}, u32[]{:S(2)}, u32[]{:S(2)}) %collective-permute-start.17) | collective-permute-done | bytes 262176 | tf_op jit(solution)/shard_map/ppermute | solution.py:139
  209.0 4.8 %all-to-all-start.11 = ((f32[4,32,512]{2,1,0:T(8,128)}), f32[4,32,512]{2,1,0:T(8,128)}, u32[]{:S(2)}, u32[]{:S(2)}) async-start(f32[4,32,512]{2,1,0:T(8,128)} %add.62), calls=%async_computation.11 | async-start | bytes 524288 | tf_op jit(solution)/shard_map/all_to_all | solution.py:142
  225.0 5.4 %collective-permute-done.14 = f32[4,32,512]{2,1,0:T(8,128)S(1)} collective-permute-done((f32[4,32,512]{2,1,0:T(8,128)S(1)}, f32[4,32,512]{2,1,0:T(8,128)S(1)}, u32[]{:S(2)}, u32[]{:S(2)}) %collective-permute-start.14) | collective-permute-done | bytes 262176 | tf_op jit(solution)/shard_map/ppermute | solution.py:139
  231.1 4.8 %all-to-all-start.9 = ((f32[4,32,512]{2,1,0:T(8,128)}), f32[4,32,512]{2,1,0:T(8,128)}, u32[]{:S(2)}, u32[]{:S(2)}) async-start(f32[4,32,512]{2,1,0:T(8,128)} %add.60), calls=%async_computation.9 | async-start | bytes 524288 | tf_op jit(solution)/shard_map/all_to_all | solution.py:142
  250.9 4.4 %all-to-all-done.12 = f32[4,32,512]{2,1,0:T(8,128)} async-done(((f32[4,32,512]{2,1,0:T(8,128)}), f32[4,32,512]{2,1,0:T(8,128)}, u32[]{:S(2)}, u32[]{:S(2)}) %all-to-all-start.12) | async-done | bytes 262176 | tf_op jit(solution)/shard_map/all_to_all | solution.py:142
  276.6 4.3 %gradients.15 = (bf16[1024,256]{1,0:T(8,128)(2,1)S(1)}, bf16[1024,256]{1,0:T(8,128)(2,1)S(1)}, bf16[256,512]{1,0:T(8,128)(2,1)S(1)}, bf16[256,512]{1,0:T(8,128)(...) custom-call(s32[2]{0:T(128)S(1)} %copy-done.68, ...), custom_call_target="tpu_custom_call" | custom-call | flops 1610612736 | bytes 2097152 | tf_op jit(solution)/shard_map/gradients/pallas_call | solution.py:82
  290.4 7.2 %collective-permute-done.20 = f32[2,64,512]{2,1,0:T(8,128)S(1)} collective-permute-done((f32[2,64,512]{2,1,0:T(8,128)S(1)}, f32[2,64,512]{2,1,0:T(8,128)S(1)}, u32[]{:S(2)}, u32[]{:S(2)}) %collective-permute-start.20) | collective-permute-done | bytes 262176 | tf_op jit(solution)/shard_map/ppermute | solution.py:139
  302.8 13.8 %all-to-all-done.13 = f32[4,64,512]{2,1,0:T(8,128)} async-done(((f32[4,64,512]{2,1,0:T(8,128)}), f32[4,64,512]{2,1,0:T(8,128)}, u32[]{:S(2)}, u32[]{:S(2)}) %all-to-all-start.13) | async-done | bytes 524320 | tf_op jit(solution)/shard_map/all_to_all | solution.py:142
  (235 shorter events, 169.1 us)
Async XLA Ops:
  40.5 12.1 %collective-permute-start = (f32[2,64,512]{2,1,0:T(8,128)S(1)}, f32[2,64,512]{2,1,0:T(8,128)S(1)}, u32[]{:S(2)}, u32[]{:S(2)}) collective-permute-start(f32[2,64,512]{2,1,0:T(8,128)S(1)} %get-tuple-element.115.refs_4_), channel_id=1, source_target_pairs={{0,1},{1,0},{2,3},{3,2},{4,5},{5,4},{6,7},{7,6},{8,9},{9,8},{10,11... | collective-permute-start | bytes 786440 | tf_op jit(solution)/shard_map/ppermute | solution.py:139
  48.6 22.4 %all-to-all-start.3 = ((f32[4,32,512]{2,1,0:T(8,128)}), f32[4,32,512]{2,1,0:T(8,128)}, u32[]{:S(2)}, u32[]{:S(2)}) async-start(f32[4,32,512]{2,1,0:T(8,128)} %add.54), calls=%async_computation.3 | async-start | bytes 524288 | tf_op jit(solution)/shard_map/all_to_all | solution.py:142
  71.0 11.9 %all-to-all-start.1 = ((f32[4,32,512]{2,1,0:T(8,128)}), f32[4,32,512]{2,1,0:T(8,128)S(1)}, u32[]{:S(2)}, u32[]{:S(2)}) async-start(f32[4,32,512]{2,1,0:T(8,128)} %add.52), calls=%async_computation.1 | async-start | bytes 524288 | tf_op jit(solution)/shard_map/all_to_all | solution.py:142
  94.5 15.8 %collective-permute-start.7 = (f32[4,32,512]{2,1,0:T(8,128)}, f32[4,32,512]{2,1,0:T(8,128)}, u32[]{:S(2)}, u32[]{:S(2)}) collective-permute-start(f32[4,32,512]{2,1,0:T(8,128)} %all-to-all-done.4), channel_id=1, source_target_pairs={{0,9},{1,8},{2,11},{3,10},{4,13},{5,12},{6,15},{7,14},{8,17},{9,16... | collective-permute-start | bytes 786440 | tf_op jit(solution)/shard_map/ppermute | solution.py:152
  94.5 15.8 %collective-permute-start.6 = (f32[4,32,512]{2,1,0:T(8,128)}, f32[4,32,512]{2,1,0:T(8,128)}, u32[]{:S(2)}, u32[]{:S(2)}) collective-permute-start(f32[4,32,512]{2,1,0:T(8,128)} %all-to-all-done.4), channel_id=1, source_target_pairs={{0,8},{1,9},{2,10},{3,11},{4,12},{5,13},{6,14},{7,15},{8,16},{9,17... | collective-permute-start | bytes 786440 | tf_op jit(solution)/shard_map/ppermute | solution.py:152
  97.8 20.7 %all-to-all-start.2 = ((f32[4,32,512]{2,1,0:T(8,128)}), f32[4,32,512]{2,1,0:T(8,128)}, u32[]{:S(2)}, u32[]{:S(2)}) async-start(f32[4,32,512]{2,1,0:T(8,128)} %broadcast_in_dim.22), calls=%async_computation.2 | async-start | bytes 524288 | tf_op jit(solution)/shard_map/all_to_all | solution.py:142
  117.0 11.4 %collective-permute-start.11 = (f32[4,32,512]{2,1,0:T(8,128)}, f32[4,32,512]{2,1,0:T(8,128)}, u32[]{:S(2)}, u32[]{:S(2)}) collective-permute-start(f32[4,32,512]{2,1,0:T(8,128)} %get-tuple-element.89), channel_id=1, source_target_pairs={{0,1},{1,0},{2,3},{3,2},{4,5},{5,4},{6,7},{7,6},{8,9},{9,8},{10,11... | collective-permute-start | bytes 786440 | tf_op jit(solution)/shard_map/ppermute | solution.py:139
  118.5 16.4 %collective-permute-start.4 = (f32[4,32,512]{2,1,0:T(8,128)}, f32[4,32,512]{2,1,0:T(8,128)}, u32[]{:S(2)}, u32[]{:S(2)}) collective-permute-start(f32[4,32,512]{2,1,0:T(8,128)} %all-to-all-done.2), channel_id=1, source_target_pairs={{0,9},{1,8},{2,11},{3,10},{4,13},{5,12},{6,15},{7,14},{8,17},{9,16... | collective-permute-start | bytes 786440 | tf_op jit(solution)/shard_map/ppermute | solution.py:152
  118.5 16.4 %collective-permute-start.3 = (f32[4,32,512]{2,1,0:T(8,128)}, f32[4,32,512]{2,1,0:T(8,128)}, u32[]{:S(2)}, u32[]{:S(2)}) collective-permute-start(f32[4,32,512]{2,1,0:T(8,128)} %all-to-all-done.2), channel_id=1, source_target_pairs={{0,8},{1,9},{2,10},{3,11},{4,12},{5,13},{6,14},{7,15},{8,16},{9,17... | collective-permute-start | bytes 786440 | tf_op jit(solution)/shard_map/ppermute | solution.py:152
  130.2 22.2 %all-to-all-start.7 = ((f32[4,32,512]{2,1,0:T(8,128)}), f32[4,32,512]{2,1,0:T(8,128)}, u32[]{:S(2)}, u32[]{:S(2)}) async-start(f32[4,32,512]{2,1,0:T(8,128)} %add.58), calls=%async_computation.7 | async-start | bytes 524288 | tf_op jit(solution)/shard_map/all_to_all | solution.py:142
  152.4 11.6 %all-to-all-start.5 = ((f32[4,32,512]{2,1,0:T(8,128)}), f32[4,32,512]{2,1,0:T(8,128)S(1)}, u32[]{:S(2)}, u32[]{:S(2)}) async-start(f32[4,32,512]{2,1,0:T(8,128)} %add.56), calls=%async_computation.5 | async-start | bytes 524288 | tf_op jit(solution)/shard_map/all_to_all | solution.py:142
  175.8 13.7 %collective-permute-start.13 = (f32[4,32,512]{2,1,0:T(8,128)}, f32[4,32,512]{2,1,0:T(8,128)}, u32[]{:S(2)}, u32[]{:S(2)}) collective-permute-start(f32[4,32,512]{2,1,0:T(8,128)} %all-to-all-done.8), channel_id=1, source_target_pairs={{0,9},{1,8},{2,11},{3,10},{4,13},{5,12},{6,15},{7,14},{8,17},{9,16... | collective-permute-start | bytes 786440 | tf_op jit(solution)/shard_map/ppermute | solution.py:152
  175.8 13.7 %collective-permute-start.12 = (f32[4,32,512]{2,1,0:T(8,128)}, f32[4,32,512]{2,1,0:T(8,128)}, u32[]{:S(2)}, u32[]{:S(2)}) collective-permute-start(f32[4,32,512]{2,1,0:T(8,128)} %all-to-all-done.8), channel_id=1, source_target_pairs={{0,8},{1,9},{2,10},{3,11},{4,12},{5,13},{6,14},{7,15},{8,16},{9,17... | collective-permute-start | bytes 786440 | tf_op jit(solution)/shard_map/ppermute | solution.py:152
  177.1 20.2 %all-to-all-start.6 = ((f32[4,32,512]{2,1,0:T(8,128)}), f32[4,32,512]{2,1,0:T(8,128)}, u32[]{:S(2)}, u32[]{:S(2)}) async-start(f32[4,32,512]{2,1,0:T(8,128)} %broadcast_in_dim.24), calls=%async_computation.6 | async-start | bytes 524288 | tf_op jit(solution)/shard_map/all_to_all | solution.py:142
  195.9 11.3 %collective-permute-start.17 = (f32[4,32,512]{2,1,0:T(8,128)}, f32[4,32,512]{2,1,0:T(8,128)}, u32[]{:S(2)}, u32[]{:S(2)}) collective-permute-start(f32[4,32,512]{2,1,0:T(8,128)} %get-tuple-element.103), channel_id=1, source_target_pairs={{0,1},{1,0},{2,3},{3,2},{4,5},{5,4},{6,7},{7,6},{8,9},{9,8},{10,11... | collective-permute-start | bytes 786440 | tf_op jit(solution)/shard_map/ppermute | solution.py:139
  197.3 16.5 %collective-permute-start.10 = (f32[4,32,512]{2,1,0:T(8,128)}, f32[4,32,512]{2,1,0:T(8,128)}, u32[]{:S(2)}, u32[]{:S(2)}) collective-permute-start(f32[4,32,512]{2,1,0:T(8,128)} %all-to-all-done.6), channel_id=1, source_target_pairs={{0,9},{1,8},{2,11},{3,10},{4,13},{5,12},{6,15},{7,14},{8,17},{9,16... | collective-permute-start | bytes 786440 | tf_op jit(solution)/shard_map/ppermute | solution.py:152
  197.3 16.5 %collective-permute-start.9 = (f32[4,32,512]{2,1,0:T(8,128)}, f32[4,32,512]{2,1,0:T(8,128)}, u32[]{:S(2)}, u32[]{:S(2)}) collective-permute-start(f32[4,32,512]{2,1,0:T(8,128)} %all-to-all-done.6), channel_id=1, source_target_pairs={{0,8},{1,9},{2,10},{3,11},{4,12},{5,13},{6,14},{7,15},{8,16},{9,17... | collective-permute-start | bytes 786440 | tf_op jit(solution)/shard_map/ppermute | solution.py:152
  209.0 22.1 %all-to-all-start.11 = ((f32[4,32,512]{2,1,0:T(8,128)}), f32[4,32,512]{2,1,0:T(8,128)}, u32[]{:S(2)}, u32[]{:S(2)}) async-start(f32[4,32,512]{2,1,0:T(8,128)} %add.62), calls=%async_computation.11 | async-start | bytes 524288 | tf_op jit(solution)/shard_map/all_to_all | solution.py:142
  231.1 11.7 %all-to-all-start.9 = ((f32[4,32,512]{2,1,0:T(8,128)}), f32[4,32,512]{2,1,0:T(8,128)}, u32[]{:S(2)}, u32[]{:S(2)}) async-start(f32[4,32,512]{2,1,0:T(8,128)} %add.60), calls=%async_computation.9 | async-start | bytes 524288 | tf_op jit(solution)/shard_map/all_to_all | solution.py:142
  260.0 16.2 %collective-permute-start.19 = (f32[4,32,512]{2,1,0:T(8,128)}, f32[4,32,512]{2,1,0:T(8,128)}, u32[]{:S(2)}, u32[]{:S(2)}) collective-permute-start(f32[4,32,512]{2,1,0:T(8,128)} %all-to-all-done.12), channel_id=1, source_target_pairs={{0,9},{1,8},{2,11},{3,10},{4,13},{5,12},{6,15},{7,14},{8,17},{9,16... | collective-permute-start | bytes 786440 | tf_op jit(solution)/shard_map/ppermute | solution.py:152
  260.1 16.2 %collective-permute-start.18 = (f32[4,32,512]{2,1,0:T(8,128)}, f32[4,32,512]{2,1,0:T(8,128)}, u32[]{:S(2)}, u32[]{:S(2)}) collective-permute-start(f32[4,32,512]{2,1,0:T(8,128)} %all-to-all-done.12), channel_id=1, source_target_pairs={{0,8},{1,9},{2,10},{3,11},{4,12},{5,13},{6,14},{7,15},{8,16},{9,17... | collective-permute-start | bytes 786440 | tf_op jit(solution)/shard_map/ppermute | solution.py:152
  266.9 16.2 %collective-permute-start.16 = (f32[4,32,512]{2,1,0:T(8,128)}, f32[4,32,512]{2,1,0:T(8,128)S(1)}, u32[]{:S(2)}, u32[]{:S(2)}) collective-permute-start(f32[4,32,512]{2,1,0:T(8,128)} %all-to-all-done.10), channel_id=1, source_target_pairs={{0,9},{1,8},{2,11},{3,10},{4,13},{5,12},{6,15},{7,14},{8,17},{9,16... | collective-permute-start | bytes 786440 | tf_op jit(solution)/shard_map/ppermute | solution.py:152
  266.9 16.2 %collective-permute-start.15 = (f32[4,32,512]{2,1,0:T(8,128)}, f32[4,32,512]{2,1,0:T(8,128)S(1)}, u32[]{:S(2)}, u32[]{:S(2)}) collective-permute-start(f32[4,32,512]{2,1,0:T(8,128)} %all-to-all-done.10), channel_id=1, source_target_pairs={{0,8},{1,9},{2,10},{3,11},{4,12},{5,13},{6,14},{7,15},{8,16},{9,17... | collective-permute-start | bytes 786440 | tf_op jit(solution)/shard_map/ppermute | solution.py:152
  298.6 18.0 %all-to-all-start.13 = ((f32[4,64,512]{2,1,0:T(8,128)}), f32[4,64,512]{2,1,0:T(8,128)}, u32[]{:S(2)}, u32[]{:S(2)}) async-start(f32[4,64,512]{2,1,0:T(8,128)} %pad_maximum_fusion), calls=%async_computation.13 | async-start | bytes 1048576 | tf_op jit(solution)/shard_map/all_to_all | solution.py:142
  (82 other events, 331.3 us)

commit v3 on v2

--- a/solution.py
+++ b/solution.py
@@ -119,44 +119,112 @@
     )(users, *[x for p in parts for x in p])
 
 
+def cut_kernel(ny, nz, *refs):
+    where, outs = refs[0], refs[-nz:]
+    terms = refs[1:-nz]
+    chunks = [terms[i:i + ny] for i in range(0, len(terms), ny)]
+    each = nz // len(chunks)
+    for t in range(nz):
+        parts = [x[t % each] for x in chunks[t // each]]
+        total = functools.reduce(jnp.add, parts)
+        for r in range(nz):
+            @pl.when((where[1] ^ t) == r)
+            def _():
+                outs[r][...] = total
+
+
+def cut(where, chunks):
+    ny = len(chunks[0])
+    each, q, rank = chunks[0][0].shape
+    nz = each * len(chunks)
+    return pl.pallas_call(
+        functools.partial(cut_kernel, ny, nz),
+        in_specs=[SMEM] + [VMEM] * (ny * len(chunks)),
+        out_specs=[VMEM] * nz,
+        out_shape=[jax.ShapeDtypeStruct((q, rank), F32)] * nz,
+        compiler_params=params(8),
+        name="cut",
+    )(where, *[x for c in chunks for x in c])
+
+
+def join_kernel(nz, *refs):
+    where, pieces, outs = refs[0], refs[1:1 + nz], refs[1 + nz:]
+    each = nz // len(outs)
+    if each == nz:
+        for r in range(nz):
+            outs[0][where[1] ^ r] = pieces[r][...]
+        return
+    for t in range(nz):
+        for r in range(nz):
+            @pl.when((where[1] ^ t) == r)
+            def _():
+                outs[t // each][t % each] = pieces[r][...]
+
+
+def join(where, pieces, chunks):
+    nz = len(pieces)
+    shape = (nz // chunks,) + pieces[0].shape
+    return pl.pallas_call(
+        functools.partial(join_kernel, nz),
+        in_specs=[SMEM] + [VMEM] * nz,
+        out_specs=[VMEM] * chunks,
+        out_shape=[jax.ShapeDtypeStruct(shape, F32)] * chunks,
+        compiler_params=params(8),
+        name="join",
+    )(where, *pieces)
+
+
+def pick_kernel(cut, *refs):
+    where, olds, out = refs[0], refs[1:-1], refs[-1]
+    for c in range(len(olds)):
+        @pl.when(lax.div(where[1], cut) == c)
+        def _():
+            out[...] = olds[c][...]
+
+
+def pick(where, olds, cut):
+    return pl.pallas_call(
+        functools.partial(pick_kernel, cut),
+        in_specs=[SMEM] + [VMEM] * len(olds),
+        out_specs=VMEM,
+        out_shape=jax.ShapeDtypeStruct(olds[0].shape, F32),
+        compiler_params=params(8),
+        name="pick",
+    )(where, *olds)
+
+
 def new_rows(old, terms):
-    return old + 0.005 * (jnp.sum(terms, axis=0) - 0.05 * old)
+    total = functools.reduce(jnp.add, terms)
+    return old + 0.005 * (total - 0.05 * old)
 
 
 def per_device(n_group, n_sub, users, items, ratings, occupancy):
     strata = ratings.shape[0]
     share, rank = items.shape
     ny = 1
-    while ny * ny * 4 <= n_sub:
+    while ny * ny * 2 <= n_sub:
         ny *= 2
     nz = n_sub // ny
     chunks = max(1, min(CHUNKS, share // 8))
     k = lax.axis_index("sub")
-    where = jnp.stack([k % ny, k // ny]).astype(jnp.int32)
-    lines = [[z * ny + y for z in range(nz)] for y in range(ny)]
+    where = jnp.stack([k & (ny - 1), k >> (ny.bit_length() - 1)]).astype(jnp.int32)
 
     def over_y(x, r):
         return lax.ppermute(x, "sub", [(i, i ^ r) for i in range(n_sub)])
 
-    def over_z(x):
-        return lax.all_to_all(x, "sub", 0, 0, axis_index_groups=lines)
-
-    def gather_z(x):
-        return over_z(jnp.broadcast_to(x, (nz,) + x.shape))
+    def over_z(x, r):
+        return lax.ppermute(x, "sub", [(i, i ^ (r * ny)) for i in range(n_sub)])
 
     def onward(x, r):
         route = []
         for g in range(n_group):
             for i in range(n_sub):
-                route.append((g * n_sub + i, (g + 1) % n_group * n_sub + (i ^ r)))
+                route.append((g * n_sub + i, (g + 1) % n_group * n_sub + (i ^ (r * ny))))
         return lax.ppermute(x, ("group", "sub"), route)
 
     q = share // chunks
-    own = gather_z(items)
-    pieces = []
-    for c in range(chunks):
-        part = own[c * (nz // chunks):(c + 1) * (nz // chunks)]
-        pieces.append([part] + [over_y(part, r) for r in range(1, ny)])
+    owns = join(where, [items] + [over_z(items, r) for r in range(1, nz)], chunks)
+    pieces = [[own] + [over_y(own, r) for r in range(1, ny)] for own in owns]
 
     for s in range(strata):
         last = s == strata - 1
@@ -165,21 +233,18 @@
             res = gradients(where, occupancy, users, ratings, pieces[c], s, c, share if last else q)
             parts.append(res[:4])
             olds.append(res[4])
-            term = res[5]
-            for r in range(1, ny):
-                term = term + over_y(res[5 + r], r)
-            grads.append(term)
+            grads.append([res[5]] + [over_y(res[5 + r], r) for r in range(1, ny)])
         new_users = user_step(users, parts)
         if last:
-            old = olds[0]
-            for c in range(1, chunks):
-                old = jnp.where(where[1] // (nz // chunks) == c, olds[c], old)
-            rows = new_rows(old, over_z(jnp.concatenate(grads)))
-            rows = lax.ppermute(rows, "group", [(g, (g + 1) % n_group) for g in range(n_group)])
+            old = onward(pick(where, olds, nz // chunks), 0)
+            cuts = cut(where, grads)
+            rows = new_rows(old, [onward(cuts[r], r) for r in range(nz)])
             return new_users, rows
         for c in range(chunks):
-            own = gather_z(new_rows(olds[c], over_z(grads[c])))
-            pieces[c] = [onward(own, r) for r in range(ny)]
+            cuts = cut(where, [grads[c]])
+            rows = new_rows(olds[c], [cuts[0]] + [over_z(cuts[r], r) for r in range(1, nz)])
+            own = join(where, [onward(rows, r) for r in range(nz)], 1)[0]
+            pieces[c] = [own] + [over_y(own, r) for r in range(1, ny)]
         users = new_users
 
 

time: 331 us -> 183 us (0.55)
  waiting for transfers between devices: 103 us -> 38.9 us
  local copies, waits for them, and re-layouts: 62.7 us -> 5.48 us
  blocking collectives: 20.6 us -> 0 us
  other arithmetic: 17.9 us -> 0.89 us
  starting transfers between devices: 81.3 us -> 89.3 us
  Pallas kernels: 41.6 us -> 47 us
    all_to_all x13 -> x0, starting transfers between devices: 56.7 us -> none  [over_z(): return lax.all_to_all(x, 'sub', 0, 0, axis_index_groups=lines)]
    all_to_all x13 -> x0, waiting for transfers between devices: 51.4 us -> none  [over_z(): return lax.all_to_all(x, 'sub', 0, 0, axis_index_groups=lines)]
    unnamed x142 -> x11, local copies, waits for them, and re-layouts: 56.3 us -> 5.48 us
    ppermute x10 -> x48, starting transfers between devices: 13 us -> 58.8 us  [over_y(): return lax.ppermute(x, 'sub', [(i, i ^ r) for i in range(n_sub)])]
    ppermute x10 -> x48, waiting for transfers between devices: 51.5 us -> 18.4 us  [over_y(): return lax.ppermute(x, 'sub', [(i, i ^ r) for i in range(n_sub)])]
    all_to_all x1 -> x0, blocking collectives: 20.6 us -> none  [over_z(): return lax.all_to_all(x, 'sub', 0, 0, axis_index_groups=lines)]
    ppermute x1 -> x7, starting transfers between devices: 0.06 us -> 15.2 us  [over_z(): return lax.ppermute(x, 'sub', [(i, i ^ r * ny) for i in range(n_sub)])]
    ppermute x1 -> x7, waiting for transfers between devices: 0.01 us -> 13.1 us  [over_z(): return lax.ppermute(x, 'sub', [(i, i ^ r * ny) for i in range(n_sub)])]
  transfers between devices with their start and end apart: 36 -> 70, of which waited for: 16 -> 25; matrix products, arithmetic and copies ran while one was open for 5% -> 1% of each run, Pallas kernels for 12% -> 25%
where the time goes in v3:
time: 183 us
  starting transfers between devices  89.3 us (49%)
  Pallas kernels  47 us (26%)
  waiting for transfers between devices  38.9 us (21%)
  local copies, waits for them, and re-layouts  5.48 us (3%)
    ppermute x48, starting transfers between devices, over_y(): return lax.ppermute(x, 'sub', [(i, i ^ r) for i in range(n_sub)])  58.8 us
    pallas_call x8, Pallas kernels, gradients(): pl.pallas_call(functools.partial(grad_kernel, ny, chunk, stratum), in_spe...  29.7 us
    ppermute x48, waiting for transfers between devices, over_y(): return lax.ppermute(x, 'sub', [(i, i ^ r) for i in range(n_sub)])  18.4 us
    ppermute x15, starting transfers between devices, onward(): return lax.ppermute(x, ('group', 'sub'), route)  15.4 us
    ppermute x7, starting transfers between devices, over_z(): return lax.ppermute(x, 'sub', [(i, i ^ r * ny) for i in range(n_sub)])  15.2 us
    ppermute x7, waiting for transfers between devices, over_z(): return lax.ppermute(x, 'sub', [(i, i ^ r * ny) for i in range(n_sub)])  13.1 us
    pallas_call x4, Pallas kernels, user_step(): pl.pallas_call(functools.partial(step_kernel, len(parts)), in_specs=[VMEM...  8.72 us
    ppermute x15, waiting for transfers between devices, onward(): return lax.ppermute(x, ('group', 'sub'), route)  7.4 us
  transfers between devices with their start and end apart: 70, of which 25 were waited for; matrix products, arithmetic and copies ran while one was open for 1% of the time, Pallas kernels for 25%

profile of v3, /device:TPU:0, one launch (start us, length us, event | category | flops | bytes accessed | tf_op | source)
XLA Modules:
  0.0 182.6 jit_solution(10904666629808231976)
XLA Ops:
  0.6 4.1 %collective-permute-start = (f32[64,512]{1,0:T(8,128)}, f32[64,512]{1,0:T(8,128)S(1)}, u32[]{:S(2)}, u32[]{:S(2)}) collective-permute-start(f32[64,512]{1,0:T(8,128)} %refs_1_.9), channel_id=1, source_target_pairs={{0,4},{1,5},{2,6},{3,7},{4,0},{5,1},{6,2},{7,3},{8,12},{9,13},{10,... | collective-permute-start | bytes 393224 | tf_op jit(solution)/shard_map/ppermute | solution.py:216
  4.8 6.4 %collective-permute-done.refs_2_ = f32[64,512]{1,0:T(8,128)S(1)} collective-permute-done((f32[64,512]{1,0:T(8,128)}, f32[64,512]{1,0:T(8,128)S(1)}, u32[]{:S(2)}, u32[]{:S(2)}) %collective-permute-start) | collective-permute-done | bytes 131104 | tf_op jit(solution)/shard_map/ppermute | solution.py:216
  20.7 2.5 %collective-permute-done.6.refs_7_ = f32[1,64,512]{2,1,0:T(8,128)S(1)} collective-permute-done((f32[1,64,512]{2,1,0:T(8,128)S(1)}, f32[1,64,512]{2,1,0:T(8,128)S(1)}, u32[]{:S(2)}, u32[]{:S(2)}) %collective-permute-start.6) | collective-permute-done | bytes 131104 | tf_op jit(solution)/shard_map/ppermute | solution.py:213
  27.0 3.7 %gradients.9 = (bf16[1024,256]{1,0:T(8,128)(2,1)S(1)}, bf16[1024,256]{1,0:T(8,128)(2,1)S(1)}, bf16[256,512]{1,0:T(8,128)(2,1)S(1)}, bf16[256,512]{1,0:T(8,128)(2...) custom-call(s32[2]{0:T(128)S(1)} %pad_add_fusion.refs_0_, ...), custom_call_target="tpu_custom_call" | custom-call | flops 1610612736 | bytes 2097152 | tf_op jit(solution)/shard_map/gradients/pallas_call | solution.py:82
  34.2 3.7 %gradients.8 = (bf16[1024,256]{1,0:T(8,128)(2,1)S(1)}, bf16[1024,256]{1,0:T(8,128)(2,1)S(1)}, bf16[256,512]{1,0:T(8,128)(2,1)S(1)}, bf16[256,512]{1,0:T(8,128)(2...) custom-call(s32[2]{0:T(128)S(1)} %pad_add_fusion.refs_0_, ...), custom_call_target="tpu_custom_call" | custom-call | flops 1610612736 | bytes 2097152 | tf_op jit(solution)/shard_map/gradients/pallas_call | solution.py:82
  42.1 2.7 %collective-permute-start.19 = (f32[32,512]{1,0:T(8,128)S(1)}, f32[32,512]{1,0:T(8,128)S(1)}, u32[]{:S(2)}, u32[]{:S(2)}) collective-permute-start(f32[32,512]{1,0:T(8,128)S(1)} %get-tuple-element.117), channel_id=1, source_target_pairs={{0,4},{1,5},{2,6},{3,7},{4,0},{5,1},{6,2},{7,3},{8,12},{9,13},{10,... | collective-permute-start | bytes 196616 | tf_op jit(solution)/shard_map/ppermute | solution.py:216
  47.1 3.7 %collective-permute-start.10 = (f32[32,512]{1,0:T(8,128)S(1)}, f32[32,512]{1,0:T(8,128)S(1)}, u32[]{:S(2)}, u32[]{:S(2)}) collective-permute-start(f32[32,512]{1,0:T(8,128)S(1)} %get-tuple-element.106), channel_id=1, source_target_pairs={{0,4},{1,5},{2,6},{3,7},{4,0},{5,1},{6,2},{7,3},{8,12},{9,13},{10,... | collective-permute-start | bytes 196616 | tf_op jit(solution)/shard_map/ppermute | solution.py:216
  53.9 4.2 %collective-permute-start.12 = (f32[32,512]{1,0:T(8,128)S(1)}, f32[32,512]{1,0:T(8,128)S(1)}, u32[]{:S(2)}, u32[]{:S(2)}) collective-permute-start(f32[32,512]{1,0:T(8,128)S(1)} %multiply_add_fusion.6), channel_id=1, source_target_pairs={{0,12},{1,13},{2,14},{3,15},{4,8},{5,9},{6,10},{7,11},{8,20},{9,21... | collective-permute-start | bytes 196616 | tf_op jit(solution)/shard_map/ppermute | solution.py:223
  59.5 3.5 %collective-permute-start.23 = (f32[2,32,512]{2,1,0:T(8,128)S(1)}, f32[2,32,512]{2,1,0:T(8,128)S(1)}, u32[]{:S(2)}, u32[]{:S(2)}) collective-permute-start(f32[2,32,512]{2,1,0:T(8,128)S(1)} %join.9.refs_4_), channel_id=1, source_target_pairs={{0,2},{1,3},{2,0},{3,1},{4,6},{5,7},{6,4},{7,5},{8,10},{9,11},{10,... | collective-permute-start | bytes 393224 | tf_op jit(solution)/shard_map/ppermute | solution.py:213
  69.2 3.7 %gradients.11 = (bf16[1024,256]{1,0:T(8,128)(2,1)S(1)}, bf16[1024,256]{1,0:T(8,128)(2,1)S(1)}, bf16[256,512]{1,0:T(8,128)(2,1)S(1)}, bf16[256,512]{1,0:T(8,128)(...) custom-call(s32[2]{0:T(128)S(1)} %pad_add_fusion.refs_0_, ...), custom_call_target="tpu_custom_call" | custom-call | flops 1610612736 | bytes 2097152 | tf_op jit(solution)/shard_map/gradients/pallas_call | solution.py:82
  76.7 3.7 %gradients.10 = (bf16[1024,256]{1,0:T(8,128)(2,1)S(1)}, bf16[1024,256]{1,0:T(8,128)(2,1)S(1)}, bf16[256,512]{1,0:T(8,128)(2,1)S(1)}, bf16[256,512]{1,0:T(8,128)(...) custom-call(s32[2]{0:T(128)S(1)} %pad_add_fusion.refs_0_, ...), custom_call_target="tpu_custom_call" | custom-call | flops 1610612736 | bytes 2097152 | tf_op jit(solution)/shard_map/gradients/pallas_call | solution.py:82
  93.5 2.8 %collective-permute-done.28 = f32[32,512]{1,0:T(8,128)S(1)} collective-permute-done((f32[32,512]{1,0:T(8,128)S(1)}, f32[32,512]{1,0:T(8,128)S(1)}, u32[]{:S(2)}, u32[]{:S(2)}) %collective-permute-start.28) | collective-permute-done | bytes 65568 | tf_op jit(solution)/shard_map/ppermute | solution.py:216
  97.8 3.2 %collective-permute-start.40 = (f32[2,32,512]{2,1,0:T(8,128)S(1)}, f32[2,32,512]{2,1,0:T(8,128)S(1)}, u32[]{:S(2)}, u32[]{:S(2)}) collective-permute-start(f32[2,32,512]{2,1,0:T(8,128)S(1)} %join.11.refs_4_), channel_id=1, source_target_pairs={{0,1},{1,0},{2,3},{3,2},{4,5},{5,4},{6,7},{7,6},{8,9},{9,8},{10,11... | collective-permute-start | bytes 393224 | tf_op jit(solution)/shard_map/ppermute | solution.py:213
  109.6 3.7 %gradients.13 = (bf16[1024,256]{1,0:T(8,128)(2,1)S(1)}, bf16[1024,256]{1,0:T(8,128)(2,1)S(1)}, bf16[256,512]{1,0:T(8,128)(2,1)S(1)}, bf16[256,512]{1,0:T(8,128)(...) custom-call(s32[2]{0:T(128)S(1)} %pad_add_fusion.refs_0_, ...), custom_call_target="tpu_custom_call" | custom-call | flops 1610612736 | bytes 2097152 | tf_op jit(solution)/shard_map/gradients/pallas_call | solution.py:82
  114.6 2.2 %collective-permute-start.54 = (f32[2,32,512]{2,1,0:T(8,128)S(1)}, f32[2,32,512]{2,1,0:T(8,128)S(1)}, u32[]{:S(2)}, u32[]{:S(2)}) collective-permute-start(f32[2,32,512]{2,1,0:T(8,128)S(1)} %get-tuple-element.159), channel_id=1, source_target_pairs={{0,3},{1,2},{2,1},{3,0},{4,7},{5,6},{6,5},{7,4},{8,11},{9,10},{10,... | collective-permute-start | bytes 393224 | tf_op jit(solution)/shard_map/ppermute | solution.py:213
  116.9 3.7 %gradients.12 = (bf16[1024,256]{1,0:T(8,128)(2,1)S(1)}, bf16[1024,256]{1,0:T(8,128)(2,1)S(1)}, bf16[256,512]{1,0:T(8,128)(2,1)S(1)}, bf16[256,512]{1,0:T(8,128)(...) custom-call(s32[2]{0:T(128)S(1)} %pad_add_fusion.refs_0_, ...), custom_call_target="tpu_custom_call" | custom-call | flops 1610612736 | bytes 2097152 | tf_op jit(solution)/shard_map/gradients/pallas_call | solution.py:82
  121.9 2.2 %collective-permute-start.45 = (f32[2,32,512]{2,1,0:T(8,128)S(1)}, f32[2,32,512]{2,1,0:T(8,128)S(1)}, u32[]{:S(2)}, u32[]{:S(2)}) collective-permute-start(f32[2,32,512]{2,1,0:T(8,128)S(1)} %get-tuple-element.148), channel_id=1, source_target_pairs={{0,3},{1,2},{2,1},{3,0},{4,7},{5,6},{6,5},{7,4},{8,11},{9,10},{10,... | collective-permute-start | bytes 393224 | tf_op jit(solution)/shard_map/ppermute | solution.py:213
  131.9 2.5 %collective-permute-start.57 = (f32[32,512]{1,0:T(8,128)S(1)}, f32[32,512]{1,0:T(8,128)S(1)}, u32[]{:S(2)}, u32[]{:S(2)}) collective-permute-start(f32[32,512]{1,0:T(8,128)S(1)} %multiply_add_fusion.1), channel_id=1, source_target_pairs={{0,12},{1,13},{2,14},{3,15},{4,8},{5,9},{6,10},{7,11},{8,20},{9,21... | collective-permute-start | bytes 196616 | tf_op jit(solution)/shard_map/ppermute | solution.py:223
  135.6 4.0 %collective-permute-start.48 = (f32[32,512]{1,0:T(8,128)S(1)}, f32[32,512]{1,0:T(8,128)S(1)}, u32[]{:S(2)}, u32[]{:S(2)}) collective-permute-start(f32[32,512]{1,0:T(8,128)S(1)} %multiply_add_fusion.2), channel_id=1, source_target_pairs={{0,12},{1,13},{2,14},{3,15},{4,8},{5,9},{6,10},{7,11},{8,20},{9,21... | collective-permute-start | bytes 196616 | tf_op jit(solution)/shard_map/ppermute | solution.py:223
  141.4 2.8 %collective-permute-start.59 = (f32[2,32,512]{2,1,0:T(8,128)S(1)}, f32[2,32,512]{2,1,0:T(8,128)S(1)}, u32[]{:S(2)}, u32[]{:S(2)}) collective-permute-start(f32[2,32,512]{2,1,0:T(8,128)S(1)} %join.13.refs_4_), channel_id=1, source_target_pairs={{0,2},{1,3},{2,0},{3,1},{4,6},{5,7},{6,4},{7,5},{8,10},{9,11},{10,... | collective-permute-start | bytes 393224 | tf_op jit(solution)/shard_map/ppermute | solution.py:213
  151.9 3.7 %gradients.15 = (bf16[1024,256]{1,0:T(8,128)(2,1)S(1)}, bf16[1024,256]{1,0:T(8,128)(2,1)S(1)}, bf16[256,512]{1,0:T(8,128)(2,1)S(1)}, bf16[256,512]{1,0:T(8,128)(...) custom-call(s32[2]{0:T(128)S(1)} %pad_add_fusion.refs_0_, ...), custom_call_target="tpu_custom_call" | custom-call | flops 1610612736 | bytes 2097152 | tf_op jit(solution)/shard_map/gradients/pallas_call | solution.py:82
  159.2 3.7 %gradients.14 = (bf16[1024,256]{1,0:T(8,128)(2,1)S(1)}, bf16[1024,256]{1,0:T(8,128)(2,1)S(1)}, bf16[256,512]{1,0:T(8,128)(2,1)S(1)}, bf16[256,512]{1,0:T(8,128)(...) custom-call(s32[2]{0:T(128)S(1)} %pad_add_fusion.refs_0_, ...), custom_call_target="tpu_custom_call" | custom-call | flops 1610612736 | bytes 2097152 | tf_op jit(solution)/shard_map/gradients/pallas_call | solution.py:82
  172.4 3.2 %user_step.7 = f32[1024,512]{1,0:T(8,128)} custom-call(f32[1024,512]{1,0:T(8,128)S(1)} %user_step.6.refs_2_.refs_0_, bf16[1024,256]{1,0:T(8,128)(2,1)S(1)} %get-tuple-element.151.refs_1_, bf16[1024,256]{1,0:T(8,128)(2,1)S(1)} %get-tuple-element.152.refs_2_, bf16[256,512]{1,0:T(8,128)(2,1)S(1)} %get-tuple-element.153.refs_3_, ...), custom_call_target="tpu_custom_call" | custom-call | flops 1610612736 | bytes 4194304 | tf_op jit(solution)/shard_map/user_step/pallas_call | solution.py:111
  176.2 5.7 %collective-permute-done.69 = f32[64,512]{1,0:T(8,128)S(1)} collective-permute-done((f32[64,512]{1,0:T(8,128)S(1)}, f32[64,512]{1,0:T(8,128)S(1)}, u32[]{:S(2)}, u32[]{:S(2)}) %collective-permute-start.69) | collective-permute-done | bytes 131104 | tf_op jit(solution)/shard_map/ppermute | solution.py:223
  (162 shorter events, 96.1 us)
Async XLA Ops:
  0.6 10.6 %collective-permute-start = (f32[64,512]{1,0:T(8,128)}, f32[64,512]{1,0:T(8,128)S(1)}, u32[]{:S(2)}, u32[]{:S(2)}) collective-permute-start(f32[64,512]{1,0:T(8,128)} %refs_1_.9), channel_id=1, source_target_pairs={{0,4},{1,5},{2,6},{3,7},{4,0},{5,1},{6,2},{7,3},{8,12},{9,13},{10,... | collective-permute-start | bytes 393224 | tf_op jit(solution)/shard_map/ppermute | solution.py:216
  17.1 16.3 %collective-permute-start.1 = (f32[1,64,512]{2,1,0:T(8,128)S(1)}, f32[1,64,512]{2,1,0:T(8,128)S(1)}, u32[]{:S(2)}, u32[]{:S(2)}) collective-permute-start(f32[1,64,512]{2,1,0:T(8,128)S(1)} %get-tuple-element.90.refs_4_), channel_id=1, source_target_pairs={{0,1},{1,0},{2,3},{3,2},{4,5},{5,4},{6,7},{7,6},{8,9},{9,8},{10,11... | collective-permute-start | bytes 393224 | tf_op jit(solution)/shard_map/ppermute | solution.py:213
  18.7 15.6 %collective-permute-start.2 = (f32[1,64,512]{2,1,0:T(8,128)S(1)}, f32[1,64,512]{2,1,0:T(8,128)S(1)}, u32[]{:S(2)}, u32[]{:S(2)}) collective-permute-start(f32[1,64,512]{2,1,0:T(8,128)S(1)} %get-tuple-element.90.refs_4_), channel_id=1, source_target_pairs={{0,2},{1,3},{2,0},{3,1},{4,6},{5,7},{6,4},{7,5},{8,10},{9,11},{10,... | collective-permute-start | bytes 393224 | tf_op jit(solution)/shard_map/ppermute | solution.py:213
  19.4 14.8 %collective-permute-start.3 = (f32[1,64,512]{2,1,0:T(8,128)S(1)}, f32[1,64,512]{2,1,0:T(8,128)S(1)}, u32[]{:S(2)}, u32[]{:S(2)}) collective-permute-start(f32[1,64,512]{2,1,0:T(8,128)S(1)} %get-tuple-element.90.refs_4_), channel_id=1, source_target_pairs={{0,3},{1,2},{2,1},{3,0},{4,7},{5,6},{6,5},{7,4},{8,11},{9,10},{10,... | collective-permute-start | bytes 393224 | tf_op jit(solution)/shard_map/ppermute | solution.py:213
  30.7 10.0 %collective-permute-start.16 = (f32[2,32,512]{2,1,0:T(8,128)S(1)}, f32[2,32,512]{2,1,0:T(8,128)S(1)}, u32[]{:S(2)}, u32[]{:S(2)}) collective-permute-start(f32[2,32,512]{2,1,0:T(8,128)S(1)} %get-tuple-element.113), channel_id=1, source_target_pairs={{0,1},{1,0},{2,3},{3,2},{4,5},{5,4},{6,7},{7,6},{8,9},{9,8},{10,11... | collective-permute-start | bytes 393224 | tf_op jit(solution)/shard_map/ppermute | solution.py:213
  53.8 11.0 %collective-permute-start.11 = (f32[32,512]{1,0:T(8,128)S(1)}, f32[32,512]{1,0:T(8,128)S(1)}, u32[]{:S(2)}, u32[]{:S(2)}) collective-permute-start(f32[32,512]{1,0:T(8,128)S(1)} %multiply_add_fusion.6), channel_id=1, source_target_pairs={{0,8},{1,9},{2,10},{3,11},{4,12},{5,13},{6,14},{7,15},{8,16},{9,17... | collective-permute-start | bytes 196616 | tf_op jit(solution)/shard_map/ppermute | solution.py:223
  53.9 10.9 %collective-permute-start.12 = (f32[32,512]{1,0:T(8,128)S(1)}, f32[32,512]{1,0:T(8,128)S(1)}, u32[]{:S(2)}, u32[]{:S(2)}) collective-permute-start(f32[32,512]{1,0:T(8,128)S(1)} %multiply_add_fusion.6), channel_id=1, source_target_pairs={{0,12},{1,13},{2,14},{3,15},{4,8},{5,9},{6,10},{7,11},{8,20},{9,21... | collective-permute-start | bytes 196616 | tf_op jit(solution)/shard_map/ppermute | solution.py:223
  59.0 9.9 %collective-permute-start.22 = (f32[2,32,512]{2,1,0:T(8,128)S(1)}, f32[2,32,512]{2,1,0:T(8,128)S(1)}, u32[]{:S(2)}, u32[]{:S(2)}) collective-permute-start(f32[2,32,512]{2,1,0:T(8,128)S(1)} %join.9.refs_4_), channel_id=1, source_target_pairs={{0,1},{1,0},{2,3},{3,2},{4,5},{5,4},{6,7},{7,6},{8,9},{9,8},{10,11... | collective-permute-start | bytes 393224 | tf_op jit(solution)/shard_map/ppermute | solution.py:213
  65.4 11.3 %collective-permute-start.13 = (f32[2,32,512]{2,1,0:T(8,128)S(1)}, f32[2,32,512]{2,1,0:T(8,128)S(1)}, u32[]{:S(2)}, u32[]{:S(2)}) collective-permute-start(f32[2,32,512]{2,1,0:T(8,128)S(1)} %join.8.refs_4_), channel_id=1, source_target_pairs={{0,1},{1,0},{2,3},{3,2},{4,5},{5,4},{6,7},{7,6},{8,9},{9,8},{10,11... | collective-permute-start | bytes 393224 | tf_op jit(solution)/shard_map/ppermute | solution.py:213
  66.9 9.8 %collective-permute-start.14 = (f32[2,32,512]{2,1,0:T(8,128)S(1)}, f32[2,32,512]{2,1,0:T(8,128)S(1)}, u32[]{:S(2)}, u32[]{:S(2)}) collective-permute-start(f32[2,32,512]{2,1,0:T(8,128)S(1)} %join.8.refs_4_), channel_id=1, source_target_pairs={{0,2},{1,3},{2,0},{3,1},{4,6},{5,7},{6,4},{7,5},{8,10},{9,11},{10,... | collective-permute-start | bytes 393224 | tf_op jit(solution)/shard_map/ppermute | solution.py:213
  72.9 11.0 %collective-permute-start.34 = (f32[2,32,512]{2,1,0:T(8,128)S(1)}, f32[2,32,512]{2,1,0:T(8,128)S(1)}, u32[]{:S(2)}, u32[]{:S(2)}) collective-permute-start(f32[2,32,512]{2,1,0:T(8,128)S(1)} %get-tuple-element.135), channel_id=1, source_target_pairs={{0,1},{1,0},{2,3},{3,2},{4,5},{5,4},{6,7},{7,6},{8,9},{9,8},{10,11... | collective-permute-start | bytes 393224 | tf_op jit(solution)/shard_map/ppermute | solution.py:213
  105.0 9.7 %collective-permute-start.31 = (f32[2,32,512]{2,1,0:T(8,128)S(1)}, f32[2,32,512]{2,1,0:T(8,128)S(1)}, u32[]{:S(2)}, u32[]{:S(2)}) collective-permute-start(f32[2,32,512]{2,1,0:T(8,128)S(1)} %join.10.refs_4_), channel_id=1, source_target_pairs={{0,1},{1,0},{2,3},{3,2},{4,5},{5,4},{6,7},{7,6},{8,9},{9,8},{10,11... | collective-permute-start | bytes 393224 | tf_op jit(solution)/shard_map/ppermute | solution.py:213
  107.0 9.9 %collective-permute-start.32 = (f32[2,32,512]{2,1,0:T(8,128)S(1)}, f32[2,32,512]{2,1,0:T(8,128)S(1)}, u32[]{:S(2)}, u32[]{:S(2)}) collective-permute-start(f32[2,32,512]{2,1,0:T(8,128)S(1)} %join.10.refs_4_), channel_id=1, source_target_pairs={{0,2},{1,3},{2,0},{3,1},{4,6},{5,7},{6,4},{7,5},{8,10},{9,11},{10,... | collective-permute-start | bytes 393224 | tf_op jit(solution)/shard_map/ppermute | solution.py:213
  107.0 9.9 %collective-permute-start.33 = (f32[2,32,512]{2,1,0:T(8,128)S(1)}, f32[2,32,512]{2,1,0:T(8,128)S(1)}, u32[]{:S(2)}, u32[]{:S(2)}) collective-permute-start(f32[2,32,512]{2,1,0:T(8,128)S(1)} %join.10.refs_4_), channel_id=1, source_target_pairs={{0,3},{1,2},{2,1},{3,0},{4,7},{5,6},{6,5},{7,4},{8,11},{9,10},{10,... | collective-permute-start | bytes 393224 | tf_op jit(solution)/shard_map/ppermute | solution.py:213
  114.3 9.8 %collective-permute-start.53 = (f32[2,32,512]{2,1,0:T(8,128)S(1)}, f32[2,32,512]{2,1,0:T(8,128)S(1)}, u32[]{:S(2)}, u32[]{:S(2)}) collective-permute-start(f32[2,32,512]{2,1,0:T(8,128)S(1)} %get-tuple-element.158), channel_id=1, source_target_pairs={{0,2},{1,3},{2,0},{3,1},{4,6},{5,7},{6,4},{7,5},{8,10},{9,11},{10,... | collective-permute-start | bytes 393224 | tf_op jit(solution)/shard_map/ppermute | solution.py:213
  114.6 9.5 %collective-permute-start.54 = (f32[2,32,512]{2,1,0:T(8,128)S(1)}, f32[2,32,512]{2,1,0:T(8,128)S(1)}, u32[]{:S(2)}, u32[]{:S(2)}) collective-permute-start(f32[2,32,512]{2,1,0:T(8,128)S(1)} %get-tuple-element.159), channel_id=1, source_target_pairs={{0,3},{1,2},{2,1},{3,0},{4,7},{5,6},{6,5},{7,4},{8,11},{9,10},{10,... | collective-permute-start | bytes 393224 | tf_op jit(solution)/shard_map/ppermute | solution.py:213
  135.5 10.6 %collective-permute-start.47 = (f32[32,512]{1,0:T(8,128)S(1)}, f32[32,512]{1,0:T(8,128)S(1)}, u32[]{:S(2)}, u32[]{:S(2)}) collective-permute-start(f32[32,512]{1,0:T(8,128)S(1)} %multiply_add_fusion.2), channel_id=1, source_target_pairs={{0,8},{1,9},{2,10},{3,11},{4,12},{5,13},{6,14},{7,15},{8,16},{9,17... | collective-permute-start | bytes 196616 | tf_op jit(solution)/shard_map/ppermute | solution.py:223
  135.6 10.5 %collective-permute-start.48 = (f32[32,512]{1,0:T(8,128)S(1)}, f32[32,512]{1,0:T(8,128)S(1)}, u32[]{:S(2)}, u32[]{:S(2)}) collective-permute-start(f32[32,512]{1,0:T(8,128)S(1)} %multiply_add_fusion.2), channel_id=1, source_target_pairs={{0,12},{1,13},{2,14},{3,15},{4,8},{5,9},{6,10},{7,11},{8,20},{9,21... | collective-permute-start | bytes 196616 | tf_op jit(solution)/shard_map/ppermute | solution.py:223
  140.4 9.8 %collective-permute-start.58 = (f32[2,32,512]{2,1,0:T(8,128)S(1)}, f32[2,32,512]{2,1,0:T(8,128)S(1)}, u32[]{:S(2)}, u32[]{:S(2)}) collective-permute-start(f32[2,32,512]{2,1,0:T(8,128)S(1)} %join.13.refs_4_), channel_id=1, source_target_pairs={{0,1},{1,0},{2,3},{3,2},{4,5},{5,4},{6,7},{7,6},{8,9},{9,8},{10,11... | collective-permute-start | bytes 393224 | tf_op jit(solution)/shard_map/ppermute | solution.py:213
  146.7 11.3 %collective-permute-start.49 = (f32[2,32,512]{2,1,0:T(8,128)S(1)}, f32[2,32,512]{2,1,0:T(8,128)S(1)}, u32[]{:S(2)}, u32[]{:S(2)}) collective-permute-start(f32[2,32,512]{2,1,0:T(8,128)S(1)} %join.12.refs_4_), channel_id=1, source_target_pairs={{0,1},{1,0},{2,3},{3,2},{4,5},{5,4},{6,7},{7,6},{8,9},{9,8},{10,11... | collective-permute-start | bytes 393224 | tf_op jit(solution)/shard_map/ppermute | solution.py:213
  148.2 11.0 %collective-permute-start.50 = (f32[2,32,512]{2,1,0:T(8,128)S(1)}, f32[2,32,512]{2,1,0:T(8,128)S(1)}, u32[]{:S(2)}, u32[]{:S(2)}) collective-permute-start(f32[2,32,512]{2,1,0:T(8,128)S(1)} %join.12.refs_4_), channel_id=1, source_target_pairs={{0,2},{1,3},{2,0},{3,1},{4,6},{5,7},{6,4},{7,5},{8,10},{9,11},{10,... | collective-permute-start | bytes 393224 | tf_op jit(solution)/shard_map/ppermute | solution.py:213
  155.6 9.6 %collective-permute-start.65 = (f32[1,64,512]{2,1,0:T(8,128)S(1)}, f32[1,64,512]{2,1,0:T(8,128)S(1)}, u32[]{:S(2)}, u32[]{:S(2)}) collective-permute-start(f32[1,64,512]{2,1,0:T(8,128)S(1)} %get-tuple-element.173), channel_id=1, source_target_pairs={{0,1},{1,0},{2,3},{3,2},{4,5},{5,4},{6,7},{7,6},{8,9},{9,8},{10,11... | collective-permute-start | bytes 393224 | tf_op jit(solution)/shard_map/ppermute | solution.py:213
  156.2 10.8 %collective-permute-start.66 = (f32[1,64,512]{2,1,0:T(8,128)S(1)}, f32[1,64,512]{2,1,0:T(8,128)S(1)}, u32[]{:S(2)}, u32[]{:S(2)}) collective-permute-start(f32[1,64,512]{2,1,0:T(8,128)S(1)} %get-tuple-element.174), channel_id=1, source_target_pairs={{0,2},{1,3},{2,0},{3,1},{4,6},{5,7},{6,4},{7,5},{8,10},{9,11},{10,... | collective-permute-start | bytes 393224 | tf_op jit(solution)/shard_map/ppermute | solution.py:213
  171.8 10.1 %collective-permute-start.69 = (f32[64,512]{1,0:T(8,128)S(1)}, f32[64,512]{1,0:T(8,128)S(1)}, u32[]{:S(2)}, u32[]{:S(2)}) collective-permute-start(f32[64,512]{1,0:T(8,128)S(1)} %get-tuple-element.177), channel_id=1, source_target_pairs={{0,12},{1,13},{2,14},{3,15},{4,8},{5,9},{6,10},{7,11},{8,20},{9,21... | collective-permute-start | bytes 393224 | tf_op jit(solution)/shard_map/ppermute | solution.py:223
  (51 other events, 370.8 us)

commit v4 on v3

--- a/solution.py
+++ b/solution.py
@@ -219,10 +219,10 @@
         route = []
         for g in range(n_group):
             for i in range(n_sub):
-                route.append((g * n_sub + i, (g + 1) % n_group * n_sub + (i ^ (r * ny))))
+                route.append((g * n_sub + i, (g + 1) % n_group * n_sub + (i ^ r)))
         return lax.ppermute(x, ("group", "sub"), route)
 
-    q = share // chunks
+    wide = nz * share // chunks
     owns = join(where, [items] + [over_z(items, r) for r in range(1, nz)], chunks)
     pieces = [[own] + [over_y(own, r) for r in range(1, ny)] for own in owns]
 
@@ -230,7 +230,7 @@
         last = s == strata - 1
         parts, grads, olds = [], [], []
         for c in range(chunks):
-            res = gradients(where, occupancy, users, ratings, pieces[c], s, c, share if last else q)
+            res = gradients(where, occupancy, users, ratings, pieces[c], s, c, share if last else wide)
             parts.append(res[:4])
             olds.append(res[4])
             grads.append([res[5]] + [over_y(res[5 + r], r) for r in range(1, ny)])
@@ -238,13 +238,14 @@
         if last:
             old = onward(pick(where, olds, nz // chunks), 0)
             cuts = cut(where, grads)
-            rows = new_rows(old, [onward(cuts[r], r) for r in range(nz)])
+            rows = new_rows(old, [onward(cuts[r], r * ny) for r in range(nz)])
             return new_users, rows
         for c in range(chunks):
-            cuts = cut(where, [grads[c]])
-            rows = new_rows(olds[c], [cuts[0]] + [over_z(cuts[r], r) for r in range(1, nz)])
-            own = join(where, [onward(rows, r) for r in range(nz)], 1)[0]
-            pieces[c] = [own] + [over_y(own, r) for r in range(1, ny)]
+            total = functools.reduce(jnp.add, grads[c])
+            for bit in range(1, nz.bit_length()):
+                total = total + over_z(total, 1 << (bit - 1))
+            rows = new_rows(olds[c].reshape(total.shape), [total])
+            pieces[c] = [onward(rows, r) for r in range(ny)]
         users = new_users
 
 

time: 183 us -> 188 us (1.027)
  waiting for transfers between devices: 38.9 us -> 65.6 us
  starting transfers between devices: 89.3 us -> 74.7 us
  Pallas kernels: 47 us -> 40.1 us
    ppermute x48 -> x30, starting transfers between devices: 58.8 us -> 38.2 us  [over_y(): return lax.ppermute(x, 'sub', [(i, i ^ r) for i in range(n_sub)])]
    ppermute x15 -> x27, waiting for transfers between devices: 7.4 us -> 27.6 us  [onward(): return lax.ppermute(x, ('group', 'sub'), route)]
    ppermute x7, waiting for transfers between devices: 13.1 us -> 21 us  [over_z(): return lax.ppermute(x, 'sub', [(i, i ^ r * ny) for i in range(n_sub)])]
    ppermute x15 -> x27, starting transfers between devices: 15.4 us -> 21.1 us  [onward(): return lax.ppermute(x, ('group', 'sub'), route)]
    pallas_call x7 -> x1, Pallas kernels: 4.12 us -> 0.61 us  [cut(): pl.pallas_call(functools.partial(cut_kernel, ny, nz), in_specs=[SMEM] + [...]
    pallas_call x7 -> x1, Pallas kernels: 3.9 us -> 0.58 us  [join(): pl.pallas_call(functools.partial(join_kernel, nz), in_specs=[SMEM] + [VME...]
    ppermute x48 -> x30, waiting for transfers between devices: 18.4 us -> 16.9 us  [over_y(): return lax.ppermute(x, 'sub', [(i, i ^ r) for i in range(n_sub)])]
  transfers between devices with their start and end apart: 70 -> 64, of which waited for: 25 -> 27; matrix products, arithmetic and copies ran while one was open for 1% -> 1% of each run, Pallas kernels for 25% -> 21%
where the time goes in v4:
time: 188 us
  starting transfers between devices  74.7 us (40%)
  waiting for transfers between devices  65.6 us (35%)
  Pallas kernels  40.1 us (21%)
  local copies, waits for them, and re-layouts  5.48 us (3%)
    ppermute x30, starting transfers between devices, over_y(): return lax.ppermute(x, 'sub', [(i, i ^ r) for i in range(n_sub)])  38.2 us
    pallas_call x8, Pallas kernels, gradients(): pl.pallas_call(functools.partial(grad_kernel, ny, chunk, stratum), in_spe...  29.7 us
    ppermute x27, waiting for transfers between devices, onward(): return lax.ppermute(x, ('group', 'sub'), route)  27.6 us
    ppermute x27, starting transfers between devices, onward(): return lax.ppermute(x, ('group', 'sub'), route)  21.1 us
    ppermute x7, waiting for transfers between devices, over_z(): return lax.ppermute(x, 'sub', [(i, i ^ r * ny) for i in range(n_sub)])  21 us
    ppermute x30, waiting for transfers between devices, over_y(): return lax.ppermute(x, 'sub', [(i, i ^ r) for i in range(n_sub)])  16.9 us
    ppermute x7, starting transfers between devices, over_z(): return lax.ppermute(x, 'sub', [(i, i ^ r * ny) for i in range(n_sub)])  15.4 us
    pallas_call x4, Pallas kernels, user_step(): pl.pallas_call(functools.partial(step_kernel, len(parts)), in_specs=[VMEM...  8.71 us
  transfers between devices with their start and end apart: 64, of which 27 were waited for; matrix products, arithmetic and copies ran while one was open for 1% of the time, Pallas kernels for 21%

profile of v4, /device:TPU:0, one launch (start us, length us, event | category | flops | bytes accessed | tf_op | source)
XLA Modules:
  0.0 188.1 jit_solution(8828448632882653463)
XLA Ops:
  0.6 4.1 %collective-permute-start = (f32[64,512]{1,0:T(8,128)}, f32[64,512]{1,0:T(8,128)S(1)}, u32[]{:S(2)}, u32[]{:S(2)}) collective-permute-start(f32[64,512]{1,0:T(8,128)} %refs_1_.9), channel_id=1, source_target_pairs={{0,4},{1,5},{2,6},{3,7},{4,0},{5,1},{6,2},{7,3},{8,12},{9,13},{10,... | collective-permute-start | bytes 393224 | tf_op jit(solution)/shard_map/ppermute | solution.py:216
  4.8 6.4 %collective-permute-done.refs_2_ = f32[64,512]{1,0:T(8,128)S(1)} collective-permute-done((f32[64,512]{1,0:T(8,128)}, f32[64,512]{1,0:T(8,128)S(1)}, u32[]{:S(2)}, u32[]{:S(2)}) %collective-permute-start) | collective-permute-done | bytes 131104 | tf_op jit(solution)/shard_map/ppermute | solution.py:216
  28.6 3.7 %gradients.9 = (bf16[1024,256]{1,0:T(8,128)(2,1)S(1)}, bf16[1024,256]{1,0:T(8,128)(2,1)S(1)}, bf16[256,512]{1,0:T(8,128)(2,1)S(1)}, bf16[256,512]{1,0:T(8,128)(2...) custom-call(s32[2]{0:T(128)S(1)} %pad_add_fusion.refs_0_, ...), custom_call_target="tpu_custom_call" | custom-call | flops 1610612736 | bytes 2097152 | tf_op jit(solution)/shard_map/gradients/pallas_call | solution.py:82
  33.6 3.7 %gradients.8 = (bf16[1024,256]{1,0:T(8,128)(2,1)S(1)}, bf16[1024,256]{1,0:T(8,128)(2,1)S(1)}, bf16[256,512]{1,0:T(8,128)(2,1)S(1)}, bf16[256,512]{1,0:T(8,128)(2...) custom-call(s32[2]{0:T(128)S(1)} %pad_add_fusion.refs_0_, ...), custom_call_target="tpu_custom_call" | custom-call | flops 1610612736 | bytes 2097152 | tf_op jit(solution)/shard_map/gradients/pallas_call | solution.py:82
  50.1 4.3 %collective-permute-start.18 = (f32[1,64,512]{2,1,0:T(8,128)S(1)}, f32[1,64,512]{2,1,0:T(8,128)S(1)}, u32[]{:S(2)}, u32[]{:S(2)}) collective-permute-start(f32[1,64,512]{2,1,0:T(8,128)S(1)} %add_add_fusion.4), channel_id=1, source_target_pairs={{0,4},{1,5},{2,6},{3,7},{4,0},{5,1},{6,2},{7,3},{8,12},{9,13},{10,... | collective-permute-start | bytes 393224 | tf_op jit(solution)/shard_map/ppermute | solution.py:216
  54.4 3.9 %collective-permute-done.10 = f32[1,64,512]{2,1,0:T(8,128)S(1)} collective-permute-done((f32[1,64,512]{2,1,0:T(8,128)S(1)}, f32[1,64,512]{2,1,0:T(8,128)S(1)}, u32[]{:S(2)}, u32[]{:S(2)}) %collective-permute-start.10) | collective-permute-done | bytes 131104 | tf_op jit(solution)/shard_map/ppermute | solution.py:216
  59.3 3.3 %collective-permute-start.11 = (f32[1,64,512]{2,1,0:T(8,128)S(1)}, f32[1,64,512]{2,1,0:T(8,128)S(1)}, u32[]{:S(2)}, u32[]{:S(2)}) collective-permute-start(f32[1,64,512]{2,1,0:T(8,128)S(1)} %fusion.11), channel_id=1, source_target_pairs={{0,8},{1,9},{2,10},{3,11},{4,12},{5,13},{6,14},{7,15},{8,16},{9,17... | collective-permute-start | bytes 393224 | tf_op jit(solution)/shard_map/ppermute | solution.py:223
  67.9 3.9 %collective-permute-done.11.refs_4_ = f32[1,64,512]{2,1,0:T(8,128)S(1)} collective-permute-done((f32[1,64,512]{2,1,0:T(8,128)S(1)}, f32[1,64,512]{2,1,0:T(8,128)S(1)}, u32[]{:S(2)}, u32[]{:S(2)}) %collective-permute-start.11) | collective-permute-done | bytes 131104 | tf_op jit(solution)/shard_map/ppermute | solution.py:223
  71.9 3.7 %gradients.10 = (bf16[1024,256]{1,0:T(8,128)(2,1)S(1)}, bf16[1024,256]{1,0:T(8,128)(2,1)S(1)}, bf16[256,512]{1,0:T(8,128)(2,1)S(1)}, bf16[256,512]{1,0:T(8,128)(...) custom-call(s32[2]{0:T(128)S(1)} %pad_add_fusion.refs_0_, ...), custom_call_target="tpu_custom_call" | custom-call | flops 1610612736 | bytes 2097152 | tf_op jit(solution)/shard_map/gradients/pallas_call | solution.py:82
  75.8 3.7 %gradients.11 = (bf16[1024,256]{1,0:T(8,128)(2,1)S(1)}, bf16[1024,256]{1,0:T(8,128)(2,1)S(1)}, bf16[256,512]{1,0:T(8,128)(2,1)S(1)}, bf16[256,512]{1,0:T(8,128)(...) custom-call(s32[2]{0:T(128)S(1)} %pad_add_fusion.refs_0_, ...), custom_call_target="tpu_custom_call" | custom-call | flops 1610612736 | bytes 2097152 | tf_op jit(solution)/shard_map/gradients/pallas_call | solution.py:82
  85.4 3.8 %collective-permute-start.25 = (f32[1,64,512]{2,1,0:T(8,128)S(1)}, f32[1,64,512]{2,1,0:T(8,128)S(1)}, u32[]{:S(2)}, u32[]{:S(2)}) collective-permute-start(f32[1,64,512]{2,1,0:T(8,128)S(1)} %get-tuple-element.110), channel_id=1, source_target_pairs={{0,3},{1,2},{2,1},{3,0},{4,7},{5,6},{6,5},{7,4},{8,11},{9,10},{10,... | collective-permute-start | bytes 393224 | tf_op jit(solution)/shard_map/ppermute | solution.py:213
  93.7 7.4 %collective-permute-done.34 = f32[1,64,512]{2,1,0:T(8,128)S(1)} collective-permute-done((f32[1,64,512]{2,1,0:T(8,128)S(1)}, f32[1,64,512]{2,1,0:T(8,128)S(1)}, u32[]{:S(2)}, u32[]{:S(2)}) %collective-permute-start.34) | collective-permute-done | bytes 131104 | tf_op jit(solution)/shard_map/ppermute | solution.py:216
  101.2 3.2 %collective-permute-start.37 = (f32[1,64,512]{2,1,0:T(8,128)S(1)}, f32[1,64,512]{2,1,0:T(8,128)S(1)}, u32[]{:S(2)}, u32[]{:S(2)}) collective-permute-start(f32[1,64,512]{2,1,0:T(8,128)S(1)} %fusion.5), channel_id=1, source_target_pairs={{0,10},{1,11},{2,8},{3,9},{4,14},{5,15},{6,12},{7,13},{8,18},{9,19... | collective-permute-start | bytes 393224 | tf_op jit(solution)/shard_map/ppermute | solution.py:223
  109.1 4.7 %collective-permute-done.36.refs_5_ = f32[1,64,512]{2,1,0:T(8,128)S(1)} collective-permute-done((f32[1,64,512]{2,1,0:T(8,128)S(1)}, f32[1,64,512]{2,1,0:T(8,128)S(1)}, u32[]{:S(2)}, u32[]{:S(2)}) %collective-permute-start.36) | collective-permute-done | bytes 131104 | tf_op jit(solution)/shard_map/ppermute | solution.py:223
  113.8 3.7 %gradients.13 = (bf16[1024,256]{1,0:T(8,128)(2,1)S(1)}, bf16[1024,256]{1,0:T(8,128)(2,1)S(1)}, bf16[256,512]{1,0:T(8,128)(2,1)S(1)}, bf16[256,512]{1,0:T(8,128)(...) custom-call(s32[2]{0:T(128)S(1)} %pad_add_fusion.refs_0_, ...), custom_call_target="tpu_custom_call" | custom-call | flops 1610612736 | bytes 2097152 | tf_op jit(solution)/shard_map/gradients/pallas_call | solution.py:82
  117.5 3.0 %collective-permute-start.47 = (f32[1,64,512]{2,1,0:T(8,128)S(1)}, f32[1,64,512]{2,1,0:T(8,128)S(1)}, u32[]{:S(2)}, u32[]{:S(2)}) collective-permute-start(f32[1,64,512]{2,1,0:T(8,128)S(1)} %get-tuple-element.135), channel_id=1, source_target_pairs={{0,1},{1,0},{2,3},{3,2},{4,5},{5,4},{6,7},{7,6},{8,9},{9,8},{10,11... | collective-permute-start | bytes 393224 | tf_op jit(solution)/shard_map/ppermute | solution.py:213
  120.6 3.7 %gradients.12 = (bf16[1024,256]{1,0:T(8,128)(2,1)S(1)}, bf16[1024,256]{1,0:T(8,128)(2,1)S(1)}, bf16[256,512]{1,0:T(8,128)(2,1)S(1)}, bf16[256,512]{1,0:T(8,128)(...) custom-call(s32[2]{0:T(128)S(1)} %pad_add_fusion.refs_0_, ...), custom_call_target="tpu_custom_call" | custom-call | flops 1610612736 | bytes 2097152 | tf_op jit(solution)/shard_map/gradients/pallas_call | solution.py:82
  138.8 3.3 %collective-permute-done.42 = f32[1,64,512]{2,1,0:T(8,128)S(1)} collective-permute-done((f32[1,64,512]{2,1,0:T(8,128)S(1)}, f32[1,64,512]{2,1,0:T(8,128)S(1)}, u32[]{:S(2)}, u32[]{:S(2)}) %collective-permute-start.42) | collective-permute-done | bytes 131104 | tf_op jit(solution)/shard_map/ppermute | solution.py:216
  142.2 6.4 %collective-permute-start.45 = (f32[1,64,512]{2,1,0:T(8,128)S(1)}, f32[1,64,512]{2,1,0:T(8,128)S(1)}, u32[]{:S(2)}, u32[]{:S(2)}) collective-permute-start(f32[1,64,512]{2,1,0:T(8,128)S(1)} %fusion.3), channel_id=1, source_target_pairs={{0,10},{1,11},{2,8},{3,9},{4,14},{5,15},{6,12},{7,13},{8,18},{9,19... | collective-permute-start | bytes 393224 | tf_op jit(solution)/shard_map/ppermute | solution.py:223
  153.2 3.5 %collective-permute-done.44.refs_5_ = f32[1,64,512]{2,1,0:T(8,128)S(1)} collective-permute-done((f32[1,64,512]{2,1,0:T(8,128)S(1)}, f32[1,64,512]{2,1,0:T(8,128)S(1)}, u32[]{:S(2)}, u32[]{:S(2)}) %collective-permute-start.44) | collective-permute-done | bytes 131104 | tf_op jit(solution)/shard_map/ppermute | solution.py:223
  158.2 3.7 %gradients.14 = (bf16[1024,256]{1,0:T(8,128)(2,1)S(1)}, bf16[1024,256]{1,0:T(8,128)(2,1)S(1)}, bf16[256,512]{1,0:T(8,128)(2,1)S(1)}, bf16[256,512]{1,0:T(8,128)(...) custom-call(s32[2]{0:T(128)S(1)} %pad_add_fusion.refs_0_, ...), custom_call_target="tpu_custom_call" | custom-call | flops 1610612736 | bytes 2097152 | tf_op jit(solution)/shard_map/gradients/pallas_call | solution.py:82
  165.4 3.7 %gradients.15 = (bf16[1024,256]{1,0:T(8,128)(2,1)S(1)}, bf16[1024,256]{1,0:T(8,128)(2,1)S(1)}, bf16[256,512]{1,0:T(8,128)(2,1)S(1)}, bf16[256,512]{1,0:T(8,128)(...) custom-call(s32[2]{0:T(128)S(1)} %pad_add_fusion.refs_0_, ...), custom_call_target="tpu_custom_call" | custom-call | flops 1610612736 | bytes 2097152 | tf_op jit(solution)/shard_map/gradients/pallas_call | solution.py:82
  179.2 3.2 %user_step.7 = f32[1024,512]{1,0:T(8,128)} custom-call(f32[1024,512]{1,0:T(8,128)S(1)} %user_step.6.refs_2_.refs_0_, bf16[1024,256]{1,0:T(8,128)(2,1)S(1)} %get-tuple-element.129.refs_1_, bf16[1024,256]{1,0:T(8,128)(2,1)S(1)} %get-tuple-element.130.refs_2_, bf16[256,512]{1,0:T(8,128)(2,1)S(1)} %get-tuple-element.131.refs_3_, ...), custom_call_target="tpu_custom_call" | custom-call | flops 1610612736 | bytes 4194304 | tf_op jit(solution)/shard_map/user_step/pallas_call | solution.py:111
  182.3 5.1 %collective-permute-done.63 = f32[64,512]{1,0:T(8,128)S(1)} collective-permute-done((f32[64,512]{1,0:T(8,128)S(1)}, f32[64,512]{1,0:T(8,128)S(1)}, u32[]{:S(2)}, u32[]{:S(2)}) %collective-permute-start.63) | collective-permute-done | bytes 131104 | tf_op jit(solution)/shard_map/ppermute | solution.py:223
  (144 shorter events, 87.9 us)
Async XLA Ops:
  0.6 10.6 %collective-permute-start = (f32[64,512]{1,0:T(8,128)}, f32[64,512]{1,0:T(8,128)S(1)}, u32[]{:S(2)}, u32[]{:S(2)}) collective-permute-start(f32[64,512]{1,0:T(8,128)} %refs_1_.9), channel_id=1, source_target_pairs={{0,4},{1,5},{2,6},{3,7},{4,0},{5,1},{6,2},{7,3},{8,12},{9,13},{10,... | collective-permute-start | bytes 393224 | tf_op jit(solution)/shard_map/ppermute | solution.py:216
  17.1 16.5 %collective-permute-start.3 = (f32[1,64,512]{2,1,0:T(8,128)S(1)}, f32[1,64,512]{2,1,0:T(8,128)S(1)}, u32[]{:S(2)}, u32[]{:S(2)}) collective-permute-start(f32[1,64,512]{2,1,0:T(8,128)S(1)} %get-tuple-element.78.refs_4_), channel_id=1, source_target_pairs={{0,3},{1,2},{2,1},{3,0},{4,7},{5,6},{6,5},{7,4},{8,11},{9,10},{10,... | collective-permute-start | bytes 393224 | tf_op jit(solution)/shard_map/ppermute | solution.py:213
  18.9 14.7 %collective-permute-start.2 = (f32[1,64,512]{2,1,0:T(8,128)S(1)}, f32[1,64,512]{2,1,0:T(8,128)S(1)}, u32[]{:S(2)}, u32[]{:S(2)}) collective-permute-start(f32[1,64,512]{2,1,0:T(8,128)S(1)} %get-tuple-element.78.refs_4_), channel_id=1, source_target_pairs={{0,2},{1,3},{2,0},{3,1},{4,6},{5,7},{6,4},{7,5},{8,10},{9,11},{10,... | collective-permute-start | bytes 393224 | tf_op jit(solution)/shard_map/ppermute | solution.py:213
  20.2 13.4 %collective-permute-start.1 = (f32[1,64,512]{2,1,0:T(8,128)S(1)}, f32[1,64,512]{2,1,0:T(8,128)S(1)}, u32[]{:S(2)}, u32[]{:S(2)}) collective-permute-start(f32[1,64,512]{2,1,0:T(8,128)S(1)} %get-tuple-element.78.refs_4_), channel_id=1, source_target_pairs={{0,1},{1,0},{2,3},{3,2},{4,5},{5,4},{6,7},{7,6},{8,9},{9,8},{10,11... | collective-permute-start | bytes 393224 | tf_op jit(solution)/shard_map/ppermute | solution.py:213
  32.3 17.7 %collective-permute-start.15 = (f32[1,64,512]{2,1,0:T(8,128)S(1)}, f32[1,64,512]{2,1,0:T(8,128)S(1)}, u32[]{:S(2)}, u32[]{:S(2)}) collective-permute-start(f32[1,64,512]{2,1,0:T(8,128)S(1)} %get-tuple-element.99), channel_id=1, source_target_pairs={{0,1},{1,0},{2,3},{3,2},{4,5},{5,4},{6,7},{7,6},{8,9},{9,8},{10,11... | collective-permute-start | bytes 393224 | tf_op jit(solution)/shard_map/ppermute | solution.py:213
  33.2 16.9 %collective-permute-start.16 = (f32[1,64,512]{2,1,0:T(8,128)S(1)}, f32[1,64,512]{2,1,0:T(8,128)S(1)}, u32[]{:S(2)}, u32[]{:S(2)}) collective-permute-start(f32[1,64,512]{2,1,0:T(8,128)S(1)} %get-tuple-element.100), channel_id=1, source_target_pairs={{0,2},{1,3},{2,0},{3,1},{4,6},{5,7},{6,4},{7,5},{8,10},{9,11},{10,... | collective-permute-start | bytes 393224 | tf_op jit(solution)/shard_map/ppermute | solution.py:213
  50.1 12.5 %collective-permute-start.18 = (f32[1,64,512]{2,1,0:T(8,128)S(1)}, f32[1,64,512]{2,1,0:T(8,128)S(1)}, u32[]{:S(2)}, u32[]{:S(2)}) collective-permute-start(f32[1,64,512]{2,1,0:T(8,128)S(1)} %add_add_fusion.4), channel_id=1, source_target_pairs={{0,4},{1,5},{2,6},{3,7},{4,0},{5,1},{6,2},{7,3},{8,12},{9,13},{10,... | collective-permute-start | bytes 393224 | tf_op jit(solution)/shard_map/ppermute | solution.py:216
  59.3 12.6 %collective-permute-start.11 = (f32[1,64,512]{2,1,0:T(8,128)S(1)}, f32[1,64,512]{2,1,0:T(8,128)S(1)}, u32[]{:S(2)}, u32[]{:S(2)}) collective-permute-start(f32[1,64,512]{2,1,0:T(8,128)S(1)} %fusion.11), channel_id=1, source_target_pairs={{0,8},{1,9},{2,10},{3,11},{4,12},{5,13},{6,14},{7,15},{8,16},{9,17... | collective-permute-start | bytes 393224 | tf_op jit(solution)/shard_map/ppermute | solution.py:223
  62.6 13.1 %collective-permute-start.22 = (f32[1,64,512]{2,1,0:T(8,128)S(1)}, f32[1,64,512]{2,1,0:T(8,128)S(1)}, u32[]{:S(2)}, u32[]{:S(2)}) collective-permute-start(f32[1,64,512]{2,1,0:T(8,128)S(1)} %fusion.9), channel_id=1, source_target_pairs={{0,11},{1,10},{2,9},{3,8},{4,15},{5,14},{6,13},{7,12},{8,19},{9,18... | collective-permute-start | bytes 393224 | tf_op jit(solution)/shard_map/ppermute | solution.py:223
  64.7 11.1 %collective-permute-start.21 = (f32[1,64,512]{2,1,0:T(8,128)S(1)}, f32[1,64,512]{2,1,0:T(8,128)S(1)}, u32[]{:S(2)}, u32[]{:S(2)}) collective-permute-start(f32[1,64,512]{2,1,0:T(8,128)S(1)} %fusion.9), channel_id=1, source_target_pairs={{0,10},{1,11},{2,8},{3,9},{4,14},{5,15},{6,12},{7,13},{8,18},{9,19... | collective-permute-start | bytes 393224 | tf_op jit(solution)/shard_map/ppermute | solution.py:223
  75.6 15.1 %collective-permute-start.23 = (f32[1,64,512]{2,1,0:T(8,128)S(1)}, f32[1,64,512]{2,1,0:T(8,128)S(1)}, u32[]{:S(2)}, u32[]{:S(2)}) collective-permute-start(f32[1,64,512]{2,1,0:T(8,128)S(1)} %get-tuple-element.108), channel_id=1, source_target_pairs={{0,1},{1,0},{2,3},{3,2},{4,5},{5,4},{6,7},{7,6},{8,9},{9,8},{10,11... | collective-permute-start | bytes 393224 | tf_op jit(solution)/shard_map/ppermute | solution.py:213
  75.7 15.0 %collective-permute-start.24 = (f32[1,64,512]{2,1,0:T(8,128)S(1)}, f32[1,64,512]{2,1,0:T(8,128)S(1)}, u32[]{:S(2)}, u32[]{:S(2)}) collective-permute-start(f32[1,64,512]{2,1,0:T(8,128)S(1)} %get-tuple-element.109), channel_id=1, source_target_pairs={{0,2},{1,3},{2,0},{3,1},{4,6},{5,7},{6,4},{7,5},{8,10},{9,11},{10,... | collective-permute-start | bytes 393224 | tf_op jit(solution)/shard_map/ppermute | solution.py:213
  90.6 10.5 %collective-permute-start.34 = (f32[1,64,512]{2,1,0:T(8,128)S(1)}, f32[1,64,512]{2,1,0:T(8,128)S(1)}, u32[]{:S(2)}, u32[]{:S(2)}) collective-permute-start(f32[1,64,512]{2,1,0:T(8,128)S(1)} %add_add_fusion.2), channel_id=1, source_target_pairs={{0,4},{1,5},{2,6},{3,7},{4,0},{5,1},{6,2},{7,3},{8,12},{9,13},{10,... | collective-permute-start | bytes 393224 | tf_op jit(solution)/shard_map/ppermute | solution.py:216
  92.4 12.9 %collective-permute-start.26 = (f32[1,64,512]{2,1,0:T(8,128)S(1)}, f32[1,64,512]{2,1,0:T(8,128)S(1)}, u32[]{:S(2)}, u32[]{:S(2)}) collective-permute-start(f32[1,64,512]{2,1,0:T(8,128)S(1)} %add_add_fusion.3), channel_id=1, source_target_pairs={{0,4},{1,5},{2,6},{3,7},{4,0},{5,1},{6,2},{7,3},{8,12},{9,13},{10,... | collective-permute-start | bytes 393224 | tf_op jit(solution)/shard_map/ppermute | solution.py:216
  105.4 15.1 %collective-permute-start.30 = (f32[1,64,512]{2,1,0:T(8,128)S(1)}, f32[1,64,512]{2,1,0:T(8,128)S(1)}, u32[]{:S(2)}, u32[]{:S(2)}) collective-permute-start(f32[1,64,512]{2,1,0:T(8,128)S(1)} %fusion.7), channel_id=1, source_target_pairs={{0,11},{1,10},{2,9},{3,8},{4,15},{5,14},{6,13},{7,12},{8,19},{9,18... | collective-permute-start | bytes 393224 | tf_op jit(solution)/shard_map/ppermute | solution.py:223
  108.3 12.3 %collective-permute-start.29 = (f32[1,64,512]{2,1,0:T(8,128)S(1)}, f32[1,64,512]{2,1,0:T(8,128)S(1)}, u32[]{:S(2)}, u32[]{:S(2)}) collective-permute-start(f32[1,64,512]{2,1,0:T(8,128)S(1)} %fusion.7), channel_id=1, source_target_pairs={{0,10},{1,11},{2,8},{3,9},{4,14},{5,15},{6,12},{7,13},{8,18},{9,19... | collective-permute-start | bytes 393224 | tf_op jit(solution)/shard_map/ppermute | solution.py:223
  109.0 11.5 %collective-permute-start.28 = (f32[1,64,512]{2,1,0:T(8,128)S(1)}, f32[1,64,512]{2,1,0:T(8,128)S(1)}, u32[]{:S(2)}, u32[]{:S(2)}) collective-permute-start(f32[1,64,512]{2,1,0:T(8,128)S(1)} %fusion.7), channel_id=1, source_target_pairs={{0,9},{1,8},{2,11},{3,10},{4,13},{5,12},{6,15},{7,14},{8,17},{9,16... | collective-permute-start | bytes 393224 | tf_op jit(solution)/shard_map/ppermute | solution.py:223
  117.5 19.6 %collective-permute-start.47 = (f32[1,64,512]{2,1,0:T(8,128)S(1)}, f32[1,64,512]{2,1,0:T(8,128)S(1)}, u32[]{:S(2)}, u32[]{:S(2)}) collective-permute-start(f32[1,64,512]{2,1,0:T(8,128)S(1)} %get-tuple-element.135), channel_id=1, source_target_pairs={{0,1},{1,0},{2,3},{3,2},{4,5},{5,4},{6,7},{7,6},{8,9},{9,8},{10,11... | collective-permute-start | bytes 393224 | tf_op jit(solution)/shard_map/ppermute | solution.py:213
  120.5 16.6 %collective-permute-start.48 = (f32[1,64,512]{2,1,0:T(8,128)S(1)}, f32[1,64,512]{2,1,0:T(8,128)S(1)}, u32[]{:S(2)}, u32[]{:S(2)}) collective-permute-start(f32[1,64,512]{2,1,0:T(8,128)S(1)} %get-tuple-element.136), channel_id=1, source_target_pairs={{0,2},{1,3},{2,0},{3,1},{4,6},{5,7},{6,4},{7,5},{8,10},{9,11},{10,... | collective-permute-start | bytes 393224 | tf_op jit(solution)/shard_map/ppermute | solution.py:213
  137.2 11.5 %collective-permute-start.50 = (f32[1,64,512]{2,1,0:T(8,128)S(1)}, f32[1,64,512]{2,1,0:T(8,128)S(1)}, u32[]{:S(2)}, u32[]{:S(2)}) collective-permute-start(f32[1,64,512]{2,1,0:T(8,128)S(1)} %add_add_fusion), channel_id=1, source_target_pairs={{0,4},{1,5},{2,6},{3,7},{4,0},{5,1},{6,2},{7,3},{8,12},{9,13},{10,... | collective-permute-start | bytes 393224 | tf_op jit(solution)/shard_map/ppermute | solution.py:216
  142.2 10.8 %collective-permute-start.45 = (f32[1,64,512]{2,1,0:T(8,128)S(1)}, f32[1,64,512]{2,1,0:T(8,128)S(1)}, u32[]{:S(2)}, u32[]{:S(2)}) collective-permute-start(f32[1,64,512]{2,1,0:T(8,128)S(1)} %fusion.3), channel_id=1, source_target_pairs={{0,10},{1,11},{2,8},{3,9},{4,14},{5,15},{6,12},{7,13},{8,18},{9,19... | collective-permute-start | bytes 393224 | tf_op jit(solution)/shard_map/ppermute | solution.py:223
  148.7 14.8 %collective-permute-start.54 = (f32[1,64,512]{2,1,0:T(8,128)S(1)}, f32[1,64,512]{2,1,0:T(8,128)S(1)}, u32[]{:S(2)}, u32[]{:S(2)}) collective-permute-start(f32[1,64,512]{2,1,0:T(8,128)S(1)} %fusion.1), channel_id=1, source_target_pairs={{0,11},{1,10},{2,9},{3,8},{4,15},{5,14},{6,13},{7,12},{8,19},{9,18... | collective-permute-start | bytes 393224 | tf_op jit(solution)/shard_map/ppermute | solution.py:223
  151.0 12.6 %collective-permute-start.53 = (f32[1,64,512]{2,1,0:T(8,128)S(1)}, f32[1,64,512]{2,1,0:T(8,128)S(1)}, u32[]{:S(2)}, u32[]{:S(2)}) collective-permute-start(f32[1,64,512]{2,1,0:T(8,128)S(1)} %fusion.1), channel_id=1, source_target_pairs={{0,10},{1,11},{2,8},{3,9},{4,14},{5,15},{6,12},{7,13},{8,18},{9,19... | collective-permute-start | bytes 393224 | tf_op jit(solution)/shard_map/ppermute | solution.py:223
  153.0 12.4 %collective-permute-start.52 = (f32[1,64,512]{2,1,0:T(8,128)S(1)}, f32[1,64,512]{2,1,0:T(8,128)S(1)}, u32[]{:S(2)}, u32[]{:S(2)}) collective-permute-start(f32[1,64,512]{2,1,0:T(8,128)S(1)} %fusion.1), channel_id=1, source_target_pairs={{0,9},{1,8},{2,11},{3,10},{4,13},{5,12},{6,15},{7,14},{8,17},{9,16... | collective-permute-start | bytes 393224 | tf_op jit(solution)/shard_map/ppermute | solution.py:223
  (45 other events, 353.9 us)

commit v5 on v4

--- a/solution.py
+++ b/solution.py
@@ -27,16 +27,22 @@
     return dot(ah, bh) + (dot(ah, bl) + dot(al, bh))
 
 
+def place(ny):
+    k = lax.axis_index("sub")
+    return k & (ny - 1), lax.shift_right_logical(k, ny.bit_length() - 1)
+
+
 def params(mib):
     return pltpu.CompilerParams(vmem_limit_bytes=mib * 1024 * 1024)
 
 
 def grad_kernel(ny, chunk, stratum, *refs):
-    where, occ, users, rate = refs[:4]
-    pieces = refs[4:4 + ny]
-    err_hi, err_lo, v_hi, v_lo, old = refs[4 + ny:9 + ny]
-    grads = refs[9 + ny:9 + 2 * ny]
-    block, total, vt_hi, vt_lo = refs[9 + 2 * ny:]
+    occ, users, rate = refs[:3]
+    where = place(ny)
+    pieces = refs[3:3 + ny]
+    err_hi, err_lo, v_hi, v_lo, old = refs[3 + ny:8 + ny]
+    grads = refs[8 + ny:8 + 2 * ny]
+    block, total, vt_hi, vt_lo = refs[8 + 2 * ny:]
     mine = where[0]
     rows, rank = total.shape
     steps, q_in, _ = pieces[0].shape
@@ -57,7 +63,7 @@
         for a in range(BLOCK // TILE):
             line = []
             for b in range(rows // TILE):
-                seen = occ[stratum, first // TILE + a, chunk * rows // TILE + b]
+                seen = occ[stratum, chunk * rows // TILE + b, first // TILE + a]
                 part = err[a * TILE:(a + 1) * TILE, b * TILE:(b + 1) * TILE]
                 line.append(jnp.where(seen == 1, part, 0.0))
             parts.append(jnp.concatenate(line, axis=1))
@@ -73,7 +79,7 @@
             grads[r][z] = total[pl.ds((z * ny + (mine ^ r)) * q, q), :]
 
 
-def gradients(where, occ, users, ratings, pieces, stratum, chunk, q):
+def gradients(occ, users, ratings, pieces, stratum, chunk, q):
     ny = len(pieces)
     steps, q_in, rank = pieces[0].shape
     rows = steps * ny * q_in
@@ -81,7 +87,7 @@
     gshape = (rows // (ny * q), q, rank)
     return pl.pallas_call(
         functools.partial(grad_kernel, ny, chunk, stratum),
-        in_specs=[SMEM, SMEM] + [VMEM] * (2 + ny),
+        in_specs=[SMEM] + [VMEM] * (2 + ny),
         out_specs=[VMEM] * (5 + ny),
         out_shape=[jax.ShapeDtypeStruct((n_users, rows), BF16)] * 2 + [jax.ShapeDtypeStruct((rows, rank), BF16)] * 2
         + [jax.ShapeDtypeStruct((q, rank), F32)] + [jax.ShapeDtypeStruct(gshape, F32)] * ny,
@@ -89,7 +95,7 @@
         compiler_params=params(24),
         cost_estimate=pl.CostEstimate(flops=12 * n_users * rows * rank, bytes_accessed=4 * n_users * rank, transcendentals=0),
         name="gradients",
-    )(where, occ, users, ratings, *pieces)
+    )(occ, users, ratings, *pieces)
 
 
 def step_kernel(n, *refs):
@@ -120,8 +126,8 @@
 
 
 def cut_kernel(ny, nz, *refs):
-    where, outs = refs[0], refs[-nz:]
-    terms = refs[1:-nz]
+    where, outs = place(ny), refs[-nz:]
+    terms = refs[:-nz]
     chunks = [terms[i:i + ny] for i in range(0, len(terms), ny)]
     each = nz // len(chunks)
     for t in range(nz):
@@ -133,22 +139,22 @@
                 outs[r][...] = total
 
 
-def cut(where, chunks):
+def cut(chunks):
     ny = len(chunks[0])
     each, q, rank = chunks[0][0].shape
     nz = each * len(chunks)
     return pl.pallas_call(
         functools.partial(cut_kernel, ny, nz),
-        in_specs=[SMEM] + [VMEM] * (ny * len(chunks)),
+        in_specs=[VMEM] * (ny * len(chunks)),
         out_specs=[VMEM] * nz,
         out_shape=[jax.ShapeDtypeStruct((q, rank), F32)] * nz,
         compiler_params=params(8),
         name="cut",
-    )(where, *[x for c in chunks for x in c])
-
-
-def join_kernel(nz, *refs):
-    where, pieces, outs = refs[0], refs[1:1 + nz], refs[1 + nz:]
+    )(*[x for c in chunks for x in c])
+
+
+def join_kernel(ny, nz, *refs):
+    where, pieces, outs = place(ny), refs[:nz], refs[nz:]
     each = nz // len(outs)
     if each == nz:
         for r in range(nz):
@@ -161,36 +167,36 @@
                 outs[t // each][t % each] = pieces[r][...]
 
 
-def join(where, pieces, chunks):
+def join(ny, pieces, chunks):
     nz = len(pieces)
     shape = (nz // chunks,) + pieces[0].shape
     return pl.pallas_call(
-        functools.partial(join_kernel, nz),
-        in_specs=[SMEM] + [VMEM] * nz,
+        functools.partial(join_kernel, ny, nz),
+        in_specs=[VMEM] * nz,
         out_specs=[VMEM] * chunks,
         out_shape=[jax.ShapeDtypeStruct(shape, F32)] * chunks,
         compiler_params=params(8),
         name="join",
-    )(where, *pieces)
-
-
-def pick_kernel(cut, *refs):
-    where, olds, out = refs[0], refs[1:-1], refs[-1]
+    )(*pieces)
+
+
+def pick_kernel(ny, cut, *refs):
+    where, olds, out = place(ny), refs[:-1], refs[-1]
     for c in range(len(olds)):
         @pl.when(lax.div(where[1], cut) == c)
         def _():
             out[...] = olds[c][...]
 
 
-def pick(where, olds, cut):
-    return pl.pallas_call(
-        functools.partial(pick_kernel, cut),
-        in_specs=[SMEM] + [VMEM] * len(olds),
+def pick(ny, olds, cut):
+    return pl.pallas_call(
+        functools.partial(pick_kernel, ny, cut),
+        in_specs=[VMEM] * len(olds),
         out_specs=VMEM,
         out_shape=jax.ShapeDtypeStruct(olds[0].shape, F32),
         compiler_params=params(8),
         name="pick",
-    )(where, *olds)
+    )(*olds)
 
 
 def new_rows(old, terms):
@@ -206,8 +212,6 @@
         ny *= 2
     nz = n_sub // ny
     chunks = max(1, min(CHUNKS, share // 8))
-    k = lax.axis_index("sub")
-    where = jnp.stack([k & (ny - 1), k >> (ny.bit_length() - 1)]).astype(jnp.int32)
 
     def over_y(x, r):
         return lax.ppermute(x, "sub", [(i, i ^ r) for i in range(n_sub)])
@@ -222,30 +226,32 @@
                 route.append((g * n_sub + i, (g + 1) % n_group * n_sub + (i ^ r)))
         return lax.ppermute(x, ("group", "sub"), route)
 
+    occupancy = occupancy.transpose(0, 2, 1)
+
     wide = nz * share // chunks
-    owns = join(where, [items] + [over_z(items, r) for r in range(1, nz)], chunks)
+    owns = join(ny, [items] + [over_z(items, r) for r in range(1, nz)], chunks)
     pieces = [[own] + [over_y(own, r) for r in range(1, ny)] for own in owns]
 
     for s in range(strata):
         last = s == strata - 1
         parts, grads, olds = [], [], []
         for c in range(chunks):
-            res = gradients(where, occupancy, users, ratings, pieces[c], s, c, share if last else wide)
+            res = gradients(occupancy, users, ratings, pieces[c], s, c, share if last else wide)
             parts.append(res[:4])
             olds.append(res[4])
             grads.append([res[5]] + [over_y(res[5 + r], r) for r in range(1, ny)])
         new_users = user_step(users, parts)
         if last:
-            old = onward(pick(where, olds, nz // chunks), 0)
-            cuts = cut(where, grads)
+            old = onward(pick(ny, olds, nz // chunks), 0)
+            cuts = cut(grads)
             rows = new_rows(old, [onward(cuts[r], r * ny) for r in range(nz)])
             return new_users, rows
         for c in range(chunks):
             total = functools.reduce(jnp.add, grads[c])
             for bit in range(1, nz.bit_length()):
                 total = total + over_z(total, 1 << (bit - 1))
-            rows = new_rows(olds[c].reshape(total.shape), [total])
-            pieces[c] = [onward(rows, r) for r in range(ny)]
+            own = onward(new_rows(olds[c].reshape(total.shape), [total]), 0)
+            pieces[c] = [own] + [over_y(own, r) for r in range(1, ny)]
         users = new_users
 
 

time: 188 us -> 180 us (0.957)
  waiting for transfers between devices: 65.6 us -> 61.9 us
  Pallas kernels: 40.1 us -> 37.4 us
    ppermute x30 -> x48, starting transfers between devices: 38.2 us -> 59.3 us  [over_y(): return lax.ppermute(x, 'sub', [(i, i ^ r) for i in range(n_sub)])]
    ppermute x27 -> x9, starting transfers between devices: 21.1 us -> 1.17 us  [onward(): return lax.ppermute(x, ('group', 'sub'), route)]
    ppermute x27 -> x9, waiting for transfers between devices: 27.6 us -> 8.49 us  [onward(): return lax.ppermute(x, ('group', 'sub'), route)]
    ppermute x30 -> x48, waiting for transfers between devices: 16.9 us -> 29.7 us  [over_y(): return lax.ppermute(x, 'sub', [(i, i ^ r) for i in range(n_sub)])]
    ppermute x7, starting transfers between devices: 15.4 us -> 12.5 us  [over_z(): return lax.ppermute(x, 'sub', [(i, i ^ r * ny) for i in range(n_sub)])]
    ppermute x7, waiting for transfers between devices: 21 us -> 23.7 us  [over_z(): return lax.ppermute(x, 'sub', [(i, i ^ r * ny) for i in range(n_sub)])]
    unnamed x11 -> x14, local copies, waits for them, and re-layouts: 5.48 us -> 5.39 us
  transfers between devices with their start and end apart: 64 -> 64, of which waited for: 27 -> 29; matrix products, arithmetic and copies ran while one was open for 1% -> 0% of each run, Pallas kernels for 21% -> 21%
where the time goes in v5:
time: 180 us
  starting transfers between devices  73 us (41%)
  waiting for transfers between devices  61.9 us (34%)
  Pallas kernels  37.4 us (21%)
  local copies, waits for them, and re-layouts  5.39 us (3%)
    ppermute x48, starting transfers between devices, over_y(): return lax.ppermute(x, 'sub', [(i, i ^ r) for i in range(n_sub)])  59.3 us
    ppermute x48, waiting for transfers between devices, over_y(): return lax.ppermute(x, 'sub', [(i, i ^ r) for i in range(n_sub)])  29.7 us
    pallas_call x8, Pallas kernels, gradients(): pl.pallas_call(functools.partial(grad_kernel, ny, chunk, stratum), in_spe...  28.6 us
    ppermute x7, waiting for transfers between devices, over_z(): return lax.ppermute(x, 'sub', [(i, i ^ r * ny) for i in range(n_sub)])  23.7 us
    ppermute x7, starting transfers between devices, over_z(): return lax.ppermute(x, 'sub', [(i, i ^ r * ny) for i in range(n_sub)])  12.5 us
    pallas_call x4, Pallas kernels, user_step(): pl.pallas_call(functools.partial(step_kernel, len(parts)), in_specs=[VMEM...  8.72 us
    ppermute x9, waiting for transfers between devices, onward(): return lax.ppermute(x, ('group', 'sub'), route)  8.49 us
    unnamed x14, local copies, waits for them, and re-layouts  5.39 us
  transfers between devices with their start and end apart: 64, of which 29 were waited for; matrix products, arithmetic and copies ran while one was open for 0% of the time, Pallas kernels for 21%

profile of v5, /device:TPU:0, one launch (start us, length us, event | category | flops | bytes accessed | tf_op | source)
XLA Modules:
  0.0 179.7 jit_solution(8845187109278250598)
XLA Ops:
  0.6 4.1 %collective-permute-start = (f32[64,512]{1,0:T(8,128)}, f32[64,512]{1,0:T(8,128)S(1)}, u32[]{:S(2)}, u32[]{:S(2)}) collective-permute-start(f32[64,512]{1,0:T(8,128)} %refs_0_.2), channel_id=1, source_target_pairs={{0,4},{1,5},{2,6},{3,7},{4,0},{5,1},{6,2},{7,3},{8,12},{9,13},{10,... | collective-permute-start | bytes 393224 | tf_op jit(solution)/shard_map/ppermute | solution.py:220
  4.7 6.5 %collective-permute-done.refs_1_ = f32[64,512]{1,0:T(8,128)S(1)} collective-permute-done((f32[64,512]{1,0:T(8,128)}, f32[64,512]{1,0:T(8,128)S(1)}, u32[]{:S(2)}, u32[]{:S(2)}) %collective-permute-start) | collective-permute-done | bytes 131104 | tf_op jit(solution)/shard_map/ppermute | solution.py:220
  29.0 3.6 %gradients.8 = (bf16[1024,256]{1,0:T(8,128)(2,1)S(1)}, bf16[1024,256]{1,0:T(8,128)(2,1)S(1)}, bf16[256,512]{1,0:T(8,128)(2,1)S(1)}, bf16[256,512]{1,0:T(8,128)(2...) custom-call(s32[4,4,8]{2,1,0:T(4,128)S(1)} %bitcast.49, ...), custom_call_target="tpu_custom_call" | custom-call | flops 1610612736 | bytes 2097152 | tf_op jit(solution)/shard_map/gradients/pallas_call | solution.py:88
  33.6 2.5 %collective-permute-start.9 = (f32[1,64,512]{2,1,0:T(8,128)S(1)}, f32[1,64,512]{2,1,0:T(8,128)S(1)}, u32[]{:S(2)}, u32[]{:S(2)}) collective-permute-start(f32[1,64,512]{2,1,0:T(8,128)S(1)} %get-tuple-element.92), channel_id=1, source_target_pairs={{0,3},{1,2},{2,1},{3,0},{4,7},{5,6},{6,5},{7,4},{8,11},{9,10},{10,... | collective-permute-start | bytes 393224 | tf_op jit(solution)/shard_map/ppermute | solution.py:217
  36.1 3.6 %gradients.9 = (bf16[1024,256]{1,0:T(8,128)(2,1)S(1)}, bf16[1024,256]{1,0:T(8,128)(2,1)S(1)}, bf16[256,512]{1,0:T(8,128)(2,1)S(1)}, bf16[256,512]{1,0:T(8,128)(2...) custom-call(s32[4,4,8]{2,1,0:T(4,128)S(1)} %bitcast.50, ...), custom_call_target="tpu_custom_call" | custom-call | flops 1610612736 | bytes 2097152 | tf_op jit(solution)/shard_map/gradients/pallas_call | solution.py:88
  40.7 2.5 %collective-permute-start.17 = (f32[1,64,512]{2,1,0:T(8,128)S(1)}, f32[1,64,512]{2,1,0:T(8,128)S(1)}, u32[]{:S(2)}, u32[]{:S(2)}) collective-permute-start(f32[1,64,512]{2,1,0:T(8,128)S(1)} %get-tuple-element.101), channel_id=1, source_target_pairs={{0,3},{1,2},{2,1},{3,0},{4,7},{5,6},{6,5},{7,4},{8,11},{9,10},{10,... | collective-permute-start | bytes 393224 | tf_op jit(solution)/shard_map/ppermute | solution.py:217
  47.9 4.0 %collective-permute-start.18 = (f32[1,64,512]{2,1,0:T(8,128)S(1)}, f32[1,64,512]{2,1,0:T(8,128)S(1)}, u32[]{:S(2)}, u32[]{:S(2)}) collective-permute-start(f32[1,64,512]{2,1,0:T(8,128)S(1)} %add_add_fusion.4), channel_id=1, source_target_pairs={{0,4},{1,5},{2,6},{3,7},{4,0},{5,1},{6,2},{7,3},{8,12},{9,13},{10,... | collective-permute-start | bytes 393224 | tf_op jit(solution)/shard_map/ppermute | solution.py:220
  53.6 2.7 %collective-permute-done.18 = f32[1,64,512]{2,1,0:T(8,128)S(1)} collective-permute-done((f32[1,64,512]{2,1,0:T(8,128)S(1)}, f32[1,64,512]{2,1,0:T(8,128)S(1)}, u32[]{:S(2)}, u32[]{:S(2)}) %collective-permute-start.18) | collective-permute-done | bytes 131104 | tf_op jit(solution)/shard_map/ppermute | solution.py:220
  68.2 3.6 %gradients.10 = (bf16[1024,256]{1,0:T(8,128)(2,1)S(1)}, bf16[1024,256]{1,0:T(8,128)(2,1)S(1)}, bf16[256,512]{1,0:T(8,128)(2,1)S(1)}, bf16[256,512]{1,0:T(8,128)(...) custom-call(s32[4,4,8]{2,1,0:T(4,128)S(1)} %bitcast.51, ...), custom_call_target="tpu_custom_call" | custom-call | flops 1610612736 | bytes 2097152 | tf_op jit(solution)/shard_map/gradients/pallas_call | solution.py:88
  72.7 2.6 %collective-permute-start.25 = (f32[1,64,512]{2,1,0:T(8,128)S(1)}, f32[1,64,512]{2,1,0:T(8,128)S(1)}, u32[]{:S(2)}, u32[]{:S(2)}) collective-permute-start(f32[1,64,512]{2,1,0:T(8,128)S(1)} %get-tuple-element.110), channel_id=1, source_target_pairs={{0,3},{1,2},{2,1},{3,0},{4,7},{5,6},{6,5},{7,4},{8,11},{9,10},{10,... | collective-permute-start | bytes 393224 | tf_op jit(solution)/shard_map/ppermute | solution.py:217
  75.3 3.6 %gradients.11 = (bf16[1024,256]{1,0:T(8,128)(2,1)S(1)}, bf16[1024,256]{1,0:T(8,128)(2,1)S(1)}, bf16[256,512]{1,0:T(8,128)(2,1)S(1)}, bf16[256,512]{1,0:T(8,128)(...) custom-call(s32[4,4,8]{2,1,0:T(4,128)S(1)} %bitcast.52, ...), custom_call_target="tpu_custom_call" | custom-call | flops 1610612736 | bytes 2097152 | tf_op jit(solution)/shard_map/gradients/pallas_call | solution.py:88
  79.8 2.6 %collective-permute-start.33 = (f32[1,64,512]{2,1,0:T(8,128)S(1)}, f32[1,64,512]{2,1,0:T(8,128)S(1)}, u32[]{:S(2)}, u32[]{:S(2)}) collective-permute-start(f32[1,64,512]{2,1,0:T(8,128)S(1)} %get-tuple-element.119), channel_id=1, source_target_pairs={{0,3},{1,2},{2,1},{3,0},{4,7},{5,6},{6,5},{7,4},{8,11},{9,10},{10,... | collective-permute-start | bytes 393224 | tf_op jit(solution)/shard_map/ppermute | solution.py:217
  86.7 3.4 %collective-permute-done.33 = f32[1,64,512]{2,1,0:T(8,128)S(1)} collective-permute-done((f32[1,64,512]{2,1,0:T(8,128)S(1)}, f32[1,64,512]{2,1,0:T(8,128)S(1)}, u32[]{:S(2)}, u32[]{:S(2)}) %collective-permute-start.33) | collective-permute-done | bytes 131104 | tf_op jit(solution)/shard_map/ppermute | solution.py:217
  92.5 4.4 %collective-permute-done.34 = f32[1,64,512]{2,1,0:T(8,128)S(1)} collective-permute-done((f32[1,64,512]{2,1,0:T(8,128)S(1)}, f32[1,64,512]{2,1,0:T(8,128)S(1)}, u32[]{:S(2)}, u32[]{:S(2)}) %collective-permute-start.34) | collective-permute-done | bytes 131104 | tf_op jit(solution)/shard_map/ppermute | solution.py:220
  107.5 3.6 %gradients.12 = (bf16[1024,256]{1,0:T(8,128)(2,1)S(1)}, bf16[1024,256]{1,0:T(8,128)(2,1)S(1)}, bf16[256,512]{1,0:T(8,128)(2,1)S(1)}, bf16[256,512]{1,0:T(8,128)(...) custom-call(s32[4,4,8]{2,1,0:T(4,128)S(1)} %bitcast.53, ...), custom_call_target="tpu_custom_call" | custom-call | flops 1610612736 | bytes 2097152 | tf_op jit(solution)/shard_map/gradients/pallas_call | solution.py:88
  114.6 3.6 %gradients.13 = (bf16[1024,256]{1,0:T(8,128)(2,1)S(1)}, bf16[1024,256]{1,0:T(8,128)(2,1)S(1)}, bf16[256,512]{1,0:T(8,128)(2,1)S(1)}, bf16[256,512]{1,0:T(8,128)(...) custom-call(s32[4,4,8]{2,1,0:T(4,128)S(1)} %bitcast.54, ...), custom_call_target="tpu_custom_call" | custom-call | flops 1610612736 | bytes 2097152 | tf_op jit(solution)/shard_map/gradients/pallas_call | solution.py:88
  126.7 2.8 %collective-permute-done.49 = f32[1,64,512]{2,1,0:T(8,128)S(1)} collective-permute-done((f32[1,64,512]{2,1,0:T(8,128)S(1)}, f32[1,64,512]{2,1,0:T(8,128)S(1)}, u32[]{:S(2)}, u32[]{:S(2)}) %collective-permute-start.49) | collective-permute-done | bytes 131104 | tf_op jit(solution)/shard_map/ppermute | solution.py:217
  131.7 4.6 %collective-permute-done.50 = f32[1,64,512]{2,1,0:T(8,128)S(1)} collective-permute-done((f32[1,64,512]{2,1,0:T(8,128)S(1)}, f32[1,64,512]{2,1,0:T(8,128)S(1)}, u32[]{:S(2)}, u32[]{:S(2)}) %collective-permute-start.50) | collective-permute-done | bytes 131104 | tf_op jit(solution)/shard_map/ppermute | solution.py:220
  146.7 3.6 %gradients.14 = (bf16[1024,256]{1,0:T(8,128)(2,1)S(1)}, bf16[1024,256]{1,0:T(8,128)(2,1)S(1)}, bf16[256,512]{1,0:T(8,128)(2,1)S(1)}, bf16[256,512]{1,0:T(8,128)(...) custom-call(s32[4,4,8]{2,1,0:T(4,128)S(1)} %bitcast.55, ...), custom_call_target="tpu_custom_call" | custom-call | flops 1610612736 | bytes 2097152 | tf_op jit(solution)/shard_map/gradients/pallas_call | solution.py:88
  150.2 3.6 %collective-permute-start.56 = (f32[1,64,512]{2,1,0:T(8,128)S(1)}, f32[1,64,512]{2,1,0:T(8,128)S(1)}, u32[]{:S(2)}, u32[]{:S(2)}) collective-permute-start(f32[1,64,512]{2,1,0:T(8,128)S(1)} %get-tuple-element.145), channel_id=1, source_target_pairs={{0,1},{1,0},{2,3},{3,2},{4,5},{5,4},{6,7},{7,6},{8,9},{9,8},{10,11... | collective-permute-start | bytes 393224 | tf_op jit(solution)/shard_map/ppermute | solution.py:217
  155.4 3.6 %gradients.15 = (bf16[1024,256]{1,0:T(8,128)(2,1)S(1)}, bf16[1024,256]{1,0:T(8,128)(2,1)S(1)}, bf16[256,512]{1,0:T(8,128)(2,1)S(1)}, bf16[256,512]{1,0:T(8,128)(...) custom-call(s32[4,4,8]{2,1,0:T(4,128)S(1)} %bitcast.56, ...), custom_call_target="tpu_custom_call" | custom-call | flops 1610612736 | bytes 2097152 | tf_op jit(solution)/shard_map/gradients/pallas_call | solution.py:88
  162.6 2.9 %collective-permute-done.59.refs_5_ = f32[1,64,512]{2,1,0:T(8,128)S(1)} collective-permute-done((f32[1,64,512]{2,1,0:T(8,128)S(1)}, f32[1,64,512]{2,1,0:T(8,128)S(1)}, u32[]{:S(2)}, u32[]{:S(2)}) %collective-permute-start.59) | collective-permute-done | bytes 131104 | tf_op jit(solution)/shard_map/ppermute | solution.py:217
  168.8 3.2 %user_step.7 = f32[1024,512]{1,0:T(8,128)} custom-call(f32[1024,512]{1,0:T(8,128)S(1)} %user_step.6.refs_1_.refs_0_, bf16[1024,256]{1,0:T(8,128)(2,1)S(1)} %get-tuple-element.129.refs_1_, bf16[1024,256]{1,0:T(8,128)(2,1)S(1)} %get-tuple-element.130.refs_2_, bf16[256,512]{1,0:T(8,128)(2,1)S(1)} %get-tuple-element.131.refs_3_, ...), custom_call_target="tpu_custom_call" | custom-call | flops 1610612736 | bytes 4194304 | tf_op jit(solution)/shard_map/user_step/pallas_call | solution.py:117
  173.1 5.9 %collective-permute-done.63 = f32[64,512]{1,0:T(8,128)S(1)} collective-permute-done((f32[64,512]{1,0:T(8,128)S(1)}, f32[64,512]{1,0:T(8,128)S(1)}, u32[]{:S(2)}, u32[]{:S(2)}) %collective-permute-start.63) | collective-permute-done | bytes 131104 | tf_op jit(solution)/shard_map/ppermute | solution.py:227
  (146 shorter events, 91.8 us)
Async XLA Ops:
  0.6 10.6 %collective-permute-start = (f32[64,512]{1,0:T(8,128)}, f32[64,512]{1,0:T(8,128)S(1)}, u32[]{:S(2)}, u32[]{:S(2)}) collective-permute-start(f32[64,512]{1,0:T(8,128)} %refs_0_.2), channel_id=1, source_target_pairs={{0,4},{1,5},{2,6},{3,7},{4,0},{5,1},{6,2},{7,3},{8,12},{9,13},{10,... | collective-permute-start | bytes 393224 | tf_op jit(solution)/shard_map/ppermute | solution.py:220
  15.7 17.8 %collective-permute-start.6 = (f32[1,64,512]{2,1,0:T(8,128)S(1)}, f32[1,64,512]{2,1,0:T(8,128)S(1)}, u32[]{:S(2)}, u32[]{:S(2)}) collective-permute-start(f32[1,64,512]{2,1,0:T(8,128)S(1)} %get-tuple-element.83.refs_3_), channel_id=1, source_target_pairs={{0,3},{1,2},{2,1},{3,0},{4,7},{5,6},{6,5},{7,4},{8,11},{9,10},{10,... | collective-permute-start | bytes 393224 | tf_op jit(solution)/shard_map/ppermute | solution.py:217
  17.5 18.6 %collective-permute-start.5 = (f32[1,64,512]{2,1,0:T(8,128)S(1)}, f32[1,64,512]{2,1,0:T(8,128)S(1)}, u32[]{:S(2)}, u32[]{:S(2)}) collective-permute-start(f32[1,64,512]{2,1,0:T(8,128)S(1)} %get-tuple-element.83.refs_3_), channel_id=1, source_target_pairs={{0,2},{1,3},{2,0},{3,1},{4,6},{5,7},{6,4},{7,5},{8,10},{9,11},{10,... | collective-permute-start | bytes 393224 | tf_op jit(solution)/shard_map/ppermute | solution.py:217
  19.6 16.5 %collective-permute-start.4 = (f32[1,64,512]{2,1,0:T(8,128)S(1)}, f32[1,64,512]{2,1,0:T(8,128)S(1)}, u32[]{:S(2)}, u32[]{:S(2)}) collective-permute-start(f32[1,64,512]{2,1,0:T(8,128)S(1)} %get-tuple-element.83.refs_3_), channel_id=1, source_target_pairs={{0,1},{1,0},{2,3},{3,2},{4,5},{5,4},{6,7},{7,6},{8,9},{9,8},{10,11... | collective-permute-start | bytes 393224 | tf_op jit(solution)/shard_map/ppermute | solution.py:217
  33.2 10.1 %collective-permute-start.8 = (f32[1,64,512]{2,1,0:T(8,128)S(1)}, f32[1,64,512]{2,1,0:T(8,128)S(1)}, u32[]{:S(2)}, u32[]{:S(2)}) collective-permute-start(f32[1,64,512]{2,1,0:T(8,128)S(1)} %get-tuple-element.91), channel_id=1, source_target_pairs={{0,2},{1,3},{2,0},{3,1},{4,6},{5,7},{6,4},{7,5},{8,10},{9,11},{10,... | collective-permute-start | bytes 393224 | tf_op jit(solution)/shard_map/ppermute | solution.py:217
  33.6 9.7 %collective-permute-start.9 = (f32[1,64,512]{2,1,0:T(8,128)S(1)}, f32[1,64,512]{2,1,0:T(8,128)S(1)}, u32[]{:S(2)}, u32[]{:S(2)}) collective-permute-start(f32[1,64,512]{2,1,0:T(8,128)S(1)} %get-tuple-element.92), channel_id=1, source_target_pairs={{0,3},{1,2},{2,1},{3,0},{4,7},{5,6},{6,5},{7,4},{8,11},{9,10},{10,... | collective-permute-start | bytes 393224 | tf_op jit(solution)/shard_map/ppermute | solution.py:217
  43.3 10.2 %collective-permute-start.10 = (f32[1,64,512]{2,1,0:T(8,128)S(1)}, f32[1,64,512]{2,1,0:T(8,128)S(1)}, u32[]{:S(2)}, u32[]{:S(2)}) collective-permute-start(f32[1,64,512]{2,1,0:T(8,128)S(1)} %add_add_fusion.5), channel_id=1, source_target_pairs={{0,4},{1,5},{2,6},{3,7},{4,0},{5,1},{6,2},{7,3},{8,12},{9,13},{10,... | collective-permute-start | bytes 393224 | tf_op jit(solution)/shard_map/ppermute | solution.py:220
  63.7 11.6 %collective-permute-start.21 = (f32[1,64,512]{2,1,0:T(8,128)S(1)}, f32[1,64,512]{2,1,0:T(8,128)S(1)}, u32[]{:S(2)}, u32[]{:S(2)}) collective-permute-start(f32[1,64,512]{2,1,0:T(8,128)S(1)} %collective-permute-done.19.refs_3_), channel_id=1, source_target_pairs={{0,2},{1,3},{2,0},{3,1},{4,6},{5,7},{6,4},{7,5},{8,10},{9,11},{10,... | collective-permute-start | bytes 393224 | tf_op jit(solution)/shard_map/ppermute | solution.py:217
  65.8 9.6 %collective-permute-start.20 = (f32[1,64,512]{2,1,0:T(8,128)S(1)}, f32[1,64,512]{2,1,0:T(8,128)S(1)}, u32[]{:S(2)}, u32[]{:S(2)}) collective-permute-start(f32[1,64,512]{2,1,0:T(8,128)S(1)} %collective-permute-done.19.refs_3_), channel_id=1, source_target_pairs={{0,1},{1,0},{2,3},{3,2},{4,5},{5,4},{6,7},{7,6},{8,9},{9,8},{10,11... | collective-permute-start | bytes 393224 | tf_op jit(solution)/shard_map/ppermute | solution.py:217
  72.7 9.8 %collective-permute-start.24 = (f32[1,64,512]{2,1,0:T(8,128)S(1)}, f32[1,64,512]{2,1,0:T(8,128)S(1)}, u32[]{:S(2)}, u32[]{:S(2)}) collective-permute-start(f32[1,64,512]{2,1,0:T(8,128)S(1)} %get-tuple-element.109), channel_id=1, source_target_pairs={{0,2},{1,3},{2,0},{3,1},{4,6},{5,7},{6,4},{7,5},{8,10},{9,11},{10,... | collective-permute-start | bytes 393224 | tf_op jit(solution)/shard_map/ppermute | solution.py:217
  72.7 9.8 %collective-permute-start.25 = (f32[1,64,512]{2,1,0:T(8,128)S(1)}, f32[1,64,512]{2,1,0:T(8,128)S(1)}, u32[]{:S(2)}, u32[]{:S(2)}) collective-permute-start(f32[1,64,512]{2,1,0:T(8,128)S(1)} %get-tuple-element.110), channel_id=1, source_target_pairs={{0,3},{1,2},{2,1},{3,0},{4,7},{5,6},{6,5},{7,4},{8,11},{9,10},{10,... | collective-permute-start | bytes 393224 | tf_op jit(solution)/shard_map/ppermute | solution.py:217
  79.8 10.3 %collective-permute-start.33 = (f32[1,64,512]{2,1,0:T(8,128)S(1)}, f32[1,64,512]{2,1,0:T(8,128)S(1)}, u32[]{:S(2)}, u32[]{:S(2)}) collective-permute-start(f32[1,64,512]{2,1,0:T(8,128)S(1)} %get-tuple-element.119), channel_id=1, source_target_pairs={{0,3},{1,2},{2,1},{3,0},{4,7},{5,6},{6,5},{7,4},{8,11},{9,10},{10,... | collective-permute-start | bytes 393224 | tf_op jit(solution)/shard_map/ppermute | solution.py:217
  82.5 9.9 %collective-permute-start.26 = (f32[1,64,512]{2,1,0:T(8,128)S(1)}, f32[1,64,512]{2,1,0:T(8,128)S(1)}, u32[]{:S(2)}, u32[]{:S(2)}) collective-permute-start(f32[1,64,512]{2,1,0:T(8,128)S(1)} %add_add_fusion.3), channel_id=1, source_target_pairs={{0,4},{1,5},{2,6},{3,7},{4,0},{5,1},{6,2},{7,3},{8,12},{9,13},{10,... | collective-permute-start | bytes 393224 | tf_op jit(solution)/shard_map/ppermute | solution.py:220
  102.7 9.6 %collective-permute-start.38 = (f32[1,64,512]{2,1,0:T(8,128)S(1)}, f32[1,64,512]{2,1,0:T(8,128)S(1)}, u32[]{:S(2)}, u32[]{:S(2)}) collective-permute-start(f32[1,64,512]{2,1,0:T(8,128)S(1)} %collective-permute-done.35.refs_3_), channel_id=1, source_target_pairs={{0,3},{1,2},{2,1},{3,0},{4,7},{5,6},{6,5},{7,4},{8,11},{9,10},{10,... | collective-permute-start | bytes 393224 | tf_op jit(solution)/shard_map/ppermute | solution.py:217
  103.3 11.4 %collective-permute-start.37 = (f32[1,64,512]{2,1,0:T(8,128)S(1)}, f32[1,64,512]{2,1,0:T(8,128)S(1)}, u32[]{:S(2)}, u32[]{:S(2)}) collective-permute-start(f32[1,64,512]{2,1,0:T(8,128)S(1)} %collective-permute-done.35.refs_3_), channel_id=1, source_target_pairs={{0,2},{1,3},{2,0},{3,1},{4,6},{5,7},{6,4},{7,5},{8,10},{9,11},{10,... | collective-permute-start | bytes 393224 | tf_op jit(solution)/shard_map/ppermute | solution.py:217
  112.2 9.5 %collective-permute-start.40 = (f32[1,64,512]{2,1,0:T(8,128)S(1)}, f32[1,64,512]{2,1,0:T(8,128)S(1)}, u32[]{:S(2)}, u32[]{:S(2)}) collective-permute-start(f32[1,64,512]{2,1,0:T(8,128)S(1)} %get-tuple-element.127), channel_id=1, source_target_pairs={{0,2},{1,3},{2,0},{3,1},{4,6},{5,7},{6,4},{7,5},{8,10},{9,11},{10,... | collective-permute-start | bytes 393224 | tf_op jit(solution)/shard_map/ppermute | solution.py:217
  112.2 9.5 %collective-permute-start.41 = (f32[1,64,512]{2,1,0:T(8,128)S(1)}, f32[1,64,512]{2,1,0:T(8,128)S(1)}, u32[]{:S(2)}, u32[]{:S(2)}) collective-permute-start(f32[1,64,512]{2,1,0:T(8,128)S(1)} %get-tuple-element.128), channel_id=1, source_target_pairs={{0,3},{1,2},{2,1},{3,0},{4,7},{5,6},{6,5},{7,4},{8,11},{9,10},{10,... | collective-permute-start | bytes 393224 | tf_op jit(solution)/shard_map/ppermute | solution.py:217
  119.4 10.1 %collective-permute-start.49 = (f32[1,64,512]{2,1,0:T(8,128)S(1)}, f32[1,64,512]{2,1,0:T(8,128)S(1)}, u32[]{:S(2)}, u32[]{:S(2)}) collective-permute-start(f32[1,64,512]{2,1,0:T(8,128)S(1)} %get-tuple-element.137), channel_id=1, source_target_pairs={{0,3},{1,2},{2,1},{3,0},{4,7},{5,6},{6,5},{7,4},{8,11},{9,10},{10,... | collective-permute-start | bytes 393224 | tf_op jit(solution)/shard_map/ppermute | solution.py:217
  121.8 9.8 %collective-permute-start.42 = (f32[1,64,512]{2,1,0:T(8,128)S(1)}, f32[1,64,512]{2,1,0:T(8,128)S(1)}, u32[]{:S(2)}, u32[]{:S(2)}) collective-permute-start(f32[1,64,512]{2,1,0:T(8,128)S(1)} %add_add_fusion.1), channel_id=1, source_target_pairs={{0,4},{1,5},{2,6},{3,7},{4,0},{5,1},{6,2},{7,3},{8,12},{9,13},{10,... | collective-permute-start | bytes 393224 | tf_op jit(solution)/shard_map/ppermute | solution.py:220
  142.1 11.7 %collective-permute-start.54 = (f32[1,64,512]{2,1,0:T(8,128)S(1)}, f32[1,64,512]{2,1,0:T(8,128)S(1)}, u32[]{:S(2)}, u32[]{:S(2)}) collective-permute-start(f32[1,64,512]{2,1,0:T(8,128)S(1)} %collective-permute-done.51.refs_3_), channel_id=1, source_target_pairs={{0,3},{1,2},{2,1},{3,0},{4,7},{5,6},{6,5},{7,4},{8,11},{9,10},{10,... | collective-permute-start | bytes 393224 | tf_op jit(solution)/shard_map/ppermute | solution.py:217
  142.3 13.1 %collective-permute-start.53 = (f32[1,64,512]{2,1,0:T(8,128)S(1)}, f32[1,64,512]{2,1,0:T(8,128)S(1)}, u32[]{:S(2)}, u32[]{:S(2)}) collective-permute-start(f32[1,64,512]{2,1,0:T(8,128)S(1)} %collective-permute-done.51.refs_3_), channel_id=1, source_target_pairs={{0,2},{1,3},{2,0},{3,1},{4,6},{5,7},{6,4},{7,5},{8,10},{9,11},{10,... | collective-permute-start | bytes 393224 | tf_op jit(solution)/shard_map/ppermute | solution.py:217
  144.2 11.2 %collective-permute-start.52 = (f32[1,64,512]{2,1,0:T(8,128)S(1)}, f32[1,64,512]{2,1,0:T(8,128)S(1)}, u32[]{:S(2)}, u32[]{:S(2)}) collective-permute-start(f32[1,64,512]{2,1,0:T(8,128)S(1)} %collective-permute-done.51.refs_3_), channel_id=1, source_target_pairs={{0,1},{1,0},{2,3},{3,2},{4,5},{5,4},{6,7},{7,6},{8,9},{9,8},{10,11... | collective-permute-start | bytes 393224 | tf_op jit(solution)/shard_map/ppermute | solution.py:217
  150.2 10.8 %collective-permute-start.56 = (f32[1,64,512]{2,1,0:T(8,128)S(1)}, f32[1,64,512]{2,1,0:T(8,128)S(1)}, u32[]{:S(2)}, u32[]{:S(2)}) collective-permute-start(f32[1,64,512]{2,1,0:T(8,128)S(1)} %get-tuple-element.145), channel_id=1, source_target_pairs={{0,1},{1,0},{2,3},{3,2},{4,5},{5,4},{6,7},{7,6},{8,9},{9,8},{10,11... | collective-permute-start | bytes 393224 | tf_op jit(solution)/shard_map/ppermute | solution.py:217
  168.7 10.3 %collective-permute-start.63 = (f32[64,512]{1,0:T(8,128)S(1)}, f32[64,512]{1,0:T(8,128)S(1)}, u32[]{:S(2)}, u32[]{:S(2)}) collective-permute-start(f32[64,512]{1,0:T(8,128)S(1)} %get-tuple-element.153), channel_id=1, source_target_pairs={{0,12},{1,13},{2,14},{3,15},{4,8},{5,9},{6,10},{7,11},{8,20},{9,21... | collective-permute-start | bytes 393224 | tf_op jit(solution)/shard_map/ppermute | solution.py:227
  (47 other events, 333.9 us)

commit v6 on v2

v6 whole, which is shorter than its diff:
```python
import functools

import jax
import jax.numpy as jnp
from jax import lax
from jax.experimental import pallas as pl
from jax.experimental.pallas import tpu as pltpu
from jax.sharding import PartitionSpec as P

TILE = 128
BLOCK = 512
VMEM = pl.BlockSpec(memory_space=pltpu.VMEM)
SMEM = pl.BlockSpec(memory_space=pltpu.SMEM)
F32 = jnp.float32
BF16 = jnp.bfloat16


def split(x):
    hi = x.astype(BF16)
    return hi, (x - hi.astype(F32)).astype(BF16)


def dot3(a, b, dims):
    (ah, al), (bh, bl) = a, b
    dot = functools.partial(lax.dot_general, dimension_numbers=(dims, ((), ())), preferred_element_type=F32)
    return dot(ah, bh) + (dot(ah, bl) + dot(al, bh))


def params(mib):
    return pltpu.CompilerParams(vmem_limit_bytes=mib * 1024 * 1024)


def load_kernel(users, ratings, users_out, ratings_out, sems):
    copies = [pltpu.make_async_copy(users, users_out, sems.at[0]), pltpu.make_async_copy(ratings, ratings_out, sems.at[1])]
    for copy in copies:
        copy.start()
    for copy in copies:
        copy.wait()


def load(users, ratings):
    return pl.pallas_call(
        load_kernel,
        in_specs=[pl.BlockSpec(memory_space=pltpu.HBM)] * 2,
        out_specs=[VMEM] * 2,
        out_shape=[jax.ShapeDtypeStruct(users.shape, F32), jax.ShapeDtypeStruct(ratings.shape, BF16)],
        scratch_shapes=[pltpu.SemaphoreType.DMA((2,))],
        compiler_params=params(12),
        cost_estimate=pl.CostEstimate(flops=0, bytes_accessed=2 * (users.size * 4 + ratings.size * 2), transcendentals=0),
        name="load",
    )(users, ratings)


def grad_kernel(ny, place, stratum, *refs):
    occ, users, rate = refs[:3]
    pieces = refs[3:3 + ny]
    err_hi, err_lo, v_hi, v_lo = refs[3 + ny:7 + ny]
    grads = refs[7 + ny:7 + 2 * ny]
    block, total, vt_hi, vt_lo = refs[7 + 2 * ny:]
    k = lax.axis_index("sub")
    mine = k & (ny - 1)
    chunk = (lax.shift_right_logical(k, ny.bit_length() - 1) + (place + stratum)) & 1
    rows, rank = total.shape
    q = pieces[0].shape[0]
    for r in range(ny):
        block[pl.ds((mine ^ r) * q, q), :] = pieces[r][...]
    v = block[...]
    v_hi[...], v_lo[...] = split(v)
    vt_hi[...], vt_lo[...] = split(v.T)
    columns = pl.ds(pl.multiple_of(chunk * rows, TILE), rows)
    for first in range(0, users.shape[0], BLOCK):
        at = slice(first, first + BLOCK)
        u = split(users[at, :])
        pred = dot3(u, (vt_hi[...], vt_lo[...]), ((1,), (0,)))
        err = rate[stratum, at, columns].astype(F32) - pred
        parts = []
        for a in range(BLOCK // TILE):
            line = []
            for b in range(rows // TILE):
                seen = occ[stratum, chunk * (rows // TILE) + b, first // TILE + a]
                part = err[a * TILE:(a + 1) * TILE, b * TILE:(b + 1) * TILE]
                line.append(jnp.where(seen == 1, part, 0.0))
            parts.append(jnp.concatenate(line, axis=1))
        err = jnp.concatenate(parts, axis=0)
        err_hi[at, :], err_lo[at, :] = split(err)
        term = dot3(split(err.T), u, ((1,), (0,)))
        if first == 0:
            total[...] = term
        else:
            total[...] += term
    for r in range(ny):
        grads[r][...] = total[pl.ds((mine ^ r) * q, q), :]


def gradients(occ, users, ratings, pieces, place, stratum):
    ny = len(pieces)
    q, rank = pieces[0].shape
    rows = ny * q
    n_users = users.shape[0]
    return pl.pallas_call(
        functools.partial(grad_kernel, ny, place, stratum),
        in_specs=[SMEM] + [VMEM] * (2 + ny),
        out_specs=[VMEM] * (4 + ny),
        out_shape=[jax.ShapeDtypeStruct((n_users, rows), BF16)] * 2 + [jax.ShapeDtypeStruct((rows, rank), BF16)] * 2
        + [jax.ShapeDtypeStruct((q, rank), F32)] * ny,
        scratch_shapes=[pltpu.VMEM((rows, rank), F32)] * 2 + [pltpu.VMEM((rank, rows), BF16)] * 2,
        compiler_params=params(24),
        cost_estimate=pl.CostEstimate(flops=12 * n_users * rows * rank, bytes_accessed=4 * n_users * rank, transcendentals=0),
        name="gradients",
    )(occ, users, ratings, *pieces)


def step_kernel(n, *refs):
    users, out = refs[0], refs[-1]
    for first in range(0, users.shape[0], BLOCK):
        at = slice(first, first + BLOCK)
        u = users[at, :]
        pull = None
        for i in range(n):
            eh, el, vh, vl = refs[1 + 4 * i:5 + 4 * i]
            part = dot3((eh[at, :], el[at, :]), (vh[...], vl[...]), ((1,), (0,)))
            pull = part if pull is None else pull + part
        out[at, :] = u + 0.02 * (pull - 0.05 * u)


def user_step(users, parts):
    n_users, rank = users.shape
    rows = sum(p[2].shape[0] for p in parts)
    return pl.pallas_call(
        functools.partial(step_kernel, len(parts)),
        in_specs=[VMEM] * (1 + 4 * len(parts)),
        out_specs=VMEM,
        out_shape=jax.ShapeDtypeStruct(users.shape, F32),
        compiler_params=params(24),
        cost_estimate=pl.CostEstimate(flops=6 * n_users * rows * rank, bytes_accessed=8 * n_users * rank, transcendentals=0),
        name="user_step",
    )(users, *[x for p in parts for x in p])


def per_device(n_group, n_sub, users, items, ratings, occupancy):
    strata = ratings.shape[0]
    ny = n_sub // 2
    occupancy = occupancy.transpose(0, 2, 1)

    def over_y(x, r):
        return lax.ppermute(x, "sub", [(i, i ^ r) for i in range(n_sub)])

    def onward(x, r):
        route = []
        for g in range(n_group):
            for i in range(n_sub):
                route.append((g * n_sub + i, (g + 1) % n_group * n_sub + (i ^ r)))
        return lax.ppermute(x, ("group", "sub"), route)

    def gathered(own):
        return [own] + [over_y(own, r) for r in range(1, ny)]

    def summed(terms):
        return functools.reduce(jnp.add, [terms[0]] + [over_y(terms[r], r) for r in range(1, ny)])

    first = gathered(items)
    second = gathered(over_y(items, ny))
    users, ratings = load(users, ratings)
    for s in range(strata):
        one = gradients(occupancy, users, ratings, first, 0, s)
        term = summed(one[4:])
        base = first[0] + 0.005 * (term - 0.05 * first[0])
        two = gradients(occupancy, users, ratings, second, 1, s)
        users = user_step(users, [one[:4], two[:4]])
        term = summed(two[4:])
        if s < strata - 1:
            near = onward(base, ny) + 0.005 * onward(term, 0)
            far = onward(base, 0) + 0.005 * onward(term, ny)
            first, second = gathered(near), gathered(far)
        elif strata % 2 == 0:
            return users, onward(base, ny) + 0.005 * onward(term, 0)
        else:
            return users, onward(base, 0) + 0.005 * onward(term, ny)


def solution(mesh):
    spec = P(("group", "sub"), None)
    third = P(None, ("group", "sub"), None)
    return jax.shard_map(
        functools.partial(per_device, mesh.shape["group"], mesh.shape["sub"]),
        mesh=mesh,
        in_specs=(spec, spec, third, third),
        out_specs=(spec, spec),
        check_vma=False,
    )
```

time: 331 us -> 162 us (0.49)
  local copies, waits for them, and re-layouts: 62.7 us -> 3.79 us
  waiting for transfers between devices: 103 us -> 47.3 us
  blocking collectives: 20.6 us -> 0 us
  other arithmetic: 17.9 us -> 1.17 us
  starting transfers between devices: 81.3 us -> 71.2 us
  Pallas kernels: 41.6 us -> 37.8 us
    all_to_all x13 -> x0, starting transfers between devices: 56.7 us -> none  [over_z(): return lax.all_to_all(x, 'sub', 0, 0, axis_index_groups=lines)]
    unnamed x142 -> x8, local copies, waits for them, and re-layouts: 56.3 us -> 3.79 us
    all_to_all x13 -> x0, waiting for transfers between devices: 51.4 us -> none  [over_z(): return lax.all_to_all(x, 'sub', 0, 0, axis_index_groups=lines)]
    ppermute x10 -> x49, starting transfers between devices: 13 us -> 60.7 us  [over_y(): return lax.ppermute(x, 'sub', [(i, i ^ r) for i in range(n_sub)])]
    ppermute x10 -> x49, waiting for transfers between devices: 51.5 us -> 25.8 us  [over_y(): return lax.ppermute(x, 'sub', [(i, i ^ r) for i in range(n_sub)])]
    ppermute x12 -> x14, waiting for transfers between devices: 0.03 us -> 21.4 us  [onward(): return lax.ppermute(x, ('group', 'sub'), route)]
    all_to_all x1 -> x0, blocking collectives: 20.6 us -> none  [over_z(): return lax.all_to_all(x, 'sub', 0, 0, axis_index_groups=lines)]
    add x15, other arithmetic: 10 us -> 1.17 us  [the longest x1 0.68 us: per_device(): return (users, onward(base, ny) + 0.005 * onward(term, 0))]
  transfers between devices with their start and end apart: 36 -> 63, of which waited for: 16 -> 23; matrix products, arithmetic and copies ran while one was open for 5% -> 0% of each run, Pallas kernels for 12% -> 23%
where the time goes in v6:
time: 162 us
  starting transfers between devices  71.2 us (44%)
  waiting for transfers between devices  47.3 us (29%)
  Pallas kernels  37.8 us (23%)
  local copies, waits for them, and re-layouts  3.79 us (2%)
    ppermute x49, starting transfers between devices, over_y(): return lax.ppermute(x, 'sub', [(i, i ^ r) for i in range(n_sub)])  60.7 us
    pallas_call x8, Pallas kernels, gradients(): pl.pallas_call(functools.partial(grad_kernel, ny, place, stratum), in_spe...  28.6 us
    ppermute x49, waiting for transfers between devices, over_y(): return lax.ppermute(x, 'sub', [(i, i ^ r) for i in range(n_sub)])  25.8 us
    ppermute x14, waiting for transfers between devices, onward(): return lax.ppermute(x, ('group', 'sub'), route)  21.4 us
    ppermute x14, starting transfers between devices, onward(): return lax.ppermute(x, ('group', 'sub'), route)  10.5 us
    pallas_call x4, Pallas kernels, user_step(): pl.pallas_call(functools.partial(step_kernel, len(parts)), in_specs=[VMEM...  8.73 us
    unnamed x8, local copies, waits for them, and re-layouts  3.79 us
  transfers between devices with their start and end apart: 63, of which 23 were waited for; matrix products, arithmetic and copies ran while one was open for 0% of the time, Pallas kernels for 23%

profile of v6, /device:TPU:0, one launch (start us, length us, event | category | flops | bytes accessed | tf_op | source)
XLA Modules:
  0.0 162.1 jit_solution(8405844802739489482)
XLA Ops:
  0.6 4.1 %collective-permute-start.3 = (f32[64,512]{1,0:T(8,128)}, f32[64,512]{1,0:T(8,128)S(1)}, u32[]{:S(2)}, u32[]{:S(2)}) collective-permute-start(f32[64,512]{1,0:T(8,128)} %refs_3_.1), channel_id=1, source_target_pairs={{0,4},{1,5},{2,6},{3,7},{4,0},{5,1},{6,2},{7,3},{8,12},{9,13},{10,... | collective-permute-start | bytes 393224 | tf_op jit(solution)/shard_map/ppermute | solution.py:146
  16.3 3.6 %gradients.8 = (bf16[1024,256]{1,0:T(8,128)(2,1)S(1)}, bf16[1024,256]{1,0:T(8,128)(2,1)S(1)}, bf16[256,512]{1,0:T(8,128)(2,1)S(1)}, bf16[256,512]{1,0:T(8,128)(2...) custom-call(s32[4,4,8]{2,1,0:T(4,128)S(1)} %bitcast.1, ...), custom_call_target="tpu_custom_call" | custom-call | flops 1610612736 | bytes 2097152 | tf_op jit(solution)/shard_map/gradients/pallas_call | solution.py:100
  23.5 3.6 %gradients.9 = (bf16[1024,256]{1,0:T(8,128)(2,1)S(1)}, bf16[1024,256]{1,0:T(8,128)(2,1)S(1)}, bf16[256,512]{1,0:T(8,128)(2,1)S(1)}, bf16[256,512]{1,0:T(8,128)(2...) custom-call(s32[4,4,8]{2,1,0:T(4,128)S(1)} %bitcast.2, ...), custom_call_target="tpu_custom_call" | custom-call | flops 1610612736 | bytes 2097152 | tf_op jit(solution)/shard_map/gradients/pallas_call | solution.py:100
  33.3 2.5 %collective-permute-done.13 = f32[64,512]{1,0:T(8,128)S(1)} collective-permute-done((f32[64,512]{1,0:T(8,128)S(1)}, f32[64,512]{1,0:T(8,128)S(1)}, u32[]{:S(2)}, u32[]{:S(2)}) %collective-permute-start.13) | collective-permute-done | bytes 131104 | tf_op jit(solution)/shard_map/ppermute | solution.py:146
  37.8 2.6 %collective-permute-start.14 = (f32[64,512]{1,0:T(8,128)S(1)}, f32[64,512]{1,0:T(8,128)S(1)}, u32[]{:S(2)}, u32[]{:S(2)}) collective-permute-start(f32[64,512]{1,0:T(8,128)S(1)} %add_add_fusion.3), channel_id=1, source_target_pairs={{0,8},{1,9},{2,10},{3,11},{4,12},{5,13},{6,14},{7,15},{8,16},{9,17... | collective-permute-start | bytes 393224 | tf_op jit(solution)/shard_map/ppermute | solution.py:153
  40.5 5.6 %collective-permute-done.19 = f32[64,512]{1,0:T(8,128)S(1)} collective-permute-done((f32[64,512]{1,0:T(8,128)S(1)}, f32[64,512]{1,0:T(8,128)S(1)}, u32[]{:S(2)}, u32[]{:S(2)}) %collective-permute-start.19) | collective-permute-done | bytes 131104 | tf_op jit(solution)/shard_map/ppermute | solution.py:153
  53.8 3.0 %collective-permute-done.22.refs_6_ = f32[64,512]{1,0:T(8,128)S(1)} collective-permute-done((f32[64,512]{1,0:T(8,128)S(1)}, f32[64,512]{1,0:T(8,128)S(1)}, u32[]{:S(2)}, u32[]{:S(2)}) %collective-permute-start.22) | collective-permute-done | bytes 131104 | tf_op jit(solution)/shard_map/ppermute | solution.py:146
  56.8 3.6 %gradients.11 = (bf16[1024,256]{1,0:T(8,128)(2,1)S(1)}, bf16[1024,256]{1,0:T(8,128)(2,1)S(1)}, bf16[256,512]{1,0:T(8,128)(2,1)S(1)}, bf16[256,512]{1,0:T(8,128)(...) custom-call(s32[4,4,8]{2,1,0:T(4,128)S(1)} %bitcast.3, ...), custom_call_target="tpu_custom_call" | custom-call | flops 1610612736 | bytes 2097152 | tf_op jit(solution)/shard_map/gradients/pallas_call | solution.py:100
  63.9 3.6 %gradients.10 = (bf16[1024,256]{1,0:T(8,128)(2,1)S(1)}, bf16[1024,256]{1,0:T(8,128)(2,1)S(1)}, bf16[256,512]{1,0:T(8,128)(2,1)S(1)}, bf16[256,512]{1,0:T(8,128)(...) custom-call(s32[4,4,8]{2,1,0:T(4,128)S(1)} %bitcast.4, ...), custom_call_target="tpu_custom_call" | custom-call | flops 1610612736 | bytes 2097152 | tf_op jit(solution)/shard_map/gradients/pallas_call | solution.py:100
  73.8 3.0 %collective-permute-done.25 = f32[64,512]{1,0:T(8,128)S(1)} collective-permute-done((f32[64,512]{1,0:T(8,128)S(1)}, f32[64,512]{1,0:T(8,128)S(1)}, u32[]{:S(2)}, u32[]{:S(2)}) %collective-permute-start.25) | collective-permute-done | bytes 131104 | tf_op jit(solution)/shard_map/ppermute | solution.py:146
  85.7 4.5 %collective-permute-done.26 = f32[64,512]{1,0:T(8,128)S(1)} collective-permute-done((f32[64,512]{1,0:T(8,128)S(1)}, f32[64,512]{1,0:T(8,128)S(1)}, u32[]{:S(2)}, u32[]{:S(2)}) %collective-permute-start.26) | collective-permute-done | bytes 131104 | tf_op jit(solution)/shard_map/ppermute | solution.py:153
  94.9 3.6 %gradients.13 = (bf16[1024,256]{1,0:T(8,128)(2,1)S(1)}, bf16[1024,256]{1,0:T(8,128)(2,1)S(1)}, bf16[256,512]{1,0:T(8,128)(2,1)S(1)}, bf16[256,512]{1,0:T(8,128)(...) custom-call(s32[4,4,8]{2,1,0:T(4,128)S(1)} %bitcast.5, ...), custom_call_target="tpu_custom_call" | custom-call | flops 1610612736 | bytes 2097152 | tf_op jit(solution)/shard_map/gradients/pallas_call | solution.py:100
  99.0 3.0 %collective-permute-start.45 = (f32[64,512]{1,0:T(8,128)S(1)}, f32[64,512]{1,0:T(8,128)S(1)}, u32[]{:S(2)}, u32[]{:S(2)}) collective-permute-start(f32[64,512]{1,0:T(8,128)S(1)} %get-tuple-element.117), channel_id=1, source_target_pairs={{0,3},{1,2},{2,1},{3,0},{4,7},{5,6},{6,5},{7,4},{8,11},{9,10},{10,... | collective-permute-start | bytes 393224 | tf_op jit(solution)/shard_map/ppermute | solution.py:146
  102.1 3.6 %gradients.12 = (bf16[1024,256]{1,0:T(8,128)(2,1)S(1)}, bf16[1024,256]{1,0:T(8,128)(2,1)S(1)}, bf16[256,512]{1,0:T(8,128)(2,1)S(1)}, bf16[256,512]{1,0:T(8,128)(...) custom-call(s32[4,4,8]{2,1,0:T(4,128)S(1)} %bitcast.6, ...), custom_call_target="tpu_custom_call" | custom-call | flops 1610612736 | bytes 2097152 | tf_op jit(solution)/shard_map/gradients/pallas_call | solution.py:100
  106.3 2.9 %collective-permute-start.41 = (f32[64,512]{1,0:T(8,128)S(1)}, f32[64,512]{1,0:T(8,128)S(1)}, u32[]{:S(2)}, u32[]{:S(2)}) collective-permute-start(f32[64,512]{1,0:T(8,128)S(1)} %get-tuple-element.113), channel_id=1, source_target_pairs={{0,3},{1,2},{2,1},{3,0},{4,7},{5,6},{6,5},{7,4},{8,11},{9,10},{10,... | collective-permute-start | bytes 393224 | tf_op jit(solution)/shard_map/ppermute | solution.py:146
  112.6 2.4 %collective-permute-done.41 = f32[64,512]{1,0:T(8,128)S(1)} collective-permute-done((f32[64,512]{1,0:T(8,128)S(1)}, f32[64,512]{1,0:T(8,128)S(1)}, u32[]{:S(2)}, u32[]{:S(2)}) %collective-permute-start.41) | collective-permute-done | bytes 131104 | tf_op jit(solution)/shard_map/ppermute | solution.py:146
  123.9 4.7 %collective-permute-done.42 = f32[64,512]{1,0:T(8,128)S(1)} collective-permute-done((f32[64,512]{1,0:T(8,128)S(1)}, f32[64,512]{1,0:T(8,128)S(1)}, u32[]{:S(2)}, u32[]{:S(2)}) %collective-permute-start.42) | collective-permute-done | bytes 131104 | tf_op jit(solution)/shard_map/ppermute | solution.py:153
  129.2 3.0 %collective-permute-start.49 = (f32[64,512]{1,0:T(8,128)S(1)}, f32[64,512]{1,0:T(8,128)S(1)}, u32[]{:S(2)}, u32[]{:S(2)}) collective-permute-start(f32[64,512]{1,0:T(8,128)S(1)} %multiply_add_fusion.3.refs_3_), channel_id=1, source_target_pairs={{0,3},{1,2},{2,1},{3,0},{4,7},{5,6},{6,5},{7,4},{8,11},{9,10},{10,... | collective-permute-start | bytes 393224 | tf_op jit(solution)/shard_map/ppermute | solution.py:146
  133.4 3.6 %gradients.15 = (bf16[1024,256]{1,0:T(8,128)(2,1)S(1)}, bf16[1024,256]{1,0:T(8,128)(2,1)S(1)}, bf16[256,512]{1,0:T(8,128)(2,1)S(1)}, bf16[256,512]{1,0:T(8,128)(...) custom-call(s32[4,4,8]{2,1,0:T(4,128)S(1)} %bitcast.7, ...), custom_call_target="tpu_custom_call" | custom-call | flops 1610612736 | bytes 2097152 | tf_op jit(solution)/shard_map/gradients/pallas_call | solution.py:100
  137.8 2.7 %collective-permute-start.61 = (f32[64,512]{1,0:T(8,128)S(1)}, f32[64,512]{1,0:T(8,128)S(1)}, u32[]{:S(2)}, u32[]{:S(2)}) collective-permute-start(f32[64,512]{1,0:T(8,128)S(1)} %get-tuple-element.133), channel_id=1, source_target_pairs={{0,3},{1,2},{2,1},{3,0},{4,7},{5,6},{6,5},{7,4},{8,11},{9,10},{10,... | collective-permute-start | bytes 393224 | tf_op jit(solution)/shard_map/ppermute | solution.py:146
  140.6 3.6 %gradients.14 = (bf16[1024,256]{1,0:T(8,128)(2,1)S(1)}, bf16[1024,256]{1,0:T(8,128)(2,1)S(1)}, bf16[256,512]{1,0:T(8,128)(2,1)S(1)}, bf16[256,512]{1,0:T(8,128)(...) custom-call(s32[4,4,8]{2,1,0:T(4,128)S(1)} %bitcast.8, ...), custom_call_target="tpu_custom_call" | custom-call | flops 1610612736 | bytes 2097152 | tf_op jit(solution)/shard_map/gradients/pallas_call | solution.py:100
  145.0 2.7 %collective-permute-start.57 = (f32[64,512]{1,0:T(8,128)S(1)}, f32[64,512]{1,0:T(8,128)S(1)}, u32[]{:S(2)}, u32[]{:S(2)}) collective-permute-start(f32[64,512]{1,0:T(8,128)S(1)} %get-tuple-element.129), channel_id=1, source_target_pairs={{0,3},{1,2},{2,1},{3,0},{4,7},{5,6},{6,5},{7,4},{8,11},{9,10},{10,... | collective-permute-start | bytes 393224 | tf_op jit(solution)/shard_map/ppermute | solution.py:146
  152.2 3.2 %user_step.7 = f32[1024,512]{1,0:T(8,128)} custom-call(f32[1024,512]{1,0:T(8,128)S(1)} %user_step.6.refs_1_.refs_0_, bf16[1024,256]{1,0:T(8,128)(2,1)S(1)} %get-tuple-element.118.refs_1_, bf16[1024,256]{1,0:T(8,128)(2,1)S(1)} %get-tuple-element.119.refs_2_, bf16[256,512]{1,0:T(8,128)(2,1)S(1)} %get-tuple-element.120.refs_3_, ...), custom_call_target="tpu_custom_call" | custom-call | flops 1610612736 | bytes 4194304 | tf_op jit(solution)/shard_map/user_step/pallas_call | solution.py:129
  155.3 6.1 %collective-permute-done.58 = f32[64,512]{1,0:T(8,128)S(1)} collective-permute-done((f32[64,512]{1,0:T(8,128)S(1)}, f32[64,512]{1,0:T(8,128)S(1)}, u32[]{:S(2)}, u32[]{:S(2)}) %collective-permute-start.58) | collective-permute-done | bytes 131104 | tf_op jit(solution)/shard_map/ppermute | solution.py:153
  (138 shorter events, 76.4 us)
Async XLA Ops:
  0.6 11.8 %collective-permute-start.3 = (f32[64,512]{1,0:T(8,128)}, f32[64,512]{1,0:T(8,128)S(1)}, u32[]{:S(2)}, u32[]{:S(2)}) collective-permute-start(f32[64,512]{1,0:T(8,128)} %refs_3_.1), channel_id=1, source_target_pairs={{0,4},{1,5},{2,6},{3,7},{4,0},{5,1},{6,2},{7,3},{8,12},{9,13},{10,... | collective-permute-start | bytes 393224 | tf_op jit(solution)/shard_map/ppermute | solution.py:146
  4.7 10.9 %collective-permute-start = (f32[64,512]{1,0:T(8,128)}, f32[64,512]{1,0:T(8,128)S(1)}, u32[]{:S(2)}, u32[]{:S(2)}) collective-permute-start(f32[64,512]{1,0:T(8,128)} %refs_3_.1), channel_id=1, source_target_pairs={{0,1},{1,0},{2,3},{3,2},{4,5},{5,4},{6,7},{7,6},{8,9},{9,8},{10,11... | collective-permute-start | bytes 393224 | tf_op jit(solution)/shard_map/ppermute | solution.py:146
  12.5 10.3 %collective-permute-start.4 = (f32[64,512]{1,0:T(8,128)S(1)}, f32[64,512]{1,0:T(8,128)S(1)}, u32[]{:S(2)}, u32[]{:S(2)}) collective-permute-start(f32[64,512]{1,0:T(8,128)S(1)} %collective-permute-done.3.refs_3_), channel_id=1, source_target_pairs={{0,1},{1,0},{2,3},{3,2},{4,5},{5,4},{6,7},{7,6},{8,9},{9,8},{10,11... | collective-permute-start | bytes 393224 | tf_op jit(solution)/shard_map/ppermute | solution.py:146
  19.9 10.1 %collective-permute-start.7 = (f32[64,512]{1,0:T(8,128)S(1)}, f32[64,512]{1,0:T(8,128)S(1)}, u32[]{:S(2)}, u32[]{:S(2)}) collective-permute-start(f32[64,512]{1,0:T(8,128)S(1)} %get-tuple-element.79), channel_id=1, source_target_pairs={{0,1},{1,0},{2,3},{3,2},{4,5},{5,4},{6,7},{7,6},{8,9},{9,8},{10,11... | collective-permute-start | bytes 393224 | tf_op jit(solution)/shard_map/ppermute | solution.py:146
  30.7 9.8 %collective-permute-start.18 = (f32[64,512]{1,0:T(8,128)S(1)}, f32[64,512]{1,0:T(8,128)S(1)}, u32[]{:S(2)}, u32[]{:S(2)}) collective-permute-start(f32[64,512]{1,0:T(8,128)S(1)} %multiply_add_fusion.10), channel_id=1, source_target_pairs={{0,8},{1,9},{2,10},{3,11},{4,12},{5,13},{6,14},{7,15},{8,16},{9,17... | collective-permute-start | bytes 393224 | tf_op jit(solution)/shard_map/ppermute | solution.py:153
  30.7 18.9 %collective-permute-start.10 = (f32[64,512]{1,0:T(8,128)S(1)}, f32[64,512]{1,0:T(8,128)S(1)}, u32[]{:S(2)}, u32[]{:S(2)}) collective-permute-start(f32[64,512]{1,0:T(8,128)S(1)} %multiply_add_fusion.10), channel_id=1, source_target_pairs={{0,12},{1,13},{2,14},{3,15},{4,8},{5,9},{6,10},{7,11},{8,20},{9,21... | collective-permute-start | bytes 393224 | tf_op jit(solution)/shard_map/ppermute | solution.py:153
  35.9 10.2 %collective-permute-start.19 = (f32[64,512]{1,0:T(8,128)S(1)}, f32[64,512]{1,0:T(8,128)S(1)}, u32[]{:S(2)}, u32[]{:S(2)}) collective-permute-start(f32[64,512]{1,0:T(8,128)S(1)} %add_add_fusion.3), channel_id=1, source_target_pairs={{0,12},{1,13},{2,14},{3,15},{4,8},{5,9},{6,10},{7,11},{8,20},{9,21... | collective-permute-start | bytes 393224 | tf_op jit(solution)/shard_map/ppermute | solution.py:153
  37.8 11.8 %collective-permute-start.14 = (f32[64,512]{1,0:T(8,128)S(1)}, f32[64,512]{1,0:T(8,128)S(1)}, u32[]{:S(2)}, u32[]{:S(2)}) collective-permute-start(f32[64,512]{1,0:T(8,128)S(1)} %add_add_fusion.3), channel_id=1, source_target_pairs={{0,8},{1,9},{2,10},{3,11},{4,12},{5,13},{6,14},{7,15},{8,16},{9,17... | collective-permute-start | bytes 393224 | tf_op jit(solution)/shard_map/ppermute | solution.py:153
  49.7 12.1 %collective-permute-start.15 = (f32[64,512]{1,0:T(8,128)S(1)}, f32[64,512]{1,0:T(8,128)S(1)}, u32[]{:S(2)}, u32[]{:S(2)}) collective-permute-start(f32[64,512]{1,0:T(8,128)S(1)} %multiply_add_fusion.9.refs_3_), channel_id=1, source_target_pairs={{0,1},{1,0},{2,3},{3,2},{4,5},{5,4},{6,7},{7,6},{8,9},{9,8},{10,11... | collective-permute-start | bytes 393224 | tf_op jit(solution)/shard_map/ppermute | solution.py:146
  51.0 12.9 %collective-permute-start.16 = (f32[64,512]{1,0:T(8,128)S(1)}, f32[64,512]{1,0:T(8,128)S(1)}, u32[]{:S(2)}, u32[]{:S(2)}) collective-permute-start(f32[64,512]{1,0:T(8,128)S(1)} %multiply_add_fusion.9.refs_3_), channel_id=1, source_target_pairs={{0,2},{1,3},{2,0},{3,1},{4,6},{5,7},{6,4},{7,5},{8,10},{9,11},{10,... | collective-permute-start | bytes 393224 | tf_op jit(solution)/shard_map/ppermute | solution.py:146
  52.1 11.8 %collective-permute-start.17 = (f32[64,512]{1,0:T(8,128)S(1)}, f32[64,512]{1,0:T(8,128)S(1)}, u32[]{:S(2)}, u32[]{:S(2)}) collective-permute-start(f32[64,512]{1,0:T(8,128)S(1)} %multiply_add_fusion.9.refs_3_), channel_id=1, source_target_pairs={{0,3},{1,2},{2,1},{3,0},{4,7},{5,6},{6,5},{7,4},{8,11},{9,10},{10,... | collective-permute-start | bytes 393224 | tf_op jit(solution)/shard_map/ppermute | solution.py:146
  71.1 11.0 %collective-permute-start.35 = (f32[64,512]{1,0:T(8,128)S(1)}, f32[64,512]{1,0:T(8,128)S(1)}, u32[]{:S(2)}, u32[]{:S(2)}) collective-permute-start(f32[64,512]{1,0:T(8,128)S(1)} %add_add_fusion.2), channel_id=1, source_target_pairs={{0,12},{1,13},{2,14},{3,15},{4,8},{5,9},{6,10},{7,11},{8,20},{9,21... | collective-permute-start | bytes 393224 | tf_op jit(solution)/shard_map/ppermute | solution.py:153
  79.8 10.4 %collective-permute-start.26 = (f32[64,512]{1,0:T(8,128)S(1)}, f32[64,512]{1,0:T(8,128)S(1)}, u32[]{:S(2)}, u32[]{:S(2)}) collective-permute-start(f32[64,512]{1,0:T(8,128)S(1)} %multiply_add_fusion.7), channel_id=1, source_target_pairs={{0,12},{1,13},{2,14},{3,15},{4,8},{5,9},{6,10},{7,11},{8,20},{9,21... | collective-permute-start | bytes 393224 | tf_op jit(solution)/shard_map/ppermute | solution.py:153
  83.4 10.4 %collective-permute-start.37 = (f32[64,512]{1,0:T(8,128)S(1)}, f32[64,512]{1,0:T(8,128)S(1)}, u32[]{:S(2)}, u32[]{:S(2)}) collective-permute-start(f32[64,512]{1,0:T(8,128)S(1)} %multiply_add_fusion.5.refs_3_), channel_id=1, source_target_pairs={{0,2},{1,3},{2,0},{3,1},{4,6},{5,7},{6,4},{7,5},{8,10},{9,11},{10,... | collective-permute-start | bytes 393224 | tf_op jit(solution)/shard_map/ppermute | solution.py:146
  91.9 10.2 %collective-permute-start.32 = (f32[64,512]{1,0:T(8,128)S(1)}, f32[64,512]{1,0:T(8,128)S(1)}, u32[]{:S(2)}, u32[]{:S(2)}) collective-permute-start(f32[64,512]{1,0:T(8,128)S(1)} %multiply_add_fusion.6.refs_3_), channel_id=1, source_target_pairs={{0,2},{1,3},{2,0},{3,1},{4,6},{5,7},{6,4},{7,5},{8,10},{9,11},{10,... | collective-permute-start | bytes 393224 | tf_op jit(solution)/shard_map/ppermute | solution.py:146
  91.9 10.2 %collective-permute-start.33 = (f32[64,512]{1,0:T(8,128)S(1)}, f32[64,512]{1,0:T(8,128)S(1)}, u32[]{:S(2)}, u32[]{:S(2)}) collective-permute-start(f32[64,512]{1,0:T(8,128)S(1)} %multiply_add_fusion.6.refs_3_), channel_id=1, source_target_pairs={{0,3},{1,2},{2,1},{3,0},{4,7},{5,6},{6,5},{7,4},{8,11},{9,10},{10,... | collective-permute-start | bytes 393224 | tf_op jit(solution)/shard_map/ppermute | solution.py:146
  99.0 10.2 %collective-permute-start.44 = (f32[64,512]{1,0:T(8,128)S(1)}, f32[64,512]{1,0:T(8,128)S(1)}, u32[]{:S(2)}, u32[]{:S(2)}) collective-permute-start(f32[64,512]{1,0:T(8,128)S(1)} %get-tuple-element.116), channel_id=1, source_target_pairs={{0,2},{1,3},{2,0},{3,1},{4,6},{5,7},{6,4},{7,5},{8,10},{9,11},{10,... | collective-permute-start | bytes 393224 | tf_op jit(solution)/shard_map/ppermute | solution.py:146
  99.0 10.2 %collective-permute-start.45 = (f32[64,512]{1,0:T(8,128)S(1)}, f32[64,512]{1,0:T(8,128)S(1)}, u32[]{:S(2)}, u32[]{:S(2)}) collective-permute-start(f32[64,512]{1,0:T(8,128)S(1)} %get-tuple-element.117), channel_id=1, source_target_pairs={{0,3},{1,2},{2,1},{3,0},{4,7},{5,6},{6,5},{7,4},{8,11},{9,10},{10,... | collective-permute-start | bytes 393224 | tf_op jit(solution)/shard_map/ppermute | solution.py:146
  121.9 10.3 %collective-permute-start.53 = (f32[64,512]{1,0:T(8,128)S(1)}, f32[64,512]{1,0:T(8,128)S(1)}, u32[]{:S(2)}, u32[]{:S(2)}) collective-permute-start(f32[64,512]{1,0:T(8,128)S(1)} %multiply_add_fusion.2.refs_3_), channel_id=1, source_target_pairs={{0,2},{1,3},{2,0},{3,1},{4,6},{5,7},{6,4},{7,5},{8,10},{9,11},{10,... | collective-permute-start | bytes 393224 | tf_op jit(solution)/shard_map/ppermute | solution.py:146
  122.5 10.9 %collective-permute-start.54 = (f32[64,512]{1,0:T(8,128)S(1)}, f32[64,512]{1,0:T(8,128)S(1)}, u32[]{:S(2)}, u32[]{:S(2)}) collective-permute-start(f32[64,512]{1,0:T(8,128)S(1)} %multiply_add_fusion.2.refs_3_), channel_id=1, source_target_pairs={{0,3},{1,2},{2,1},{3,0},{4,7},{5,6},{6,5},{7,4},{8,11},{9,10},{10,... | collective-permute-start | bytes 393224 | tf_op jit(solution)/shard_map/ppermute | solution.py:146
  129.2 11.4 %collective-permute-start.48 = (f32[64,512]{1,0:T(8,128)S(1)}, f32[64,512]{1,0:T(8,128)S(1)}, u32[]{:S(2)}, u32[]{:S(2)}) collective-permute-start(f32[64,512]{1,0:T(8,128)S(1)} %multiply_add_fusion.3.refs_3_), channel_id=1, source_target_pairs={{0,2},{1,3},{2,0},{3,1},{4,6},{5,7},{6,4},{7,5},{8,10},{9,11},{10,... | collective-permute-start | bytes 393224 | tf_op jit(solution)/shard_map/ppermute | solution.py:146
  129.2 11.4 %collective-permute-start.49 = (f32[64,512]{1,0:T(8,128)S(1)}, f32[64,512]{1,0:T(8,128)S(1)}, u32[]{:S(2)}, u32[]{:S(2)}) collective-permute-start(f32[64,512]{1,0:T(8,128)S(1)} %multiply_add_fusion.3.refs_3_), channel_id=1, source_target_pairs={{0,3},{1,2},{2,1},{3,0},{4,7},{5,6},{6,5},{7,4},{8,11},{9,10},{10,... | collective-permute-start | bytes 393224 | tf_op jit(solution)/shard_map/ppermute | solution.py:146
  137.8 9.9 %collective-permute-start.60 = (f32[64,512]{1,0:T(8,128)S(1)}, f32[64,512]{1,0:T(8,128)S(1)}, u32[]{:S(2)}, u32[]{:S(2)}) collective-permute-start(f32[64,512]{1,0:T(8,128)S(1)} %get-tuple-element.132), channel_id=1, source_target_pairs={{0,2},{1,3},{2,0},{3,1},{4,6},{5,7},{6,4},{7,5},{8,10},{9,11},{10,... | collective-permute-start | bytes 393224 | tf_op jit(solution)/shard_map/ppermute | solution.py:146
  137.8 9.9 %collective-permute-start.61 = (f32[64,512]{1,0:T(8,128)S(1)}, f32[64,512]{1,0:T(8,128)S(1)}, u32[]{:S(2)}, u32[]{:S(2)}) collective-permute-start(f32[64,512]{1,0:T(8,128)S(1)} %get-tuple-element.133), channel_id=1, source_target_pairs={{0,3},{1,2},{2,1},{3,0},{4,7},{5,6},{6,5},{7,4},{8,11},{9,10},{10,... | collective-permute-start | bytes 393224 | tf_op jit(solution)/shard_map/ppermute | solution.py:146
  (43 other events, 310.7 us)

commit v7 on v6

v7 whole, which is shorter than its diff:
```python
import functools

import jax
import jax.numpy as jnp
from jax import lax
from jax.experimental import pallas as pl
from jax.experimental.pallas import tpu as pltpu
from jax.sharding import PartitionSpec as P

TILE = 128
BLOCK = 512
VMEM = pl.BlockSpec(memory_space=pltpu.VMEM)
SMEM = pl.BlockSpec(memory_space=pltpu.SMEM)
F32 = jnp.float32
BF16 = jnp.bfloat16


def split(x):
    hi = x.astype(BF16)
    return hi, (x - hi.astype(F32)).astype(BF16)


def dot3(a, b, dims):
    (ah, al), (bh, bl) = a, b
    dot = functools.partial(lax.dot_general, dimension_numbers=(dims, ((), ())), preferred_element_type=F32)
    return dot(ah, bh) + (dot(ah, bl) + dot(al, bh))


def params(mib):
    return pltpu.CompilerParams(vmem_limit_bytes=mib * 1024 * 1024)


def load_kernel(users, ratings, users_out, turned, held, sems):
    strata = ratings.shape[0]
    copies = [pltpu.make_async_copy(ratings.at[s], held.at[s], sems.at[s]) for s in range(strata)]
    copies.append(pltpu.make_async_copy(users, users_out, sems.at[strata]))
    for copy in copies:
        copy.start()
    for s in range(strata):
        copies[s].wait()
        turned[s] = held[s].T
    copies[strata].wait()


def load(users, ratings):
    strata, n_users, items = ratings.shape
    return pl.pallas_call(
        load_kernel,
        in_specs=[pl.BlockSpec(memory_space=pl.ANY)] * 2,
        out_specs=[VMEM] * 2,
        out_shape=[jax.ShapeDtypeStruct(users.shape, F32), jax.ShapeDtypeStruct((strata, items, n_users), BF16)],
        scratch_shapes=[pltpu.VMEM(ratings.shape, BF16), pltpu.SemaphoreType.DMA((strata + 1,))],
        compiler_params=params(44),
        cost_estimate=pl.CostEstimate(flops=0, bytes_accessed=2 * (users.size * 4 + ratings.size * 2), transcendentals=0),
        name="load",
    )(users, ratings)


def grad_kernel(ny, place, stratum, *refs):
    occ, users, rate = refs[:3]
    pieces = refs[3:3 + ny]
    err_hi, err_lo, v_hi, v_lo = refs[3 + ny:7 + ny]
    grads = refs[7 + ny:7 + 2 * ny]
    block, total = refs[7 + 2 * ny:]
    k = lax.axis_index("sub")
    mine = k & (ny - 1)
    chunk = (lax.shift_right_logical(k, ny.bit_length() - 1) + (place + stratum)) & 1
    rows, rank = total.shape
    q = pieces[0].shape[0]
    for r in range(ny):
        block[pl.ds((mine ^ r) * q, q), :] = pieces[r][...]
    v_hi[...], v_lo[...] = split(block[...])
    u = split(users[...])
    pred = dot3((v_hi[...], v_lo[...]), u, ((1,), (1,)))
    at = pl.ds(pl.multiple_of(chunk * rows, TILE), rows)
    err = rate[stratum, at, :].astype(F32) - pred
    parts = []
    for b in range(rows // TILE):
        line = []
        for a in range(err.shape[1] // TILE):
            seen = occ[stratum, chunk * (rows // TILE) + b, a]
            part = err[b * TILE:(b + 1) * TILE, a * TILE:(a + 1) * TILE]
            line.append(jnp.where(seen == 1, part, 0.0))
        parts.append(jnp.concatenate(line, axis=1))
    e = split(jnp.concatenate(parts, axis=0))
    err_hi[...], err_lo[...] = e
    total[...] = dot3(e, u, ((1,), (0,)))
    for r in range(ny):
        grads[r][...] = total[pl.ds((mine ^ r) * q, q), :]


def gradients(occ, users, ratings, pieces, place, stratum):
    ny = len(pieces)
    q, rank = pieces[0].shape
    rows = ny * q
    n_users = users.shape[0]
    return pl.pallas_call(
        functools.partial(grad_kernel, ny, place, stratum),
        in_specs=[SMEM] + [VMEM] * (2 + ny),
        out_specs=[VMEM] * (4 + ny),
        out_shape=[jax.ShapeDtypeStruct((rows, n_users), BF16)] * 2 + [jax.ShapeDtypeStruct((rows, rank), BF16)] * 2
        + [jax.ShapeDtypeStruct((q, rank), F32)] * ny,
        scratch_shapes=[pltpu.VMEM((rows, rank), F32)] * 2,
        compiler_params=params(24),
        cost_estimate=pl.CostEstimate(flops=12 * n_users * rows * rank, bytes_accessed=4 * n_users * rank, transcendentals=0),
        name="gradients",
    )(occ, users, ratings, *pieces)


def step_kernel(n, *refs):
    users, out = refs[0], refs[-1]
    for first in range(0, users.shape[0], BLOCK):
        at = slice(first, first + BLOCK)
        u = users[at, :]
        pull = None
        for i in range(n):
            eh, el, vh, vl = refs[1 + 4 * i:5 + 4 * i]
            part = dot3((eh[:, at], el[:, at]), (vh[...], vl[...]), ((0,), (0,)))
            pull = part if pull is None else pull + part
        out[at, :] = u + 0.02 * (pull - 0.05 * u)


def user_step(users, parts):
    n_users, rank = users.shape
    rows = sum(p[2].shape[0] for p in parts)
    return pl.pallas_call(
        functools.partial(step_kernel, len(parts)),
        in_specs=[VMEM] * (1 + 4 * len(parts)),
        out_specs=VMEM,
        out_shape=jax.ShapeDtypeStruct(users.shape, F32),
        compiler_params=params(24),
        cost_estimate=pl.CostEstimate(flops=6 * n_users * rows * rank, bytes_accessed=8 * n_users * rank, transcendentals=0),
        name="user_step",
    )(users, *[x for p in parts for x in p])


def per_device(n_group, n_sub, users, items, ratings, occupancy):
    strata = ratings.shape[0]
    ny = n_sub // 2
    occupancy = occupancy.transpose(0, 2, 1)

    def over_y(x, r):
        return lax.ppermute(x, "sub", [(i, i ^ r) for i in range(n_sub)])

    def onward(x, r):
        route = []
        for g in range(n_group):
            for i in range(n_sub):
                route.append((g * n_sub + i, (g + 1) % n_group * n_sub + (i ^ r)))
        return lax.ppermute(x, ("group", "sub"), route)

    def gathered(own):
        return [own] + [over_y(own, r) for r in range(1, ny)]

    def arrived(terms):
        return [terms[0]] + [over_y(terms[r], r) for r in range(1, ny)]

    first = gathered(items)
    second = gathered(over_y(items, ny))
    users, ratings = load(users, ratings)
    for s in range(strata):
        last = s == strata - 1
        one = gradients(occupancy, users, ratings, first, 0, s)
        second, _ = lax.optimization_barrier((second, one[4]))
        two = gradients(occupancy, users, ratings, second, 1, s)
        term = arrived(one[4:])
        users, term[1] = lax.optimization_barrier((users, term[1]))
        users = user_step(users, [one[:4], two[:4]])
        term, users = lax.optimization_barrier((functools.reduce(jnp.add, term), users))
        base = first[0] + 0.005 * (term - 0.05 * first[0])
        term = functools.reduce(jnp.add, arrived(two[4:]))
        flip = strata % 2 if last else 0
        near = onward(base, 0 if flip else ny) + 0.005 * onward(term, ny if flip else 0)
        if last:
            return users, near
        far = onward(base, 0) + 0.005 * onward(term, ny)
        first, second = gathered(near), gathered(far)


def solution(mesh):
    spec = P(("group", "sub"), None)
    third = P(None, ("group", "sub"), None)
    return jax.shard_map(
        functools.partial(per_device, mesh.shape["group"], mesh.shape["sub"]),
        mesh=mesh,
        in_specs=(spec, spec, third, third),
        out_specs=(spec, spec),
        check_vma=False,
    )
```

time: 162 us -> 163 us (level)
  waiting for transfers between devices: 47.3 us -> 61.1 us
  starting transfers between devices: 71.2 us -> 65.5 us
  Pallas kernels: 37.8 us -> 32.7 us
  local copies, waits for them, and re-layouts: 3.79 us -> 1.6 us
    ppermute x49, waiting for transfers between devices: 25.8 us -> 35.3 us  [over_y(): return lax.ppermute(x, 'sub', [(i, i ^ r) for i in range(n_sub)])]
    pallas_call x8, Pallas kernels: 28.6 us -> 21 us  [gradients(): pl.pallas_call(functools.partial(grad_kernel, ny, place, stratum), in_spe...]
    ppermute x14, waiting for transfers between devices: 21.4 us -> 25.8 us  [onward(): return lax.ppermute(x, ('group', 'sub'), route)]
    ppermute x14, starting transfers between devices: 10.5 us -> 6.77 us  [onward(): return lax.ppermute(x, ('group', 'sub'), route)]
    pallas_call x1, Pallas kernels: 0.44 us -> 2.7 us  [load(): pl.pallas_call(load_kernel, in_specs=[pl.BlockSpec(memory_space=pl.ANY)]...]
    unnamed x8 -> x6, local copies, waits for them, and re-layouts: 3.79 us -> 1.6 us
    ppermute x49, starting transfers between devices: 60.7 us -> 58.7 us  [over_y(): return lax.ppermute(x, 'sub', [(i, i ^ r) for i in range(n_sub)])]
  transfers between devices with their start and end apart: 63 -> 63, of which waited for: 23 -> 34; matrix products, arithmetic and copies ran while one was open for 0% -> 0% of each run, Pallas kernels for 23% -> 18%
where the time goes in v7:
time: 163 us
  starting transfers between devices  65.5 us (40%)
  waiting for transfers between devices  61.1 us (37%)
  Pallas kernels  32.7 us (20%)
    ppermute x49, starting transfers between devices, over_y(): return lax.ppermute(x, 'sub', [(i, i ^ r) for i in range(n_sub)])  58.7 us
    ppermute x49, waiting for transfers between devices, over_y(): return lax.ppermute(x, 'sub', [(i, i ^ r) for i in range(n_sub)])  35.3 us
    ppermute x14, waiting for transfers between devices, onward(): return lax.ppermute(x, ('group', 'sub'), route)  25.8 us
    pallas_call x8, Pallas kernels, gradients(): pl.pallas_call(functools.partial(grad_kernel, ny, place, stratum), in_spe...  21 us
    pallas_call x4, Pallas kernels, user_step(): pl.pallas_call(functools.partial(step_kernel, len(parts)), in_specs=[VMEM...  8.97 us
    ppermute x14, starting transfers between devices, onward(): return lax.ppermute(x, ('group', 'sub'), route)  6.77 us
  transfers between devices with their start and end apart: 63, of which 34 were waited for; matrix products, arithmetic and copies ran while one was open for 0% of the time, Pallas kernels for 18%

profile of v7, /device:TPU:0, one launch (start us, length us, event | category | flops | bytes accessed | tf_op | source)
XLA Modules:
  0.0 163.2 jit_solution(15056705095331711910)
XLA Ops:
  0.6 4.1 %collective-permute-start.6 = (f32[64,512]{1,0:T(8,128)}, f32[64,512]{1,0:T(8,128)S(1)}, u32[]{:S(2)}, u32[]{:S(2)}) collective-permute-start(f32[64,512]{1,0:T(8,128)} %refs_3_.1), channel_id=1, source_target_pairs={{0,4},{1,5},{2,6},{3,7},{4,0},{5,1},{6,2},{7,3},{8,12},{9,13},{10,... | collective-permute-start | bytes 393224 | tf_op jit(solution)/shard_map/ppermute | solution.py:143
  9.8 2.7 %load.1 = (f32[1024,512]{1,0:T(8,128)S(1)}, bf16[4,512,1024]{2,1,0:T(8,128)(2,1)S(1)}) custom-call(f32[1024,512]{1,0:T(8,128)S(1)} %copy-done, bf16[4,1024,512]{2,1,0:T(8,128)(2,1)} %ratings.1), custom_call_target="tpu_custom_call" | custom-call | bytes 12582912 | tf_op jit(solution)/shard_map/load/pallas_call | solution.py:47
  12.5 2.6 %collective-permute-start.9 = (f32[64,512]{1,0:T(8,128)S(1)}, f32[64,512]{1,0:T(8,128)S(1)}, u32[]{:S(2)}, u32[]{:S(2)}) collective-permute-start(f32[64,512]{1,0:T(8,128)S(1)} %collective-permute-done.6.refs_3_), channel_id=1, source_target_pairs={{0,3},{1,2},{2,1},{3,0},{4,7},{5,6},{6,5},{7,4},{8,11},{9,10},{10,... | collective-permute-start | bytes 393224 | tf_op jit(solution)/shard_map/ppermute | solution.py:143
  16.1 2.6 %gradients.8 = (bf16[256,1024]{1,0:T(8,128)(2,1)S(1)}, bf16[256,1024]{1,0:T(8,128)(2,1)S(1)}, bf16[256,512]{1,0:T(8,128)(2,1)S(1)}, bf16[256,512]{1,0:T(8,128)(2...) custom-call(s32[4,4,8]{2,1,0:T(4,128)S(1)} %bitcast.1, ...), custom_call_target="tpu_custom_call" | custom-call | flops 1610612736 | bytes 2097152 | tf_op jit(solution)/shard_map/gradients/pallas_call | solution.py:97
  22.3 2.9 %collective-permute-done.3 = f32[64,512]{1,0:T(8,128)S(1)} collective-permute-done((f32[64,512]{1,0:T(8,128)S(1)}, f32[64,512]{1,0:T(8,128)S(1)}, u32[]{:S(2)}, u32[]{:S(2)}) %collective-permute-start.3) | collective-permute-done | bytes 131104 | tf_op jit(solution)/shard_map/ppermute | solution.py:143
  25.2 2.6 %gradients.9 = (bf16[256,1024]{1,0:T(8,128)(2,1)S(1)}, bf16[256,1024]{1,0:T(8,128)(2,1)S(1)}, bf16[256,512]{1,0:T(8,128)(2,1)S(1)}, bf16[256,512]{1,0:T(8,128)(2...) custom-call(s32[4,4,8]{2,1,0:T(4,128)S(1)} %bitcast.2, ...), custom_call_target="tpu_custom_call" | custom-call | flops 1610612736 | bytes 2097152 | tf_op jit(solution)/shard_map/gradients/pallas_call | solution.py:97
  36.3 4.5 %collective-permute-done.13 = f32[64,512]{1,0:T(8,128)S(1)} collective-permute-done((f32[64,512]{1,0:T(8,128)S(1)}, f32[64,512]{1,0:T(8,128)S(1)}, u32[]{:S(2)}, u32[]{:S(2)}) %collective-permute-start.13) | collective-permute-done | bytes 131104 | tf_op jit(solution)/shard_map/ppermute | solution.py:143
  48.8 2.8 %collective-permute-done.22 = f32[64,512]{1,0:T(8,128)S(1)} collective-permute-done((f32[64,512]{1,0:T(8,128)S(1)}, f32[64,512]{1,0:T(8,128)S(1)}, u32[]{:S(2)}, u32[]{:S(2)}) %collective-permute-start.22) | collective-permute-done | bytes 131104 | tf_op jit(solution)/shard_map/ppermute | solution.py:150
  56.9 2.6 %gradients.10 = (bf16[256,1024]{1,0:T(8,128)(2,1)S(1)}, bf16[256,1024]{1,0:T(8,128)(2,1)S(1)}, bf16[256,512]{1,0:T(8,128)(2,1)S(1)}, bf16[256,512]{1,0:T(8,128)(...) custom-call(s32[4,4,8]{2,1,0:T(4,128)S(1)} %bitcast.3, ...), custom_call_target="tpu_custom_call" | custom-call | flops 1610612736 | bytes 2097152 | tf_op jit(solution)/shard_map/gradients/pallas_call | solution.py:97
  62.6 2.7 %collective-permute-start.20 = (f32[64,512]{1,0:T(8,128)S(1)}, f32[64,512]{1,0:T(8,128)S(1)}, u32[]{:S(2)}, u32[]{:S(2)}) collective-permute-start(f32[64,512]{1,0:T(8,128)S(1)} %get-tuple-element.130), channel_id=1, source_target_pairs={{0,3},{1,2},{2,1},{3,0},{4,7},{5,6},{6,5},{7,4},{8,11},{9,10},{10,... | collective-permute-start | bytes 393224 | tf_op jit(solution)/shard_map/ppermute | solution.py:143
  65.3 2.6 %gradients.11 = (bf16[256,1024]{1,0:T(8,128)(2,1)S(1)}, bf16[256,1024]{1,0:T(8,128)(2,1)S(1)}, bf16[256,512]{1,0:T(8,128)(2,1)S(1)}, bf16[256,512]{1,0:T(8,128)(...) custom-call(s32[4,4,8]{2,1,0:T(4,128)S(1)} %bitcast.4, ...), custom_call_target="tpu_custom_call" | custom-call | flops 1610612736 | bytes 2097152 | tf_op jit(solution)/shard_map/gradients/pallas_call | solution.py:97
  68.8 2.7 %collective-permute-start.29 = (f32[64,512]{1,0:T(8,128)S(1)}, f32[64,512]{1,0:T(8,128)S(1)}, u32[]{:S(2)}, u32[]{:S(2)}) collective-permute-start(f32[64,512]{1,0:T(8,128)S(1)} %get-tuple-element.149), channel_id=1, source_target_pairs={{0,3},{1,2},{2,1},{3,0},{4,7},{5,6},{6,5},{7,4},{8,11},{9,10},{10,... | collective-permute-start | bytes 393224 | tf_op jit(solution)/shard_map/ppermute | solution.py:143
  78.9 3.1 %collective-permute-done.26 = f32[64,512]{1,0:T(8,128)S(1)} collective-permute-done((f32[64,512]{1,0:T(8,128)S(1)}, f32[64,512]{1,0:T(8,128)S(1)}, u32[]{:S(2)}, u32[]{:S(2)}) %collective-permute-start.26) | collective-permute-done | bytes 131104 | tf_op jit(solution)/shard_map/ppermute | solution.py:150
  93.5 2.6 %gradients.12 = (bf16[256,1024]{1,0:T(8,128)(2,1)S(1)}, bf16[256,1024]{1,0:T(8,128)(2,1)S(1)}, bf16[256,512]{1,0:T(8,128)(2,1)S(1)}, bf16[256,512]{1,0:T(8,128)(...) custom-call(s32[4,4,8]{2,1,0:T(4,128)S(1)} %bitcast.5, ...), custom_call_target="tpu_custom_call" | custom-call | flops 1610612736 | bytes 2097152 | tf_op jit(solution)/shard_map/gradients/pallas_call | solution.py:97
  99.7 2.7 %collective-permute-start.36 = (f32[64,512]{1,0:T(8,128)S(1)}, f32[64,512]{1,0:T(8,128)S(1)}, u32[]{:S(2)}, u32[]{:S(2)}) collective-permute-start(f32[64,512]{1,0:T(8,128)S(1)} %get-tuple-element.154), channel_id=1, source_target_pairs={{0,3},{1,2},{2,1},{3,0},{4,7},{5,6},{6,5},{7,4},{8,11},{9,10},{10,... | collective-permute-start | bytes 393224 | tf_op jit(solution)/shard_map/ppermute | solution.py:143
  102.3 2.6 %gradients.13 = (bf16[256,1024]{1,0:T(8,128)(2,1)S(1)}, bf16[256,1024]{1,0:T(8,128)(2,1)S(1)}, bf16[256,512]{1,0:T(8,128)(2,1)S(1)}, bf16[256,512]{1,0:T(8,128)(...) custom-call(s32[4,4,8]{2,1,0:T(4,128)S(1)} %bitcast.6, ...), custom_call_target="tpu_custom_call" | custom-call | flops 1610612736 | bytes 2097152 | tf_op jit(solution)/shard_map/gradients/pallas_call | solution.py:97
  105.9 2.7 %collective-permute-start.45 = (f32[64,512]{1,0:T(8,128)S(1)}, f32[64,512]{1,0:T(8,128)S(1)}, u32[]{:S(2)}, u32[]{:S(2)}) collective-permute-start(f32[64,512]{1,0:T(8,128)S(1)} %get-tuple-element.173), channel_id=1, source_target_pairs={{0,3},{1,2},{2,1},{3,0},{4,7},{5,6},{6,5},{7,4},{8,11},{9,10},{10,... | collective-permute-start | bytes 393224 | tf_op jit(solution)/shard_map/ppermute | solution.py:143
  115.2 3.3 %collective-permute-done.42 = f32[64,512]{1,0:T(8,128)S(1)} collective-permute-done((f32[64,512]{1,0:T(8,128)S(1)}, f32[64,512]{1,0:T(8,128)S(1)}, u32[]{:S(2)}, u32[]{:S(2)}) %collective-permute-start.42) | collective-permute-done | bytes 131104 | tf_op jit(solution)/shard_map/ppermute | solution.py:150
  129.9 2.6 %gradients.14 = (bf16[256,1024]{1,0:T(8,128)(2,1)S(1)}, bf16[256,1024]{1,0:T(8,128)(2,1)S(1)}, bf16[256,512]{1,0:T(8,128)(2,1)S(1)}, bf16[256,512]{1,0:T(8,128)(...) custom-call(s32[4,4,8]{2,1,0:T(4,128)S(1)} %bitcast.7, ...), custom_call_target="tpu_custom_call" | custom-call | flops 1610612736 | bytes 2097152 | tf_op jit(solution)/shard_map/gradients/pallas_call | solution.py:97
  135.0 2.6 %gradients.15 = (bf16[256,1024]{1,0:T(8,128)(2,1)S(1)}, bf16[256,1024]{1,0:T(8,128)(2,1)S(1)}, bf16[256,512]{1,0:T(8,128)(2,1)S(1)}, bf16[256,512]{1,0:T(8,128)(...) custom-call(s32[4,4,8]{2,1,0:T(4,128)S(1)} %bitcast.8, ...), custom_call_target="tpu_custom_call" | custom-call | flops 1610612736 | bytes 2097152 | tf_op jit(solution)/shard_map/gradients/pallas_call | solution.py:97
  138.5 2.7 %collective-permute-start.61 = (f32[64,512]{1,0:T(8,128)S(1)}, f32[64,512]{1,0:T(8,128)S(1)}, u32[]{:S(2)}, u32[]{:S(2)}) collective-permute-start(f32[64,512]{1,0:T(8,128)S(1)} %get-tuple-element.197), channel_id=1, source_target_pairs={{0,3},{1,2},{2,1},{3,0},{4,7},{5,6},{6,5},{7,4},{8,11},{9,10},{10,... | collective-permute-start | bytes 393224 | tf_op jit(solution)/shard_map/ppermute | solution.py:143
  144.9 3.5 %collective-permute-done.61 = f32[64,512]{1,0:T(8,128)S(1)} collective-permute-done((f32[64,512]{1,0:T(8,128)S(1)}, f32[64,512]{1,0:T(8,128)S(1)}, u32[]{:S(2)}, u32[]{:S(2)}) %collective-permute-start.61) | collective-permute-done | bytes 131104 | tf_op jit(solution)/shard_map/ppermute | solution.py:143
  148.8 3.2 %user_step.7 = f32[1024,512]{1,0:T(8,128)} custom-call(f32[1024,512]{1,0:T(8,128)S(1)} %user_step.6.refs_1_.refs_0_, bf16[256,1024]{1,0:T(8,128)(2,1)S(1)} %get-tuple-element.180.refs_1_, bf16[256,1024]{1,0:T(8,128)(2,1)S(1)} %get-tuple-element.181.refs_2_, bf16[256,512]{1,0:T(8,128)(2,1)S(1)} %get-tuple-element.182.refs_3_, ...), custom_call_target="tpu_custom_call" | custom-call | flops 1610612736 | bytes 4194304 | tf_op jit(solution)/shard_map/user_step/pallas_call | solution.py:126
  153.0 9.5 %collective-permute-done.58 = f32[64,512]{1,0:T(8,128)S(1)} collective-permute-done((f32[64,512]{1,0:T(8,128)S(1)}, f32[64,512]{1,0:T(8,128)S(1)}, u32[]{:S(2)}, u32[]{:S(2)}) %collective-permute-start.58) | collective-permute-done | bytes 131104 | tf_op jit(solution)/shard_map/ppermute | solution.py:150
  (140 shorter events, 85.5 us)
Async XLA Ops:
  0.6 11.9 %collective-permute-start.6 = (f32[64,512]{1,0:T(8,128)}, f32[64,512]{1,0:T(8,128)S(1)}, u32[]{:S(2)}, u32[]{:S(2)}) collective-permute-start(f32[64,512]{1,0:T(8,128)} %refs_3_.1), channel_id=1, source_target_pairs={{0,4},{1,5},{2,6},{3,7},{4,0},{5,1},{6,2},{7,3},{8,12},{9,13},{10,... | collective-permute-start | bytes 393224 | tf_op jit(solution)/shard_map/ppermute | solution.py:143
  4.7 10.9 %collective-permute-start.2 = (f32[64,512]{1,0:T(8,128)}, f32[64,512]{1,0:T(8,128)S(1)}, u32[]{:S(2)}, u32[]{:S(2)}) collective-permute-start(f32[64,512]{1,0:T(8,128)} %refs_3_.1), channel_id=1, source_target_pairs={{0,3},{1,2},{2,1},{3,0},{4,7},{5,6},{6,5},{7,4},{8,11},{9,10},{10,... | collective-permute-start | bytes 393224 | tf_op jit(solution)/shard_map/ppermute | solution.py:143
  12.5 9.4 %collective-permute-start.9 = (f32[64,512]{1,0:T(8,128)S(1)}, f32[64,512]{1,0:T(8,128)S(1)}, u32[]{:S(2)}, u32[]{:S(2)}) collective-permute-start(f32[64,512]{1,0:T(8,128)S(1)} %collective-permute-done.6.refs_3_), channel_id=1, source_target_pairs={{0,3},{1,2},{2,1},{3,0},{4,7},{5,6},{6,5},{7,4},{8,11},{9,10},{10,... | collective-permute-start | bytes 393224 | tf_op jit(solution)/shard_map/ppermute | solution.py:143
  20.3 9.4 %collective-permute-start.4 = (f32[64,512]{1,0:T(8,128)S(1)}, f32[64,512]{1,0:T(8,128)S(1)}, u32[]{:S(2)}, u32[]{:S(2)}) collective-permute-start(f32[64,512]{1,0:T(8,128)S(1)} %get-tuple-element.105), channel_id=1, source_target_pairs={{0,2},{1,3},{2,0},{3,1},{4,6},{5,7},{6,4},{7,5},{8,10},{9,11},{10,... | collective-permute-start | bytes 393224 | tf_op jit(solution)/shard_map/ppermute | solution.py:143
  33.3 10.1 %collective-permute-start.10 = (f32[64,512]{1,0:T(8,128)S(1)}, f32[64,512]{1,0:T(8,128)S(1)}, u32[]{:S(2)}, u32[]{:S(2)}) collective-permute-start(f32[64,512]{1,0:T(8,128)S(1)} %multiply_add_fusion.10), channel_id=1, source_target_pairs={{0,12},{1,13},{2,14},{3,15},{4,8},{5,9},{6,10},{7,11},{8,20},{9,21... | collective-permute-start | bytes 393224 | tf_op jit(solution)/shard_map/ppermute | solution.py:150
  42.0 9.7 %collective-permute-start.22 = (f32[64,512]{1,0:T(8,128)S(1)}, f32[64,512]{1,0:T(8,128)S(1)}, u32[]{:S(2)}, u32[]{:S(2)}) collective-permute-start(f32[64,512]{1,0:T(8,128)S(1)} %add_add_fusion.6), channel_id=1, source_target_pairs={{0,12},{1,13},{2,14},{3,15},{4,8},{5,9},{6,10},{7,11},{8,20},{9,21... | collective-permute-start | bytes 393224 | tf_op jit(solution)/shard_map/ppermute | solution.py:150
  45.3 9.2 %collective-permute-start.17 = (f32[64,512]{1,0:T(8,128)S(1)}, f32[64,512]{1,0:T(8,128)S(1)}, u32[]{:S(2)}, u32[]{:S(2)}) collective-permute-start(f32[64,512]{1,0:T(8,128)S(1)} %multiply_add_fusion.9.refs_3_), channel_id=1, source_target_pairs={{0,3},{1,2},{2,1},{3,0},{4,7},{5,6},{6,5},{7,4},{8,11},{9,10},{10,... | collective-permute-start | bytes 393224 | tf_op jit(solution)/shard_map/ppermute | solution.py:143
  46.2 10.7 %collective-permute-start.16 = (f32[64,512]{1,0:T(8,128)S(1)}, f32[64,512]{1,0:T(8,128)S(1)}, u32[]{:S(2)}, u32[]{:S(2)}) collective-permute-start(f32[64,512]{1,0:T(8,128)S(1)} %multiply_add_fusion.9.refs_3_), channel_id=1, source_target_pairs={{0,2},{1,3},{2,0},{3,1},{4,6},{5,7},{6,4},{7,5},{8,10},{9,11},{10,... | collective-permute-start | bytes 393224 | tf_op jit(solution)/shard_map/ppermute | solution.py:143
  51.9 9.9 %collective-permute-start.24 = (f32[64,512]{1,0:T(8,128)S(1)}, f32[64,512]{1,0:T(8,128)S(1)}, u32[]{:S(2)}, u32[]{:S(2)}) collective-permute-start(f32[64,512]{1,0:T(8,128)S(1)} %multiply_add_fusion.8.refs_3_), channel_id=1, source_target_pairs={{0,2},{1,3},{2,0},{3,1},{4,6},{5,7},{6,4},{7,5},{8,10},{9,11},{10,... | collective-permute-start | bytes 393224 | tf_op jit(solution)/shard_map/ppermute | solution.py:143
  62.5 10.9 %collective-permute-start.19 = (f32[64,512]{1,0:T(8,128)S(1)}, f32[64,512]{1,0:T(8,128)S(1)}, u32[]{:S(2)}, u32[]{:S(2)}) collective-permute-start(f32[64,512]{1,0:T(8,128)S(1)} %get-tuple-element.129), channel_id=1, source_target_pairs={{0,2},{1,3},{2,0},{3,1},{4,6},{5,7},{6,4},{7,5},{8,10},{9,11},{10,... | collective-permute-start | bytes 393224 | tf_op jit(solution)/shard_map/ppermute | solution.py:143
  62.6 10.9 %collective-permute-start.20 = (f32[64,512]{1,0:T(8,128)S(1)}, f32[64,512]{1,0:T(8,128)S(1)}, u32[]{:S(2)}, u32[]{:S(2)}) collective-permute-start(f32[64,512]{1,0:T(8,128)S(1)} %get-tuple-element.130), channel_id=1, source_target_pairs={{0,3},{1,2},{2,1},{3,0},{4,7},{5,6},{6,5},{7,4},{8,11},{9,10},{10,... | collective-permute-start | bytes 393224 | tf_op jit(solution)/shard_map/ppermute | solution.py:143
  76.5 9.3 %collective-permute-start.37 = (f32[64,512]{1,0:T(8,128)S(1)}, f32[64,512]{1,0:T(8,128)S(1)}, u32[]{:S(2)}, u32[]{:S(2)}) collective-permute-start(f32[64,512]{1,0:T(8,128)S(1)} %multiply_add_fusion.7), channel_id=1, source_target_pairs={{0,8},{1,9},{2,10},{3,11},{4,12},{5,13},{6,14},{7,15},{8,16},{9,17... | collective-permute-start | bytes 393224 | tf_op jit(solution)/shard_map/ppermute | solution.py:150
  78.9 9.0 %collective-permute-start.38 = (f32[64,512]{1,0:T(8,128)S(1)}, f32[64,512]{1,0:T(8,128)S(1)}, u32[]{:S(2)}, u32[]{:S(2)}) collective-permute-start(f32[64,512]{1,0:T(8,128)S(1)} %add_add_fusion.4), channel_id=1, source_target_pairs={{0,12},{1,13},{2,14},{3,15},{4,8},{5,9},{6,10},{7,11},{8,20},{9,21... | collective-permute-start | bytes 393224 | tf_op jit(solution)/shard_map/ppermute | solution.py:150
  82.4 11.0 %collective-permute-start.32 = (f32[64,512]{1,0:T(8,128)S(1)}, f32[64,512]{1,0:T(8,128)S(1)}, u32[]{:S(2)}, u32[]{:S(2)}) collective-permute-start(f32[64,512]{1,0:T(8,128)S(1)} %multiply_add_fusion.6.refs_3_), channel_id=1, source_target_pairs={{0,2},{1,3},{2,0},{3,1},{4,6},{5,7},{6,4},{7,5},{8,10},{9,11},{10,... | collective-permute-start | bytes 393224 | tf_op jit(solution)/shard_map/ppermute | solution.py:143
  84.3 9.2 %collective-permute-start.31 = (f32[64,512]{1,0:T(8,128)S(1)}, f32[64,512]{1,0:T(8,128)S(1)}, u32[]{:S(2)}, u32[]{:S(2)}) collective-permute-start(f32[64,512]{1,0:T(8,128)S(1)} %multiply_add_fusion.6.refs_3_), channel_id=1, source_target_pairs={{0,1},{1,0},{2,3},{3,2},{4,5},{5,4},{6,7},{7,6},{8,9},{9,8},{10,11... | collective-permute-start | bytes 393224 | tf_op jit(solution)/shard_map/ppermute | solution.py:143
  88.0 10.1 %collective-permute-start.40 = (f32[64,512]{1,0:T(8,128)S(1)}, f32[64,512]{1,0:T(8,128)S(1)}, u32[]{:S(2)}, u32[]{:S(2)}) collective-permute-start(f32[64,512]{1,0:T(8,128)S(1)} %multiply_add_fusion.5.refs_3_), channel_id=1, source_target_pairs={{0,2},{1,3},{2,0},{3,1},{4,6},{5,7},{6,4},{7,5},{8,10},{9,11},{10,... | collective-permute-start | bytes 393224 | tf_op jit(solution)/shard_map/ppermute | solution.py:143
  99.7 10.8 %collective-permute-start.35 = (f32[64,512]{1,0:T(8,128)S(1)}, f32[64,512]{1,0:T(8,128)S(1)}, u32[]{:S(2)}, u32[]{:S(2)}) collective-permute-start(f32[64,512]{1,0:T(8,128)S(1)} %get-tuple-element.153), channel_id=1, source_target_pairs={{0,2},{1,3},{2,0},{3,1},{4,6},{5,7},{6,4},{7,5},{8,10},{9,11},{10,... | collective-permute-start | bytes 393224 | tf_op jit(solution)/shard_map/ppermute | solution.py:143
  99.7 10.8 %collective-permute-start.36 = (f32[64,512]{1,0:T(8,128)S(1)}, f32[64,512]{1,0:T(8,128)S(1)}, u32[]{:S(2)}, u32[]{:S(2)}) collective-permute-start(f32[64,512]{1,0:T(8,128)S(1)} %get-tuple-element.154), channel_id=1, source_target_pairs={{0,3},{1,2},{2,1},{3,0},{4,7},{5,6},{6,5},{7,4},{8,11},{9,10},{10,... | collective-permute-start | bytes 393224 | tf_op jit(solution)/shard_map/ppermute | solution.py:143
  114.6 10.5 %collective-permute-start.54 = (f32[64,512]{1,0:T(8,128)S(1)}, f32[64,512]{1,0:T(8,128)S(1)}, u32[]{:S(2)}, u32[]{:S(2)}) collective-permute-start(f32[64,512]{1,0:T(8,128)S(1)} %add_add_fusion.2), channel_id=1, source_target_pairs={{0,12},{1,13},{2,14},{3,15},{4,8},{5,9},{6,10},{7,11},{8,20},{9,21... | collective-permute-start | bytes 393224 | tf_op jit(solution)/shard_map/ppermute | solution.py:150
  119.9 9.9 %collective-permute-start.48 = (f32[64,512]{1,0:T(8,128)S(1)}, f32[64,512]{1,0:T(8,128)S(1)}, u32[]{:S(2)}, u32[]{:S(2)}) collective-permute-start(f32[64,512]{1,0:T(8,128)S(1)} %multiply_add_fusion.3.refs_3_), channel_id=1, source_target_pairs={{0,2},{1,3},{2,0},{3,1},{4,6},{5,7},{6,4},{7,5},{8,10},{9,11},{10,... | collective-permute-start | bytes 393224 | tf_op jit(solution)/shard_map/ppermute | solution.py:143
  125.2 9.7 %collective-permute-start.56 = (f32[64,512]{1,0:T(8,128)S(1)}, f32[64,512]{1,0:T(8,128)S(1)}, u32[]{:S(2)}, u32[]{:S(2)}) collective-permute-start(f32[64,512]{1,0:T(8,128)S(1)} %multiply_add_fusion.2.refs_3_), channel_id=1, source_target_pairs={{0,2},{1,3},{2,0},{3,1},{4,6},{5,7},{6,4},{7,5},{8,10},{9,11},{10,... | collective-permute-start | bytes 393224 | tf_op jit(solution)/shard_map/ppermute | solution.py:143
  138.5 10.0 %collective-permute-start.61 = (f32[64,512]{1,0:T(8,128)S(1)}, f32[64,512]{1,0:T(8,128)S(1)}, u32[]{:S(2)}, u32[]{:S(2)}) collective-permute-start(f32[64,512]{1,0:T(8,128)S(1)} %get-tuple-element.197), channel_id=1, source_target_pairs={{0,3},{1,2},{2,1},{3,0},{4,7},{5,6},{6,5},{7,4},{8,11},{9,10},{10,... | collective-permute-start | bytes 393224 | tf_op jit(solution)/shard_map/ppermute | solution.py:143
  142.0 10.1 %collective-permute-start.51 = (f32[64,512]{1,0:T(8,128)S(1)}, f32[64,512]{1,0:T(8,128)S(1)}, u32[]{:S(2)}, u32[]{:S(2)}) collective-permute-start(f32[64,512]{1,0:T(8,128)S(1)} %get-tuple-element.177), channel_id=1, source_target_pairs={{0,2},{1,3},{2,0},{3,1},{4,6},{5,7},{6,4},{7,5},{8,10},{9,11},{10,... | collective-permute-start | bytes 393224 | tf_op jit(solution)/shard_map/ppermute | solution.py:143
  152.3 10.1 %collective-permute-start.58 = (f32[64,512]{1,0:T(8,128)S(1)}, f32[64,512]{1,0:T(8,128)S(1)}, u32[]{:S(2)}, u32[]{:S(2)}) collective-permute-start(f32[64,512]{1,0:T(8,128)S(1)} %multiply_add_fusion.1), channel_id=1, source_target_pairs={{0,12},{1,13},{2,14},{3,15},{4,8},{5,9},{6,10},{7,11},{8,20},{9,21... | collective-permute-start | bytes 393224 | tf_op jit(solution)/shard_map/ppermute | solution.py:150
  (42 other events, 297.5 us)

commit v8 on v7

--- a/solution.py
+++ b/solution.py
@@ -161,19 +161,17 @@
     for s in range(strata):
         last = s == strata - 1
         one = gradients(occupancy, users, ratings, first, 0, s)
-        second, _ = lax.optimization_barrier((second, one[4]))
         two = gradients(occupancy, users, ratings, second, 1, s)
-        term = arrived(one[4:])
-        users, term[1] = lax.optimization_barrier((users, term[1]))
-        users = user_step(users, [one[:4], two[:4]])
-        term, users = lax.optimization_barrier((functools.reduce(jnp.add, term), users))
-        base = first[0] + 0.005 * (term - 0.05 * first[0])
+        base = functools.reduce(jnp.add, arrived(one[4:]))
+        base = first[0] + 0.005 * (base - 0.05 * first[0])
         term = functools.reduce(jnp.add, arrived(two[4:]))
         flip = strata % 2 if last else 0
         near = onward(base, 0 if flip else ny) + 0.005 * onward(term, ny if flip else 0)
         if last:
-            return users, near
+            return user_step(users, [one[:4], two[:4]]), near
         far = onward(base, 0) + 0.005 * onward(term, ny)
+        users, base = lax.optimization_barrier((users, base))
+        users = user_step(users, [one[:4], two[:4]])
         first, second = gathered(near), gathered(far)
 
 

time: 163 us -> 153 us (0.939)
  waiting for transfers between devices: 61.1 us -> 42.6 us
  starting transfers between devices: 65.5 us -> 73.8 us
    ppermute x49, waiting for transfers between devices: 35.3 us -> 23.8 us  [over_y(): return lax.ppermute(x, 'sub', [(i, i ^ r) for i in range(n_sub)])]
    ppermute x14, waiting for transfers between devices: 25.8 us -> 18.8 us  [onward(): return lax.ppermute(x, ('group', 'sub'), route)]
    ppermute x14, starting transfers between devices: 6.77 us -> 12.6 us  [onward(): return lax.ppermute(x, ('group', 'sub'), route)]
    ppermute x49, starting transfers between devices: 58.7 us -> 61.2 us  [over_y(): return lax.ppermute(x, 'sub', [(i, i ^ r) for i in range(n_sub)])]
  transfers between devices with their start and end apart: 63 -> 63, of which waited for: 34 -> 20; matrix products, arithmetic and copies ran while one was open for 0% -> 0% of each run, Pallas kernels for 18% -> 21%
where the time goes in v8:
time: 153 us
  starting transfers between devices  73.8 us (48%)
  waiting for transfers between devices  42.6 us (28%)
  Pallas kernels  32.7 us (21%)
  local copies, waits for them, and re-layouts  1.6 us (1%)
    ppermute x49, starting transfers between devices, over_y(): return lax.ppermute(x, 'sub', [(i, i ^ r) for i in range(n_sub)])  61.2 us
    ppermute x49, waiting for transfers between devices, over_y(): return lax.ppermute(x, 'sub', [(i, i ^ r) for i in range(n_sub)])  23.8 us
    pallas_call x8, Pallas kernels, gradients(): pl.pallas_call(functools.partial(grad_kernel, ny, place, stratum), in_spe...  21.1 us
    ppermute x14, waiting for transfers between devices, onward(): return lax.ppermute(x, ('group', 'sub'), route)  18.8 us
    ppermute x14, starting transfers between devices, onward(): return lax.ppermute(x, ('group', 'sub'), route)  12.6 us
    pallas_call x4, Pallas kernels, user_step(): pl.pallas_call(functools.partial(step_kernel, len(parts)), in_specs=[VMEM...  8.95 us
  transfers between devices with their start and end apart: 63, of which 20 were waited for; matrix products, arithmetic and copies ran while one was open for 0% of the time, Pallas kernels for 21%

profile of v8, /device:TPU:0, one launch (start us, length us, event | category | flops | bytes accessed | tf_op | source)
XLA Modules:
  0.0 152.8 jit_solution(16287897807125659749)
XLA Ops:
  0.6 4.1 %collective-permute-start.6 = (f32[64,512]{1,0:T(8,128)}, f32[64,512]{1,0:T(8,128)S(1)}, u32[]{:S(2)}, u32[]{:S(2)}) collective-permute-start(f32[64,512]{1,0:T(8,128)} %refs_3_.1), channel_id=1, source_target_pairs={{0,4},{1,5},{2,6},{3,7},{4,0},{5,1},{6,2},{7,3},{8,12},{9,13},{10,... | collective-permute-start | bytes 393224 | tf_op jit(solution)/shard_map/ppermute | solution.py:143
  4.7 2.5 %collective-permute-start.2 = (f32[64,512]{1,0:T(8,128)}, f32[64,512]{1,0:T(8,128)S(1)}, u32[]{:S(2)}, u32[]{:S(2)}) collective-permute-start(f32[64,512]{1,0:T(8,128)} %refs_3_.1), channel_id=1, source_target_pairs={{0,3},{1,2},{2,1},{3,0},{4,7},{5,6},{6,5},{7,4},{8,11},{9,10},{10,... | collective-permute-start | bytes 393224 | tf_op jit(solution)/shard_map/ppermute | solution.py:143
  9.8 2.7 %load.1 = (f32[1024,512]{1,0:T(8,128)S(1)}, bf16[4,512,1024]{2,1,0:T(8,128)(2,1)S(1)}) custom-call(f32[1024,512]{1,0:T(8,128)S(1)} %copy-done, bf16[4,1024,512]{2,1,0:T(8,128)(2,1)} %ratings.1), custom_call_target="tpu_custom_call" | custom-call | bytes 12582912 | tf_op jit(solution)/shard_map/load/pallas_call | solution.py:47
  12.5 2.6 %collective-permute-start.9 = (f32[64,512]{1,0:T(8,128)S(1)}, f32[64,512]{1,0:T(8,128)S(1)}, u32[]{:S(2)}, u32[]{:S(2)}) collective-permute-start(f32[64,512]{1,0:T(8,128)S(1)} %collective-permute-done.6.refs_3_), channel_id=1, source_target_pairs={{0,3},{1,2},{2,1},{3,0},{4,7},{5,6},{6,5},{7,4},{8,11},{9,10},{10,... | collective-permute-start | bytes 393224 | tf_op jit(solution)/shard_map/ppermute | solution.py:143
  16.1 2.6 %gradients.8 = (bf16[256,1024]{1,0:T(8,128)(2,1)S(1)}, bf16[256,1024]{1,0:T(8,128)(2,1)S(1)}, bf16[256,512]{1,0:T(8,128)(2,1)S(1)}, bf16[256,512]{1,0:T(8,128)(2...) custom-call(s32[4,4,8]{2,1,0:T(4,128)S(1)} %bitcast.1, ...), custom_call_target="tpu_custom_call" | custom-call | flops 1610612736 | bytes 2097152 | tf_op jit(solution)/shard_map/gradients/pallas_call | solution.py:97
  22.3 2.6 %gradients.9 = (bf16[256,1024]{1,0:T(8,128)(2,1)S(1)}, bf16[256,1024]{1,0:T(8,128)(2,1)S(1)}, bf16[256,512]{1,0:T(8,128)(2,1)S(1)}, bf16[256,512]{1,0:T(8,128)(2...) custom-call(s32[4,4,8]{2,1,0:T(4,128)S(1)} %bitcast.2, ...), custom_call_target="tpu_custom_call" | custom-call | flops 1610612736 | bytes 2097152 | tf_op jit(solution)/shard_map/gradients/pallas_call | solution.py:97
  36.2 3.0 %collective-permute-start.14 = (f32[64,512]{1,0:T(8,128)S(1)}, f32[64,512]{1,0:T(8,128)S(1)}, u32[]{:S(2)}, u32[]{:S(2)}) collective-permute-start(f32[64,512]{1,0:T(8,128)S(1)} %add_add_fusion.3), channel_id=1, source_target_pairs={{0,8},{1,9},{2,10},{3,11},{4,12},{5,13},{6,14},{7,15},{8,16},{9,17... | collective-permute-start | bytes 393224 | tf_op jit(solution)/shard_map/ppermute | solution.py:150
  39.2 5.8 %collective-permute-done.22 = f32[64,512]{1,0:T(8,128)S(1)} collective-permute-done((f32[64,512]{1,0:T(8,128)S(1)}, f32[64,512]{1,0:T(8,128)S(1)}, u32[]{:S(2)}, u32[]{:S(2)}) %collective-permute-start.22) | collective-permute-done | bytes 131104 | tf_op jit(solution)/shard_map/ppermute | solution.py:150
  55.2 2.6 %gradients.11 = (bf16[256,1024]{1,0:T(8,128)(2,1)S(1)}, bf16[256,1024]{1,0:T(8,128)(2,1)S(1)}, bf16[256,512]{1,0:T(8,128)(2,1)S(1)}, bf16[256,512]{1,0:T(8,128)(...) custom-call(s32[4,4,8]{2,1,0:T(4,128)S(1)} %bitcast.3, ...), custom_call_target="tpu_custom_call" | custom-call | flops 1610612736 | bytes 2097152 | tf_op jit(solution)/shard_map/gradients/pallas_call | solution.py:97
  58.5 2.9 %collective-permute-start.29 = (f32[64,512]{1,0:T(8,128)S(1)}, f32[64,512]{1,0:T(8,128)S(1)}, u32[]{:S(2)}, u32[]{:S(2)}) collective-permute-start(f32[64,512]{1,0:T(8,128)S(1)} %get-tuple-element.106), channel_id=1, source_target_pairs={{0,3},{1,2},{2,1},{3,0},{4,7},{5,6},{6,5},{7,4},{8,11},{9,10},{10,... | collective-permute-start | bytes 393224 | tf_op jit(solution)/shard_map/ppermute | solution.py:143
  61.4 2.6 %gradients.10 = (bf16[256,1024]{1,0:T(8,128)(2,1)S(1)}, bf16[256,1024]{1,0:T(8,128)(2,1)S(1)}, bf16[256,512]{1,0:T(8,128)(2,1)S(1)}, bf16[256,512]{1,0:T(8,128)(...) custom-call(s32[4,4,8]{2,1,0:T(4,128)S(1)} %bitcast.4, ...), custom_call_target="tpu_custom_call" | custom-call | flops 1610612736 | bytes 2097152 | tf_op jit(solution)/shard_map/gradients/pallas_call | solution.py:97
  64.7 2.9 %collective-permute-start.20 = (f32[64,512]{1,0:T(8,128)S(1)}, f32[64,512]{1,0:T(8,128)S(1)}, u32[]{:S(2)}, u32[]{:S(2)}) collective-permute-start(f32[64,512]{1,0:T(8,128)S(1)} %get-tuple-element.93), channel_id=1, source_target_pairs={{0,3},{1,2},{2,1},{3,0},{4,7},{5,6},{6,5},{7,4},{8,11},{9,10},{10,... | collective-permute-start | bytes 393224 | tf_op jit(solution)/shard_map/ppermute | solution.py:143
  67.7 3.6 %collective-permute-start.30 = (f32[64,512]{1,0:T(8,128)S(1)}, f32[64,512]{1,0:T(8,128)S(1)}, u32[]{:S(2)}, u32[]{:S(2)}) collective-permute-start(f32[64,512]{1,0:T(8,128)S(1)} %add_add_fusion.2), channel_id=1, source_target_pairs={{0,8},{1,9},{2,10},{3,11},{4,12},{5,13},{6,14},{7,15},{8,16},{9,17... | collective-permute-start | bytes 393224 | tf_op jit(solution)/shard_map/ppermute | solution.py:150
  71.3 2.8 %collective-permute-done.20 = f32[64,512]{1,0:T(8,128)S(1)} collective-permute-done((f32[64,512]{1,0:T(8,128)S(1)}, f32[64,512]{1,0:T(8,128)S(1)}, u32[]{:S(2)}, u32[]{:S(2)}) %collective-permute-start.20) | collective-permute-done | bytes 131104 | tf_op jit(solution)/shard_map/ppermute | solution.py:143
  74.3 2.5 %collective-permute-start.26 = (f32[64,512]{1,0:T(8,128)S(1)}, f32[64,512]{1,0:T(8,128)S(1)}, u32[]{:S(2)}, u32[]{:S(2)}) collective-permute-start(f32[64,512]{1,0:T(8,128)S(1)} %multiply_add_fusion.8), channel_id=1, source_target_pairs={{0,12},{1,13},{2,14},{3,15},{4,8},{5,9},{6,10},{7,11},{8,20},{9,21... | collective-permute-start | bytes 393224 | tf_op jit(solution)/shard_map/ppermute | solution.py:150
  91.7 2.6 %gradients.13 = (bf16[256,1024]{1,0:T(8,128)(2,1)S(1)}, bf16[256,1024]{1,0:T(8,128)(2,1)S(1)}, bf16[256,512]{1,0:T(8,128)(2,1)S(1)}, bf16[256,512]{1,0:T(8,128)(...) custom-call(s32[4,4,8]{2,1,0:T(4,128)S(1)} %bitcast.5, ...), custom_call_target="tpu_custom_call" | custom-call | flops 1610612736 | bytes 2097152 | tf_op jit(solution)/shard_map/gradients/pallas_call | solution.py:97
  97.9 2.6 %gradients.12 = (bf16[256,1024]{1,0:T(8,128)(2,1)S(1)}, bf16[256,1024]{1,0:T(8,128)(2,1)S(1)}, bf16[256,512]{1,0:T(8,128)(2,1)S(1)}, bf16[256,512]{1,0:T(8,128)(...) custom-call(s32[4,4,8]{2,1,0:T(4,128)S(1)} %bitcast.6, ...), custom_call_target="tpu_custom_call" | custom-call | flops 1610612736 | bytes 2097152 | tf_op jit(solution)/shard_map/gradients/pallas_call | solution.py:97
  107.0 3.2 %collective-permute-done.36 = f32[64,512]{1,0:T(8,128)S(1)} collective-permute-done((f32[64,512]{1,0:T(8,128)S(1)}, f32[64,512]{1,0:T(8,128)S(1)}, u32[]{:S(2)}, u32[]{:S(2)}) %collective-permute-start.36) | collective-permute-done | bytes 131104 | tf_op jit(solution)/shard_map/ppermute | solution.py:143
  120.4 3.1 %collective-permute-start.48 = (f32[64,512]{1,0:T(8,128)S(1)}, f32[64,512]{1,0:T(8,128)S(1)}, u32[]{:S(2)}, u32[]{:S(2)}) collective-permute-start(f32[64,512]{1,0:T(8,128)S(1)} %multiply_add_fusion.3.refs_3_), channel_id=1, source_target_pairs={{0,2},{1,3},{2,0},{3,1},{4,6},{5,7},{6,4},{7,5},{8,10},{9,11},{10,... | collective-permute-start | bytes 393224 | tf_op jit(solution)/shard_map/ppermute | solution.py:143
  125.0 2.6 %gradients.15 = (bf16[256,1024]{1,0:T(8,128)(2,1)S(1)}, bf16[256,1024]{1,0:T(8,128)(2,1)S(1)}, bf16[256,512]{1,0:T(8,128)(2,1)S(1)}, bf16[256,512]{1,0:T(8,128)(...) custom-call(s32[4,4,8]{2,1,0:T(4,128)S(1)} %bitcast.7, ...), custom_call_target="tpu_custom_call" | custom-call | flops 1610612736 | bytes 2097152 | tf_op jit(solution)/shard_map/gradients/pallas_call | solution.py:97
  131.2 2.6 %gradients.14 = (bf16[256,1024]{1,0:T(8,128)(2,1)S(1)}, bf16[256,1024]{1,0:T(8,128)(2,1)S(1)}, bf16[256,512]{1,0:T(8,128)(2,1)S(1)}, bf16[256,512]{1,0:T(8,128)(...) custom-call(s32[4,4,8]{2,1,0:T(4,128)S(1)} %bitcast.8, ...), custom_call_target="tpu_custom_call" | custom-call | flops 1610612736 | bytes 2097152 | tf_op jit(solution)/shard_map/gradients/pallas_call | solution.py:97
  137.5 2.4 %collective-permute-done.55 = f32[64,512]{1,0:T(8,128)S(1)} collective-permute-done((f32[64,512]{1,0:T(8,128)S(1)}, f32[64,512]{1,0:T(8,128)S(1)}, u32[]{:S(2)}, u32[]{:S(2)}) %collective-permute-start.55) | collective-permute-done | bytes 131104 | tf_op jit(solution)/shard_map/ppermute | solution.py:143
  141.9 3.2 %user_step.7 = f32[1024,512]{1,0:T(8,128)} custom-call(f32[1024,512]{1,0:T(8,128)S(1)} %user_step.6.refs_1_.refs_0_, bf16[256,1024]{1,0:T(8,128)(2,1)S(1)} %get-tuple-element.124.refs_1_, bf16[256,1024]{1,0:T(8,128)(2,1)S(1)} %get-tuple-element.125.refs_2_, bf16[256,512]{1,0:T(8,128)(2,1)S(1)} %get-tuple-element.126.refs_3_, ...), custom_call_target="tpu_custom_call" | custom-call | flops 1610612736 | bytes 4194304 | tf_op jit(solution)/shard_map/user_step/pallas_call | solution.py:126
  145.1 7.1 %collective-permute-done.58 = f32[64,512]{1,0:T(8,128)S(1)} collective-permute-done((f32[64,512]{1,0:T(8,128)S(1)}, f32[64,512]{1,0:T(8,128)S(1)}, u32[]{:S(2)}, u32[]{:S(2)}) %collective-permute-start.58) | collective-permute-done | bytes 131104 | tf_op jit(solution)/shard_map/ppermute | solution.py:150
  (136 shorter events, 76.4 us)
Async XLA Ops:
  0.6 11.9 %collective-permute-start.6 = (f32[64,512]{1,0:T(8,128)}, f32[64,512]{1,0:T(8,128)S(1)}, u32[]{:S(2)}, u32[]{:S(2)}) collective-permute-start(f32[64,512]{1,0:T(8,128)} %refs_3_.1), channel_id=1, source_target_pairs={{0,4},{1,5},{2,6},{3,7},{4,0},{5,1},{6,2},{7,3},{8,12},{9,13},{10,... | collective-permute-start | bytes 393224 | tf_op jit(solution)/shard_map/ppermute | solution.py:143
  4.7 10.9 %collective-permute-start.2 = (f32[64,512]{1,0:T(8,128)}, f32[64,512]{1,0:T(8,128)S(1)}, u32[]{:S(2)}, u32[]{:S(2)}) collective-permute-start(f32[64,512]{1,0:T(8,128)} %refs_3_.1), channel_id=1, source_target_pairs={{0,3},{1,2},{2,1},{3,0},{4,7},{5,6},{6,5},{7,4},{8,11},{9,10},{10,... | collective-permute-start | bytes 393224 | tf_op jit(solution)/shard_map/ppermute | solution.py:143
  12.5 9.4 %collective-permute-start.9 = (f32[64,512]{1,0:T(8,128)S(1)}, f32[64,512]{1,0:T(8,128)S(1)}, u32[]{:S(2)}, u32[]{:S(2)}) collective-permute-start(f32[64,512]{1,0:T(8,128)S(1)} %collective-permute-done.6.refs_3_), channel_id=1, source_target_pairs={{0,3},{1,2},{2,1},{3,0},{4,7},{5,6},{6,5},{7,4},{8,11},{9,10},{10,... | collective-permute-start | bytes 393224 | tf_op jit(solution)/shard_map/ppermute | solution.py:143
  18.7 9.4 %collective-permute-start.3 = (f32[64,512]{1,0:T(8,128)S(1)}, f32[64,512]{1,0:T(8,128)S(1)}, u32[]{:S(2)}, u32[]{:S(2)}) collective-permute-start(f32[64,512]{1,0:T(8,128)S(1)} %get-tuple-element.74), channel_id=1, source_target_pairs={{0,1},{1,0},{2,3},{3,2},{4,5},{5,4},{6,7},{7,6},{8,9},{9,8},{10,11... | collective-permute-start | bytes 393224 | tf_op jit(solution)/shard_map/ppermute | solution.py:143
  29.3 9.8 %collective-permute-start.21 = (f32[64,512]{1,0:T(8,128)S(1)}, f32[64,512]{1,0:T(8,128)S(1)}, u32[]{:S(2)}, u32[]{:S(2)}) collective-permute-start(f32[64,512]{1,0:T(8,128)S(1)} %multiply_add_fusion.10), channel_id=1, source_target_pairs={{0,8},{1,9},{2,10},{3,11},{4,12},{5,13},{6,14},{7,15},{8,16},{9,17... | collective-permute-start | bytes 393224 | tf_op jit(solution)/shard_map/ppermute | solution.py:150
  29.4 19.2 %collective-permute-start.10 = (f32[64,512]{1,0:T(8,128)S(1)}, f32[64,512]{1,0:T(8,128)S(1)}, u32[]{:S(2)}, u32[]{:S(2)}) collective-permute-start(f32[64,512]{1,0:T(8,128)S(1)} %multiply_add_fusion.10), channel_id=1, source_target_pairs={{0,12},{1,13},{2,14},{3,15},{4,8},{5,9},{6,10},{7,11},{8,20},{9,21... | collective-permute-start | bytes 393224 | tf_op jit(solution)/shard_map/ppermute | solution.py:150
  34.0 11.0 %collective-permute-start.22 = (f32[64,512]{1,0:T(8,128)S(1)}, f32[64,512]{1,0:T(8,128)S(1)}, u32[]{:S(2)}, u32[]{:S(2)}) collective-permute-start(f32[64,512]{1,0:T(8,128)S(1)} %add_add_fusion.3), channel_id=1, source_target_pairs={{0,12},{1,13},{2,14},{3,15},{4,8},{5,9},{6,10},{7,11},{8,20},{9,21... | collective-permute-start | bytes 393224 | tf_op jit(solution)/shard_map/ppermute | solution.py:150
  36.2 12.4 %collective-permute-start.14 = (f32[64,512]{1,0:T(8,128)S(1)}, f32[64,512]{1,0:T(8,128)S(1)}, u32[]{:S(2)}, u32[]{:S(2)}) collective-permute-start(f32[64,512]{1,0:T(8,128)S(1)} %add_add_fusion.3), channel_id=1, source_target_pairs={{0,8},{1,9},{2,10},{3,11},{4,12},{5,13},{6,14},{7,15},{8,16},{9,17... | collective-permute-start | bytes 393224 | tf_op jit(solution)/shard_map/ppermute | solution.py:150
  48.6 9.9 %collective-permute-start.17 = (f32[64,512]{1,0:T(8,128)S(1)}, f32[64,512]{1,0:T(8,128)S(1)}, u32[]{:S(2)}, u32[]{:S(2)}) collective-permute-start(f32[64,512]{1,0:T(8,128)S(1)} %multiply_add_fusion.9.refs_3_), channel_id=1, source_target_pairs={{0,3},{1,2},{2,1},{3,0},{4,7},{5,6},{6,5},{7,4},{8,11},{9,10},{10,... | collective-permute-start | bytes 393224 | tf_op jit(solution)/shard_map/ppermute | solution.py:143
  48.7 12.7 %collective-permute-start.16 = (f32[64,512]{1,0:T(8,128)S(1)}, f32[64,512]{1,0:T(8,128)S(1)}, u32[]{:S(2)}, u32[]{:S(2)}) collective-permute-start(f32[64,512]{1,0:T(8,128)S(1)} %multiply_add_fusion.9.refs_3_), channel_id=1, source_target_pairs={{0,2},{1,3},{2,0},{3,1},{4,6},{5,7},{6,4},{7,5},{8,10},{9,11},{10,... | collective-permute-start | bytes 393224 | tf_op jit(solution)/shard_map/ppermute | solution.py:143
  64.7 9.4 %collective-permute-start.20 = (f32[64,512]{1,0:T(8,128)S(1)}, f32[64,512]{1,0:T(8,128)S(1)}, u32[]{:S(2)}, u32[]{:S(2)}) collective-permute-start(f32[64,512]{1,0:T(8,128)S(1)} %get-tuple-element.93), channel_id=1, source_target_pairs={{0,3},{1,2},{2,1},{3,0},{4,7},{5,6},{6,5},{7,4},{8,11},{9,10},{10,... | collective-permute-start | bytes 393224 | tf_op jit(solution)/shard_map/ppermute | solution.py:143
  67.7 11.0 %collective-permute-start.38 = (f32[64,512]{1,0:T(8,128)S(1)}, f32[64,512]{1,0:T(8,128)S(1)}, u32[]{:S(2)}, u32[]{:S(2)}) collective-permute-start(f32[64,512]{1,0:T(8,128)S(1)} %add_add_fusion.2), channel_id=1, source_target_pairs={{0,12},{1,13},{2,14},{3,15},{4,8},{5,9},{6,10},{7,11},{8,20},{9,21... | collective-permute-start | bytes 393224 | tf_op jit(solution)/shard_map/ppermute | solution.py:150
  67.7 15.8 %collective-permute-start.30 = (f32[64,512]{1,0:T(8,128)S(1)}, f32[64,512]{1,0:T(8,128)S(1)}, u32[]{:S(2)}, u32[]{:S(2)}) collective-permute-start(f32[64,512]{1,0:T(8,128)S(1)} %add_add_fusion.2), channel_id=1, source_target_pairs={{0,8},{1,9},{2,10},{3,11},{4,12},{5,13},{6,14},{7,15},{8,16},{9,17... | collective-permute-start | bytes 393224 | tf_op jit(solution)/shard_map/ppermute | solution.py:150
  74.3 10.5 %collective-permute-start.26 = (f32[64,512]{1,0:T(8,128)S(1)}, f32[64,512]{1,0:T(8,128)S(1)}, u32[]{:S(2)}, u32[]{:S(2)}) collective-permute-start(f32[64,512]{1,0:T(8,128)S(1)} %multiply_add_fusion.8), channel_id=1, source_target_pairs={{0,12},{1,13},{2,14},{3,15},{4,8},{5,9},{6,10},{7,11},{8,20},{9,21... | collective-permute-start | bytes 393224 | tf_op jit(solution)/shard_map/ppermute | solution.py:150
  78.9 9.6 %collective-permute-start.41 = (f32[64,512]{1,0:T(8,128)S(1)}, f32[64,512]{1,0:T(8,128)S(1)}, u32[]{:S(2)}, u32[]{:S(2)}) collective-permute-start(f32[64,512]{1,0:T(8,128)S(1)} %multiply_add_fusion.4.refs_3_), channel_id=1, source_target_pairs={{0,3},{1,2},{2,1},{3,0},{4,7},{5,6},{6,5},{7,4},{8,11},{9,10},{10,... | collective-permute-start | bytes 393224 | tf_op jit(solution)/shard_map/ppermute | solution.py:143
  81.0 10.6 %collective-permute-start.40 = (f32[64,512]{1,0:T(8,128)S(1)}, f32[64,512]{1,0:T(8,128)S(1)}, u32[]{:S(2)}, u32[]{:S(2)}) collective-permute-start(f32[64,512]{1,0:T(8,128)S(1)} %multiply_add_fusion.4.refs_3_), channel_id=1, source_target_pairs={{0,2},{1,3},{2,0},{3,1},{4,6},{5,7},{6,4},{7,5},{8,10},{9,11},{10,... | collective-permute-start | bytes 393224 | tf_op jit(solution)/shard_map/ppermute | solution.py:143
  82.1 9.5 %collective-permute-start.39 = (f32[64,512]{1,0:T(8,128)S(1)}, f32[64,512]{1,0:T(8,128)S(1)}, u32[]{:S(2)}, u32[]{:S(2)}) collective-permute-start(f32[64,512]{1,0:T(8,128)S(1)} %multiply_add_fusion.4.refs_3_), channel_id=1, source_target_pairs={{0,1},{1,0},{2,3},{3,2},{4,5},{5,4},{6,7},{7,6},{8,9},{9,8},{10,11... | collective-permute-start | bytes 393224 | tf_op jit(solution)/shard_map/ppermute | solution.py:143
  84.8 11.9 %collective-permute-start.33 = (f32[64,512]{1,0:T(8,128)S(1)}, f32[64,512]{1,0:T(8,128)S(1)}, u32[]{:S(2)}, u32[]{:S(2)}) collective-permute-start(f32[64,512]{1,0:T(8,128)S(1)} %multiply_add_fusion.6.refs_3_), channel_id=1, source_target_pairs={{0,3},{1,2},{2,1},{3,0},{4,7},{5,6},{6,5},{7,4},{8,11},{9,10},{10,... | collective-permute-start | bytes 393224 | tf_op jit(solution)/shard_map/ppermute | solution.py:143
  85.2 12.7 %collective-permute-start.32 = (f32[64,512]{1,0:T(8,128)S(1)}, f32[64,512]{1,0:T(8,128)S(1)}, u32[]{:S(2)}, u32[]{:S(2)}) collective-permute-start(f32[64,512]{1,0:T(8,128)S(1)} %multiply_add_fusion.6.refs_3_), channel_id=1, source_target_pairs={{0,2},{1,3},{2,0},{3,1},{4,6},{5,7},{6,4},{7,5},{8,10},{9,11},{10,... | collective-permute-start | bytes 393224 | tf_op jit(solution)/shard_map/ppermute | solution.py:143
  94.6 9.5 %collective-permute-start.44 = (f32[64,512]{1,0:T(8,128)S(1)}, f32[64,512]{1,0:T(8,128)S(1)}, u32[]{:S(2)}, u32[]{:S(2)}) collective-permute-start(f32[64,512]{1,0:T(8,128)S(1)} %get-tuple-element.122), channel_id=1, source_target_pairs={{0,2},{1,3},{2,0},{3,1},{4,6},{5,7},{6,4},{7,5},{8,10},{9,11},{10,... | collective-permute-start | bytes 393224 | tf_op jit(solution)/shard_map/ppermute | solution.py:143
  104.2 14.0 %collective-permute-start.46 = (f32[64,512]{1,0:T(8,128)S(1)}, f32[64,512]{1,0:T(8,128)S(1)}, u32[]{:S(2)}, u32[]{:S(2)}) collective-permute-start(f32[64,512]{1,0:T(8,128)S(1)} %add_add_fusion.1), channel_id=1, source_target_pairs={{0,8},{1,9},{2,10},{3,11},{4,12},{5,13},{6,14},{7,15},{8,16},{9,17... | collective-permute-start | bytes 393224 | tf_op jit(solution)/shard_map/ppermute | solution.py:150
  110.3 10.1 %collective-permute-start.42 = (f32[64,512]{1,0:T(8,128)S(1)}, f32[64,512]{1,0:T(8,128)S(1)}, u32[]{:S(2)}, u32[]{:S(2)}) collective-permute-start(f32[64,512]{1,0:T(8,128)S(1)} %multiply_add_fusion.5), channel_id=1, source_target_pairs={{0,12},{1,13},{2,14},{3,15},{4,8},{5,9},{6,10},{7,11},{8,20},{9,21... | collective-permute-start | bytes 393224 | tf_op jit(solution)/shard_map/ppermute | solution.py:150
  120.4 10.7 %collective-permute-start.48 = (f32[64,512]{1,0:T(8,128)S(1)}, f32[64,512]{1,0:T(8,128)S(1)}, u32[]{:S(2)}, u32[]{:S(2)}) collective-permute-start(f32[64,512]{1,0:T(8,128)S(1)} %multiply_add_fusion.3.refs_3_), channel_id=1, source_target_pairs={{0,2},{1,3},{2,0},{3,1},{4,6},{5,7},{6,4},{7,5},{8,10},{9,11},{10,... | collective-permute-start | bytes 393224 | tf_op jit(solution)/shard_map/ppermute | solution.py:143
  141.8 10.4 %collective-permute-start.58 = (f32[64,512]{1,0:T(8,128)S(1)}, f32[64,512]{1,0:T(8,128)S(1)}, u32[]{:S(2)}, u32[]{:S(2)}) collective-permute-start(f32[64,512]{1,0:T(8,128)S(1)} %multiply_add_fusion.1), channel_id=1, source_target_pairs={{0,12},{1,13},{2,14},{3,15},{4,8},{5,9},{6,10},{7,11},{8,20},{9,21... | collective-permute-start | bytes 393224 | tf_op jit(solution)/shard_map/ppermute | solution.py:150
  (42 other events, 305.8 us)

commit v9 on v8

--- a/solution.py
+++ b/solution.py
@@ -170,7 +170,10 @@
         if last:
             return user_step(users, [one[:4], two[:4]]), near
         far = onward(base, 0) + 0.005 * onward(term, ny)
-        users, base = lax.optimization_barrier((users, base))
+        if s == 0:
+            users, term = lax.optimization_barrier((users, term))
+        else:
+            users, base = lax.optimization_barrier((users, base))
         users = user_step(users, [one[:4], two[:4]])
         first, second = gathered(near), gathered(far)
 

time: 153 us -> 144 us (0.941)
  waiting for transfers between devices: 42.6 us -> 32.3 us
    ppermute x14, waiting for transfers between devices: 18.8 us -> 9.39 us  [onward(): return lax.ppermute(x, ('group', 'sub'), route)]
  transfers between devices with their start and end apart: 63 -> 63, of which waited for: 20 -> 24; matrix products, arithmetic and copies ran while one was open for 0% -> 0% of each run, Pallas kernels for 21% -> 23%
where the time goes in v9:
time: 144 us; the launch traced here: 143 us
  starting transfers between devices  74.7 us (52%)
  Pallas kernels  32.7 us (23%)
  waiting for transfers between devices  32.3 us (22%)
  local copies, waits for them, and re-layouts  1.6 us (1%)
    ppermute x49, starting transfers between devices, over_y(): return lax.ppermute(x, 'sub', [(i, i ^ r) for i in range(n_sub)])  62.2 us
    ppermute x49, waiting for transfers between devices, over_y(): return lax.ppermute(x, 'sub', [(i, i ^ r) for i in range(n_sub)])  22.9 us
    pallas_call x8, Pallas kernels, gradients(): pl.pallas_call(functools.partial(grad_kernel, ny, place, stratum), in_spe...  21 us
    ppermute x14, starting transfers between devices, onward(): return lax.ppermute(x, ('group', 'sub'), route)  12.5 us
    ppermute x14, waiting for transfers between devices, onward(): return lax.ppermute(x, ('group', 'sub'), route)  9.39 us
    pallas_call x4, Pallas kernels, user_step(): pl.pallas_call(functools.partial(step_kernel, len(parts)), in_specs=[VMEM...  8.96 us
  transfers between devices with their start and end apart: 63, of which 24 were waited for; matrix products, arithmetic and copies ran while one was open for 0% of the time, Pallas kernels for 23%

profile of v9, /device:TPU:0, one launch (start us, length us, event | category | flops | bytes accessed | tf_op | source)
XLA Modules:
  0.0 143.4 jit_solution(10910154890309911770)
XLA Ops:
  0.6 4.1 %collective-permute-start = (f32[64,512]{1,0:T(8,128)}, f32[64,512]{1,0:T(8,128)S(1)}, u32[]{:S(2)}, u32[]{:S(2)}) collective-permute-start(f32[64,512]{1,0:T(8,128)} %refs_3_.1), channel_id=1, source_target_pairs={{0,4},{1,5},{2,6},{3,7},{4,0},{5,1},{6,2},{7,3},{8,12},{9,13},{10,... | collective-permute-start | bytes 393224 | tf_op jit(solution)/shard_map/ppermute | solution.py:143
  9.8 2.7 %load.1 = (f32[1024,512]{1,0:T(8,128)S(1)}, bf16[4,512,1024]{2,1,0:T(8,128)(2,1)S(1)}) custom-call(f32[1024,512]{1,0:T(8,128)S(1)} %copy-done, bf16[4,1024,512]{2,1,0:T(8,128)(2,1)} %ratings.1), custom_call_target="tpu_custom_call" | custom-call | bytes 12582912 | tf_op jit(solution)/shard_map/load/pallas_call | solution.py:47
  16.2 2.6 %gradients.9 = (bf16[256,1024]{1,0:T(8,128)(2,1)S(1)}, bf16[256,1024]{1,0:T(8,128)(2,1)S(1)}, bf16[256,512]{1,0:T(8,128)(2,1)S(1)}, bf16[256,512]{1,0:T(8,128)(2...) custom-call(s32[4,4,8]{2,1,0:T(4,128)S(1)} %bitcast.1, ...), custom_call_target="tpu_custom_call" | custom-call | flops 1610612736 | bytes 2097152 | tf_op jit(solution)/shard_map/gradients/pallas_call | solution.py:97
  18.9 2.5 %collective-permute-start.12 = (f32[64,512]{1,0:T(8,128)S(1)}, f32[64,512]{1,0:T(8,128)S(1)}, u32[]{:S(2)}, u32[]{:S(2)}) collective-permute-start(f32[64,512]{1,0:T(8,128)S(1)} %get-tuple-element.89), channel_id=1, source_target_pairs={{0,3},{1,2},{2,1},{3,0},{4,7},{5,6},{6,5},{7,4},{8,11},{9,10},{10,... | collective-permute-start | bytes 393224 | tf_op jit(solution)/shard_map/ppermute | solution.py:143
  22.4 2.6 %gradients.8 = (bf16[256,1024]{1,0:T(8,128)(2,1)S(1)}, bf16[256,1024]{1,0:T(8,128)(2,1)S(1)}, bf16[256,512]{1,0:T(8,128)(2,1)S(1)}, bf16[256,512]{1,0:T(8,128)(2...) custom-call(s32[4,4,8]{2,1,0:T(4,128)S(1)} %bitcast.2, ...), custom_call_target="tpu_custom_call" | custom-call | flops 1610612736 | bytes 2097152 | tf_op jit(solution)/shard_map/gradients/pallas_call | solution.py:97
  25.0 2.5 %collective-permute-start.6 = (f32[64,512]{1,0:T(8,128)S(1)}, f32[64,512]{1,0:T(8,128)S(1)}, u32[]{:S(2)}, u32[]{:S(2)}) collective-permute-start(f32[64,512]{1,0:T(8,128)S(1)} %get-tuple-element.76), channel_id=1, source_target_pairs={{0,3},{1,2},{2,1},{3,0},{4,7},{5,6},{6,5},{7,4},{8,11},{9,10},{10,... | collective-permute-start | bytes 393224 | tf_op jit(solution)/shard_map/ppermute | solution.py:143
  31.4 2.9 %collective-permute-done.5 = f32[64,512]{1,0:T(8,128)S(1)} collective-permute-done((f32[64,512]{1,0:T(8,128)S(1)}, f32[64,512]{1,0:T(8,128)S(1)}, u32[]{:S(2)}, u32[]{:S(2)}) %collective-permute-start.5) | collective-permute-done | bytes 131104 | tf_op jit(solution)/shard_map/ppermute | solution.py:143
  45.4 2.8 %collective-permute-start.25 = (f32[64,512]{1,0:T(8,128)S(1)}, f32[64,512]{1,0:T(8,128)S(1)}, u32[]{:S(2)}, u32[]{:S(2)}) collective-permute-start(f32[64,512]{1,0:T(8,128)S(1)} %multiply_add_fusion.7.refs_3_), channel_id=1, source_target_pairs={{0,3},{1,2},{2,1},{3,0},{4,7},{5,6},{6,5},{7,4},{8,11},{9,10},{10,... | collective-permute-start | bytes 393224 | tf_op jit(solution)/shard_map/ppermute | solution.py:143
  50.6 2.6 %gradients.10 = (bf16[256,1024]{1,0:T(8,128)(2,1)S(1)}, bf16[256,1024]{1,0:T(8,128)(2,1)S(1)}, bf16[256,512]{1,0:T(8,128)(2,1)S(1)}, bf16[256,512]{1,0:T(8,128)(...) custom-call(s32[4,4,8]{2,1,0:T(4,128)S(1)} %bitcast.3, ...), custom_call_target="tpu_custom_call" | custom-call | flops 1610612736 | bytes 2097152 | tf_op jit(solution)/shard_map/gradients/pallas_call | solution.py:97
  53.8 3.1 %collective-permute-start.19 = (f32[64,512]{1,0:T(8,128)S(1)}, f32[64,512]{1,0:T(8,128)S(1)}, u32[]{:S(2)}, u32[]{:S(2)}) collective-permute-start(f32[64,512]{1,0:T(8,128)S(1)} %get-tuple-element.92), channel_id=1, source_target_pairs={{0,2},{1,3},{2,0},{3,1},{4,6},{5,7},{6,4},{7,5},{8,10},{9,11},{10,... | collective-permute-start | bytes 393224 | tf_op jit(solution)/shard_map/ppermute | solution.py:143
  56.9 2.6 %gradients.11 = (bf16[256,1024]{1,0:T(8,128)(2,1)S(1)}, bf16[256,1024]{1,0:T(8,128)(2,1)S(1)}, bf16[256,512]{1,0:T(8,128)(2,1)S(1)}, bf16[256,512]{1,0:T(8,128)(...) custom-call(s32[4,4,8]{2,1,0:T(4,128)S(1)} %bitcast.4, ...), custom_call_target="tpu_custom_call" | custom-call | flops 1610612736 | bytes 2097152 | tf_op jit(solution)/shard_map/gradients/pallas_call | solution.py:97
  79.3 3.1 %collective-permute-start.41 = (f32[64,512]{1,0:T(8,128)S(1)}, f32[64,512]{1,0:T(8,128)S(1)}, u32[]{:S(2)}, u32[]{:S(2)}) collective-permute-start(f32[64,512]{1,0:T(8,128)S(1)} %multiply_add_fusion.4.refs_3_), channel_id=1, source_target_pairs={{0,3},{1,2},{2,1},{3,0},{4,7},{5,6},{6,5},{7,4},{8,11},{9,10},{10,... | collective-permute-start | bytes 393224 | tf_op jit(solution)/shard_map/ppermute | solution.py:143
  83.7 2.6 %gradients.12 = (bf16[256,1024]{1,0:T(8,128)(2,1)S(1)}, bf16[256,1024]{1,0:T(8,128)(2,1)S(1)}, bf16[256,512]{1,0:T(8,128)(2,1)S(1)}, bf16[256,512]{1,0:T(8,128)(...) custom-call(s32[4,4,8]{2,1,0:T(4,128)S(1)} %bitcast.5, ...), custom_call_target="tpu_custom_call" | custom-call | flops 1610612736 | bytes 2097152 | tf_op jit(solution)/shard_map/gradients/pallas_call | solution.py:97
  90.1 2.6 %gradients.13 = (bf16[256,1024]{1,0:T(8,128)(2,1)S(1)}, bf16[256,1024]{1,0:T(8,128)(2,1)S(1)}, bf16[256,512]{1,0:T(8,128)(2,1)S(1)}, bf16[256,512]{1,0:T(8,128)(...) custom-call(s32[4,4,8]{2,1,0:T(4,128)S(1)} %bitcast.6, ...), custom_call_target="tpu_custom_call" | custom-call | flops 1610612736 | bytes 2097152 | tf_op jit(solution)/shard_map/gradients/pallas_call | solution.py:97
  96.6 2.9 %collective-permute-start.50 = (f32[64,512]{1,0:T(8,128)S(1)}, f32[64,512]{1,0:T(8,128)S(1)}, u32[]{:S(2)}, u32[]{:S(2)}) collective-permute-start(f32[64,512]{1,0:T(8,128)S(1)} %multiply_add_fusion.5), channel_id=1, source_target_pairs={{0,8},{1,9},{2,10},{3,11},{4,12},{5,13},{6,14},{7,15},{8,16},{9,17... | collective-permute-start | bytes 393224 | tf_op jit(solution)/shard_map/ppermute | solution.py:150
  100.0 2.8 %collective-permute-done.44 = f32[64,512]{1,0:T(8,128)S(1)} collective-permute-done((f32[64,512]{1,0:T(8,128)S(1)}, f32[64,512]{1,0:T(8,128)S(1)}, u32[]{:S(2)}, u32[]{:S(2)}) %collective-permute-start.44) | collective-permute-done | bytes 131104 | tf_op jit(solution)/shard_map/ppermute | solution.py:143
  103.0 2.3 %collective-permute-start.51 = (f32[64,512]{1,0:T(8,128)S(1)}, f32[64,512]{1,0:T(8,128)S(1)}, u32[]{:S(2)}, u32[]{:S(2)}) collective-permute-start(f32[64,512]{1,0:T(8,128)S(1)} %add_add_fusion.1), channel_id=1, source_target_pairs={{0,12},{1,13},{2,14},{3,15},{4,8},{5,9},{6,10},{7,11},{8,20},{9,21... | collective-permute-start | bytes 393224 | tf_op jit(solution)/shard_map/ppermute | solution.py:150
  107.9 3.0 %collective-permute-start.47 = (f32[64,512]{1,0:T(8,128)S(1)}, f32[64,512]{1,0:T(8,128)S(1)}, u32[]{:S(2)}, u32[]{:S(2)}) collective-permute-start(f32[64,512]{1,0:T(8,128)S(1)} %multiply_add_fusion.3.refs_3_), channel_id=1, source_target_pairs={{0,1},{1,0},{2,3},{3,2},{4,5},{5,4},{6,7},{7,6},{8,9},{9,8},{10,11... | collective-permute-start | bytes 393224 | tf_op jit(solution)/shard_map/ppermute | solution.py:143
  117.4 2.5 %collective-permute-done.49.refs_6_ = f32[64,512]{1,0:T(8,128)S(1)} collective-permute-done((f32[64,512]{1,0:T(8,128)S(1)}, f32[64,512]{1,0:T(8,128)S(1)}, u32[]{:S(2)}, u32[]{:S(2)}) %collective-permute-start.49) | collective-permute-done | bytes 131104 | tf_op jit(solution)/shard_map/ppermute | solution.py:143
  119.8 2.6 %gradients.14 = (bf16[256,1024]{1,0:T(8,128)(2,1)S(1)}, bf16[256,1024]{1,0:T(8,128)(2,1)S(1)}, bf16[256,512]{1,0:T(8,128)(2,1)S(1)}, bf16[256,512]{1,0:T(8,128)(...) custom-call(s32[4,4,8]{2,1,0:T(4,128)S(1)} %bitcast.7, ...), custom_call_target="tpu_custom_call" | custom-call | flops 1610612736 | bytes 2097152 | tf_op jit(solution)/shard_map/gradients/pallas_call | solution.py:97
  122.6 3.3 %collective-permute-start.56 = (f32[64,512]{1,0:T(8,128)S(1)}, f32[64,512]{1,0:T(8,128)S(1)}, u32[]{:S(2)}, u32[]{:S(2)}) collective-permute-start(f32[64,512]{1,0:T(8,128)S(1)} %get-tuple-element.134), channel_id=1, source_target_pairs={{0,2},{1,3},{2,0},{3,1},{4,6},{5,7},{6,4},{7,5},{8,10},{9,11},{10,... | collective-permute-start | bytes 393224 | tf_op jit(solution)/shard_map/ppermute | solution.py:143
  126.0 2.6 %gradients.15 = (bf16[256,1024]{1,0:T(8,128)(2,1)S(1)}, bf16[256,1024]{1,0:T(8,128)(2,1)S(1)}, bf16[256,512]{1,0:T(8,128)(2,1)S(1)}, bf16[256,512]{1,0:T(8,128)(...) custom-call(s32[4,4,8]{2,1,0:T(4,128)S(1)} %bitcast.8, ...), custom_call_target="tpu_custom_call" | custom-call | flops 1610612736 | bytes 2097152 | tf_op jit(solution)/shard_map/gradients/pallas_call | solution.py:97
  132.4 2.7 %collective-permute-done.61 = f32[64,512]{1,0:T(8,128)S(1)} collective-permute-done((f32[64,512]{1,0:T(8,128)S(1)}, f32[64,512]{1,0:T(8,128)S(1)}, u32[]{:S(2)}, u32[]{:S(2)}) %collective-permute-start.61) | collective-permute-done | bytes 131104 | tf_op jit(solution)/shard_map/ppermute | solution.py:143
  137.4 3.2 %user_step.7 = f32[1024,512]{1,0:T(8,128)} custom-call(f32[1024,512]{1,0:T(8,128)S(1)} %user_step.6.refs_1_.refs_0_, bf16[256,1024]{1,0:T(8,128)(2,1)S(1)} %get-tuple-element.124.refs_1_, bf16[256,1024]{1,0:T(8,128)(2,1)S(1)} %get-tuple-element.125.refs_2_, bf16[256,512]{1,0:T(8,128)(2,1)S(1)} %get-tuple-element.126.refs_3_, ...), custom_call_target="tpu_custom_call" | custom-call | flops 1610612736 | bytes 4194304 | tf_op jit(solution)/shard_map/user_step/pallas_call | solution.py:126
  (136 shorter events, 75.0 us)
Async XLA Ops:
  0.6 11.9 %collective-permute-start = (f32[64,512]{1,0:T(8,128)}, f32[64,512]{1,0:T(8,128)S(1)}, u32[]{:S(2)}, u32[]{:S(2)}) collective-permute-start(f32[64,512]{1,0:T(8,128)} %refs_3_.1), channel_id=1, source_target_pairs={{0,4},{1,5},{2,6},{3,7},{4,0},{5,1},{6,2},{7,3},{8,12},{9,13},{10,... | collective-permute-start | bytes 393224 | tf_op jit(solution)/shard_map/ppermute | solution.py:143
  4.7 11.0 %collective-permute-start.7 = (f32[64,512]{1,0:T(8,128)}, f32[64,512]{1,0:T(8,128)S(1)}, u32[]{:S(2)}, u32[]{:S(2)}) collective-permute-start(f32[64,512]{1,0:T(8,128)} %refs_3_.1), channel_id=1, source_target_pairs={{0,1},{1,0},{2,3},{3,2},{4,5},{5,4},{6,7},{7,6},{8,9},{9,8},{10,11... | collective-permute-start | bytes 393224 | tf_op jit(solution)/shard_map/ppermute | solution.py:143
  6.3 9.8 %collective-permute-start.8 = (f32[64,512]{1,0:T(8,128)}, f32[64,512]{1,0:T(8,128)S(1)}, u32[]{:S(2)}, u32[]{:S(2)}) collective-permute-start(f32[64,512]{1,0:T(8,128)} %refs_3_.1), channel_id=1, source_target_pairs={{0,2},{1,3},{2,0},{3,1},{4,6},{5,7},{6,4},{7,5},{8,10},{9,11},{10,... | collective-permute-start | bytes 393224 | tf_op jit(solution)/shard_map/ppermute | solution.py:143
  28.7 9.9 %collective-permute-start.13 = (f32[64,512]{1,0:T(8,128)S(1)}, f32[64,512]{1,0:T(8,128)S(1)}, u32[]{:S(2)}, u32[]{:S(2)}) collective-permute-start(f32[64,512]{1,0:T(8,128)S(1)} %multiply_add_fusion.10), channel_id=1, source_target_pairs={{0,12},{1,13},{2,14},{3,15},{4,8},{5,9},{6,10},{7,11},{8,20},{9,21... | collective-permute-start | bytes 393224 | tf_op jit(solution)/shard_map/ppermute | solution.py:150
  28.7 13.9 %collective-permute-start.21 = (f32[64,512]{1,0:T(8,128)S(1)}, f32[64,512]{1,0:T(8,128)S(1)}, u32[]{:S(2)}, u32[]{:S(2)}) collective-permute-start(f32[64,512]{1,0:T(8,128)S(1)} %multiply_add_fusion.10), channel_id=1, source_target_pairs={{0,8},{1,9},{2,10},{3,11},{4,12},{5,13},{6,14},{7,15},{8,16},{9,17... | collective-permute-start | bytes 393224 | tf_op jit(solution)/shard_map/ppermute | solution.py:150
  34.4 10.2 %collective-permute-start.22 = (f32[64,512]{1,0:T(8,128)S(1)}, f32[64,512]{1,0:T(8,128)S(1)}, u32[]{:S(2)}, u32[]{:S(2)}) collective-permute-start(f32[64,512]{1,0:T(8,128)S(1)} %add_add_fusion.3), channel_id=1, source_target_pairs={{0,12},{1,13},{2,14},{3,15},{4,8},{5,9},{6,10},{7,11},{8,20},{9,21... | collective-permute-start | bytes 393224 | tf_op jit(solution)/shard_map/ppermute | solution.py:150
  44.6 12.3 %collective-permute-start.23 = (f32[64,512]{1,0:T(8,128)S(1)}, f32[64,512]{1,0:T(8,128)S(1)}, u32[]{:S(2)}, u32[]{:S(2)}) collective-permute-start(f32[64,512]{1,0:T(8,128)S(1)} %multiply_add_fusion.7.refs_3_), channel_id=1, source_target_pairs={{0,1},{1,0},{2,3},{3,2},{4,5},{5,4},{6,7},{7,6},{8,9},{9,8},{10,11... | collective-permute-start | bytes 393224 | tf_op jit(solution)/shard_map/ppermute | solution.py:143
  45.4 11.5 %collective-permute-start.24 = (f32[64,512]{1,0:T(8,128)S(1)}, f32[64,512]{1,0:T(8,128)S(1)}, u32[]{:S(2)}, u32[]{:S(2)}) collective-permute-start(f32[64,512]{1,0:T(8,128)S(1)} %multiply_add_fusion.7.refs_3_), channel_id=1, source_target_pairs={{0,2},{1,3},{2,0},{3,1},{4,6},{5,7},{6,4},{7,5},{8,10},{9,11},{10,... | collective-permute-start | bytes 393224 | tf_op jit(solution)/shard_map/ppermute | solution.py:143
  45.4 11.5 %collective-permute-start.25 = (f32[64,512]{1,0:T(8,128)S(1)}, f32[64,512]{1,0:T(8,128)S(1)}, u32[]{:S(2)}, u32[]{:S(2)}) collective-permute-start(f32[64,512]{1,0:T(8,128)S(1)} %multiply_add_fusion.7.refs_3_), channel_id=1, source_target_pairs={{0,3},{1,2},{2,1},{3,0},{4,7},{5,6},{6,5},{7,4},{8,11},{9,10},{10,... | collective-permute-start | bytes 393224 | tf_op jit(solution)/shard_map/ppermute | solution.py:143
  53.2 9.9 %collective-permute-start.20 = (f32[64,512]{1,0:T(8,128)S(1)}, f32[64,512]{1,0:T(8,128)S(1)}, u32[]{:S(2)}, u32[]{:S(2)}) collective-permute-start(f32[64,512]{1,0:T(8,128)S(1)} %get-tuple-element.93), channel_id=1, source_target_pairs={{0,3},{1,2},{2,1},{3,0},{4,7},{5,6},{6,5},{7,4},{8,11},{9,10},{10,... | collective-permute-start | bytes 393224 | tf_op jit(solution)/shard_map/ppermute | solution.py:143
  63.3 13.5 %collective-permute-start.37 = (f32[64,512]{1,0:T(8,128)S(1)}, f32[64,512]{1,0:T(8,128)S(1)}, u32[]{:S(2)}, u32[]{:S(2)}) collective-permute-start(f32[64,512]{1,0:T(8,128)S(1)} %multiply_add_fusion.8), channel_id=1, source_target_pairs={{0,8},{1,9},{2,10},{3,11},{4,12},{5,13},{6,14},{7,15},{8,16},{9,17... | collective-permute-start | bytes 393224 | tf_op jit(solution)/shard_map/ppermute | solution.py:150
  68.2 10.6 %collective-permute-start.38 = (f32[64,512]{1,0:T(8,128)S(1)}, f32[64,512]{1,0:T(8,128)S(1)}, u32[]{:S(2)}, u32[]{:S(2)}) collective-permute-start(f32[64,512]{1,0:T(8,128)S(1)} %add_add_fusion.2), channel_id=1, source_target_pairs={{0,12},{1,13},{2,14},{3,15},{4,8},{5,9},{6,10},{7,11},{8,20},{9,21... | collective-permute-start | bytes 393224 | tf_op jit(solution)/shard_map/ppermute | solution.py:150
  78.8 11.2 %collective-permute-start.39 = (f32[64,512]{1,0:T(8,128)S(1)}, f32[64,512]{1,0:T(8,128)S(1)}, u32[]{:S(2)}, u32[]{:S(2)}) collective-permute-start(f32[64,512]{1,0:T(8,128)S(1)} %multiply_add_fusion.4.refs_3_), channel_id=1, source_target_pairs={{0,1},{1,0},{2,3},{3,2},{4,5},{5,4},{6,7},{7,6},{8,9},{9,8},{10,11... | collective-permute-start | bytes 393224 | tf_op jit(solution)/shard_map/ppermute | solution.py:143
  79.3 10.7 %collective-permute-start.40 = (f32[64,512]{1,0:T(8,128)S(1)}, f32[64,512]{1,0:T(8,128)S(1)}, u32[]{:S(2)}, u32[]{:S(2)}) collective-permute-start(f32[64,512]{1,0:T(8,128)S(1)} %multiply_add_fusion.4.refs_3_), channel_id=1, source_target_pairs={{0,2},{1,3},{2,0},{3,1},{4,6},{5,7},{6,4},{7,5},{8,10},{9,11},{10,... | collective-permute-start | bytes 393224 | tf_op jit(solution)/shard_map/ppermute | solution.py:143
  79.3 10.7 %collective-permute-start.41 = (f32[64,512]{1,0:T(8,128)S(1)}, f32[64,512]{1,0:T(8,128)S(1)}, u32[]{:S(2)}, u32[]{:S(2)}) collective-permute-start(f32[64,512]{1,0:T(8,128)S(1)} %multiply_add_fusion.4.refs_3_), channel_id=1, source_target_pairs={{0,3},{1,2},{2,1},{3,0},{4,7},{5,6},{6,5},{7,4},{8,11},{9,10},{10,... | collective-permute-start | bytes 393224 | tf_op jit(solution)/shard_map/ppermute | solution.py:143
  86.4 9.9 %collective-permute-start.36 = (f32[64,512]{1,0:T(8,128)S(1)}, f32[64,512]{1,0:T(8,128)S(1)}, u32[]{:S(2)}, u32[]{:S(2)}) collective-permute-start(f32[64,512]{1,0:T(8,128)S(1)} %get-tuple-element.110), channel_id=1, source_target_pairs={{0,3},{1,2},{2,1},{3,0},{4,7},{5,6},{6,5},{7,4},{8,11},{9,10},{10,... | collective-permute-start | bytes 393224 | tf_op jit(solution)/shard_map/ppermute | solution.py:143
  96.6 10.6 %collective-permute-start.42 = (f32[64,512]{1,0:T(8,128)S(1)}, f32[64,512]{1,0:T(8,128)S(1)}, u32[]{:S(2)}, u32[]{:S(2)}) collective-permute-start(f32[64,512]{1,0:T(8,128)S(1)} %multiply_add_fusion.5), channel_id=1, source_target_pairs={{0,12},{1,13},{2,14},{3,15},{4,8},{5,9},{6,10},{7,11},{8,20},{9,21... | collective-permute-start | bytes 393224 | tf_op jit(solution)/shard_map/ppermute | solution.py:150
  96.6 15.8 %collective-permute-start.50 = (f32[64,512]{1,0:T(8,128)S(1)}, f32[64,512]{1,0:T(8,128)S(1)}, u32[]{:S(2)}, u32[]{:S(2)}) collective-permute-start(f32[64,512]{1,0:T(8,128)S(1)} %multiply_add_fusion.5), channel_id=1, source_target_pairs={{0,8},{1,9},{2,10},{3,11},{4,12},{5,13},{6,14},{7,15},{8,16},{9,17... | collective-permute-start | bytes 393224 | tf_op jit(solution)/shard_map/ppermute | solution.py:150
  103.0 9.5 %collective-permute-start.51 = (f32[64,512]{1,0:T(8,128)S(1)}, f32[64,512]{1,0:T(8,128)S(1)}, u32[]{:S(2)}, u32[]{:S(2)}) collective-permute-start(f32[64,512]{1,0:T(8,128)S(1)} %add_add_fusion.1), channel_id=1, source_target_pairs={{0,12},{1,13},{2,14},{3,15},{4,8},{5,9},{6,10},{7,11},{8,20},{9,21... | collective-permute-start | bytes 393224 | tf_op jit(solution)/shard_map/ppermute | solution.py:150
  112.5 13.3 %collective-permute-start.52 = (f32[64,512]{1,0:T(8,128)S(1)}, f32[64,512]{1,0:T(8,128)S(1)}, u32[]{:S(2)}, u32[]{:S(2)}) collective-permute-start(f32[64,512]{1,0:T(8,128)S(1)} %multiply_add_fusion.2.refs_3_), channel_id=1, source_target_pairs={{0,1},{1,0},{2,3},{3,2},{4,5},{5,4},{6,7},{7,6},{8,9},{9,8},{10,11... | collective-permute-start | bytes 393224 | tf_op jit(solution)/shard_map/ppermute | solution.py:143
  114.5 11.5 %collective-permute-start.53 = (f32[64,512]{1,0:T(8,128)S(1)}, f32[64,512]{1,0:T(8,128)S(1)}, u32[]{:S(2)}, u32[]{:S(2)}) collective-permute-start(f32[64,512]{1,0:T(8,128)S(1)} %multiply_add_fusion.2.refs_3_), channel_id=1, source_target_pairs={{0,2},{1,3},{2,0},{3,1},{4,6},{5,7},{6,4},{7,5},{8,10},{9,11},{10,... | collective-permute-start | bytes 393224 | tf_op jit(solution)/shard_map/ppermute | solution.py:143
  114.5 11.5 %collective-permute-start.54 = (f32[64,512]{1,0:T(8,128)S(1)}, f32[64,512]{1,0:T(8,128)S(1)}, u32[]{:S(2)}, u32[]{:S(2)}) collective-permute-start(f32[64,512]{1,0:T(8,128)S(1)} %multiply_add_fusion.2.refs_3_), channel_id=1, source_target_pairs={{0,3},{1,2},{2,1},{3,0},{4,7},{5,6},{6,5},{7,4},{8,11},{9,10},{10,... | collective-permute-start | bytes 393224 | tf_op jit(solution)/shard_map/ppermute | solution.py:143
  122.5 9.6 %collective-permute-start.57 = (f32[64,512]{1,0:T(8,128)S(1)}, f32[64,512]{1,0:T(8,128)S(1)}, u32[]{:S(2)}, u32[]{:S(2)}) collective-permute-start(f32[64,512]{1,0:T(8,128)S(1)} %get-tuple-element.135), channel_id=1, source_target_pairs={{0,3},{1,2},{2,1},{3,0},{4,7},{5,6},{6,5},{7,4},{8,11},{9,10},{10,... | collective-permute-start | bytes 393224 | tf_op jit(solution)/shard_map/ppermute | solution.py:143
  122.6 9.7 %collective-permute-start.56 = (f32[64,512]{1,0:T(8,128)S(1)}, f32[64,512]{1,0:T(8,128)S(1)}, u32[]{:S(2)}, u32[]{:S(2)}) collective-permute-start(f32[64,512]{1,0:T(8,128)S(1)} %get-tuple-element.134), channel_id=1, source_target_pairs={{0,2},{1,3},{2,0},{3,1},{4,6},{5,7},{6,4},{7,5},{8,10},{9,11},{10,... | collective-permute-start | bytes 393224 | tf_op jit(solution)/shard_map/ppermute | solution.py:143
  (42 other events, 291.4 us)

commit v10 on v8

--- a/solution.py
+++ b/solution.py
@@ -165,14 +165,17 @@
         base = functools.reduce(jnp.add, arrived(one[4:]))
         base = first[0] + 0.005 * (base - 0.05 * first[0])
         term = functools.reduce(jnp.add, arrived(two[4:]))
-        flip = strata % 2 if last else 0
-        near = onward(base, 0 if flip else ny) + 0.005 * onward(term, ny if flip else 0)
+        early = over_y(base, ny)
+        rows = early + 0.005 * term
         if last:
-            return user_step(users, [one[:4], two[:4]]), near
-        far = onward(base, 0) + 0.005 * onward(term, ny)
+            users = user_step(users, [one[:4], two[:4]])
+            return users, onward(rows, ny if strata % 2 else 0)
+        near = onward(rows, 0)
+        far = onward(rows, ny)
         users, base = lax.optimization_barrier((users, base))
         users = user_step(users, [one[:4], two[:4]])
-        first, second = gathered(near), gathered(far)
+        first = gathered(near)
+        second = gathered(far)
 
 
 def solution(mesh):

time: 153 us -> 148 us (0.967)
  starting transfers between devices: 73.8 us -> 67.7 us
    ppermute x49 -> x53, waiting for transfers between devices: 23.8 us -> 34.4 us  [over_y(): return lax.ppermute(x, 'sub', [(i, i ^ r) for i in range(n_sub)])]
    ppermute x14 -> x7, waiting for transfers between devices: 18.8 us -> 9.66 us  [onward(): return lax.ppermute(x, ('group', 'sub'), route)]
    ppermute x14 -> x7, starting transfers between devices: 12.6 us -> 5.35 us  [onward(): return lax.ppermute(x, ('group', 'sub'), route)]
    ppermute x49 -> x53, starting transfers between devices: 61.2 us -> 62.4 us  [over_y(): return lax.ppermute(x, 'sub', [(i, i ^ r) for i in range(n_sub)])]
  transfers between devices with their start and end apart: 63 -> 60, of which waited for: 20 -> 27; matrix products, arithmetic and copies ran while one was open for 0% -> 0% of each run, Pallas kernels for 21% -> 22%
where the time goes in v10:
time: 148 us
  starting transfers between devices  67.7 us (46%)
  waiting for transfers between devices  44 us (30%)
  Pallas kernels  32.7 us (22%)
  local copies, waits for them, and re-layouts  2.25 us (2%)
    ppermute x53, starting transfers between devices, over_y(): return lax.ppermute(x, 'sub', [(i, i ^ r) for i in range(n_sub)])  62.4 us
    ppermute x53, waiting for transfers between devices, over_y(): return lax.ppermute(x, 'sub', [(i, i ^ r) for i in range(n_sub)])  34.4 us
    pallas_call x8, Pallas kernels, gradients(): pl.pallas_call(functools.partial(grad_kernel, ny, place, stratum), in_spe...  21 us
    ppermute x7, waiting for transfers between devices, onward(): return lax.ppermute(x, ('group', 'sub'), route)  9.66 us
    pallas_call x4, Pallas kernels, user_step(): pl.pallas_call(functools.partial(step_kernel, len(parts)), in_specs=[VMEM...  8.97 us
    ppermute x7, starting transfers between devices, onward(): return lax.ppermute(x, ('group', 'sub'), route)  5.35 us
  transfers between devices with their start and end apart: 60, of which 27 were waited for; matrix products, arithmetic and copies ran while one was open for 0% of the time, Pallas kernels for 22%

profile of v10, /device:TPU:0, one launch (start us, length us, event | category | flops | bytes accessed | tf_op | source)
XLA Modules:
  0.0 148.0 jit_solution(2592430301873620401)
XLA Ops:
  0.6 4.1 %collective-permute-start.6 = (f32[64,512]{1,0:T(8,128)}, f32[64,512]{1,0:T(8,128)S(1)}, u32[]{:S(2)}, u32[]{:S(2)}) collective-permute-start(f32[64,512]{1,0:T(8,128)} %refs_3_.1), channel_id=1, source_target_pairs={{0,4},{1,5},{2,6},{3,7},{4,0},{5,1},{6,2},{7,3},{8,12},{9,13},{10,... | collective-permute-start | bytes 393224 | tf_op jit(solution)/shard_map/ppermute | solution.py:143
  4.7 2.5 %collective-permute-start.2 = (f32[64,512]{1,0:T(8,128)}, f32[64,512]{1,0:T(8,128)S(1)}, u32[]{:S(2)}, u32[]{:S(2)}) collective-permute-start(f32[64,512]{1,0:T(8,128)} %refs_3_.1), channel_id=1, source_target_pairs={{0,3},{1,2},{2,1},{3,0},{4,7},{5,6},{6,5},{7,4},{8,11},{9,10},{10,... | collective-permute-start | bytes 393224 | tf_op jit(solution)/shard_map/ppermute | solution.py:143
  9.8 2.7 %load.1 = (f32[1024,512]{1,0:T(8,128)S(1)}, bf16[4,512,1024]{2,1,0:T(8,128)(2,1)S(1)}) custom-call(f32[1024,512]{1,0:T(8,128)S(1)} %copy-done, bf16[4,1024,512]{2,1,0:T(8,128)(2,1)} %ratings.1), custom_call_target="tpu_custom_call" | custom-call | bytes 12582912 | tf_op jit(solution)/shard_map/load/pallas_call | solution.py:47
  12.5 2.6 %collective-permute-start.9 = (f32[64,512]{1,0:T(8,128)S(1)}, f32[64,512]{1,0:T(8,128)S(1)}, u32[]{:S(2)}, u32[]{:S(2)}) collective-permute-start(f32[64,512]{1,0:T(8,128)S(1)} %collective-permute-done.6.refs_3_), channel_id=1, source_target_pairs={{0,3},{1,2},{2,1},{3,0},{4,7},{5,6},{6,5},{7,4},{8,11},{9,10},{10,... | collective-permute-start | bytes 393224 | tf_op jit(solution)/shard_map/ppermute | solution.py:143
  16.1 2.6 %gradients.8 = (bf16[256,1024]{1,0:T(8,128)(2,1)S(1)}, bf16[256,1024]{1,0:T(8,128)(2,1)S(1)}, bf16[256,512]{1,0:T(8,128)(2,1)S(1)}, bf16[256,512]{1,0:T(8,128)(2...) custom-call(s32[4,4,8]{2,1,0:T(4,128)S(1)} %bitcast.1, ...), custom_call_target="tpu_custom_call" | custom-call | flops 1610612736 | bytes 2097152 | tf_op jit(solution)/shard_map/gradients/pallas_call | solution.py:97
  22.3 2.6 %gradients.9 = (bf16[256,1024]{1,0:T(8,128)(2,1)S(1)}, bf16[256,1024]{1,0:T(8,128)(2,1)S(1)}, bf16[256,512]{1,0:T(8,128)(2,1)S(1)}, bf16[256,512]{1,0:T(8,128)(2...) custom-call(s32[4,4,8]{2,1,0:T(4,128)S(1)} %bitcast.2, ...), custom_call_target="tpu_custom_call" | custom-call | flops 1610612736 | bytes 2097152 | tf_op jit(solution)/shard_map/gradients/pallas_call | solution.py:97
  32.5 2.8 %collective-permute-done.13 = f32[64,512]{1,0:T(8,128)S(1)} collective-permute-done((f32[64,512]{1,0:T(8,128)S(1)}, f32[64,512]{1,0:T(8,128)S(1)}, u32[]{:S(2)}, u32[]{:S(2)}) %collective-permute-start.13) | collective-permute-done | bytes 131104 | tf_op jit(solution)/shard_map/ppermute | solution.py:143
  39.3 2.7 %collective-permute-done.14.refs_3_ = f32[64,512]{1,0:T(8,128)S(1)} collective-permute-done((f32[64,512]{1,0:T(8,128)S(1)}, f32[64,512]{1,0:T(8,128)S(1)}, u32[]{:S(2)}, u32[]{:S(2)}) %collective-permute-start.14) | collective-permute-done | bytes 131104 | tf_op jit(solution)/shard_map/ppermute | solution.py:150
  53.7 2.6 %gradients.10 = (bf16[256,1024]{1,0:T(8,128)(2,1)S(1)}, bf16[256,1024]{1,0:T(8,128)(2,1)S(1)}, bf16[256,512]{1,0:T(8,128)(2,1)S(1)}, bf16[256,512]{1,0:T(8,128)(...) custom-call(s32[4,4,8]{2,1,0:T(4,128)S(1)} %bitcast.3, ...), custom_call_target="tpu_custom_call" | custom-call | flops 1610612736 | bytes 2097152 | tf_op jit(solution)/shard_map/gradients/pallas_call | solution.py:97
  59.9 2.6 %gradients.11 = (bf16[256,1024]{1,0:T(8,128)(2,1)S(1)}, bf16[256,1024]{1,0:T(8,128)(2,1)S(1)}, bf16[256,512]{1,0:T(8,128)(2,1)S(1)}, bf16[256,512]{1,0:T(8,128)(...) custom-call(s32[4,4,8]{2,1,0:T(4,128)S(1)} %bitcast.4, ...), custom_call_target="tpu_custom_call" | custom-call | flops 1610612736 | bytes 2097152 | tf_op jit(solution)/shard_map/gradients/pallas_call | solution.py:97
  74.5 3.5 %collective-permute-done.29.refs_3_ = f32[64,512]{1,0:T(8,128)S(1)} collective-permute-done((f32[64,512]{1,0:T(8,128)S(1)}, f32[64,512]{1,0:T(8,128)S(1)}, u32[]{:S(2)}, u32[]{:S(2)}) %collective-permute-start.29) | collective-permute-done | bytes 131104 | tf_op jit(solution)/shard_map/ppermute | solution.py:150
  78.0 2.5 %collective-permute-start.31 = (f32[64,512]{1,0:T(8,128)S(1)}, f32[64,512]{1,0:T(8,128)S(1)}, u32[]{:S(2)}, u32[]{:S(2)}) collective-permute-start(f32[64,512]{1,0:T(8,128)S(1)} %collective-permute-done.29.refs_3_), channel_id=1, source_target_pairs={{0,2},{1,3},{2,0},{3,1},{4,6},{5,7},{6,4},{7,5},{8,10},{9,11},{10,... | collective-permute-start | bytes 393224 | tf_op jit(solution)/shard_map/ppermute | solution.py:143
  88.0 2.6 %gradients.12 = (bf16[256,1024]{1,0:T(8,128)(2,1)S(1)}, bf16[256,1024]{1,0:T(8,128)(2,1)S(1)}, bf16[256,512]{1,0:T(8,128)(2,1)S(1)}, bf16[256,512]{1,0:T(8,128)(...) custom-call(s32[4,4,8]{2,1,0:T(4,128)S(1)} %bitcast.5, ...), custom_call_target="tpu_custom_call" | custom-call | flops 1610612736 | bytes 2097152 | tf_op jit(solution)/shard_map/gradients/pallas_call | solution.py:97
  91.7 2.5 %collective-permute-start.35 = (f32[64,512]{1,0:T(8,128)S(1)}, f32[64,512]{1,0:T(8,128)S(1)}, u32[]{:S(2)}, u32[]{:S(2)}) collective-permute-start(f32[64,512]{1,0:T(8,128)S(1)} %get-tuple-element.110), channel_id=1, source_target_pairs={{0,3},{1,2},{2,1},{3,0},{4,7},{5,6},{6,5},{7,4},{8,11},{9,10},{10,... | collective-permute-start | bytes 393224 | tf_op jit(solution)/shard_map/ppermute | solution.py:143
  94.2 2.6 %gradients.13 = (bf16[256,1024]{1,0:T(8,128)(2,1)S(1)}, bf16[256,1024]{1,0:T(8,128)(2,1)S(1)}, bf16[256,512]{1,0:T(8,128)(2,1)S(1)}, bf16[256,512]{1,0:T(8,128)(...) custom-call(s32[4,4,8]{2,1,0:T(4,128)S(1)} %bitcast.6, ...), custom_call_target="tpu_custom_call" | custom-call | flops 1610612736 | bytes 2097152 | tf_op jit(solution)/shard_map/gradients/pallas_call | solution.py:97
  97.9 2.5 %collective-permute-start.43 = (f32[64,512]{1,0:T(8,128)S(1)}, f32[64,512]{1,0:T(8,128)S(1)}, u32[]{:S(2)}, u32[]{:S(2)}) collective-permute-start(f32[64,512]{1,0:T(8,128)S(1)} %get-tuple-element.123), channel_id=1, source_target_pairs={{0,3},{1,2},{2,1},{3,0},{4,7},{5,6},{6,5},{7,4},{8,11},{9,10},{10,... | collective-permute-start | bytes 393224 | tf_op jit(solution)/shard_map/ppermute | solution.py:143
  100.6 3.4 %collective-permute-done.41 = f32[64,512]{1,0:T(8,128)S(1)} collective-permute-done((f32[64,512]{1,0:T(8,128)S(1)}, f32[64,512]{1,0:T(8,128)S(1)}, u32[]{:S(2)}, u32[]{:S(2)}) %collective-permute-start.41) | collective-permute-done | bytes 131104 | tf_op jit(solution)/shard_map/ppermute | solution.py:143
  107.9 2.5 %collective-permute-start.48 = (f32[64,512]{1,0:T(8,128)S(1)}, f32[64,512]{1,0:T(8,128)S(1)}, u32[]{:S(2)}, u32[]{:S(2)}) collective-permute-start(f32[64,512]{1,0:T(8,128)S(1)} %multiply_add_fusion.2), channel_id=1, source_target_pairs={{0,12},{1,13},{2,14},{3,15},{4,8},{5,9},{6,10},{7,11},{8,20},{9,21... | collective-permute-start | bytes 393224 | tf_op jit(solution)/shard_map/ppermute | solution.py:150
  123.0 2.6 %gradients.14 = (bf16[256,1024]{1,0:T(8,128)(2,1)S(1)}, bf16[256,1024]{1,0:T(8,128)(2,1)S(1)}, bf16[256,512]{1,0:T(8,128)(2,1)S(1)}, bf16[256,512]{1,0:T(8,128)(...) custom-call(s32[4,4,8]{2,1,0:T(4,128)S(1)} %bitcast.7, ...), custom_call_target="tpu_custom_call" | custom-call | flops 1610612736 | bytes 2097152 | tf_op jit(solution)/shard_map/gradients/pallas_call | solution.py:97
  126.8 2.5 %collective-permute-start.54 = (f32[64,512]{1,0:T(8,128)S(1)}, f32[64,512]{1,0:T(8,128)S(1)}, u32[]{:S(2)}, u32[]{:S(2)}) collective-permute-start(f32[64,512]{1,0:T(8,128)S(1)} %get-tuple-element.135), channel_id=1, source_target_pairs={{0,3},{1,2},{2,1},{3,0},{4,7},{5,6},{6,5},{7,4},{8,11},{9,10},{10,... | collective-permute-start | bytes 393224 | tf_op jit(solution)/shard_map/ppermute | solution.py:143
  129.2 2.6 %gradients.15 = (bf16[256,1024]{1,0:T(8,128)(2,1)S(1)}, bf16[256,1024]{1,0:T(8,128)(2,1)S(1)}, bf16[256,512]{1,0:T(8,128)(2,1)S(1)}, bf16[256,512]{1,0:T(8,128)(...) custom-call(s32[4,4,8]{2,1,0:T(4,128)S(1)} %bitcast.8, ...), custom_call_target="tpu_custom_call" | custom-call | flops 1610612736 | bytes 2097152 | tf_op jit(solution)/shard_map/gradients/pallas_call | solution.py:97
  133.0 2.5 %collective-permute-start.58 = (f32[64,512]{1,0:T(8,128)S(1)}, f32[64,512]{1,0:T(8,128)S(1)}, u32[]{:S(2)}, u32[]{:S(2)}) collective-permute-start(f32[64,512]{1,0:T(8,128)S(1)} %get-tuple-element.139), channel_id=1, source_target_pairs={{0,3},{1,2},{2,1},{3,0},{4,7},{5,6},{6,5},{7,4},{8,11},{9,10},{10,... | collective-permute-start | bytes 393224 | tf_op jit(solution)/shard_map/ppermute | solution.py:143
  139.4 2.6 %collective-permute-done.58 = f32[64,512]{1,0:T(8,128)S(1)} collective-permute-done((f32[64,512]{1,0:T(8,128)S(1)}, f32[64,512]{1,0:T(8,128)S(1)}, u32[]{:S(2)}, u32[]{:S(2)}) %collective-permute-start.58) | collective-permute-done | bytes 131104 | tf_op jit(solution)/shard_map/ppermute | solution.py:143
  143.0 3.2 %user_step.7 = f32[1024,512]{1,0:T(8,128)} custom-call(f32[1024,512]{1,0:T(8,128)S(1)} %user_step.6.refs_1_.refs_0_, bf16[256,1024]{1,0:T(8,128)(2,1)S(1)} %get-tuple-element.124.refs_1_, bf16[256,1024]{1,0:T(8,128)(2,1)S(1)} %get-tuple-element.125.refs_2_, bf16[256,512]{1,0:T(8,128)(2,1)S(1)} %get-tuple-element.126.refs_3_, ...), custom_call_target="tpu_custom_call" | custom-call | flops 1610612736 | bytes 4194304 | tf_op jit(solution)/shard_map/user_step/pallas_call | solution.py:126
  (124 shorter events, 81.0 us)
Async XLA Ops:
  0.6 11.9 %collective-permute-start.6 = (f32[64,512]{1,0:T(8,128)}, f32[64,512]{1,0:T(8,128)S(1)}, u32[]{:S(2)}, u32[]{:S(2)}) collective-permute-start(f32[64,512]{1,0:T(8,128)} %refs_3_.1), channel_id=1, source_target_pairs={{0,4},{1,5},{2,6},{3,7},{4,0},{5,1},{6,2},{7,3},{8,12},{9,13},{10,... | collective-permute-start | bytes 393224 | tf_op jit(solution)/shard_map/ppermute | solution.py:143
  4.7 10.9 %collective-permute-start.2 = (f32[64,512]{1,0:T(8,128)}, f32[64,512]{1,0:T(8,128)S(1)}, u32[]{:S(2)}, u32[]{:S(2)}) collective-permute-start(f32[64,512]{1,0:T(8,128)} %refs_3_.1), channel_id=1, source_target_pairs={{0,3},{1,2},{2,1},{3,0},{4,7},{5,6},{6,5},{7,4},{8,11},{9,10},{10,... | collective-permute-start | bytes 393224 | tf_op jit(solution)/shard_map/ppermute | solution.py:143
  7.3 8.8 %collective-permute-start.1 = (f32[64,512]{1,0:T(8,128)}, f32[64,512]{1,0:T(8,128)S(1)}, u32[]{:S(2)}, u32[]{:S(2)}) collective-permute-start(f32[64,512]{1,0:T(8,128)} %refs_3_.1), channel_id=1, source_target_pairs={{0,2},{1,3},{2,0},{3,1},{4,6},{5,7},{6,4},{7,5},{8,10},{9,11},{10,... | collective-permute-start | bytes 393224 | tf_op jit(solution)/shard_map/ppermute | solution.py:143
  12.5 9.4 %collective-permute-start.9 = (f32[64,512]{1,0:T(8,128)S(1)}, f32[64,512]{1,0:T(8,128)S(1)}, u32[]{:S(2)}, u32[]{:S(2)}) collective-permute-start(f32[64,512]{1,0:T(8,128)S(1)} %collective-permute-done.6.refs_3_), channel_id=1, source_target_pairs={{0,3},{1,2},{2,1},{3,0},{4,7},{5,6},{6,5},{7,4},{8,11},{9,10},{10,... | collective-permute-start | bytes 393224 | tf_op jit(solution)/shard_map/ppermute | solution.py:143
  18.7 9.4 %collective-permute-start.3 = (f32[64,512]{1,0:T(8,128)S(1)}, f32[64,512]{1,0:T(8,128)S(1)}, u32[]{:S(2)}, u32[]{:S(2)}) collective-permute-start(f32[64,512]{1,0:T(8,128)S(1)} %get-tuple-element.74), channel_id=1, source_target_pairs={{0,1},{1,0},{2,3},{3,2},{4,5},{5,4},{6,7},{7,6},{8,9},{9,8},{10,11... | collective-permute-start | bytes 393224 | tf_op jit(solution)/shard_map/ppermute | solution.py:143
  37.6 10.3 %collective-permute-start.21 = (f32[64,512]{1,0:T(8,128)S(1)}, f32[64,512]{1,0:T(8,128)S(1)}, u32[]{:S(2)}, u32[]{:S(2)}) collective-permute-start(f32[64,512]{1,0:T(8,128)S(1)} %multiply_add_fusion.6), channel_id=1, source_target_pairs={{0,12},{1,13},{2,14},{3,15},{4,8},{5,9},{6,10},{7,11},{8,20},{9,21... | collective-permute-start | bytes 393224 | tf_op jit(solution)/shard_map/ppermute | solution.py:150
  42.0 9.4 %collective-permute-start.17 = (f32[64,512]{1,0:T(8,128)S(1)}, f32[64,512]{1,0:T(8,128)S(1)}, u32[]{:S(2)}, u32[]{:S(2)}) collective-permute-start(f32[64,512]{1,0:T(8,128)S(1)} %collective-permute-done.14.refs_3_), channel_id=1, source_target_pairs={{0,3},{1,2},{2,1},{3,0},{4,7},{5,6},{6,5},{7,4},{8,11},{9,10},{10,... | collective-permute-start | bytes 393224 | tf_op jit(solution)/shard_map/ppermute | solution.py:143
  43.0 10.6 %collective-permute-start.16 = (f32[64,512]{1,0:T(8,128)S(1)}, f32[64,512]{1,0:T(8,128)S(1)}, u32[]{:S(2)}, u32[]{:S(2)}) collective-permute-start(f32[64,512]{1,0:T(8,128)S(1)} %collective-permute-done.14.refs_3_), channel_id=1, source_target_pairs={{0,2},{1,3},{2,0},{3,1},{4,6},{5,7},{6,4},{7,5},{8,10},{9,11},{10,... | collective-permute-start | bytes 393224 | tf_op jit(solution)/shard_map/ppermute | solution.py:143
  44.7 9.0 %collective-permute-start.15 = (f32[64,512]{1,0:T(8,128)S(1)}, f32[64,512]{1,0:T(8,128)S(1)}, u32[]{:S(2)}, u32[]{:S(2)}) collective-permute-start(f32[64,512]{1,0:T(8,128)S(1)} %collective-permute-done.14.refs_3_), channel_id=1, source_target_pairs={{0,1},{1,0},{2,3},{3,2},{4,5},{5,4},{6,7},{7,6},{8,9},{9,8},{10,11... | collective-permute-start | bytes 393224 | tf_op jit(solution)/shard_map/ppermute | solution.py:143
  47.8 9.6 %collective-permute-start.24 = (f32[64,512]{1,0:T(8,128)S(1)}, f32[64,512]{1,0:T(8,128)S(1)}, u32[]{:S(2)}, u32[]{:S(2)}) collective-permute-start(f32[64,512]{1,0:T(8,128)S(1)} %collective-permute-done.21.refs_3_), channel_id=1, source_target_pairs={{0,3},{1,2},{2,1},{3,0},{4,7},{5,6},{6,5},{7,4},{8,11},{9,10},{10,... | collective-permute-start | bytes 393224 | tf_op jit(solution)/shard_map/ppermute | solution.py:143
  48.5 11.4 %collective-permute-start.23 = (f32[64,512]{1,0:T(8,128)S(1)}, f32[64,512]{1,0:T(8,128)S(1)}, u32[]{:S(2)}, u32[]{:S(2)}) collective-permute-start(f32[64,512]{1,0:T(8,128)S(1)} %collective-permute-done.21.refs_3_), channel_id=1, source_target_pairs={{0,2},{1,3},{2,0},{3,1},{4,6},{5,7},{6,4},{7,5},{8,10},{9,11},{10,... | collective-permute-start | bytes 393224 | tf_op jit(solution)/shard_map/ppermute | solution.py:143
  73.6 9.8 %collective-permute-start.36 = (f32[64,512]{1,0:T(8,128)S(1)}, f32[64,512]{1,0:T(8,128)S(1)}, u32[]{:S(2)}, u32[]{:S(2)}) collective-permute-start(f32[64,512]{1,0:T(8,128)S(1)} %multiply_add_fusion.4), channel_id=1, source_target_pairs={{0,12},{1,13},{2,14},{3,15},{4,8},{5,9},{6,10},{7,11},{8,20},{9,21... | collective-permute-start | bytes 393224 | tf_op jit(solution)/shard_map/ppermute | solution.py:150
  78.0 10.0 %collective-permute-start.31 = (f32[64,512]{1,0:T(8,128)S(1)}, f32[64,512]{1,0:T(8,128)S(1)}, u32[]{:S(2)}, u32[]{:S(2)}) collective-permute-start(f32[64,512]{1,0:T(8,128)S(1)} %collective-permute-done.29.refs_3_), channel_id=1, source_target_pairs={{0,2},{1,3},{2,0},{3,1},{4,6},{5,7},{6,4},{7,5},{8,10},{9,11},{10,... | collective-permute-start | bytes 393224 | tf_op jit(solution)/shard_map/ppermute | solution.py:143
  84.0 10.2 %collective-permute-start.38 = (f32[64,512]{1,0:T(8,128)S(1)}, f32[64,512]{1,0:T(8,128)S(1)}, u32[]{:S(2)}, u32[]{:S(2)}) collective-permute-start(f32[64,512]{1,0:T(8,128)S(1)} %collective-permute-done.36.refs_3_), channel_id=1, source_target_pairs={{0,2},{1,3},{2,0},{3,1},{4,6},{5,7},{6,4},{7,5},{8,10},{9,11},{10,... | collective-permute-start | bytes 393224 | tf_op jit(solution)/shard_map/ppermute | solution.py:143
  91.7 8.7 %collective-permute-start.34 = (f32[64,512]{1,0:T(8,128)S(1)}, f32[64,512]{1,0:T(8,128)S(1)}, u32[]{:S(2)}, u32[]{:S(2)}) collective-permute-start(f32[64,512]{1,0:T(8,128)S(1)} %get-tuple-element.109), channel_id=1, source_target_pairs={{0,2},{1,3},{2,0},{3,1},{4,6},{5,7},{6,4},{7,5},{8,10},{9,11},{10,... | collective-permute-start | bytes 393224 | tf_op jit(solution)/shard_map/ppermute | solution.py:143
  91.7 8.7 %collective-permute-start.35 = (f32[64,512]{1,0:T(8,128)S(1)}, f32[64,512]{1,0:T(8,128)S(1)}, u32[]{:S(2)}, u32[]{:S(2)}) collective-permute-start(f32[64,512]{1,0:T(8,128)S(1)} %get-tuple-element.110), channel_id=1, source_target_pairs={{0,3},{1,2},{2,1},{3,0},{4,7},{5,6},{6,5},{7,4},{8,11},{9,10},{10,... | collective-permute-start | bytes 393224 | tf_op jit(solution)/shard_map/ppermute | solution.py:143
  97.9 8.9 %collective-permute-start.43 = (f32[64,512]{1,0:T(8,128)S(1)}, f32[64,512]{1,0:T(8,128)S(1)}, u32[]{:S(2)}, u32[]{:S(2)}) collective-permute-start(f32[64,512]{1,0:T(8,128)S(1)} %get-tuple-element.123), channel_id=1, source_target_pairs={{0,3},{1,2},{2,1},{3,0},{4,7},{5,6},{6,5},{7,4},{8,11},{9,10},{10,... | collective-permute-start | bytes 393224 | tf_op jit(solution)/shard_map/ppermute | solution.py:143
  107.9 9.8 %collective-permute-start.48 = (f32[64,512]{1,0:T(8,128)S(1)}, f32[64,512]{1,0:T(8,128)S(1)}, u32[]{:S(2)}, u32[]{:S(2)}) collective-permute-start(f32[64,512]{1,0:T(8,128)S(1)} %multiply_add_fusion.2), channel_id=1, source_target_pairs={{0,12},{1,13},{2,14},{3,15},{4,8},{5,9},{6,10},{7,11},{8,20},{9,21... | collective-permute-start | bytes 393224 | tf_op jit(solution)/shard_map/ppermute | solution.py:150
  112.5 10.5 %collective-permute-start.46 = (f32[64,512]{1,0:T(8,128)S(1)}, f32[64,512]{1,0:T(8,128)S(1)}, u32[]{:S(2)}, u32[]{:S(2)}) collective-permute-start(f32[64,512]{1,0:T(8,128)S(1)} %collective-permute-done.44.refs_3_), channel_id=1, source_target_pairs={{0,2},{1,3},{2,0},{3,1},{4,6},{5,7},{6,4},{7,5},{8,10},{9,11},{10,... | collective-permute-start | bytes 393224 | tf_op jit(solution)/shard_map/ppermute | solution.py:143
  117.7 9.1 %collective-permute-start.51 = (f32[64,512]{1,0:T(8,128)S(1)}, f32[64,512]{1,0:T(8,128)S(1)}, u32[]{:S(2)}, u32[]{:S(2)}) collective-permute-start(f32[64,512]{1,0:T(8,128)S(1)} %collective-permute-done.48.refs_3_), channel_id=1, source_target_pairs={{0,3},{1,2},{2,1},{3,0},{4,7},{5,6},{6,5},{7,4},{8,11},{9,10},{10,... | collective-permute-start | bytes 393224 | tf_op jit(solution)/shard_map/ppermute | solution.py:143
  118.2 11.0 %collective-permute-start.50 = (f32[64,512]{1,0:T(8,128)S(1)}, f32[64,512]{1,0:T(8,128)S(1)}, u32[]{:S(2)}, u32[]{:S(2)}) collective-permute-start(f32[64,512]{1,0:T(8,128)S(1)} %collective-permute-done.48.refs_3_), channel_id=1, source_target_pairs={{0,2},{1,3},{2,0},{3,1},{4,6},{5,7},{6,4},{7,5},{8,10},{9,11},{10,... | collective-permute-start | bytes 393224 | tf_op jit(solution)/shard_map/ppermute | solution.py:143
  126.8 8.7 %collective-permute-start.53 = (f32[64,512]{1,0:T(8,128)S(1)}, f32[64,512]{1,0:T(8,128)S(1)}, u32[]{:S(2)}, u32[]{:S(2)}) collective-permute-start(f32[64,512]{1,0:T(8,128)S(1)} %get-tuple-element.134), channel_id=1, source_target_pairs={{0,2},{1,3},{2,0},{3,1},{4,6},{5,7},{6,4},{7,5},{8,10},{9,11},{10,... | collective-permute-start | bytes 393224 | tf_op jit(solution)/shard_map/ppermute | solution.py:143
  126.8 8.7 %collective-permute-start.54 = (f32[64,512]{1,0:T(8,128)S(1)}, f32[64,512]{1,0:T(8,128)S(1)}, u32[]{:S(2)}, u32[]{:S(2)}) collective-permute-start(f32[64,512]{1,0:T(8,128)S(1)} %get-tuple-element.135), channel_id=1, source_target_pairs={{0,3},{1,2},{2,1},{3,0},{4,7},{5,6},{6,5},{7,4},{8,11},{9,10},{10,... | collective-permute-start | bytes 393224 | tf_op jit(solution)/shard_map/ppermute | solution.py:143
  133.0 9.1 %collective-permute-start.58 = (f32[64,512]{1,0:T(8,128)S(1)}, f32[64,512]{1,0:T(8,128)S(1)}, u32[]{:S(2)}, u32[]{:S(2)}) collective-permute-start(f32[64,512]{1,0:T(8,128)S(1)} %get-tuple-element.139), channel_id=1, source_target_pairs={{0,3},{1,2},{2,1},{3,0},{4,7},{5,6},{6,5},{7,4},{8,11},{9,10},{10,... | collective-permute-start | bytes 393224 | tf_op jit(solution)/shard_map/ppermute | solution.py:143
  (39 other events, 270.7 us)

commit v11 on v8

--- a/solution.py
+++ b/solution.py
@@ -166,13 +166,16 @@
         base = first[0] + 0.005 * (base - 0.05 * first[0])
         term = functools.reduce(jnp.add, arrived(two[4:]))
         flip = strata % 2 if last else 0
-        near = onward(base, 0 if flip else ny) + 0.005 * onward(term, ny if flip else 0)
+        near = onward(base, 0 if flip else ny)
+        late = onward(term, ny if flip else 0)
+        near = near + 0.005 * late
         if last:
             return user_step(users, [one[:4], two[:4]]), near
-        far = onward(base, 0) + 0.005 * onward(term, ny)
         users, base = lax.optimization_barrier((users, base))
         users = user_step(users, [one[:4], two[:4]])
-        first, second = gathered(near), gathered(far)
+        far = over_y(near, ny)
+        first = gathered(near)
+        second = gathered(far)
 
 
 def solution(mesh):

time: 153 us -> 148 us (0.967)
  starting transfers between devices: 73.8 us -> 63.6 us
  waiting for transfers between devices: 42.6 us -> 47.5 us
    ppermute x14 -> x8, starting transfers between devices: 12.6 us -> 0.64 us  [onward(): return lax.ppermute(x, ('group', 'sub'), route)]
    ppermute x49 -> x52, waiting for transfers between devices: 23.8 us -> 32.4 us  [over_y(): return lax.ppermute(x, 'sub', [(i, i ^ r) for i in range(n_sub)])]
    ppermute x14 -> x8, waiting for transfers between devices: 18.8 us -> 15.1 us  [onward(): return lax.ppermute(x, ('group', 'sub'), route)]
    ppermute x49 -> x52, starting transfers between devices: 61.2 us -> 63 us  [over_y(): return lax.ppermute(x, 'sub', [(i, i ^ r) for i in range(n_sub)])]
  transfers between devices with their start and end apart: 63 -> 60, of which waited for: 20 -> 25; matrix products, arithmetic and copies ran while one was open for 0% -> 0% of each run, Pallas kernels for 21% -> 22%
where the time goes in v11:
time: 148 us; the launch traced here: 147 us
  starting transfers between devices  63.6 us (43%)
  waiting for transfers between devices  47.5 us (32%)
  Pallas kernels  32.7 us (22%)
  local copies, waits for them, and re-layouts  1.6 us (1%)
    ppermute x52, starting transfers between devices, over_y(): return lax.ppermute(x, 'sub', [(i, i ^ r) for i in range(n_sub)])  63 us
    ppermute x52, waiting for transfers between devices, over_y(): return lax.ppermute(x, 'sub', [(i, i ^ r) for i in range(n_sub)])  32.4 us
    pallas_call x8, Pallas kernels, gradients(): pl.pallas_call(functools.partial(grad_kernel, ny, place, stratum), in_spe...  21.1 us
    ppermute x8, waiting for transfers between devices, onward(): return lax.ppermute(x, ('group', 'sub'), route)  15.1 us
    pallas_call x4, Pallas kernels, user_step(): pl.pallas_call(functools.partial(step_kernel, len(parts)), in_specs=[VMEM...  8.97 us
  transfers between devices with their start and end apart: 60, of which 25 were waited for; matrix products, arithmetic and copies ran while one was open for 0% of the time, Pallas kernels for 22%

profile of v11, /device:TPU:0, one launch (start us, length us, event | category | flops | bytes accessed | tf_op | source)
XLA Modules:
  0.0 147.5 jit_solution(9044596010523992414)
XLA Ops:
  0.6 4.1 %collective-permute-start.6 = (f32[64,512]{1,0:T(8,128)}, f32[64,512]{1,0:T(8,128)S(1)}, u32[]{:S(2)}, u32[]{:S(2)}) collective-permute-start(f32[64,512]{1,0:T(8,128)} %refs_3_.1), channel_id=1, source_target_pairs={{0,4},{1,5},{2,6},{3,7},{4,0},{5,1},{6,2},{7,3},{8,12},{9,13},{10,... | collective-permute-start | bytes 393224 | tf_op jit(solution)/shard_map/ppermute | solution.py:143
  9.8 2.7 %load.1 = (f32[1024,512]{1,0:T(8,128)S(1)}, bf16[4,512,1024]{2,1,0:T(8,128)(2,1)S(1)}) custom-call(f32[1024,512]{1,0:T(8,128)S(1)} %copy-done, bf16[4,1024,512]{2,1,0:T(8,128)(2,1)} %ratings.1), custom_call_target="tpu_custom_call" | custom-call | bytes 12582912 | tf_op jit(solution)/shard_map/load/pallas_call | solution.py:47
  12.5 2.6 %collective-permute-start.9 = (f32[64,512]{1,0:T(8,128)S(1)}, f32[64,512]{1,0:T(8,128)S(1)}, u32[]{:S(2)}, u32[]{:S(2)}) collective-permute-start(f32[64,512]{1,0:T(8,128)S(1)} %collective-permute-done.6.refs_3_), channel_id=1, source_target_pairs={{0,3},{1,2},{2,1},{3,0},{4,7},{5,6},{6,5},{7,4},{8,11},{9,10},{10,... | collective-permute-start | bytes 393224 | tf_op jit(solution)/shard_map/ppermute | solution.py:143
  16.1 2.6 %gradients.8 = (bf16[256,1024]{1,0:T(8,128)(2,1)S(1)}, bf16[256,1024]{1,0:T(8,128)(2,1)S(1)}, bf16[256,512]{1,0:T(8,128)(2,1)S(1)}, bf16[256,512]{1,0:T(8,128)(2...) custom-call(s32[4,4,8]{2,1,0:T(4,128)S(1)} %bitcast.1, ...), custom_call_target="tpu_custom_call" | custom-call | flops 1610612736 | bytes 2097152 | tf_op jit(solution)/shard_map/gradients/pallas_call | solution.py:97
  22.3 2.6 %gradients.9 = (bf16[256,1024]{1,0:T(8,128)(2,1)S(1)}, bf16[256,1024]{1,0:T(8,128)(2,1)S(1)}, bf16[256,512]{1,0:T(8,128)(2,1)S(1)}, bf16[256,512]{1,0:T(8,128)(2...) custom-call(s32[4,4,8]{2,1,0:T(4,128)S(1)} %bitcast.2, ...), custom_call_target="tpu_custom_call" | custom-call | flops 1610612736 | bytes 2097152 | tf_op jit(solution)/shard_map/gradients/pallas_call | solution.py:97
  31.7 3.8 %collective-permute-done.13 = f32[64,512]{1,0:T(8,128)S(1)} collective-permute-done((f32[64,512]{1,0:T(8,128)S(1)}, f32[64,512]{1,0:T(8,128)S(1)}, u32[]{:S(2)}, u32[]{:S(2)}) %collective-permute-start.13) | collective-permute-done | bytes 131104 | tf_op jit(solution)/shard_map/ppermute | solution.py:143
  35.6 2.8 %collective-permute-done.10 = f32[64,512]{1,0:T(8,128)S(1)} collective-permute-done((f32[64,512]{1,0:T(8,128)S(1)}, f32[64,512]{1,0:T(8,128)S(1)}, u32[]{:S(2)}, u32[]{:S(2)}) %collective-permute-start.10) | collective-permute-done | bytes 131104 | tf_op jit(solution)/shard_map/ppermute | solution.py:150
  40.7 3.4 %collective-permute-start.17 = (f32[64,512]{1,0:T(8,128)S(1)}, f32[64,512]{1,0:T(8,128)S(1)}, u32[]{:S(2)}, u32[]{:S(2)}) collective-permute-start(f32[64,512]{1,0:T(8,128)S(1)} %multiply_add_fusion.6.refs_3_), channel_id=1, source_target_pairs={{0,3},{1,2},{2,1},{3,0},{4,7},{5,6},{6,5},{7,4},{8,11},{9,10},{10,... | collective-permute-start | bytes 393224 | tf_op jit(solution)/shard_map/ppermute | solution.py:143
  51.4 2.6 %gradients.10 = (bf16[256,1024]{1,0:T(8,128)(2,1)S(1)}, bf16[256,1024]{1,0:T(8,128)(2,1)S(1)}, bf16[256,512]{1,0:T(8,128)(2,1)S(1)}, bf16[256,512]{1,0:T(8,128)(...) custom-call(s32[4,4,8]{2,1,0:T(4,128)S(1)} %bitcast.3, ...), custom_call_target="tpu_custom_call" | custom-call | flops 1610612736 | bytes 2097152 | tf_op jit(solution)/shard_map/gradients/pallas_call | solution.py:97
  54.1 2.5 %collective-permute-start.18 = (f32[64,512]{1,0:T(8,128)S(1)}, f32[64,512]{1,0:T(8,128)S(1)}, u32[]{:S(2)}, u32[]{:S(2)}) collective-permute-start(f32[64,512]{1,0:T(8,128)S(1)} %get-tuple-element.91), channel_id=1, source_target_pairs={{0,1},{1,0},{2,3},{3,2},{4,5},{5,4},{6,7},{7,6},{8,9},{9,8},{10,11... | collective-permute-start | bytes 393224 | tf_op jit(solution)/shard_map/ppermute | solution.py:143
  58.4 2.6 %gradients.11 = (bf16[256,1024]{1,0:T(8,128)(2,1)S(1)}, bf16[256,1024]{1,0:T(8,128)(2,1)S(1)}, bf16[256,512]{1,0:T(8,128)(2,1)S(1)}, bf16[256,512]{1,0:T(8,128)(...) custom-call(s32[4,4,8]{2,1,0:T(4,128)S(1)} %bitcast.4, ...), custom_call_target="tpu_custom_call" | custom-call | flops 1610612736 | bytes 2097152 | tf_op jit(solution)/shard_map/gradients/pallas_call | solution.py:97
  64.7 3.0 %collective-permute-done.26 = f32[64,512]{1,0:T(8,128)S(1)} collective-permute-done((f32[64,512]{1,0:T(8,128)S(1)}, f32[64,512]{1,0:T(8,128)S(1)}, u32[]{:S(2)}, u32[]{:S(2)}) %collective-permute-start.26) | collective-permute-done | bytes 131104 | tf_op jit(solution)/shard_map/ppermute | solution.py:143
  71.1 3.5 %collective-permute-done.25 = f32[64,512]{1,0:T(8,128)S(1)} collective-permute-done((f32[64,512]{1,0:T(8,128)S(1)}, f32[64,512]{1,0:T(8,128)S(1)}, u32[]{:S(2)}, u32[]{:S(2)}) %collective-permute-start.25) | collective-permute-done | bytes 131104 | tf_op jit(solution)/shard_map/ppermute | solution.py:150
  75.9 2.7 %collective-permute-start.32 = (f32[64,512]{1,0:T(8,128)S(1)}, f32[64,512]{1,0:T(8,128)S(1)}, u32[]{:S(2)}, u32[]{:S(2)}) collective-permute-start(f32[64,512]{1,0:T(8,128)S(1)} %multiply_add_fusion.4.refs_3_), channel_id=1, source_target_pairs={{0,3},{1,2},{2,1},{3,0},{4,7},{5,6},{6,5},{7,4},{8,11},{9,10},{10,... | collective-permute-start | bytes 393224 | tf_op jit(solution)/shard_map/ppermute | solution.py:143
  84.0 2.6 %collective-permute-start.38 = (f32[64,512]{1,0:T(8,128)S(1)}, f32[64,512]{1,0:T(8,128)S(1)}, u32[]{:S(2)}, u32[]{:S(2)}) collective-permute-start(f32[64,512]{1,0:T(8,128)S(1)} %collective-permute-done.36.refs_3_), channel_id=1, source_target_pairs={{0,2},{1,3},{2,0},{3,1},{4,6},{5,7},{6,4},{7,5},{8,10},{9,11},{10,... | collective-permute-start | bytes 393224 | tf_op jit(solution)/shard_map/ppermute | solution.py:143
  87.1 2.6 %gradients.12 = (bf16[256,1024]{1,0:T(8,128)(2,1)S(1)}, bf16[256,1024]{1,0:T(8,128)(2,1)S(1)}, bf16[256,512]{1,0:T(8,128)(2,1)S(1)}, bf16[256,512]{1,0:T(8,128)(...) custom-call(s32[4,4,8]{2,1,0:T(4,128)S(1)} %bitcast.5, ...), custom_call_target="tpu_custom_call" | custom-call | flops 1610612736 | bytes 2097152 | tf_op jit(solution)/shard_map/gradients/pallas_call | solution.py:97
  93.8 2.6 %gradients.13 = (bf16[256,1024]{1,0:T(8,128)(2,1)S(1)}, bf16[256,1024]{1,0:T(8,128)(2,1)S(1)}, bf16[256,512]{1,0:T(8,128)(2,1)S(1)}, bf16[256,512]{1,0:T(8,128)(...) custom-call(s32[4,4,8]{2,1,0:T(4,128)S(1)} %bitcast.6, ...), custom_call_target="tpu_custom_call" | custom-call | flops 1610612736 | bytes 2097152 | tf_op jit(solution)/shard_map/gradients/pallas_call | solution.py:97
  100.2 2.6 %collective-permute-done.41 = f32[64,512]{1,0:T(8,128)S(1)} collective-permute-done((f32[64,512]{1,0:T(8,128)S(1)}, f32[64,512]{1,0:T(8,128)S(1)}, u32[]{:S(2)}, u32[]{:S(2)}) %collective-permute-start.41) | collective-permute-done | bytes 131104 | tf_op jit(solution)/shard_map/ppermute | solution.py:143
  104.8 2.8 %collective-permute-done.43 = f32[64,512]{1,0:T(8,128)S(1)} collective-permute-done((f32[64,512]{1,0:T(8,128)S(1)}, f32[64,512]{1,0:T(8,128)S(1)}, u32[]{:S(2)}, u32[]{:S(2)}) %collective-permute-start.43) | collective-permute-done | bytes 131104 | tf_op jit(solution)/shard_map/ppermute | solution.py:143
  123.1 2.6 %gradients.14 = (bf16[256,1024]{1,0:T(8,128)(2,1)S(1)}, bf16[256,1024]{1,0:T(8,128)(2,1)S(1)}, bf16[256,512]{1,0:T(8,128)(2,1)S(1)}, bf16[256,512]{1,0:T(8,128)(...) custom-call(s32[4,4,8]{2,1,0:T(4,128)S(1)} %bitcast.7, ...), custom_call_target="tpu_custom_call" | custom-call | flops 1610612736 | bytes 2097152 | tf_op jit(solution)/shard_map/gradients/pallas_call | solution.py:97
  129.3 2.6 %gradients.15 = (bf16[256,1024]{1,0:T(8,128)(2,1)S(1)}, bf16[256,1024]{1,0:T(8,128)(2,1)S(1)}, bf16[256,512]{1,0:T(8,128)(2,1)S(1)}, bf16[256,512]{1,0:T(8,128)(...) custom-call(s32[4,4,8]{2,1,0:T(4,128)S(1)} %bitcast.8, ...), custom_call_target="tpu_custom_call" | custom-call | flops 1610612736 | bytes 2097152 | tf_op jit(solution)/shard_map/gradients/pallas_call | solution.py:97
  135.6 3.0 %collective-permute-done.56 = f32[64,512]{1,0:T(8,128)S(1)} collective-permute-done((f32[64,512]{1,0:T(8,128)S(1)}, f32[64,512]{1,0:T(8,128)S(1)}, u32[]{:S(2)}, u32[]{:S(2)}) %collective-permute-start.56) | collective-permute-done | bytes 131104 | tf_op jit(solution)/shard_map/ppermute | solution.py:143
  138.6 3.2 %collective-permute-done.58 = f32[64,512]{1,0:T(8,128)S(1)} collective-permute-done((f32[64,512]{1,0:T(8,128)S(1)}, f32[64,512]{1,0:T(8,128)S(1)}, u32[]{:S(2)}, u32[]{:S(2)}) %collective-permute-start.58) | collective-permute-done | bytes 131104 | tf_op jit(solution)/shard_map/ppermute | solution.py:143
  141.9 3.2 %user_step.7 = f32[1024,512]{1,0:T(8,128)} custom-call(f32[1024,512]{1,0:T(8,128)S(1)} %user_step.6.refs_1_.refs_0_, bf16[256,1024]{1,0:T(8,128)(2,1)S(1)} %get-tuple-element.124.refs_1_, bf16[256,1024]{1,0:T(8,128)(2,1)S(1)} %get-tuple-element.125.refs_2_, bf16[256,512]{1,0:T(8,128)(2,1)S(1)} %get-tuple-element.126.refs_3_, ...), custom_call_target="tpu_custom_call" | custom-call | flops 1610612736 | bytes 4194304 | tf_op jit(solution)/shard_map/user_step/pallas_call | solution.py:126
  (127 shorter events, 77.1 us)
Async XLA Ops:
  0.6 11.9 %collective-permute-start.6 = (f32[64,512]{1,0:T(8,128)}, f32[64,512]{1,0:T(8,128)S(1)}, u32[]{:S(2)}, u32[]{:S(2)}) collective-permute-start(f32[64,512]{1,0:T(8,128)} %refs_3_.1), channel_id=1, source_target_pairs={{0,4},{1,5},{2,6},{3,7},{4,0},{5,1},{6,2},{7,3},{8,12},{9,13},{10,... | collective-permute-start | bytes 393224 | tf_op jit(solution)/shard_map/ppermute | solution.py:143
  4.7 10.9 %collective-permute-start.2 = (f32[64,512]{1,0:T(8,128)}, f32[64,512]{1,0:T(8,128)S(1)}, u32[]{:S(2)}, u32[]{:S(2)}) collective-permute-start(f32[64,512]{1,0:T(8,128)} %refs_3_.1), channel_id=1, source_target_pairs={{0,3},{1,2},{2,1},{3,0},{4,7},{5,6},{6,5},{7,4},{8,11},{9,10},{10,... | collective-permute-start | bytes 393224 | tf_op jit(solution)/shard_map/ppermute | solution.py:143
  7.3 8.8 %collective-permute-start.1 = (f32[64,512]{1,0:T(8,128)}, f32[64,512]{1,0:T(8,128)S(1)}, u32[]{:S(2)}, u32[]{:S(2)}) collective-permute-start(f32[64,512]{1,0:T(8,128)} %refs_3_.1), channel_id=1, source_target_pairs={{0,2},{1,3},{2,0},{3,1},{4,6},{5,7},{6,4},{7,5},{8,10},{9,11},{10,... | collective-permute-start | bytes 393224 | tf_op jit(solution)/shard_map/ppermute | solution.py:143
  7.7 8.4 %collective-permute-start = (f32[64,512]{1,0:T(8,128)}, f32[64,512]{1,0:T(8,128)S(1)}, u32[]{:S(2)}, u32[]{:S(2)}) collective-permute-start(f32[64,512]{1,0:T(8,128)} %refs_3_.1), channel_id=1, source_target_pairs={{0,1},{1,0},{2,3},{3,2},{4,5},{5,4},{6,7},{7,6},{8,9},{9,8},{10,11... | collective-permute-start | bytes 393224 | tf_op jit(solution)/shard_map/ppermute | solution.py:143
  12.5 9.4 %collective-permute-start.9 = (f32[64,512]{1,0:T(8,128)S(1)}, f32[64,512]{1,0:T(8,128)S(1)}, u32[]{:S(2)}, u32[]{:S(2)}) collective-permute-start(f32[64,512]{1,0:T(8,128)S(1)} %collective-permute-done.6.refs_3_), channel_id=1, source_target_pairs={{0,3},{1,2},{2,1},{3,0},{4,7},{5,6},{6,5},{7,4},{8,11},{9,10},{10,... | collective-permute-start | bytes 393224 | tf_op jit(solution)/shard_map/ppermute | solution.py:143
  18.7 9.4 %collective-permute-start.3 = (f32[64,512]{1,0:T(8,128)S(1)}, f32[64,512]{1,0:T(8,128)S(1)}, u32[]{:S(2)}, u32[]{:S(2)}) collective-permute-start(f32[64,512]{1,0:T(8,128)S(1)} %get-tuple-element.74), channel_id=1, source_target_pairs={{0,1},{1,0},{2,3},{3,2},{4,5},{5,4},{6,7},{7,6},{8,9},{9,8},{10,11... | collective-permute-start | bytes 393224 | tf_op jit(solution)/shard_map/ppermute | solution.py:143
  29.3 9.1 %collective-permute-start.10 = (f32[64,512]{1,0:T(8,128)S(1)}, f32[64,512]{1,0:T(8,128)S(1)}, u32[]{:S(2)}, u32[]{:S(2)}) collective-permute-start(f32[64,512]{1,0:T(8,128)S(1)} %multiply_add_fusion.7), channel_id=1, source_target_pairs={{0,12},{1,13},{2,14},{3,15},{4,8},{5,9},{6,10},{7,11},{8,20},{9,21... | collective-permute-start | bytes 393224 | tf_op jit(solution)/shard_map/ppermute | solution.py:150
  40.7 10.6 %collective-permute-start.17 = (f32[64,512]{1,0:T(8,128)S(1)}, f32[64,512]{1,0:T(8,128)S(1)}, u32[]{:S(2)}, u32[]{:S(2)}) collective-permute-start(f32[64,512]{1,0:T(8,128)S(1)} %multiply_add_fusion.6.refs_3_), channel_id=1, source_target_pairs={{0,3},{1,2},{2,1},{3,0},{4,7},{5,6},{6,5},{7,4},{8,11},{9,10},{10,... | collective-permute-start | bytes 393224 | tf_op jit(solution)/shard_map/ppermute | solution.py:143
  47.8 8.8 %collective-permute-start.24 = (f32[64,512]{1,0:T(8,128)S(1)}, f32[64,512]{1,0:T(8,128)S(1)}, u32[]{:S(2)}, u32[]{:S(2)}) collective-permute-start(f32[64,512]{1,0:T(8,128)S(1)} %collective-permute-done.21.refs_3_), channel_id=1, source_target_pairs={{0,3},{1,2},{2,1},{3,0},{4,7},{5,6},{6,5},{7,4},{8,11},{9,10},{10,... | collective-permute-start | bytes 393224 | tf_op jit(solution)/shard_map/ppermute | solution.py:143
  49.6 8.5 %collective-permute-start.23 = (f32[64,512]{1,0:T(8,128)S(1)}, f32[64,512]{1,0:T(8,128)S(1)}, u32[]{:S(2)}, u32[]{:S(2)}) collective-permute-start(f32[64,512]{1,0:T(8,128)S(1)} %collective-permute-done.21.refs_3_), channel_id=1, source_target_pairs={{0,2},{1,3},{2,0},{3,1},{4,6},{5,7},{6,4},{7,5},{8,10},{9,11},{10,... | collective-permute-start | bytes 393224 | tf_op jit(solution)/shard_map/ppermute | solution.py:143
  54.1 8.8 %collective-permute-start.18 = (f32[64,512]{1,0:T(8,128)S(1)}, f32[64,512]{1,0:T(8,128)S(1)}, u32[]{:S(2)}, u32[]{:S(2)}) collective-permute-start(f32[64,512]{1,0:T(8,128)S(1)} %get-tuple-element.91), channel_id=1, source_target_pairs={{0,1},{1,0},{2,3},{3,2},{4,5},{5,4},{6,7},{7,6},{8,9},{9,8},{10,11... | collective-permute-start | bytes 393224 | tf_op jit(solution)/shard_map/ppermute | solution.py:143
  64.7 9.9 %collective-permute-start.25 = (f32[64,512]{1,0:T(8,128)S(1)}, f32[64,512]{1,0:T(8,128)S(1)}, u32[]{:S(2)}, u32[]{:S(2)}) collective-permute-start(f32[64,512]{1,0:T(8,128)S(1)} %multiply_add_fusion.5), channel_id=1, source_target_pairs={{0,12},{1,13},{2,14},{3,15},{4,8},{5,9},{6,10},{7,11},{8,20},{9,21... | collective-permute-start | bytes 393224 | tf_op jit(solution)/shard_map/ppermute | solution.py:150
  75.9 10.8 %collective-permute-start.32 = (f32[64,512]{1,0:T(8,128)S(1)}, f32[64,512]{1,0:T(8,128)S(1)}, u32[]{:S(2)}, u32[]{:S(2)}) collective-permute-start(f32[64,512]{1,0:T(8,128)S(1)} %multiply_add_fusion.4.refs_3_), channel_id=1, source_target_pairs={{0,3},{1,2},{2,1},{3,0},{4,7},{5,6},{6,5},{7,4},{8,11},{9,10},{10,... | collective-permute-start | bytes 393224 | tf_op jit(solution)/shard_map/ppermute | solution.py:143
  78.5 8.6 %collective-permute-start.31 = (f32[64,512]{1,0:T(8,128)S(1)}, f32[64,512]{1,0:T(8,128)S(1)}, u32[]{:S(2)}, u32[]{:S(2)}) collective-permute-start(f32[64,512]{1,0:T(8,128)S(1)} %multiply_add_fusion.4.refs_3_), channel_id=1, source_target_pairs={{0,2},{1,3},{2,0},{3,1},{4,6},{5,7},{6,4},{7,5},{8,10},{9,11},{10,... | collective-permute-start | bytes 393224 | tf_op jit(solution)/shard_map/ppermute | solution.py:143
  84.0 9.3 %collective-permute-start.38 = (f32[64,512]{1,0:T(8,128)S(1)}, f32[64,512]{1,0:T(8,128)S(1)}, u32[]{:S(2)}, u32[]{:S(2)}) collective-permute-start(f32[64,512]{1,0:T(8,128)S(1)} %collective-permute-done.36.refs_3_), channel_id=1, source_target_pairs={{0,2},{1,3},{2,0},{3,1},{4,6},{5,7},{6,4},{7,5},{8,10},{9,11},{10,... | collective-permute-start | bytes 393224 | tf_op jit(solution)/shard_map/ppermute | solution.py:143
  91.7 8.3 %collective-permute-start.34 = (f32[64,512]{1,0:T(8,128)S(1)}, f32[64,512]{1,0:T(8,128)S(1)}, u32[]{:S(2)}, u32[]{:S(2)}) collective-permute-start(f32[64,512]{1,0:T(8,128)S(1)} %get-tuple-element.109), channel_id=1, source_target_pairs={{0,2},{1,3},{2,0},{3,1},{4,6},{5,7},{6,4},{7,5},{8,10},{9,11},{10,... | collective-permute-start | bytes 393224 | tf_op jit(solution)/shard_map/ppermute | solution.py:143
  97.9 9.7 %collective-permute-start.43 = (f32[64,512]{1,0:T(8,128)S(1)}, f32[64,512]{1,0:T(8,128)S(1)}, u32[]{:S(2)}, u32[]{:S(2)}) collective-permute-start(f32[64,512]{1,0:T(8,128)S(1)} %get-tuple-element.123), channel_id=1, source_target_pairs={{0,3},{1,2},{2,1},{3,0},{4,7},{5,6},{6,5},{7,4},{8,11},{9,10},{10,... | collective-permute-start | bytes 393224 | tf_op jit(solution)/shard_map/ppermute | solution.py:143
  100.1 9.8 %collective-permute-start.40 = (f32[64,512]{1,0:T(8,128)S(1)}, f32[64,512]{1,0:T(8,128)S(1)}, u32[]{:S(2)}, u32[]{:S(2)}) collective-permute-start(f32[64,512]{1,0:T(8,128)S(1)} %multiply_add_fusion.3), channel_id=1, source_target_pairs={{0,12},{1,13},{2,14},{3,15},{4,8},{5,9},{6,10},{7,11},{8,20},{9,21... | collective-permute-start | bytes 393224 | tf_op jit(solution)/shard_map/ppermute | solution.py:150
  112.2 9.1 %collective-permute-start.47 = (f32[64,512]{1,0:T(8,128)S(1)}, f32[64,512]{1,0:T(8,128)S(1)}, u32[]{:S(2)}, u32[]{:S(2)}) collective-permute-start(f32[64,512]{1,0:T(8,128)S(1)} %multiply_add_fusion.2.refs_3_), channel_id=1, source_target_pairs={{0,3},{1,2},{2,1},{3,0},{4,7},{5,6},{6,5},{7,4},{8,11},{9,10},{10,... | collective-permute-start | bytes 393224 | tf_op jit(solution)/shard_map/ppermute | solution.py:143
  114.6 8.5 %collective-permute-start.46 = (f32[64,512]{1,0:T(8,128)S(1)}, f32[64,512]{1,0:T(8,128)S(1)}, u32[]{:S(2)}, u32[]{:S(2)}) collective-permute-start(f32[64,512]{1,0:T(8,128)S(1)} %multiply_add_fusion.2.refs_3_), channel_id=1, source_target_pairs={{0,2},{1,3},{2,0},{3,1},{4,6},{5,7},{6,4},{7,5},{8,10},{9,11},{10,... | collective-permute-start | bytes 393224 | tf_op jit(solution)/shard_map/ppermute | solution.py:143
  114.6 8.5 %collective-permute-start.45 = (f32[64,512]{1,0:T(8,128)S(1)}, f32[64,512]{1,0:T(8,128)S(1)}, u32[]{:S(2)}, u32[]{:S(2)}) collective-permute-start(f32[64,512]{1,0:T(8,128)S(1)} %multiply_add_fusion.2.refs_3_), channel_id=1, source_target_pairs={{0,1},{1,0},{2,3},{3,2},{4,5},{5,4},{6,7},{7,6},{8,9},{9,8},{10,11... | collective-permute-start | bytes 393224 | tf_op jit(solution)/shard_map/ppermute | solution.py:143
  118.9 8.6 %collective-permute-start.51 = (f32[64,512]{1,0:T(8,128)S(1)}, f32[64,512]{1,0:T(8,128)S(1)}, u32[]{:S(2)}, u32[]{:S(2)}) collective-permute-start(f32[64,512]{1,0:T(8,128)S(1)} %collective-permute-done.48.refs_3_), channel_id=1, source_target_pairs={{0,3},{1,2},{2,1},{3,0},{4,7},{5,6},{6,5},{7,4},{8,11},{9,10},{10,... | collective-permute-start | bytes 393224 | tf_op jit(solution)/shard_map/ppermute | solution.py:143
  120.1 9.2 %collective-permute-start.50 = (f32[64,512]{1,0:T(8,128)S(1)}, f32[64,512]{1,0:T(8,128)S(1)}, u32[]{:S(2)}, u32[]{:S(2)}) collective-permute-start(f32[64,512]{1,0:T(8,128)S(1)} %collective-permute-done.48.refs_3_), channel_id=1, source_target_pairs={{0,2},{1,3},{2,0},{3,1},{4,6},{5,7},{6,4},{7,5},{8,10},{9,11},{10,... | collective-permute-start | bytes 393224 | tf_op jit(solution)/shard_map/ppermute | solution.py:143
  135.5 10.4 %collective-permute-start.55 = (f32[64,512]{1,0:T(8,128)S(1)}, f32[64,512]{1,0:T(8,128)S(1)}, u32[]{:S(2)}, u32[]{:S(2)}) collective-permute-start(f32[64,512]{1,0:T(8,128)S(1)} %multiply_add_fusion.1), channel_id=1, source_target_pairs={{0,12},{1,13},{2,14},{3,15},{4,8},{5,9},{6,10},{7,11},{8,20},{9,21... | collective-permute-start | bytes 393224 | tf_op jit(solution)/shard_map/ppermute | solution.py:150
  (39 other events, 267.8 us)

commit v12 on v9

--- a/solution.py
+++ b/solution.py
@@ -68,7 +68,7 @@
     rows, rank = total.shape
     q = pieces[0].shape[0]
     for r in range(ny):
-        block[pl.ds((mine ^ r) * q, q), :] = pieces[r][...]
+        block[pl.ds((mine ^ r) * q, q), :] = pieces[-r % ny][...]
     v_hi[...], v_lo[...] = split(block[...])
     u = split(users[...])
     pred = dot3((v_hi[...], v_lo[...]), u, ((1,), (1,)))
@@ -150,7 +150,7 @@
         return lax.ppermute(x, ("group", "sub"), route)
 
     def gathered(own):
-        return [own] + [over_y(own, r) for r in range(1, ny)]
+        return [own] + [over_y(own, r) for r in range(ny - 1, 0, -1)]
 
     def arrived(terms):
         return [terms[0]] + [over_y(terms[r], r) for r in range(1, ny)]

time: 144 us -> 143 us (level)
  starting transfers between devices: 74.7 us -> 71.2 us
  waiting for transfers between devices: 32.3 us -> 35.1 us
    ppermute x49, waiting for transfers between devices: 22.9 us -> 26.5 us  [over_y(): return lax.ppermute(x, 'sub', [(i, i ^ r) for i in range(n_sub)])]
    ppermute x14, starting transfers between devices: 12.5 us -> 9.78 us  [onward(): return lax.ppermute(x, ('group', 'sub'), route)]
  transfers between devices with their start and end apart: 63 -> 63, of which waited for: 24 -> 23; matrix products, arithmetic and copies ran while one was open for 0% -> 0% of each run, Pallas kernels for 23% -> 23%
where the time goes in v12:
time: 143 us
  starting transfers between devices  71.2 us (50%)
  waiting for transfers between devices  35.1 us (25%)
  Pallas kernels  32.7 us (23%)
  local copies, waits for them, and re-layouts  1.6 us (1%)
    ppermute x49, starting transfers between devices, over_y(): return lax.ppermute(x, 'sub', [(i, i ^ r) for i in range(n_sub)])  61.4 us
    ppermute x49, waiting for transfers between devices, over_y(): return lax.ppermute(x, 'sub', [(i, i ^ r) for i in range(n_sub)])  26.5 us
    pallas_call x8, Pallas kernels, gradients(): pl.pallas_call(functools.partial(grad_kernel, ny, place, stratum), in_spe...  21 us
    ppermute x14, starting transfers between devices, onward(): return lax.ppermute(x, ('group', 'sub'), route)  9.78 us
    pallas_call x4, Pallas kernels, user_step(): pl.pallas_call(functools.partial(step_kernel, len(parts)), in_specs=[VMEM...  8.97 us
    ppermute x14, waiting for transfers between devices, onward(): return lax.ppermute(x, ('group', 'sub'), route)  8.59 us
  transfers between devices with their start and end apart: 63, of which 23 were waited for; matrix products, arithmetic and copies ran while one was open for 0% of the time, Pallas kernels for 23%

profile of v12, /device:TPU:0, one launch (start us, length us, event | category | flops | bytes accessed | tf_op | source)
XLA Modules:
  0.0 142.8 jit_solution(3379691731173482015)
XLA Ops:
  0.6 4.1 %collective-permute-start = (f32[64,512]{1,0:T(8,128)}, f32[64,512]{1,0:T(8,128)S(1)}, u32[]{:S(2)}, u32[]{:S(2)}) collective-permute-start(f32[64,512]{1,0:T(8,128)} %refs_3_.1), channel_id=1, source_target_pairs={{0,4},{1,5},{2,6},{3,7},{4,0},{5,1},{6,2},{7,3},{8,12},{9,13},{10,... | collective-permute-start | bytes 393224 | tf_op jit(solution)/shard_map/ppermute | solution.py:143
  4.7 2.5 %collective-permute-start.7 = (f32[64,512]{1,0:T(8,128)}, f32[64,512]{1,0:T(8,128)S(1)}, u32[]{:S(2)}, u32[]{:S(2)}) collective-permute-start(f32[64,512]{1,0:T(8,128)} %refs_3_.1), channel_id=1, source_target_pairs={{0,3},{1,2},{2,1},{3,0},{4,7},{5,6},{6,5},{7,4},{8,11},{9,10},{10,... | collective-permute-start | bytes 393224 | tf_op jit(solution)/shard_map/ppermute | solution.py:143
  9.8 2.7 %load.1 = (f32[1024,512]{1,0:T(8,128)S(1)}, bf16[4,512,1024]{2,1,0:T(8,128)(2,1)S(1)}) custom-call(f32[1024,512]{1,0:T(8,128)S(1)} %copy-done, bf16[4,1024,512]{2,1,0:T(8,128)(2,1)} %ratings.1), custom_call_target="tpu_custom_call" | custom-call | bytes 12582912 | tf_op jit(solution)/shard_map/load/pallas_call | solution.py:47
  12.5 2.6 %collective-permute-start.1 = (f32[64,512]{1,0:T(8,128)S(1)}, f32[64,512]{1,0:T(8,128)S(1)}, u32[]{:S(2)}, u32[]{:S(2)}) collective-permute-start(f32[64,512]{1,0:T(8,128)S(1)} %collective-permute-done.refs_3_), channel_id=1, source_target_pairs={{0,3},{1,2},{2,1},{3,0},{4,7},{5,6},{6,5},{7,4},{8,11},{9,10},{10,... | collective-permute-start | bytes 393224 | tf_op jit(solution)/shard_map/ppermute | solution.py:143
  16.1 2.6 %gradients.9 = (bf16[256,1024]{1,0:T(8,128)(2,1)S(1)}, bf16[256,1024]{1,0:T(8,128)(2,1)S(1)}, bf16[256,512]{1,0:T(8,128)(2,1)S(1)}, bf16[256,512]{1,0:T(8,128)(2...) custom-call(s32[4,4,8]{2,1,0:T(4,128)S(1)} %bitcast.1, ...), custom_call_target="tpu_custom_call" | custom-call | flops 1610612736 | bytes 2097152 | tf_op jit(solution)/shard_map/gradients/pallas_call | solution.py:97
  18.7 2.6 %collective-permute-start.12 = (f32[64,512]{1,0:T(8,128)S(1)}, f32[64,512]{1,0:T(8,128)S(1)}, u32[]{:S(2)}, u32[]{:S(2)}) collective-permute-start(f32[64,512]{1,0:T(8,128)S(1)} %get-tuple-element.89), channel_id=1, source_target_pairs={{0,3},{1,2},{2,1},{3,0},{4,7},{5,6},{6,5},{7,4},{8,11},{9,10},{10,... | collective-permute-start | bytes 393224 | tf_op jit(solution)/shard_map/ppermute | solution.py:143
  22.3 2.6 %gradients.8 = (bf16[256,1024]{1,0:T(8,128)(2,1)S(1)}, bf16[256,1024]{1,0:T(8,128)(2,1)S(1)}, bf16[256,512]{1,0:T(8,128)(2,1)S(1)}, bf16[256,512]{1,0:T(8,128)(2...) custom-call(s32[4,4,8]{2,1,0:T(4,128)S(1)} %bitcast.2, ...), custom_call_target="tpu_custom_call" | custom-call | flops 1610612736 | bytes 2097152 | tf_op jit(solution)/shard_map/gradients/pallas_call | solution.py:97
  24.9 2.6 %collective-permute-start.6 = (f32[64,512]{1,0:T(8,128)S(1)}, f32[64,512]{1,0:T(8,128)S(1)}, u32[]{:S(2)}, u32[]{:S(2)}) collective-permute-start(f32[64,512]{1,0:T(8,128)S(1)} %get-tuple-element.76), channel_id=1, source_target_pairs={{0,3},{1,2},{2,1},{3,0},{4,7},{5,6},{6,5},{7,4},{8,11},{9,10},{10,... | collective-permute-start | bytes 393224 | tf_op jit(solution)/shard_map/ppermute | solution.py:143
  31.0 3.6 %collective-permute-done.5 = f32[64,512]{1,0:T(8,128)S(1)} collective-permute-done((f32[64,512]{1,0:T(8,128)S(1)}, f32[64,512]{1,0:T(8,128)S(1)}, u32[]{:S(2)}, u32[]{:S(2)}) %collective-permute-start.5) | collective-permute-done | bytes 131104 | tf_op jit(solution)/shard_map/ppermute | solution.py:143
  34.7 2.2 %collective-permute-start.22 = (f32[64,512]{1,0:T(8,128)S(1)}, f32[64,512]{1,0:T(8,128)S(1)}, u32[]{:S(2)}, u32[]{:S(2)}) collective-permute-start(f32[64,512]{1,0:T(8,128)S(1)} %add_add_fusion.3), channel_id=1, source_target_pairs={{0,12},{1,13},{2,14},{3,15},{4,8},{5,9},{6,10},{7,11},{8,20},{9,21... | collective-permute-start | bytes 393224 | tf_op jit(solution)/shard_map/ppermute | solution.py:150
  47.8 2.2 %collective-permute-start.25 = (f32[64,512]{1,0:T(8,128)S(1)}, f32[64,512]{1,0:T(8,128)S(1)}, u32[]{:S(2)}, u32[]{:S(2)}) collective-permute-start(f32[64,512]{1,0:T(8,128)S(1)} %multiply_add_fusion.7.refs_3_), channel_id=1, source_target_pairs={{0,1},{1,0},{2,3},{3,2},{4,5},{5,4},{6,7},{7,6},{8,9},{9,8},{10,11... | collective-permute-start | bytes 393224 | tf_op jit(solution)/shard_map/ppermute | solution.py:143
  51.4 2.6 %gradients.10 = (bf16[256,1024]{1,0:T(8,128)(2,1)S(1)}, bf16[256,1024]{1,0:T(8,128)(2,1)S(1)}, bf16[256,512]{1,0:T(8,128)(2,1)S(1)}, bf16[256,512]{1,0:T(8,128)(...) custom-call(s32[4,4,8]{2,1,0:T(4,128)S(1)} %bitcast.3, ...), custom_call_target="tpu_custom_call" | custom-call | flops 1610612736 | bytes 2097152 | tf_op jit(solution)/shard_map/gradients/pallas_call | solution.py:97
  57.6 2.6 %gradients.11 = (bf16[256,1024]{1,0:T(8,128)(2,1)S(1)}, bf16[256,1024]{1,0:T(8,128)(2,1)S(1)}, bf16[256,512]{1,0:T(8,128)(2,1)S(1)}, bf16[256,512]{1,0:T(8,128)(...) custom-call(s32[4,4,8]{2,1,0:T(4,128)S(1)} %bitcast.4, ...), custom_call_target="tpu_custom_call" | custom-call | flops 1610612736 | bytes 2097152 | tf_op jit(solution)/shard_map/gradients/pallas_call | solution.py:97
  85.0 2.6 %gradients.12 = (bf16[256,1024]{1,0:T(8,128)(2,1)S(1)}, bf16[256,1024]{1,0:T(8,128)(2,1)S(1)}, bf16[256,512]{1,0:T(8,128)(2,1)S(1)}, bf16[256,512]{1,0:T(8,128)(...) custom-call(s32[4,4,8]{2,1,0:T(4,128)S(1)} %bitcast.5, ...), custom_call_target="tpu_custom_call" | custom-call | flops 1610612736 | bytes 2097152 | tf_op jit(solution)/shard_map/gradients/pallas_call | solution.py:97
  91.2 2.6 %gradients.13 = (bf16[256,1024]{1,0:T(8,128)(2,1)S(1)}, bf16[256,1024]{1,0:T(8,128)(2,1)S(1)}, bf16[256,512]{1,0:T(8,128)(2,1)S(1)}, bf16[256,512]{1,0:T(8,128)(...) custom-call(s32[4,4,8]{2,1,0:T(4,128)S(1)} %bitcast.6, ...), custom_call_target="tpu_custom_call" | custom-call | flops 1610612736 | bytes 2097152 | tf_op jit(solution)/shard_map/gradients/pallas_call | solution.py:97
  98.6 2.5 %collective-permute-done.45 = f32[64,512]{1,0:T(8,128)S(1)} collective-permute-done((f32[64,512]{1,0:T(8,128)S(1)}, f32[64,512]{1,0:T(8,128)S(1)}, u32[]{:S(2)}, u32[]{:S(2)}) %collective-permute-start.45) | collective-permute-done | bytes 131104 | tf_op jit(solution)/shard_map/ppermute | solution.py:143
  107.8 2.2 %collective-permute-start.48 = (f32[64,512]{1,0:T(8,128)S(1)}, f32[64,512]{1,0:T(8,128)S(1)}, u32[]{:S(2)}, u32[]{:S(2)}) collective-permute-start(f32[64,512]{1,0:T(8,128)S(1)} %multiply_add_fusion.3.refs_3_), channel_id=1, source_target_pairs={{0,2},{1,3},{2,0},{3,1},{4,6},{5,7},{6,4},{7,5},{8,10},{9,11},{10,... | collective-permute-start | bytes 393224 | tf_op jit(solution)/shard_map/ppermute | solution.py:143
  112.7 2.3 %collective-permute-start.53 = (f32[64,512]{1,0:T(8,128)S(1)}, f32[64,512]{1,0:T(8,128)S(1)}, u32[]{:S(2)}, u32[]{:S(2)}) collective-permute-start(f32[64,512]{1,0:T(8,128)S(1)} %multiply_add_fusion.2.refs_3_), channel_id=1, source_target_pairs={{0,2},{1,3},{2,0},{3,1},{4,6},{5,7},{6,4},{7,5},{8,10},{9,11},{10,... | collective-permute-start | bytes 393224 | tf_op jit(solution)/shard_map/ppermute | solution.py:143
  114.9 2.5 %collective-permute-done.47.refs_4_ = f32[64,512]{1,0:T(8,128)S(1)} collective-permute-done((f32[64,512]{1,0:T(8,128)S(1)}, f32[64,512]{1,0:T(8,128)S(1)}, u32[]{:S(2)}, u32[]{:S(2)}) %collective-permute-start.47) | collective-permute-done | bytes 131104 | tf_op jit(solution)/shard_map/ppermute | solution.py:143
  119.9 2.6 %gradients.14 = (bf16[256,1024]{1,0:T(8,128)(2,1)S(1)}, bf16[256,1024]{1,0:T(8,128)(2,1)S(1)}, bf16[256,512]{1,0:T(8,128)(2,1)S(1)}, bf16[256,512]{1,0:T(8,128)(...) custom-call(s32[4,4,8]{2,1,0:T(4,128)S(1)} %bitcast.7, ...), custom_call_target="tpu_custom_call" | custom-call | flops 1610612736 | bytes 2097152 | tf_op jit(solution)/shard_map/gradients/pallas_call | solution.py:97
  122.6 2.4 %collective-permute-start.56 = (f32[64,512]{1,0:T(8,128)S(1)}, f32[64,512]{1,0:T(8,128)S(1)}, u32[]{:S(2)}, u32[]{:S(2)}) collective-permute-start(f32[64,512]{1,0:T(8,128)S(1)} %get-tuple-element.134), channel_id=1, source_target_pairs={{0,2},{1,3},{2,0},{3,1},{4,6},{5,7},{6,4},{7,5},{8,10},{9,11},{10,... | collective-permute-start | bytes 393224 | tf_op jit(solution)/shard_map/ppermute | solution.py:143
  126.1 2.6 %gradients.15 = (bf16[256,1024]{1,0:T(8,128)(2,1)S(1)}, bf16[256,1024]{1,0:T(8,128)(2,1)S(1)}, bf16[256,512]{1,0:T(8,128)(2,1)S(1)}, bf16[256,512]{1,0:T(8,128)(...) custom-call(s32[4,4,8]{2,1,0:T(4,128)S(1)} %bitcast.8, ...), custom_call_target="tpu_custom_call" | custom-call | flops 1610612736 | bytes 2097152 | tf_op jit(solution)/shard_map/gradients/pallas_call | solution.py:97
  132.4 3.3 %collective-permute-done.61 = f32[64,512]{1,0:T(8,128)S(1)} collective-permute-done((f32[64,512]{1,0:T(8,128)S(1)}, f32[64,512]{1,0:T(8,128)S(1)}, u32[]{:S(2)}, u32[]{:S(2)}) %collective-permute-start.61) | collective-permute-done | bytes 131104 | tf_op jit(solution)/shard_map/ppermute | solution.py:143
  137.7 3.2 %user_step.7 = f32[1024,512]{1,0:T(8,128)} custom-call(f32[1024,512]{1,0:T(8,128)S(1)} %user_step.6.refs_1_.refs_0_, bf16[256,1024]{1,0:T(8,128)(2,1)S(1)} %get-tuple-element.124.refs_1_, bf16[256,1024]{1,0:T(8,128)(2,1)S(1)} %get-tuple-element.125.refs_2_, bf16[256,512]{1,0:T(8,128)(2,1)S(1)} %get-tuple-element.126.refs_3_, ...), custom_call_target="tpu_custom_call" | custom-call | flops 1610612736 | bytes 4194304 | tf_op jit(solution)/shard_map/user_step/pallas_call | solution.py:126
  (136 shorter events, 77.2 us)
Async XLA Ops:
  0.6 11.9 %collective-permute-start = (f32[64,512]{1,0:T(8,128)}, f32[64,512]{1,0:T(8,128)S(1)}, u32[]{:S(2)}, u32[]{:S(2)}) collective-permute-start(f32[64,512]{1,0:T(8,128)} %refs_3_.1), channel_id=1, source_target_pairs={{0,4},{1,5},{2,6},{3,7},{4,0},{5,1},{6,2},{7,3},{8,12},{9,13},{10,... | collective-permute-start | bytes 393224 | tf_op jit(solution)/shard_map/ppermute | solution.py:143
  4.7 10.9 %collective-permute-start.7 = (f32[64,512]{1,0:T(8,128)}, f32[64,512]{1,0:T(8,128)S(1)}, u32[]{:S(2)}, u32[]{:S(2)}) collective-permute-start(f32[64,512]{1,0:T(8,128)} %refs_3_.1), channel_id=1, source_target_pairs={{0,3},{1,2},{2,1},{3,0},{4,7},{5,6},{6,5},{7,4},{8,11},{9,10},{10,... | collective-permute-start | bytes 393224 | tf_op jit(solution)/shard_map/ppermute | solution.py:143
  28.5 10.3 %collective-permute-start.13 = (f32[64,512]{1,0:T(8,128)S(1)}, f32[64,512]{1,0:T(8,128)S(1)}, u32[]{:S(2)}, u32[]{:S(2)}) collective-permute-start(f32[64,512]{1,0:T(8,128)S(1)} %multiply_add_fusion.10), channel_id=1, source_target_pairs={{0,12},{1,13},{2,14},{3,15},{4,8},{5,9},{6,10},{7,11},{8,20},{9,21... | collective-permute-start | bytes 393224 | tf_op jit(solution)/shard_map/ppermute | solution.py:150
  28.6 14.2 %collective-permute-start.21 = (f32[64,512]{1,0:T(8,128)S(1)}, f32[64,512]{1,0:T(8,128)S(1)}, u32[]{:S(2)}, u32[]{:S(2)}) collective-permute-start(f32[64,512]{1,0:T(8,128)S(1)} %multiply_add_fusion.10), channel_id=1, source_target_pairs={{0,8},{1,9},{2,10},{3,11},{4,12},{5,13},{6,14},{7,15},{8,16},{9,17... | collective-permute-start | bytes 393224 | tf_op jit(solution)/shard_map/ppermute | solution.py:150
  34.7 10.1 %collective-permute-start.22 = (f32[64,512]{1,0:T(8,128)S(1)}, f32[64,512]{1,0:T(8,128)S(1)}, u32[]{:S(2)}, u32[]{:S(2)}) collective-permute-start(f32[64,512]{1,0:T(8,128)S(1)} %add_add_fusion.3), channel_id=1, source_target_pairs={{0,12},{1,13},{2,14},{3,15},{4,8},{5,9},{6,10},{7,11},{8,20},{9,21... | collective-permute-start | bytes 393224 | tf_op jit(solution)/shard_map/ppermute | solution.py:150
  40.6 10.8 %collective-permute-start.16 = (f32[64,512]{1,0:T(8,128)S(1)}, f32[64,512]{1,0:T(8,128)S(1)}, u32[]{:S(2)}, u32[]{:S(2)}) collective-permute-start(f32[64,512]{1,0:T(8,128)S(1)} %multiply_add_fusion.9.refs_3_), channel_id=1, source_target_pairs={{0,2},{1,3},{2,0},{3,1},{4,6},{5,7},{6,4},{7,5},{8,10},{9,11},{10,... | collective-permute-start | bytes 393224 | tf_op jit(solution)/shard_map/ppermute | solution.py:143
  41.6 9.8 %collective-permute-start.17 = (f32[64,512]{1,0:T(8,128)S(1)}, f32[64,512]{1,0:T(8,128)S(1)}, u32[]{:S(2)}, u32[]{:S(2)}) collective-permute-start(f32[64,512]{1,0:T(8,128)S(1)} %multiply_add_fusion.9.refs_3_), channel_id=1, source_target_pairs={{0,1},{1,0},{2,3},{3,2},{4,5},{5,4},{6,7},{7,6},{8,9},{9,8},{10,11... | collective-permute-start | bytes 393224 | tf_op jit(solution)/shard_map/ppermute | solution.py:143
  44.8 10.7 %collective-permute-start.23 = (f32[64,512]{1,0:T(8,128)S(1)}, f32[64,512]{1,0:T(8,128)S(1)}, u32[]{:S(2)}, u32[]{:S(2)}) collective-permute-start(f32[64,512]{1,0:T(8,128)S(1)} %multiply_add_fusion.7.refs_3_), channel_id=1, source_target_pairs={{0,3},{1,2},{2,1},{3,0},{4,7},{5,6},{6,5},{7,4},{8,11},{9,10},{10,... | collective-permute-start | bytes 393224 | tf_op jit(solution)/shard_map/ppermute | solution.py:143
  44.9 12.7 %collective-permute-start.24 = (f32[64,512]{1,0:T(8,128)S(1)}, f32[64,512]{1,0:T(8,128)S(1)}, u32[]{:S(2)}, u32[]{:S(2)}) collective-permute-start(f32[64,512]{1,0:T(8,128)S(1)} %multiply_add_fusion.7.refs_3_), channel_id=1, source_target_pairs={{0,2},{1,3},{2,0},{3,1},{4,6},{5,7},{6,4},{7,5},{8,10},{9,11},{10,... | collective-permute-start | bytes 393224 | tf_op jit(solution)/shard_map/ppermute | solution.py:143
  47.8 9.8 %collective-permute-start.25 = (f32[64,512]{1,0:T(8,128)S(1)}, f32[64,512]{1,0:T(8,128)S(1)}, u32[]{:S(2)}, u32[]{:S(2)}) collective-permute-start(f32[64,512]{1,0:T(8,128)S(1)} %multiply_add_fusion.7.refs_3_), channel_id=1, source_target_pairs={{0,1},{1,0},{2,3},{3,2},{4,5},{5,4},{6,7},{7,6},{8,9},{9,8},{10,11... | collective-permute-start | bytes 393224 | tf_op jit(solution)/shard_map/ppermute | solution.py:143
  64.0 14.0 %collective-permute-start.37 = (f32[64,512]{1,0:T(8,128)S(1)}, f32[64,512]{1,0:T(8,128)S(1)}, u32[]{:S(2)}, u32[]{:S(2)}) collective-permute-start(f32[64,512]{1,0:T(8,128)S(1)} %multiply_add_fusion.8), channel_id=1, source_target_pairs={{0,8},{1,9},{2,10},{3,11},{4,12},{5,13},{6,14},{7,15},{8,16},{9,17... | collective-permute-start | bytes 393224 | tf_op jit(solution)/shard_map/ppermute | solution.py:150
  67.7 10.3 %collective-permute-start.38 = (f32[64,512]{1,0:T(8,128)S(1)}, f32[64,512]{1,0:T(8,128)S(1)}, u32[]{:S(2)}, u32[]{:S(2)}) collective-permute-start(f32[64,512]{1,0:T(8,128)S(1)} %add_add_fusion.2), channel_id=1, source_target_pairs={{0,12},{1,13},{2,14},{3,15},{4,8},{5,9},{6,10},{7,11},{8,20},{9,21... | collective-permute-start | bytes 393224 | tf_op jit(solution)/shard_map/ppermute | solution.py:150
  78.0 12.0 %collective-permute-start.39 = (f32[64,512]{1,0:T(8,128)S(1)}, f32[64,512]{1,0:T(8,128)S(1)}, u32[]{:S(2)}, u32[]{:S(2)}) collective-permute-start(f32[64,512]{1,0:T(8,128)S(1)} %multiply_add_fusion.4.refs_3_), channel_id=1, source_target_pairs={{0,3},{1,2},{2,1},{3,0},{4,7},{5,6},{6,5},{7,4},{8,11},{9,10},{10,... | collective-permute-start | bytes 393224 | tf_op jit(solution)/shard_map/ppermute | solution.py:143
  78.6 12.7 %collective-permute-start.40 = (f32[64,512]{1,0:T(8,128)S(1)}, f32[64,512]{1,0:T(8,128)S(1)}, u32[]{:S(2)}, u32[]{:S(2)}) collective-permute-start(f32[64,512]{1,0:T(8,128)S(1)} %multiply_add_fusion.4.refs_3_), channel_id=1, source_target_pairs={{0,2},{1,3},{2,0},{3,1},{4,6},{5,7},{6,4},{7,5},{8,10},{9,11},{10,... | collective-permute-start | bytes 393224 | tf_op jit(solution)/shard_map/ppermute | solution.py:143
  81.6 9.6 %collective-permute-start.41 = (f32[64,512]{1,0:T(8,128)S(1)}, f32[64,512]{1,0:T(8,128)S(1)}, u32[]{:S(2)}, u32[]{:S(2)}) collective-permute-start(f32[64,512]{1,0:T(8,128)S(1)} %multiply_add_fusion.4.refs_3_), channel_id=1, source_target_pairs={{0,1},{1,0},{2,3},{3,2},{4,5},{5,4},{6,7},{7,6},{8,9},{9,8},{10,11... | collective-permute-start | bytes 393224 | tf_op jit(solution)/shard_map/ppermute | solution.py:143
  87.9 9.6 %collective-permute-start.35 = (f32[64,512]{1,0:T(8,128)S(1)}, f32[64,512]{1,0:T(8,128)S(1)}, u32[]{:S(2)}, u32[]{:S(2)}) collective-permute-start(f32[64,512]{1,0:T(8,128)S(1)} %get-tuple-element.109), channel_id=1, source_target_pairs={{0,2},{1,3},{2,0},{3,1},{4,6},{5,7},{6,4},{7,5},{8,10},{9,11},{10,... | collective-permute-start | bytes 393224 | tf_op jit(solution)/shard_map/ppermute | solution.py:143
  97.6 13.7 %collective-permute-start.50 = (f32[64,512]{1,0:T(8,128)S(1)}, f32[64,512]{1,0:T(8,128)S(1)}, u32[]{:S(2)}, u32[]{:S(2)}) collective-permute-start(f32[64,512]{1,0:T(8,128)S(1)} %multiply_add_fusion.5), channel_id=1, source_target_pairs={{0,8},{1,9},{2,10},{3,11},{4,12},{5,13},{6,14},{7,15},{8,16},{9,17... | collective-permute-start | bytes 393224 | tf_op jit(solution)/shard_map/ppermute | solution.py:150
  102.8 9.8 %collective-permute-start.51 = (f32[64,512]{1,0:T(8,128)S(1)}, f32[64,512]{1,0:T(8,128)S(1)}, u32[]{:S(2)}, u32[]{:S(2)}) collective-permute-start(f32[64,512]{1,0:T(8,128)S(1)} %add_add_fusion.1), channel_id=1, source_target_pairs={{0,12},{1,13},{2,14},{3,15},{4,8},{5,9},{6,10},{7,11},{8,20},{9,21... | collective-permute-start | bytes 393224 | tf_op jit(solution)/shard_map/ppermute | solution.py:150
  107.7 9.7 %collective-permute-start.47 = (f32[64,512]{1,0:T(8,128)S(1)}, f32[64,512]{1,0:T(8,128)S(1)}, u32[]{:S(2)}, u32[]{:S(2)}) collective-permute-start(f32[64,512]{1,0:T(8,128)S(1)} %multiply_add_fusion.3.refs_3_), channel_id=1, source_target_pairs={{0,3},{1,2},{2,1},{3,0},{4,7},{5,6},{6,5},{7,4},{8,11},{9,10},{10,... | collective-permute-start | bytes 393224 | tf_op jit(solution)/shard_map/ppermute | solution.py:143
  107.8 12.1 %collective-permute-start.48 = (f32[64,512]{1,0:T(8,128)S(1)}, f32[64,512]{1,0:T(8,128)S(1)}, u32[]{:S(2)}, u32[]{:S(2)}) collective-permute-start(f32[64,512]{1,0:T(8,128)S(1)} %multiply_add_fusion.3.refs_3_), channel_id=1, source_target_pairs={{0,2},{1,3},{2,0},{3,1},{4,6},{5,7},{6,4},{7,5},{8,10},{9,11},{10,... | collective-permute-start | bytes 393224 | tf_op jit(solution)/shard_map/ppermute | solution.py:143
  110.0 9.9 %collective-permute-start.49 = (f32[64,512]{1,0:T(8,128)S(1)}, f32[64,512]{1,0:T(8,128)S(1)}, u32[]{:S(2)}, u32[]{:S(2)}) collective-permute-start(f32[64,512]{1,0:T(8,128)S(1)} %multiply_add_fusion.3.refs_3_), channel_id=1, source_target_pairs={{0,1},{1,0},{2,3},{3,2},{4,5},{5,4},{6,7},{7,6},{8,9},{9,8},{10,11... | collective-permute-start | bytes 393224 | tf_op jit(solution)/shard_map/ppermute | solution.py:143
  112.6 12.4 %collective-permute-start.52 = (f32[64,512]{1,0:T(8,128)S(1)}, f32[64,512]{1,0:T(8,128)S(1)}, u32[]{:S(2)}, u32[]{:S(2)}) collective-permute-start(f32[64,512]{1,0:T(8,128)S(1)} %multiply_add_fusion.2.refs_3_), channel_id=1, source_target_pairs={{0,3},{1,2},{2,1},{3,0},{4,7},{5,6},{6,5},{7,4},{8,11},{9,10},{10,... | collective-permute-start | bytes 393224 | tf_op jit(solution)/shard_map/ppermute | solution.py:143
  112.7 13.4 %collective-permute-start.53 = (f32[64,512]{1,0:T(8,128)S(1)}, f32[64,512]{1,0:T(8,128)S(1)}, u32[]{:S(2)}, u32[]{:S(2)}) collective-permute-start(f32[64,512]{1,0:T(8,128)S(1)} %multiply_add_fusion.2.refs_3_), channel_id=1, source_target_pairs={{0,2},{1,3},{2,0},{3,1},{4,6},{5,7},{6,4},{7,5},{8,10},{9,11},{10,... | collective-permute-start | bytes 393224 | tf_op jit(solution)/shard_map/ppermute | solution.py:143
  122.6 9.7 %collective-permute-start.56 = (f32[64,512]{1,0:T(8,128)S(1)}, f32[64,512]{1,0:T(8,128)S(1)}, u32[]{:S(2)}, u32[]{:S(2)}) collective-permute-start(f32[64,512]{1,0:T(8,128)S(1)} %get-tuple-element.134), channel_id=1, source_target_pairs={{0,2},{1,3},{2,0},{3,1},{4,6},{5,7},{6,4},{7,5},{8,10},{9,11},{10,... | collective-permute-start | bytes 393224 | tf_op jit(solution)/shard_map/ppermute | solution.py:143
  (42 other events, 304.7 us)

commit v13 on v12

--- a/solution.py
+++ b/solution.py
@@ -60,33 +60,30 @@
     occ, users, rate = refs[:3]
     pieces = refs[3:3 + ny]
     err_hi, err_lo, v_hi, v_lo = refs[3 + ny:7 + ny]
-    grads = refs[7 + ny:7 + 2 * ny]
-    block, total = refs[7 + 2 * ny:]
+    grads = refs[7 + ny:]
     k = lax.axis_index("sub")
     mine = k & (ny - 1)
     chunk = (lax.shift_right_logical(k, ny.bit_length() - 1) + (place + stratum)) & 1
-    rows, rank = total.shape
     q = pieces[0].shape[0]
     for r in range(ny):
-        block[pl.ds((mine ^ r) * q, q), :] = pieces[-r % ny][...]
-    v_hi[...], v_lo[...] = split(block[...])
+        at = slice(r * q, r * q + q)
+        v_hi[at, :], v_lo[at, :] = split(pieces[-r % ny][...])
     u = split(users[...])
     pred = dot3((v_hi[...], v_lo[...]), u, ((1,), (1,)))
-    at = pl.ds(pl.multiple_of(chunk * rows, TILE), rows)
-    err = rate[stratum, at, :].astype(F32) - pred
     parts = []
-    for b in range(rows // TILE):
+    for r in range(ny):
+        row = (chunk * ny + (mine ^ r)) * q
+        err = rate[stratum, pl.ds(pl.multiple_of(row, q), q), :].astype(F32) - pred[r * q:r * q + q]
         line = []
         for a in range(err.shape[1] // TILE):
-            seen = occ[stratum, chunk * (rows // TILE) + b, a]
-            part = err[b * TILE:(b + 1) * TILE, a * TILE:(a + 1) * TILE]
-            line.append(jnp.where(seen == 1, part, 0.0))
+            seen = occ[stratum, lax.div(row, TILE), a]
+            line.append(jnp.where(seen == 1, err[:, a * TILE:(a + 1) * TILE], 0.0))
         parts.append(jnp.concatenate(line, axis=1))
     e = split(jnp.concatenate(parts, axis=0))
     err_hi[...], err_lo[...] = e
-    total[...] = dot3(e, u, ((1,), (0,)))
+    term = dot3(e, u, ((1,), (0,)))
     for r in range(ny):
-        grads[r][...] = total[pl.ds((mine ^ r) * q, q), :]
+        grads[r][...] = term[r * q:r * q + q]
 
 
 def gradients(occ, users, ratings, pieces, place, stratum):
@@ -100,7 +97,6 @@
         out_specs=[VMEM] * (4 + ny),
         out_shape=[jax.ShapeDtypeStruct((rows, n_users), BF16)] * 2 + [jax.ShapeDtypeStruct((rows, rank), BF16)] * 2
         + [jax.ShapeDtypeStruct((q, rank), F32)] * ny,
-        scratch_shapes=[pltpu.VMEM((rows, rank), F32)] * 2,
         compiler_params=params(24),
         cost_estimate=pl.CostEstimate(flops=12 * n_users * rows * rank, bytes_accessed=4 * n_users * rank, transcendentals=0),
         name="gradients",

time: 143 us -> 143 us (level)
  waiting for transfers between devices: 35.1 us -> 37.4 us
  starting transfers between devices: 71.2 us -> 69.3 us
    ppermute x14, waiting for transfers between devices: 8.59 us -> 10.9 us  [onward(): return lax.ppermute(x, ('group', 'sub'), route)]
  transfers between devices with their start and end apart: 63 -> 63, of which waited for: 23 -> 26; matrix products, arithmetic and copies ran while one was open for 0% -> 0% of each run, Pallas kernels for 23% -> 23%
where the time goes in v13:
time: 143 us
  starting transfers between devices  69.3 us (48%)
  waiting for transfers between devices  37.4 us (26%)
  Pallas kernels  32.3 us (23%)
  local copies, waits for them, and re-layouts  1.6 us (1%)
    ppermute x49, starting transfers between devices, over_y(): return lax.ppermute(x, 'sub', [(i, i ^ r) for i in range(n_sub)])  60.7 us
    ppermute x49, waiting for transfers between devices, over_y(): return lax.ppermute(x, 'sub', [(i, i ^ r) for i in range(n_sub)])  26.4 us
    pallas_call x8, Pallas kernels, gradients(): pl.pallas_call(functools.partial(grad_kernel, ny, place, stratum), in_spe...  20.7 us
    ppermute x14, waiting for transfers between devices, onward(): return lax.ppermute(x, ('group', 'sub'), route)  10.9 us
    pallas_call x4, Pallas kernels, user_step(): pl.pallas_call(functools.partial(step_kernel, len(parts)), in_specs=[VMEM...  8.96 us
    ppermute x14, starting transfers between devices, onward(): return lax.ppermute(x, ('group', 'sub'), route)  8.52 us
  transfers between devices with their start and end apart: 63, of which 26 were waited for; matrix products, arithmetic and copies ran while one was open for 0% of the time, Pallas kernels for 23%

profile of v13, /device:TPU:0, one launch (start us, length us, event | category | flops | bytes accessed | tf_op | source)
XLA Modules:
  0.0 142.7 jit_solution(11455446856502946942)
XLA Ops:
  0.6 4.1 %collective-permute-start = (f32[64,512]{1,0:T(8,128)}, f32[64,512]{1,0:T(8,128)S(1)}, u32[]{:S(2)}, u32[]{:S(2)}) collective-permute-start(f32[64,512]{1,0:T(8,128)} %refs_3_.1), channel_id=1, source_target_pairs={{0,4},{1,5},{2,6},{3,7},{4,0},{5,1},{6,2},{7,3},{8,12},{9,13},{10,... | collective-permute-start | bytes 393224 | tf_op jit(solution)/shard_map/ppermute | solution.py:139
  4.7 2.5 %collective-permute-start.7 = (f32[64,512]{1,0:T(8,128)}, f32[64,512]{1,0:T(8,128)S(1)}, u32[]{:S(2)}, u32[]{:S(2)}) collective-permute-start(f32[64,512]{1,0:T(8,128)} %refs_3_.1), channel_id=1, source_target_pairs={{0,3},{1,2},{2,1},{3,0},{4,7},{5,6},{6,5},{7,4},{8,11},{9,10},{10,... | collective-permute-start | bytes 393224 | tf_op jit(solution)/shard_map/ppermute | solution.py:139
  9.8 2.7 %load.1 = (f32[1024,512]{1,0:T(8,128)S(1)}, bf16[4,512,1024]{2,1,0:T(8,128)(2,1)S(1)}) custom-call(f32[1024,512]{1,0:T(8,128)S(1)} %copy-done, bf16[4,1024,512]{2,1,0:T(8,128)(2,1)} %ratings.1), custom_call_target="tpu_custom_call" | custom-call | bytes 12582912 | tf_op jit(solution)/shard_map/load/pallas_call | solution.py:47
  12.5 2.6 %collective-permute-start.1 = (f32[64,512]{1,0:T(8,128)S(1)}, f32[64,512]{1,0:T(8,128)S(1)}, u32[]{:S(2)}, u32[]{:S(2)}) collective-permute-start(f32[64,512]{1,0:T(8,128)S(1)} %collective-permute-done.refs_3_), channel_id=1, source_target_pairs={{0,3},{1,2},{2,1},{3,0},{4,7},{5,6},{6,5},{7,4},{8,11},{9,10},{10,... | collective-permute-start | bytes 393224 | tf_op jit(solution)/shard_map/ppermute | solution.py:139
  16.1 2.6 %gradients.9 = (bf16[256,1024]{1,0:T(8,128)(2,1)S(1)}, bf16[256,1024]{1,0:T(8,128)(2,1)S(1)}, bf16[256,512]{1,0:T(8,128)(2,1)S(1)}, bf16[256,512]{1,0:T(8,128)(2...) custom-call(s32[4,4,8]{2,1,0:T(4,128)S(1)} %bitcast.1, ...), custom_call_target="tpu_custom_call" | custom-call | flops 1610612736 | bytes 2097152 | tf_op jit(solution)/shard_map/gradients/pallas_call | solution.py:94
  18.7 2.6 %collective-permute-start.12 = (f32[64,512]{1,0:T(8,128)S(1)}, f32[64,512]{1,0:T(8,128)S(1)}, u32[]{:S(2)}, u32[]{:S(2)}) collective-permute-start(f32[64,512]{1,0:T(8,128)S(1)} %get-tuple-element.89), channel_id=1, source_target_pairs={{0,3},{1,2},{2,1},{3,0},{4,7},{5,6},{6,5},{7,4},{8,11},{9,10},{10,... | collective-permute-start | bytes 393224 | tf_op jit(solution)/shard_map/ppermute | solution.py:139
  22.2 2.5 %gradients.8 = (bf16[256,1024]{1,0:T(8,128)(2,1)S(1)}, bf16[256,1024]{1,0:T(8,128)(2,1)S(1)}, bf16[256,512]{1,0:T(8,128)(2,1)S(1)}, bf16[256,512]{1,0:T(8,128)(2...) custom-call(s32[4,4,8]{2,1,0:T(4,128)S(1)} %bitcast.2, ...), custom_call_target="tpu_custom_call" | custom-call | flops 1610612736 | bytes 2097152 | tf_op jit(solution)/shard_map/gradients/pallas_call | solution.py:94
  24.8 2.6 %collective-permute-start.6 = (f32[64,512]{1,0:T(8,128)S(1)}, f32[64,512]{1,0:T(8,128)S(1)}, u32[]{:S(2)}, u32[]{:S(2)}) collective-permute-start(f32[64,512]{1,0:T(8,128)S(1)} %get-tuple-element.76), channel_id=1, source_target_pairs={{0,3},{1,2},{2,1},{3,0},{4,7},{5,6},{6,5},{7,4},{8,11},{9,10},{10,... | collective-permute-start | bytes 393224 | tf_op jit(solution)/shard_map/ppermute | solution.py:139
  30.9 3.6 %collective-permute-done.5 = f32[64,512]{1,0:T(8,128)S(1)} collective-permute-done((f32[64,512]{1,0:T(8,128)S(1)}, f32[64,512]{1,0:T(8,128)S(1)}, u32[]{:S(2)}, u32[]{:S(2)}) %collective-permute-start.5) | collective-permute-done | bytes 131104 | tf_op jit(solution)/shard_map/ppermute | solution.py:139
  34.5 2.2 %collective-permute-start.22 = (f32[64,512]{1,0:T(8,128)S(1)}, f32[64,512]{1,0:T(8,128)S(1)}, u32[]{:S(2)}, u32[]{:S(2)}) collective-permute-start(f32[64,512]{1,0:T(8,128)S(1)} %add_add_fusion.3), channel_id=1, source_target_pairs={{0,12},{1,13},{2,14},{3,15},{4,8},{5,9},{6,10},{7,11},{8,20},{9,21... | collective-permute-start | bytes 393224 | tf_op jit(solution)/shard_map/ppermute | solution.py:146
  51.3 2.6 %gradients.10 = (bf16[256,1024]{1,0:T(8,128)(2,1)S(1)}, bf16[256,1024]{1,0:T(8,128)(2,1)S(1)}, bf16[256,512]{1,0:T(8,128)(2,1)S(1)}, bf16[256,512]{1,0:T(8,128)(...) custom-call(s32[4,4,8]{2,1,0:T(4,128)S(1)} %bitcast.3, ...), custom_call_target="tpu_custom_call" | custom-call | flops 1610612736 | bytes 2097152 | tf_op jit(solution)/shard_map/gradients/pallas_call | solution.py:94
  57.5 2.6 %gradients.11 = (bf16[256,1024]{1,0:T(8,128)(2,1)S(1)}, bf16[256,1024]{1,0:T(8,128)(2,1)S(1)}, bf16[256,512]{1,0:T(8,128)(2,1)S(1)}, bf16[256,512]{1,0:T(8,128)(...) custom-call(s32[4,4,8]{2,1,0:T(4,128)S(1)} %bitcast.4, ...), custom_call_target="tpu_custom_call" | custom-call | flops 1610612736 | bytes 2097152 | tf_op jit(solution)/shard_map/gradients/pallas_call | solution.py:94
  78.3 2.2 %collective-permute-start.40 = (f32[64,512]{1,0:T(8,128)S(1)}, f32[64,512]{1,0:T(8,128)S(1)}, u32[]{:S(2)}, u32[]{:S(2)}) collective-permute-start(f32[64,512]{1,0:T(8,128)S(1)} %multiply_add_fusion.4.refs_3_), channel_id=1, source_target_pairs={{0,2},{1,3},{2,0},{3,1},{4,6},{5,7},{6,4},{7,5},{8,10},{9,11},{10,... | collective-permute-start | bytes 393224 | tf_op jit(solution)/shard_map/ppermute | solution.py:139
  84.8 2.6 %gradients.12 = (bf16[256,1024]{1,0:T(8,128)(2,1)S(1)}, bf16[256,1024]{1,0:T(8,128)(2,1)S(1)}, bf16[256,512]{1,0:T(8,128)(2,1)S(1)}, bf16[256,512]{1,0:T(8,128)(...) custom-call(s32[4,4,8]{2,1,0:T(4,128)S(1)} %bitcast.5, ...), custom_call_target="tpu_custom_call" | custom-call | flops 1610612736 | bytes 2097152 | tf_op jit(solution)/shard_map/gradients/pallas_call | solution.py:94
  91.0 2.6 %gradients.13 = (bf16[256,1024]{1,0:T(8,128)(2,1)S(1)}, bf16[256,1024]{1,0:T(8,128)(2,1)S(1)}, bf16[256,512]{1,0:T(8,128)(2,1)S(1)}, bf16[256,512]{1,0:T(8,128)(...) custom-call(s32[4,4,8]{2,1,0:T(4,128)S(1)} %bitcast.6, ...), custom_call_target="tpu_custom_call" | custom-call | flops 1610612736 | bytes 2097152 | tf_op jit(solution)/shard_map/gradients/pallas_call | solution.py:94
  98.3 2.5 %collective-permute-done.45 = f32[64,512]{1,0:T(8,128)S(1)} collective-permute-done((f32[64,512]{1,0:T(8,128)S(1)}, f32[64,512]{1,0:T(8,128)S(1)}, u32[]{:S(2)}, u32[]{:S(2)}) %collective-permute-start.45) | collective-permute-done | bytes 131104 | tf_op jit(solution)/shard_map/ppermute | solution.py:139
  107.5 2.2 %collective-permute-start.48 = (f32[64,512]{1,0:T(8,128)S(1)}, f32[64,512]{1,0:T(8,128)S(1)}, u32[]{:S(2)}, u32[]{:S(2)}) collective-permute-start(f32[64,512]{1,0:T(8,128)S(1)} %multiply_add_fusion.3.refs_3_), channel_id=1, source_target_pairs={{0,2},{1,3},{2,0},{3,1},{4,6},{5,7},{6,4},{7,5},{8,10},{9,11},{10,... | collective-permute-start | bytes 393224 | tf_op jit(solution)/shard_map/ppermute | solution.py:139
  112.4 2.2 %collective-permute-start.53 = (f32[64,512]{1,0:T(8,128)S(1)}, f32[64,512]{1,0:T(8,128)S(1)}, u32[]{:S(2)}, u32[]{:S(2)}) collective-permute-start(f32[64,512]{1,0:T(8,128)S(1)} %multiply_add_fusion.2.refs_3_), channel_id=1, source_target_pairs={{0,2},{1,3},{2,0},{3,1},{4,6},{5,7},{6,4},{7,5},{8,10},{9,11},{10,... | collective-permute-start | bytes 393224 | tf_op jit(solution)/shard_map/ppermute | solution.py:139
  114.6 2.9 %collective-permute-done.47.refs_4_ = f32[64,512]{1,0:T(8,128)S(1)} collective-permute-done((f32[64,512]{1,0:T(8,128)S(1)}, f32[64,512]{1,0:T(8,128)S(1)}, u32[]{:S(2)}, u32[]{:S(2)}) %collective-permute-start.47) | collective-permute-done | bytes 131104 | tf_op jit(solution)/shard_map/ppermute | solution.py:139
  119.6 2.6 %gradients.14 = (bf16[256,1024]{1,0:T(8,128)(2,1)S(1)}, bf16[256,1024]{1,0:T(8,128)(2,1)S(1)}, bf16[256,512]{1,0:T(8,128)(2,1)S(1)}, bf16[256,512]{1,0:T(8,128)(...) custom-call(s32[4,4,8]{2,1,0:T(4,128)S(1)} %bitcast.7, ...), custom_call_target="tpu_custom_call" | custom-call | flops 1610612736 | bytes 2097152 | tf_op jit(solution)/shard_map/gradients/pallas_call | solution.py:94
  122.5 2.5 %collective-permute-start.56 = (f32[64,512]{1,0:T(8,128)S(1)}, f32[64,512]{1,0:T(8,128)S(1)}, u32[]{:S(2)}, u32[]{:S(2)}) collective-permute-start(f32[64,512]{1,0:T(8,128)S(1)} %get-tuple-element.134), channel_id=1, source_target_pairs={{0,2},{1,3},{2,0},{3,1},{4,6},{5,7},{6,4},{7,5},{8,10},{9,11},{10,... | collective-permute-start | bytes 393224 | tf_op jit(solution)/shard_map/ppermute | solution.py:139
  125.7 2.6 %gradients.15 = (bf16[256,1024]{1,0:T(8,128)(2,1)S(1)}, bf16[256,1024]{1,0:T(8,128)(2,1)S(1)}, bf16[256,512]{1,0:T(8,128)(2,1)S(1)}, bf16[256,512]{1,0:T(8,128)(...) custom-call(s32[4,4,8]{2,1,0:T(4,128)S(1)} %bitcast.8, ...), custom_call_target="tpu_custom_call" | custom-call | flops 1610612736 | bytes 2097152 | tf_op jit(solution)/shard_map/gradients/pallas_call | solution.py:94
  132.0 2.9 %collective-permute-done.61 = f32[64,512]{1,0:T(8,128)S(1)} collective-permute-done((f32[64,512]{1,0:T(8,128)S(1)}, f32[64,512]{1,0:T(8,128)S(1)}, u32[]{:S(2)}, u32[]{:S(2)}) %collective-permute-start.61) | collective-permute-done | bytes 131104 | tf_op jit(solution)/shard_map/ppermute | solution.py:139
  136.5 3.2 %user_step.7 = f32[1024,512]{1,0:T(8,128)} custom-call(f32[1024,512]{1,0:T(8,128)S(1)} %user_step.6.refs_1_.refs_0_, bf16[256,1024]{1,0:T(8,128)(2,1)S(1)} %get-tuple-element.124.refs_1_, bf16[256,1024]{1,0:T(8,128)(2,1)S(1)} %get-tuple-element.125.refs_2_, bf16[256,512]{1,0:T(8,128)(2,1)S(1)} %get-tuple-element.126.refs_3_, ...), custom_call_target="tpu_custom_call" | custom-call | flops 1610612736 | bytes 4194304 | tf_op jit(solution)/shard_map/user_step/pallas_call | solution.py:122
  (136 shorter events, 77.4 us)
Async XLA Ops:
  0.6 11.9 %collective-permute-start = (f32[64,512]{1,0:T(8,128)}, f32[64,512]{1,0:T(8,128)S(1)}, u32[]{:S(2)}, u32[]{:S(2)}) collective-permute-start(f32[64,512]{1,0:T(8,128)} %refs_3_.1), channel_id=1, source_target_pairs={{0,4},{1,5},{2,6},{3,7},{4,0},{5,1},{6,2},{7,3},{8,12},{9,13},{10,... | collective-permute-start | bytes 393224 | tf_op jit(solution)/shard_map/ppermute | solution.py:139
  4.7 10.9 %collective-permute-start.7 = (f32[64,512]{1,0:T(8,128)}, f32[64,512]{1,0:T(8,128)S(1)}, u32[]{:S(2)}, u32[]{:S(2)}) collective-permute-start(f32[64,512]{1,0:T(8,128)} %refs_3_.1), channel_id=1, source_target_pairs={{0,3},{1,2},{2,1},{3,0},{4,7},{5,6},{6,5},{7,4},{8,11},{9,10},{10,... | collective-permute-start | bytes 393224 | tf_op jit(solution)/shard_map/ppermute | solution.py:139
  28.4 10.3 %collective-permute-start.13 = (f32[64,512]{1,0:T(8,128)S(1)}, f32[64,512]{1,0:T(8,128)S(1)}, u32[]{:S(2)}, u32[]{:S(2)}) collective-permute-start(f32[64,512]{1,0:T(8,128)S(1)} %multiply_add_fusion.10), channel_id=1, source_target_pairs={{0,12},{1,13},{2,14},{3,15},{4,8},{5,9},{6,10},{7,11},{8,20},{9,21... | collective-permute-start | bytes 393224 | tf_op jit(solution)/shard_map/ppermute | solution.py:146
  28.5 14.2 %collective-permute-start.21 = (f32[64,512]{1,0:T(8,128)S(1)}, f32[64,512]{1,0:T(8,128)S(1)}, u32[]{:S(2)}, u32[]{:S(2)}) collective-permute-start(f32[64,512]{1,0:T(8,128)S(1)} %multiply_add_fusion.10), channel_id=1, source_target_pairs={{0,8},{1,9},{2,10},{3,11},{4,12},{5,13},{6,14},{7,15},{8,16},{9,17... | collective-permute-start | bytes 393224 | tf_op jit(solution)/shard_map/ppermute | solution.py:146
  34.5 10.0 %collective-permute-start.22 = (f32[64,512]{1,0:T(8,128)S(1)}, f32[64,512]{1,0:T(8,128)S(1)}, u32[]{:S(2)}, u32[]{:S(2)}) collective-permute-start(f32[64,512]{1,0:T(8,128)S(1)} %add_add_fusion.3), channel_id=1, source_target_pairs={{0,12},{1,13},{2,14},{3,15},{4,8},{5,9},{6,10},{7,11},{8,20},{9,21... | collective-permute-start | bytes 393224 | tf_op jit(solution)/shard_map/ppermute | solution.py:146
  40.6 10.7 %collective-permute-start.16 = (f32[64,512]{1,0:T(8,128)S(1)}, f32[64,512]{1,0:T(8,128)S(1)}, u32[]{:S(2)}, u32[]{:S(2)}) collective-permute-start(f32[64,512]{1,0:T(8,128)S(1)} %multiply_add_fusion.9.refs_3_), channel_id=1, source_target_pairs={{0,2},{1,3},{2,0},{3,1},{4,6},{5,7},{6,4},{7,5},{8,10},{9,11},{10,... | collective-permute-start | bytes 393224 | tf_op jit(solution)/shard_map/ppermute | solution.py:139
  41.7 9.6 %collective-permute-start.17 = (f32[64,512]{1,0:T(8,128)S(1)}, f32[64,512]{1,0:T(8,128)S(1)}, u32[]{:S(2)}, u32[]{:S(2)}) collective-permute-start(f32[64,512]{1,0:T(8,128)S(1)} %multiply_add_fusion.9.refs_3_), channel_id=1, source_target_pairs={{0,1},{1,0},{2,3},{3,2},{4,5},{5,4},{6,7},{7,6},{8,9},{9,8},{10,11... | collective-permute-start | bytes 393224 | tf_op jit(solution)/shard_map/ppermute | solution.py:139
  44.6 10.7 %collective-permute-start.23 = (f32[64,512]{1,0:T(8,128)S(1)}, f32[64,512]{1,0:T(8,128)S(1)}, u32[]{:S(2)}, u32[]{:S(2)}) collective-permute-start(f32[64,512]{1,0:T(8,128)S(1)} %multiply_add_fusion.7.refs_3_), channel_id=1, source_target_pairs={{0,3},{1,2},{2,1},{3,0},{4,7},{5,6},{6,5},{7,4},{8,11},{9,10},{10,... | collective-permute-start | bytes 393224 | tf_op jit(solution)/shard_map/ppermute | solution.py:139
  44.7 12.8 %collective-permute-start.24 = (f32[64,512]{1,0:T(8,128)S(1)}, f32[64,512]{1,0:T(8,128)S(1)}, u32[]{:S(2)}, u32[]{:S(2)}) collective-permute-start(f32[64,512]{1,0:T(8,128)S(1)} %multiply_add_fusion.7.refs_3_), channel_id=1, source_target_pairs={{0,2},{1,3},{2,0},{3,1},{4,6},{5,7},{6,4},{7,5},{8,10},{9,11},{10,... | collective-permute-start | bytes 393224 | tf_op jit(solution)/shard_map/ppermute | solution.py:139
  47.8 9.6 %collective-permute-start.25 = (f32[64,512]{1,0:T(8,128)S(1)}, f32[64,512]{1,0:T(8,128)S(1)}, u32[]{:S(2)}, u32[]{:S(2)}) collective-permute-start(f32[64,512]{1,0:T(8,128)S(1)} %multiply_add_fusion.7.refs_3_), channel_id=1, source_target_pairs={{0,1},{1,0},{2,3},{3,2},{4,5},{5,4},{6,7},{7,6},{8,9},{9,8},{10,11... | collective-permute-start | bytes 393224 | tf_op jit(solution)/shard_map/ppermute | solution.py:139
  63.8 14.1 %collective-permute-start.37 = (f32[64,512]{1,0:T(8,128)S(1)}, f32[64,512]{1,0:T(8,128)S(1)}, u32[]{:S(2)}, u32[]{:S(2)}) collective-permute-start(f32[64,512]{1,0:T(8,128)S(1)} %multiply_add_fusion.8), channel_id=1, source_target_pairs={{0,8},{1,9},{2,10},{3,11},{4,12},{5,13},{6,14},{7,15},{8,16},{9,17... | collective-permute-start | bytes 393224 | tf_op jit(solution)/shard_map/ppermute | solution.py:146
  67.7 10.2 %collective-permute-start.38 = (f32[64,512]{1,0:T(8,128)S(1)}, f32[64,512]{1,0:T(8,128)S(1)}, u32[]{:S(2)}, u32[]{:S(2)}) collective-permute-start(f32[64,512]{1,0:T(8,128)S(1)} %add_add_fusion.2), channel_id=1, source_target_pairs={{0,12},{1,13},{2,14},{3,15},{4,8},{5,9},{6,10},{7,11},{8,20},{9,21... | collective-permute-start | bytes 393224 | tf_op jit(solution)/shard_map/ppermute | solution.py:146
  74.6 9.5 %collective-permute-start.32 = (f32[64,512]{1,0:T(8,128)S(1)}, f32[64,512]{1,0:T(8,128)S(1)}, u32[]{:S(2)}, u32[]{:S(2)}) collective-permute-start(f32[64,512]{1,0:T(8,128)S(1)} %multiply_add_fusion.6.refs_3_), channel_id=1, source_target_pairs={{0,2},{1,3},{2,0},{3,1},{4,6},{5,7},{6,4},{7,5},{8,10},{9,11},{10,... | collective-permute-start | bytes 393224 | tf_op jit(solution)/shard_map/ppermute | solution.py:139
  77.9 11.8 %collective-permute-start.39 = (f32[64,512]{1,0:T(8,128)S(1)}, f32[64,512]{1,0:T(8,128)S(1)}, u32[]{:S(2)}, u32[]{:S(2)}) collective-permute-start(f32[64,512]{1,0:T(8,128)S(1)} %multiply_add_fusion.4.refs_3_), channel_id=1, source_target_pairs={{0,3},{1,2},{2,1},{3,0},{4,7},{5,6},{6,5},{7,4},{8,11},{9,10},{10,... | collective-permute-start | bytes 393224 | tf_op jit(solution)/shard_map/ppermute | solution.py:139
  78.3 12.7 %collective-permute-start.40 = (f32[64,512]{1,0:T(8,128)S(1)}, f32[64,512]{1,0:T(8,128)S(1)}, u32[]{:S(2)}, u32[]{:S(2)}) collective-permute-start(f32[64,512]{1,0:T(8,128)S(1)} %multiply_add_fusion.4.refs_3_), channel_id=1, source_target_pairs={{0,2},{1,3},{2,0},{3,1},{4,6},{5,7},{6,4},{7,5},{8,10},{9,11},{10,... | collective-permute-start | bytes 393224 | tf_op jit(solution)/shard_map/ppermute | solution.py:139
  81.5 9.5 %collective-permute-start.41 = (f32[64,512]{1,0:T(8,128)S(1)}, f32[64,512]{1,0:T(8,128)S(1)}, u32[]{:S(2)}, u32[]{:S(2)}) collective-permute-start(f32[64,512]{1,0:T(8,128)S(1)} %multiply_add_fusion.4.refs_3_), channel_id=1, source_target_pairs={{0,1},{1,0},{2,3},{3,2},{4,5},{5,4},{6,7},{7,6},{8,9},{9,8},{10,11... | collective-permute-start | bytes 393224 | tf_op jit(solution)/shard_map/ppermute | solution.py:139
  87.6 9.5 %collective-permute-start.35 = (f32[64,512]{1,0:T(8,128)S(1)}, f32[64,512]{1,0:T(8,128)S(1)}, u32[]{:S(2)}, u32[]{:S(2)}) collective-permute-start(f32[64,512]{1,0:T(8,128)S(1)} %get-tuple-element.109), channel_id=1, source_target_pairs={{0,2},{1,3},{2,0},{3,1},{4,6},{5,7},{6,4},{7,5},{8,10},{9,11},{10,... | collective-permute-start | bytes 393224 | tf_op jit(solution)/shard_map/ppermute | solution.py:139
  97.3 13.7 %collective-permute-start.50 = (f32[64,512]{1,0:T(8,128)S(1)}, f32[64,512]{1,0:T(8,128)S(1)}, u32[]{:S(2)}, u32[]{:S(2)}) collective-permute-start(f32[64,512]{1,0:T(8,128)S(1)} %multiply_add_fusion.5), channel_id=1, source_target_pairs={{0,8},{1,9},{2,10},{3,11},{4,12},{5,13},{6,14},{7,15},{8,16},{9,17... | collective-permute-start | bytes 393224 | tf_op jit(solution)/shard_map/ppermute | solution.py:146
  102.4 9.9 %collective-permute-start.51 = (f32[64,512]{1,0:T(8,128)S(1)}, f32[64,512]{1,0:T(8,128)S(1)}, u32[]{:S(2)}, u32[]{:S(2)}) collective-permute-start(f32[64,512]{1,0:T(8,128)S(1)} %add_add_fusion.1), channel_id=1, source_target_pairs={{0,12},{1,13},{2,14},{3,15},{4,8},{5,9},{6,10},{7,11},{8,20},{9,21... | collective-permute-start | bytes 393224 | tf_op jit(solution)/shard_map/ppermute | solution.py:146
  107.4 10.1 %collective-permute-start.47 = (f32[64,512]{1,0:T(8,128)S(1)}, f32[64,512]{1,0:T(8,128)S(1)}, u32[]{:S(2)}, u32[]{:S(2)}) collective-permute-start(f32[64,512]{1,0:T(8,128)S(1)} %multiply_add_fusion.3.refs_3_), channel_id=1, source_target_pairs={{0,3},{1,2},{2,1},{3,0},{4,7},{5,6},{6,5},{7,4},{8,11},{9,10},{10,... | collective-permute-start | bytes 393224 | tf_op jit(solution)/shard_map/ppermute | solution.py:139
  107.5 12.1 %collective-permute-start.48 = (f32[64,512]{1,0:T(8,128)S(1)}, f32[64,512]{1,0:T(8,128)S(1)}, u32[]{:S(2)}, u32[]{:S(2)}) collective-permute-start(f32[64,512]{1,0:T(8,128)S(1)} %multiply_add_fusion.3.refs_3_), channel_id=1, source_target_pairs={{0,2},{1,3},{2,0},{3,1},{4,6},{5,7},{6,4},{7,5},{8,10},{9,11},{10,... | collective-permute-start | bytes 393224 | tf_op jit(solution)/shard_map/ppermute | solution.py:139
  109.7 9.8 %collective-permute-start.49 = (f32[64,512]{1,0:T(8,128)S(1)}, f32[64,512]{1,0:T(8,128)S(1)}, u32[]{:S(2)}, u32[]{:S(2)}) collective-permute-start(f32[64,512]{1,0:T(8,128)S(1)} %multiply_add_fusion.3.refs_3_), channel_id=1, source_target_pairs={{0,1},{1,0},{2,3},{3,2},{4,5},{5,4},{6,7},{7,6},{8,9},{9,8},{10,11... | collective-permute-start | bytes 393224 | tf_op jit(solution)/shard_map/ppermute | solution.py:139
  112.3 12.7 %collective-permute-start.52 = (f32[64,512]{1,0:T(8,128)S(1)}, f32[64,512]{1,0:T(8,128)S(1)}, u32[]{:S(2)}, u32[]{:S(2)}) collective-permute-start(f32[64,512]{1,0:T(8,128)S(1)} %multiply_add_fusion.2.refs_3_), channel_id=1, source_target_pairs={{0,3},{1,2},{2,1},{3,0},{4,7},{5,6},{6,5},{7,4},{8,11},{9,10},{10,... | collective-permute-start | bytes 393224 | tf_op jit(solution)/shard_map/ppermute | solution.py:139
  112.4 13.3 %collective-permute-start.53 = (f32[64,512]{1,0:T(8,128)S(1)}, f32[64,512]{1,0:T(8,128)S(1)}, u32[]{:S(2)}, u32[]{:S(2)}) collective-permute-start(f32[64,512]{1,0:T(8,128)S(1)} %multiply_add_fusion.2.refs_3_), channel_id=1, source_target_pairs={{0,2},{1,3},{2,0},{3,1},{4,6},{5,7},{6,4},{7,5},{8,10},{9,11},{10,... | collective-permute-start | bytes 393224 | tf_op jit(solution)/shard_map/ppermute | solution.py:139
  (42 other events, 302.1 us)
